TPU v7x, 32 devices: a whole 2x2x4 slice. The times are simulated.
32 devices in a mesh: groups: 2 (over y), row: 4 (over z), col: 4 (over x, core).
Axes of the slice: x: 2, y: 2, z: 4, core: 2. Of those that a mesh axis runs over, the one named last changes fastest.
Arguments:
- acq_data: bfloat16 [12288, 4, 3072], P(('groups', 'row', 'col')), parts along dimension 0, may hold values from -6 to 6
- grid_row: int32 [12288], P(('groups', 'row', 'col')), parts along dimension 0, may hold values from 0 to 3071, as said below
- counts: int32 [32], P(('groups', 'row', 'col')), parts along dimension 0, may hold values from 0 to 384, as said below
Outputs:
- multiples: bfloat16 [4, 4, 3072, 3072], P('groups', None, 'row', 'col'), parts along dimension 0
There are 2 independent parts, one for each index of `groups`. A program takes and returns all parts, laid end to end along the dimension named above; each array names one. Nothing has to cross between parts.
Inputs may be any that keep to these rules, and one draw needn't show every extreme that they name: Over the live slots of all owners grid_row takes every value from 0 to 3071 exactly once; entries of slots that are not live are arbitrary values in the range. Of one owner's live slots at most 96 fall into one block of 768 consecutive grid rows; in each block exactly 4 owners have 96 there, and one owner has 96 in every block. The counts add up to 3072; the largest equals 384. `acq_data`: rows of slots that are not live carry no meaning.
All inputs are finite; a program needn't handle non-finite values.
Results may differ from a plain program's by a relative error of at most 0.004.
Values may be sent and summed in bfloat16 or wider, within the bound.
No kernel may reach another device: no remote copies, remote signals or barrier semaphores. Data moves between devices by JAX's collectives and lax.ppermute only.
A program may use at most 192 MiB of HBM per device.

v0:
```python
import math

import jax
import jax.numpy as jnp
from jax import lax
from jax.sharding import PartitionSpec as P

NS = 3072
ORDERS = 2


def complex_product(left_side, right_side):
    freq_count = left_side.shape[0] // 2
    row_count = left_side.shape[1]
    inner_depth = left_side.shape[2]
    split_left = left_side.reshape(freq_count, 2, row_count, inner_depth)
    real_row = jnp.concatenate([split_left[:, 0], -split_left[:, 1]], axis=2)
    imag_row = jnp.concatenate([split_left[:, 1], split_left[:, 0]], axis=2)
    stacked_left = jnp.stack([real_row, imag_row], axis=1)
    stacked_right = right_side.reshape(freq_count, 2 * inner_depth, right_side.shape[2])
    result = jnp.einsum(
        "fpmk,fkn->fpmn", stacked_left, stacked_right, preferred_element_type=jnp.float32
    )
    return result.reshape(2 * freq_count, row_count, right_side.shape[2])


def gather_rows(current):
    return lax.all_gather(current, "col", axis=2, tiled=True)


def bin_tiles(acq_data, grid_row, counts):
    n_row = lax.axis_size("row")
    n_col = lax.axis_size("col")
    own_cap, planes, matrix_order = acq_data.shape
    block_rows = matrix_order // n_row
    tile_cols = matrix_order // n_col
    block_cap = own_cap // n_row
    slot_index = jnp.arange(own_cap, dtype=jnp.int32)
    live_slot = slot_index < counts[0]
    target_block = jnp.where(live_slot, grid_row // block_rows, n_row)
    block_hits = (target_block[:, None] == jnp.arange(n_row, dtype=jnp.int32)[None, :]).astype(
        jnp.int32
    )
    block_rank = jnp.sum((jnp.cumsum(block_hits, axis=0) - block_hits) * block_hits, axis=1)
    picked = (
        jnp.full((n_row, block_cap), own_cap, jnp.int32)
        .at[target_block, block_rank]
        .set(slot_index, mode="drop")
    )
    target_spots = (
        jnp.full((n_row, block_cap), block_rows, jnp.int32)
        .at[target_block, block_rank]
        .set(grid_row % block_rows, mode="drop")
    )
    padded = jnp.concatenate(
        [acq_data, jnp.zeros((1, planes, matrix_order), acq_data.dtype)], axis=0
    )
    outgoing = padded[picked]
    pieces = (
        outgoing.reshape(n_row, block_cap, planes, n_col, tile_cols)
        .transpose(0, 3, 1, 2, 4)
        .reshape(n_row * n_col, block_cap, planes, tile_cols)
    )
    labels = jnp.broadcast_to(target_spots[:, None, :], (n_row, n_col, block_cap)).reshape(
        n_row * n_col, block_cap
    )
    received, places = (
        lax.all_to_all(pieces, ("row", "col"), split_axis=0, concat_axis=0, tiled=True),
        lax.all_to_all(labels, ("row", "col"), split_axis=0, concat_axis=0, tiled=True),
    )
    received = received.reshape(-1, planes, tile_cols)
    places = places.reshape(-1)
    source = (
        jnp.zeros((block_rows,), jnp.int32)
        .at[places]
        .set(jnp.arange(places.shape[0], dtype=jnp.int32), mode="drop")
    )
    return jnp.transpose(received[source], (1, 0, 2))


def per_device(acq_data, grid_row, counts):
    data_tile = bin_tiles(acq_data, grid_row, counts)
    weight = 1.0 / math.sqrt(2.0 * NS)
    results = []
    current = data_tile
    column_panel = lax.all_gather(data_tile, "row", axis=1, tiled=True)
    for order_index in range(ORDERS):
        current = (complex_product(gather_rows(current), column_panel) * weight).astype(
            jnp.bfloat16
        )
        results.append(current)
    return jnp.stack(results, axis=0)


def solution(mesh):
    placed = (
        P(("groups", "row", "col"), None, None),
        P(("groups", "row", "col")),
        P(("groups", "row", "col")),
    )
    return jax.shard_map(
        per_device,
        mesh=mesh,
        in_specs=placed,
        out_specs=P("groups", None, "row", "col"),
        check_vma=False,
    )
```

profile of v0, /device:TPU:0, one launch (start us, length us, event | category | flops | bytes accessed | tf_op | source)
XLA Modules:
  0.0 1067.8 jit_solution(3954581518839253936)
XLA Ops:
  9.7 18.3 %scatter_fusion.1 = s32[4,96]{1,0:T(4,128)S(1)} fusion(s32[4,96]{1,0:T(4,128)S(1)} %broadcast_in_dim.36, s32[384]{0:T(512)S(1)} %fusion.22, s32[384]{0:T(512)S(1)} %get-tuple-element.19), kind=kCustom, calls=%fused_computation.3 | custom fusion | bytes 7680 | tf_op jit(solution)/shard_map/scatter | solution.py:53
  28.5 7.4 all-to-all-start.1
  35.9 18.3 %scatter_fusion = s32[4,96]{1,0:T(4,128)S(1)} fusion(s32[4,96]{1,0:T(4,128)S(1)} %broadcast_in_dim.16, s32[384]{0:T(512)S(1)} %fusion.22, s32[384]{0:T(512)S(1)} %iota.17), kind=kCustom, calls=%fused_computation.2 | custom fusion | bytes 7680 | tf_op jit(solution)/shard_map/scatter | solution.py:48
  54.3 8.8 concatenate.22
  63.1 20.3 %gather_fusion = bf16[384,4,3072]{2,1,0:T(4,128)(2,1)} fusion(bf16[385,4,3072]{2,1,0:T(4,128)(2,1)} %concatenate.22, s32[1024]{0:T(1024)S(1)} %pad_clamp_fusion.1), kind=kCustom, calls=%fused_computation | custom fusion | bytes 18875904 | tf_op jit(solution)/shard_map/gather | solution.py:58
  83.4 6.1 fusion.28
  89.5 37.9 %pad_maximum_fusion = bf16[4,384,4,768]{3,2,1,0:T(4,128)(2,1)} fusion(bf16[4,96,4,768]{3,2,1,0:T(4,128)(2,1)S(1)} %get-tuple-element.18, bf16[4,96,4,768]{3,2,1,0:T(4,128)(2,1)S(1)} %get-tuple-element.16, bf16[4,96,4,768]{3,2,1,0:T(4,128)(2,1)S(1)} %get-tuple-element.17, bf16[4,96,4,768]{3,2,1,0:T(4,128)(2,1)S(1)} %get-tuple-element.15), kind=kLoop, calls=%fused_computation.21 | loop fusion | flops 14155776 | bytes 18874368 | tf_op jit(solution)/shard_map/concatenate
  135.0 6.2 scatter_custom_fusion.2
  141.2 161.1 %all-to-all-done = bf16[16,96,4,768]{3,2,1,0:T(4,128)(2,1)} async-done(((bf16[16,96,4,768]{3,2,1,0:T(4,128)(2,1)}), bf16[16,96,4,768]{3,2,1,0:T(4,128)(2,1)}, u32[]{:S(2)}, u32[]{:S(2)}) %all-to-all-start) | async-done | bytes 9437216 | tf_op jit(solution)/shard_map/all_to_all | solution.py:68
  302.3 11.7 %gather_fusion.1 = bf16[768,4,768]{2,1,0:T(4,128)(2,1)} fusion(bf16[1536,4,768]{2,1,0:T(4,128)(2,1)} %bitcast.5, s32[1024]{0:T(1024)S(1)} %pad_clamp_fusion), kind=kCustom, calls=%fused_computation.1 | custom fusion | bytes 9440256 | tf_op jit(solution)/shard_map/gather | solution.py:78
  314.8 155.3 %all-gather.4.cloned.1.call-done = bf16[4,768,3072]{2,0,1:T(4,128)(2,1)} async-done(((bf16[4,768,768]{2,0,1:T(4,128)(2,1)}), bf16[4,768,3072]{2,0,1:T(4,128)(2,1)}) %all-gather.4.cloned.1.call-update) | async-done | bytes 18874384 | tf_op jit(solution)/shard_map/all_gather | solution.py:28
  470.1 21.1 %copy.14 = bf16[4,768,3072]{2,1,0:T(8,128)(2,1)} copy(bf16[4,768,3072]{2,0,1:T(4,128)(2,1)} %all-gather.4.cloned.1.call-done) | data formatting | bytes 37748736 | tf_op jit(solution)/shard_map/all_gather | solution.py:28
  491.2 8.4 fusion.25
  499.6 14.1 %slice_bitcast_fusion.2 = (bf16[2,768,3072]{2,1,0:T(8,128)(2,1)}, bf16[2,768,3072]{2,1,0:T(8,128)(2,1)}) fusion(bf16[2,2,768,3072]{3,2,1,0:T(8,128)(2,1)} %bitcast.75), kind=kLoop, calls=%fused_computation.19 | loop fusion | bytes 37748736 | tf_op jit(solution)/shard_map/squeeze | solution.py:17
  513.7 25.5 %maximum_bitcast_fusion = (bf16[2,1,768,6144]{3,2,1,0:T(8,128)(2,1)}, bf16[2,1,768,6144]{3,2,1,0:T(8,128)(2,1)}) fusion(bf16[2,768,3072]{2,1,0:T(8,128)(2,1)} %fusion.25, bf16[2,768,3072]{2,1,0:T(8,128)(2,1)} %get-tuple-element.10, bf16[2,768,3072]{2,1,0:T(8,128)(2,1)} %get-tuple-element.9), kind=kLoop, calls=%fused_computation.13 | loop fusion | flops 75497472 | bytes 66060288 | tf_op jit(solution)/shard_map/stack | solution.py:19
  539.2 255.1 %all-gather.6.cloned.1.call-done = bf16[4,3072,768]{2,0,1:T(4,128)(2,1)} async-done(((bf16[4,768,768]{2,0,1:T(4,128)(2,1)}), bf16[4,3072,768]{2,0,1:T(4,128)(2,1)}) %all-gather.6.cloned.1.call-update) | async-done | bytes 18874384 | tf_op jit(solution)/shard_map/all_gather | solution.py:86
  794.3 18.2 %copy.18 = bf16[4,3072,768]{2,1,0:T(8,128)(2,1)} copy(bf16[4,3072,768]{2,0,1:T(4,128)(2,1)} %all-gather.6.cloned.1.call-done) | data formatting | bytes 37748736 | tf_op jit(solution)/shard_map/all_gather | solution.py:86
  812.5 37.4 %multiply_convert_fusion.1 = bf16[2,2,768,768]{3,2,1,0:T(8,128)(2,1)} fusion(bf16[2,6144,768,1]{2,1,3,0:T(8,128)(2,1)} %bitcast.82, bf16[2,1,768,6144]{3,2,1,0:T(8,128)(2,1)} %get-tuple-element.14, bf16[2,1,768,6144]{3,2,1,0:T(8,128)(2,1)} %get-tuple-element.13), kind=kOutput, calls=%fused_computation.24 | convolution fusion | flops 29014622208 | bytes 61341696 | tf_op jit(solution)/shard_map/fpmk,fkn->fpmn/dot_general | solution.py:21
  849.9 119.0 %all-gather.8.cloned.1.call-done = bf16[4,768,3072]{2,1,0:T(8,128)(2,1)} async-done(((bf16[4,768,768]{2,1,0:T(8,128)(2,1)}), bf16[4,768,3072]{2,1,0:T(8,128)(2,1)}) %all-gather.8.cloned.1.call-update) | async-done | bytes 18874384 | tf_op jit(solution)/shard_map/all_gather | solution.py:28
  968.9 8.0 fusion.26
  976.9 14.1 %slice_bitcast_fusion = (bf16[2,768,3072]{2,1,0:T(8,128)(2,1)}, bf16[2,768,3072]{2,1,0:T(8,128)(2,1)}) fusion(bf16[2,2,768,3072]{3,2,1,0:T(8,128)(2,1)} %bitcast.77), kind=kLoop, calls=%fused_computation.17 | loop fusion | bytes 37748736 | tf_op jit(solution)/shard_map/squeeze | solution.py:17
  991.0 24.3 %maximum_bitcast_fusion.2 = (bf16[2,1,768,6144]{3,2,1,0:T(8,128)(2,1)}, bf16[2,1,768,6144]{3,2,1,0:T(8,128)(2,1)}) fusion(bf16[2,768,3072]{2,1,0:T(8,128)(2,1)} %fusion.26, bf16[2,768,3072]{2,1,0:T(8,128)(2,1)} %get-tuple-element.8, bf16[2,768,3072]{2,1,0:T(8,128)(2,1)} %get-tuple-element.7), kind=kLoop, calls=%fused_computation.15 | loop fusion | flops 75497472 | bytes 66060288 | tf_op jit(solution)/shard_map/stack | solution.py:19
  1015.3 37.6 %multiply_convert_fusion = bf16[2,2,768,768]{3,2,1,0:T(8,128)(2,1)} fusion(bf16[2,6144,768,1]{2,1,3,0:T(8,128)(2,1)} %bitcast.83, bf16[2,1,768,6144]{3,2,1,0:T(8,128)(2,1)} %get-tuple-element.12, bf16[2,1,768,6144]{3,2,1,0:T(8,128)(2,1)} %get-tuple-element.11), kind=kOutput, calls=%fused_computation.23 | convolution fusion | flops 29014622208 | bytes 61341696 | tf_op jit(solution)/shard_map/fpmk,fkn->fpmn/dot_general | solution.py:21
  1052.9 8.4 pad_maximum_fusion.1
  (30 shorter events, 11.6 us)
Async XLA Ops:
  28.5 98.8 %all-to-all-start.1 = ((s32[16,1,96]{2,1,0:T(1,128)}), s32[16,1,96]{2,1,0:T(1,128)S(1)}, u32[]{:S(2)}, u32[]{:S(2)}) async-start(s32[16,1,96]{2,1,0:T(1,128)} %bitcast.6), calls=%async_computation.1 | async-start | bytes 16384 | tf_op jit(solution)/shard_map/all_to_all | solution.py:69
  127.3 174.9 %all-to-all-start = ((bf16[16,96,4,768]{3,2,1,0:T(4,128)(2,1)}), bf16[16,96,4,768]{3,2,1,0:T(4,128)(2,1)}, u32[]{:S(2)}, u32[]{:S(2)}) async-start(bf16[16,96,4,768]{3,2,1,0:T(4,128)(2,1)} %bitcast.80), calls=%async_computation | async-start | bytes 18874368 | tf_op jit(solution)/shard_map/all_to_all | solution.py:68
  133.3 336.8 %all-gather.4.cloned.1.call-start = ((), (), s32[]{:S(2)}) async-start(), calls=%async_computation.2 | async-start | bytes 23592960 | tf_op jit(solution)/shard_map/all_gather | solution.py:28
  314.0 480.3 %all-gather.6.cloned.1.call-start = ((), (), s32[]{:S(2)}) async-start(), calls=%async_computation.3 | async-start | bytes 23592960 | tf_op jit(solution)/shard_map/all_gather | solution.py:86
  314.7 654.2 %all-gather.8.cloned.1.call-start = ((), (), s32[]{:S(2)}) async-start(), calls=%async_computation.4 | async-start | bytes 23592960 | tf_op jit(solution)/shard_map/all_gather | solution.py:28
Sparse Core Ops, SparseCore 0:
  314.1 155.9 all-gather.3
  471.7 322.5 all-gather.5
  850.0 118.8 all-gather.7
where the time goes:
time: 1070 us
  waiting for transfers between devices  691 us (65%)
  local copies, waits for them, and re-layouts  159 us (15%)
  other arithmetic  115 us (11%)
  matrix products  75 us (7%)
  between operations  13.9 us (1%)
  starting transfers between devices  13.6 us (1%)
    all_gather x2, waiting for transfers between devices, gather_rows(): return lax.all_gather(current, 'col', axis=2, tiled=True)  274 us
    all_gather x1, waiting for transfers between devices, per_device(): column_panel = lax.all_gather(data_tile, 'row', axis=1, tiled=True)  255 us
    all_to_all x1, waiting for transfers between devices, bin_tiles(): lax.all_to_all(pieces, ('row', 'col'), split_axis=0, concat_axis=0, tiled...  161 us
    dot_general x2, matrix products, complex_product(): jnp.einsum('fpmk,fkn->fpmn', stacked_left, stacked_right, preferred_eleme...  75 us
    another operation x2, other arithmetic, complex_product(): stacked_left = jnp.stack([real_row, imag_row], axis=1)  49.8 us
    concatenate x1, other arithmetic  37.9 us
    squeeze x2, local copies, waits for them, and re-layouts, complex_product(): real_row = jnp.concatenate([split_left[:, 0], -split_left[:, 1]], axis=2)  28.2 us
  transfers between devices with their start and end apart: 5, of which 4 were waited for; matrix products, arithmetic and copies ran while one was open for 16% of the time, Pallas kernels for 0%

commit v1 on v0

v1 whole, which is shorter than its diff:
```python
import functools
import math

import jax
import jax.numpy as jnp
from jax import lax
from jax.experimental import pallas as pl
from jax.experimental.pallas import tpu as pltpu
from jax.sharding import PartitionSpec as P

NS = 3072
ORDERS = 2
FREQ = 2
THIRDS = 3
BF16 = jnp.bfloat16
F32 = jnp.float32


def bits_of(n_col):
    bit_list = []
    bit = n_col // 2
    while bit:
        bit_list.append(bit)
        bit //= 2
    return bit_list


def gather_cols(piece, n_col):
    held = {0: piece}
    for bit in bits_of(n_col):
        pairs = [(c, c ^ bit) for c in range(n_col)]
        arrived = {d ^ bit: lax.ppermute(a, "col", pairs) for d, a in held.items()}
        held.update(arrived)
    return held


def product_kernel(depths, weight, offs, *refs):
    count = len(depths)
    lefts, right, out = refs[:count], refs[count], refs[count + 1]
    width = right.shape[1] // 2
    rows = out.shape[0]
    by_real = jnp.zeros((rows, 2 * width), F32)
    by_imag = jnp.zeros((rows, 2 * width), F32)
    for i, depth in enumerate(depths):
        start = pl.multiple_of(offs[i], 128)
        block = right[pl.ds(start, depth), :]
        by_real += jnp.dot(lefts[i][:, :depth], block, preferred_element_type=F32)
        by_imag += jnp.dot(lefts[i][:, depth:], block, preferred_element_type=F32)
    real = by_real[:, :width] - by_imag[:, width:]
    imag = by_real[:, width:] + by_imag[:, :width]
    out[:, :width] = (real * weight).astype(BF16)
    out[:, width:] = (imag * weight).astype(BF16)


def complex_product(offs, lefts, right, weight):
    rows = lefts[0].shape[0]
    tile = 256 if rows % 256 == 0 else rows
    depths = [a.shape[1] // 2 for a in lefts]
    wide = right.shape[1]
    spec = pltpu.PrefetchScalarGridSpec(
        num_scalar_prefetch=1,
        grid=(rows // tile,),
        in_specs=[pl.BlockSpec((tile, a.shape[1]), lambda i, s: (i, 0)) for a in lefts]
        + [pl.BlockSpec(right.shape, lambda i, s: (0, 0))],
        out_specs=pl.BlockSpec((tile, wide), lambda i, s: (i, 0)),
    )
    return pl.pallas_call(
        functools.partial(product_kernel, depths, weight),
        grid_spec=spec,
        out_shape=jax.ShapeDtypeStruct((rows, wide), BF16),
        compiler_params=pltpu.CompilerParams(vmem_limit_bytes=40 * 2**20),
        cost_estimate=pl.CostEstimate(
            flops=4 * rows * NS * wide, bytes_accessed=2 * NS * (wide + 2 * rows), transcendentals=0
        ),
    )(offs, *lefts, right)


def per_device(acq_data, grid_row, counts):
    n_row = lax.axis_size("row")
    n_col = lax.axis_size("col")
    own_cap, planes, order = acq_data.shape
    block_rows = order // n_row
    tile_cols = order // n_col
    cap = own_cap // n_row
    slots = n_row * cap
    sub = tile_cols // THIRDS
    weight = 1.0 / math.sqrt(2.0 * NS)
    me = lax.axis_index("col")

    slot_index = jnp.arange(own_cap, dtype=jnp.int32)
    block = jnp.where(slot_index < counts[0], grid_row // block_rows, n_row)
    earlier = (block[None, :] == block[:, None]) & (slot_index[None, :] < slot_index[:, None])
    rank = jnp.sum(earlier.astype(jnp.int32), axis=1)
    leaving = jnp.where(block < n_row, block * cap + rank, -1)
    hit = jnp.arange(slots, dtype=jnp.int32)[:, None] == leaving[None, :]
    spots = jnp.sum(jnp.where(hit, (grid_row % block_rows)[None, :] + 1, 0), axis=1) - 1
    labels = jnp.broadcast_to(spots.reshape(n_row, 1, cap), (n_row, n_col, cap))
    places = lax.all_to_all(
        labels.reshape(n_row * n_col, cap), ("row", "col"), split_axis=0, concat_axis=0, tiled=True
    ).reshape(-1)
    picker = hit.astype(BF16)
    placer = (jnp.arange(block_rows, dtype=jnp.int32)[:, None] == places[None, :]).astype(BF16)

    tiles = []
    for f in range(FREQ):
        raw = acq_data[:, 2 * f : 2 * f + 2, :].reshape(own_cap, 2 * order)
        sent = jnp.dot(picker, raw, preferred_element_type=F32).astype(BF16)
        sent = sent.reshape(n_row, cap, 2, n_col, tile_cols).transpose(0, 3, 1, 2, 4)
        sent = sent.reshape(n_row * n_col, cap, 2 * tile_cols)
        got = lax.all_to_all(sent, ("row", "col"), split_axis=0, concat_axis=0, tiled=True)
        tile = jnp.dot(placer, got.reshape(-1, 2 * tile_cols), preferred_element_type=F32)
        tiles.append(tile.astype(BF16))

    rights = []
    for f in range(FREQ):
        rights.append([])
        for j in range(THIRDS):
            real = tiles[f][:, j * sub : (j + 1) * sub]
            imag = tiles[f][:, tile_cols + j * sub : tile_cols + (j + 1) * sub]
            rights[f].append(
                lax.all_gather(jnp.concatenate([real, imag], axis=1), "row", axis=0, tiled=True)
            )

    keys = list(range(n_col))
    tile_offs = jnp.stack([(me ^ d) * tile_cols for d in keys])
    sub_offs = jnp.stack([(me ^ d) * tile_cols + j * sub for j in range(THIRDS) for d in keys])
    outs = [[], []]
    for f in range(FREQ):
        held = gather_cols(tiles[f], n_col)
        lefts = [held[d] for d in keys]
        first = []
        gathered = []
        for j in range(THIRDS):
            piece = complex_product(tile_offs, lefts, rights[f][j], weight)
            first.append(piece)
            held = gather_cols(piece, n_col)
            gathered += [held[d] for d in keys]
        second = [complex_product(sub_offs, gathered, rights[f][j], weight) for j in range(THIRDS)]
        for k, pieces in enumerate((first, second)):
            outs[k].append(jnp.concatenate([p[:, :sub] for p in pieces], axis=1))
            outs[k].append(jnp.concatenate([p[:, sub:] for p in pieces], axis=1))
    return jnp.stack([jnp.stack(o, axis=0) for o in outs], axis=0)


def solution(mesh):
    placed = (
        P(("groups", "row", "col"), None, None),
        P(("groups", "row", "col")),
        P(("groups", "row", "col")),
    )
    return jax.shard_map(
        per_device,
        mesh=mesh,
        in_specs=placed,
        out_specs=P("groups", None, "row", "col"),
        check_vma=False,
    )
```

time: 1070 us -> 785 us (0.73)
  waiting for transfers between devices: 691 us -> 432 us
  Pallas kernels: 0 us -> 91.6 us
  other arithmetic: 115 us -> 23.9 us
  matrix products: 75 us -> 27.5 us
  starting transfers between devices: 13.6 us -> 59.1 us
  local copies, waits for them, and re-layouts: 159 us -> 127 us
    all_gather x3 -> x6, waiting for transfers between devices: 529 us -> 78.2 us  [per_device(): lax.all_gather(jnp.concatenate([real, imag], axis=1), 'row', axis=0, tile...]
    ppermute x0 -> x24, waiting for transfers between devices: none -> 134 us  [gather_cols(): arrived = {d ^ bit: lax.ppermute(a, 'col', pairs) for d, a in held.items()}]
    pallas_call x0 -> x12, Pallas kernels: none -> 91.6 us  [complex_product(): pl.pallas_call(functools.partial(product_kernel, depths, weight), grid_sp...]
    all_to_all x2 -> x3, waiting for transfers between devices: 161 us -> 220 us  [the longest x2 220 us: per_device(): lax.all_to_all(sent, ('row', 'col'), split_axis=0, concat_axis=0, tiled=T...]
    reshape x1 -> x6, local copies, waits for them, and re-layouts: 0.08 us -> 56.1 us  [the longest x4 33.6 us: per_device(): sent.reshape(n_row, cap, 2, n_col, tile_cols).transpose(0, 3, 1, 2, 4)]
    dot_general x2 -> x4, matrix products: 75 us -> 27.5 us  [the longest x2 14.8 us: per_device(): sent = jnp.dot(picker, raw, preferred_element_type=F32).astype(BF16)]
    unnamed x0 -> x72, local copies, waits for them, and re-layouts: none -> 46.3 us
    another operation x5 -> x8, other arithmetic: 59.6 us -> 14.4 us  [the longest x7 14.3 us: per_device(): return jnp.stack([jnp.stack(o, axis=0) for o in outs], axis=0)]
  transfers between devices with their start and end apart: 5 -> 33, of which waited for: 4 -> 9; matrix products, arithmetic and copies ran while one was open for 16% -> 17% of each run, Pallas kernels for 0% -> 9%
where the time goes in v1:
time: 785 us; the launch traced here: 776 us
  waiting for transfers between devices  432 us (55%)
  local copies, waits for them, and re-layouts  127 us (16%)
  Pallas kernels  91.6 us (12%)
  starting transfers between devices  59.1 us (8%)
  matrix products  27.5 us (4%)
  other arithmetic  23.9 us (3%)
  between operations  15.1 us (2%)
    all_to_all x2, waiting for transfers between devices, per_device(): lax.all_to_all(sent, ('row', 'col'), split_axis=0, concat_axis=0, tiled=T...  220 us
    ppermute x24, waiting for transfers between devices, gather_cols(): arrived = {d ^ bit: lax.ppermute(a, 'col', pairs) for d, a in held.items()}  134 us
    pallas_call x12, Pallas kernels, complex_product(): pl.pallas_call(functools.partial(product_kernel, depths, weight), grid_sp...  91.6 us
    all_gather x6, waiting for transfers between devices, per_device(): lax.all_gather(jnp.concatenate([real, imag], axis=1), 'row', axis=0, tile...  78.2 us
    unnamed x72, local copies, waits for them, and re-layouts  46.3 us
    reshape x4, local copies, waits for them, and re-layouts, per_device(): sent.reshape(n_row, cap, 2, n_col, tile_cols).transpose(0, 3, 1, 2, 4)  33.6 us
    all_to_all x2, starting transfers between devices, per_device(): lax.all_to_all(sent, ('row', 'col'), split_axis=0, concat_axis=0, tiled=T...  27.9 us
    ppermute x24, starting transfers between devices, gather_cols(): arrived = {d ^ bit: lax.ppermute(a, 'col', pairs) for d, a in held.items()}  23.5 us
  transfers between devices with their start and end apart: 33, of which 9 were waited for; matrix products, arithmetic and copies ran while one was open for 17% of the time, Pallas kernels for 9%

profile of v1, /device:TPU:0, one launch (start us, length us, event | category | flops | bytes accessed | tf_op | source)
XLA Modules:
  0.0 775.8 jit_solution(11296569453850384145)
XLA Ops:
  16.3 12.3 %fusion.12 = (bf16[384,2,3072]{2,1,0:T(2,128)(2,1)}, bf16[384,2,3072]{2,1,0:T(2,128)(2,1)}) fusion(bf16[384,4,3072]{2,1,0:T(4,128)(2,1)} %param.3), kind=kLoop, calls=%fused_computation.46 | loop fusion | bytes 18874368 | tf_op jit(solution)/shard_map/slice | solution.py:106
  28.6 12.5 %copy.16 = bf16[384,2,3072]{0,2,1:T(8,128)(2,1)} copy(bf16[384,2,3072]{2,1,0:T(2,128)(2,1)} %get-tuple-element.5) | data formatting | bytes 9437184
  48.6 8.2 %reshape.44 = bf16[4,96,2,4,768]{4,3,2,1,0:T(4,128)(2,1)} reshape(bf16[384,6144]{1,0:T(8,128)(2,1)} %convolution_convert_fusion.1) | data formatting | bytes 9437184 | tf_op jit(solution)/shard_map/reshape | solution.py:108
  56.8 8.5 %copy.21 = bf16[4,96,2,4,768]{4,2,1,3,0:T(2,128)(2,1)} copy(bf16[4,96,2,4,768]{4,3,2,1,0:T(4,128)(2,1)} %reshape.44) | data formatting | bytes 9437184 | tf_op jit(solution)/shard_map/reshape | solution.py:108
  65.3 11.3 %reshape.45 = bf16[16,96,1536]{2,1,0:T(8,128)(2,1)} reshape(bf16[4,4,96,2,768]{4,3,2,1,0:T(2,128)(2,1)} %bitcast.51) | data formatting | bytes 9437184 | tf_op jit(solution)/shard_map/reshape | solution.py:109
  84.1 85.3 %all-to-all-done.1 = bf16[16,96,1536]{2,1,0:T(8,128)(2,1)} async-done(((bf16[16,96,1536]{2,1,0:T(8,128)(2,1)}), bf16[16,96,1536]{2,1,0:T(8,128)(2,1)}, u32[]{:S(2)}, u32[]{:S(2)}) %all-to-all-start.1) | async-done | bytes 4718624 | tf_op jit(solution)/shard_map/all_to_all | solution.py:110
  177.7 12.4 %copy.17 = bf16[384,2,3072]{0,2,1:T(8,128)(2,1)} copy(bf16[384,2,3072]{2,1,0:T(2,128)(2,1)} %get-tuple-element.6) | data formatting | bytes 9437184
  197.6 8.4 %reshape.48 = bf16[4,96,2,4,768]{4,3,2,1,0:T(4,128)(2,1)} reshape(bf16[384,6144]{1,0:T(8,128)(2,1)} %convolution_convert_fusion) | data formatting | bytes 9437184 | tf_op jit(solution)/shard_map/reshape | solution.py:108
  205.9 8.5 %copy.20 = bf16[4,96,2,4,768]{4,2,1,3,0:T(2,128)(2,1)} copy(bf16[4,96,2,4,768]{4,3,2,1,0:T(4,128)(2,1)} %reshape.48) | data formatting | bytes 9437184 | tf_op jit(solution)/shard_map/reshape | solution.py:108
  214.4 11.3 %reshape.49 = bf16[16,96,1536]{2,1,0:T(8,128)(2,1)} reshape(bf16[4,4,96,2,768]{4,3,2,1,0:T(2,128)(2,1)} %bitcast.52) | data formatting | bytes 9437184 | tf_op jit(solution)/shard_map/reshape | solution.py:109
  225.7 21.8 %all-to-all-start.2 = ((bf16[16,96,1536]{2,1,0:T(8,128)(2,1)}), bf16[16,96,1536]{2,1,0:T(8,128)(2,1)}, u32[]{:S(2)}, u32[]{:S(2)}) async-start(bf16[16,96,1536]{2,1,0:T(8,128)(2,1)} %reshape.49), calls=%async_computation.2 | async-start | bytes 9437184 | tf_op jit(solution)/shard_map/all_to_all | solution.py:110
  250.6 134.2 %all-to-all-done.2 = bf16[16,96,1536]{2,1,0:T(8,128)(2,1)} async-done(((bf16[16,96,1536]{2,1,0:T(8,128)(2,1)}), bf16[16,96,1536]{2,1,0:T(8,128)(2,1)}, u32[]{:S(2)}, u32[]{:S(2)}) %all-to-all-start.2) | async-done | bytes 4718624 | tf_op jit(solution)/shard_map/all_to_all | solution.py:110
  395.8 13.3 %collective-permute-start.1 = (bf16[768,1536]{1,0:T(8,128)(2,1)S(1)}, bf16[768,1536]{1,0:T(8,128)(2,1)}, u32[]{:S(2)}, u32[]{:S(2)}) collective-permute-start(bf16[768,1536]{1,0:T(8,128)(2,1)S(1)} %fusion.2.refs_0_), channel_id=1, source_target_pairs={{0,2},{1,3},{2,0},{3,1},{4,6},{5,7},{6,4},{7,5},{8,10},{9,11},{10,... | collective-permute-start | bytes 7077896 | tf_op jit(solution)/shard_map/ppermute | solution.py:32
  409.1 52.1 %collective-permute-done.1.refs_2_ = bf16[768,1536]{1,0:T(8,128)(2,1)} collective-permute-done((bf16[768,1536]{1,0:T(8,128)(2,1)S(1)}, bf16[768,1536]{1,0:T(8,128)(2,1)}, u32[]{:S(2)}, u32[]{:S(2)}) %collective-permute-start.1) | collective-permute-done | bytes 2359328 | tf_op jit(solution)/shard_map/ppermute | solution.py:32
  462.7 48.5 %collective-permute-done.4.refs_2_ = bf16[768,1536]{1,0:T(8,128)(2,1)} collective-permute-done((bf16[768,1536]{1,0:T(8,128)(2,1)}, bf16[768,1536]{1,0:T(8,128)(2,1)}, u32[]{:S(2)}, u32[]{:S(2)}) %collective-permute-start.4) | collective-permute-done | bytes 2359328 | tf_op jit(solution)/shard_map/ppermute | solution.py:32
  513.3 7.8 %shard_map.37.refs_0_ = bf16[768,512]{1,0:T(8,128)(2,1)S(1)} custom-call(s32[4]{0:T(128)S(1)} %pad_add_fusion.offs, bf16[768,1536]{1,0:T(8,128)(2,1)S(1)} %fusion.2.refs_0_, bf16[768,1536]{1,0:T(8,128)(2,1)} %collective-permute-done.refs_1_, bf16[768,1536]{1,0:T(8,128)(2,1)} %collective-permute-done.1.refs_2_, ...), custom_call_target="tpu_custom_call" | custom-call | flops 4831838208 | bytes 12582912 | tf_op jit(solution)/shard_map/pallas_call | solution.py:67
  525.0 8.3 %shard_map.38.refs_4_ = bf16[768,512]{1,0:T(8,128)(2,1)} custom-call(s32[4]{0:T(128)S(1)} %pad_add_fusion.offs, bf16[768,1536]{1,0:T(8,128)(2,1)S(1)} %fusion.2.refs_0_, bf16[768,1536]{1,0:T(8,128)(2,1)} %collective-permute-done.refs_1_, bf16[768,1536]{1,0:T(8,128)(2,1)} %collective-permute-done.1.refs_2_, bf16[768,1536]{1,0:T(8,128)(2,1)} %collective-permute-done.2.refs_3_, ...), custom_call_target="tpu_custom_call" | custom-call | flops 4831838208 | bytes 12582912 | tf_op jit(solution)/shard_map/pallas_call | solution.py:67
  538.7 8.3 %shard_map.39.refs_8_ = bf16[768,512]{1,0:T(8,128)(2,1)} custom-call(s32[4]{0:T(128)S(1)} %pad_add_fusion.offs, bf16[768,1536]{1,0:T(8,128)(2,1)S(1)} %fusion.2.refs_0_, bf16[768,1536]{1,0:T(8,128)(2,1)} %collective-permute-done.refs_1_, bf16[768,1536]{1,0:T(8,128)(2,1)} %collective-permute-done.1.refs_2_, bf16[768,1536]{1,0:T(8,128)(2,1)} %collective-permute-done.2.refs_3_, ...), custom_call_target="tpu_custom_call" | custom-call | flops 4831838208 | bytes 12582912 | tf_op jit(solution)/shard_map/pallas_call | solution.py:67
  563.0 28.6 %all-gather.13.cloned.1.call-done.refs_4_.refs_12_ = bf16[3072,512]{1,0:T(8,128)(2,1)} async-done(((bf16[768,512]{1,0:T(8,128)(2,1)}), bf16[3072,512]{1,0:T(8,128)(2,1)}) %all-gather.13.cloned.1.call-update) | async-done | bytes 3145744 | tf_op jit(solution)/shard_map/all_gather | solution.py:121
  605.5 49.6 %all-gather.17.cloned.1.call-done.refs_4_.refs_12_ = bf16[3072,512]{1,0:T(8,128)(2,1)} async-done(((bf16[768,512]{1,0:T(8,128)(2,1)}), bf16[3072,512]{1,0:T(8,128)(2,1)}) %all-gather.17.cloned.1.call-update) | async-done | bytes 3145744 | tf_op jit(solution)/shard_map/all_gather | solution.py:121
  692.8 16.3 %collective-permute-done.19.refs_6_ = bf16[768,512]{1,0:T(8,128)(2,1)S(1)} collective-permute-done((bf16[768,512]{1,0:T(8,128)(2,1)S(1)}, bf16[768,512]{1,0:T(8,128)(2,1)S(1)}, u32[]{:S(2)}, u32[]{:S(2)}) %collective-permute-start.19) | collective-permute-done | bytes 786464 | tf_op jit(solution)/shard_map/ppermute | solution.py:32
  709.1 16.1 %collective-permute-done.22.refs_10_ = bf16[768,512]{1,0:T(8,128)(2,1)} collective-permute-done((bf16[768,512]{1,0:T(8,128)(2,1)S(1)}, bf16[768,512]{1,0:T(8,128)(2,1)}, u32[]{:S(2)}, u32[]{:S(2)}) %collective-permute-start.22) | collective-permute-done | bytes 786464 | tf_op jit(solution)/shard_map/ppermute | solution.py:32
  726.2 8.0 %shard_map.45 = bf16[768,512]{1,0:T(8,128)(2,1)S(1)} custom-call(s32[12]{0:T(128)S(1)} %stack.104.offs, bf16[768,512]{1,0:T(8,128)(2,1)S(1)} %shard_map.37.refs_0_, bf16[768,512]{1,0:T(8,128)(2,1)} %collective-permute-done.6.refs_1_, bf16[768,512]{1,0:T(8,128)(2,1)} %collective-permute-done.7.refs_2_, bf16[768,512]{1,0:T(8,128)(2,1)S(1)} %collective-permute-done.8.refs_3_, ...), custom_call_target="tpu_custom_call" | custom-call | flops 4831838208 | bytes 12582912 | tf_op jit(solution)/shard_map/pallas_call | solution.py:67
  760.2 8.4 %pad_maximum_fusion = bf16[2,4,768,768]{3,2,1,0:T(8,128)(2,1)} fusion(bf16[1,4,768,768]{3,2,1,0:T(8,128)(2,1)} %maximum_bitcast_fusion.1, bf16[1,4,768,768]{3,2,1,0:T(8,128)(2,1)} %maximum_bitcast_fusion), kind=kLoop, calls=%fused_computation | loop fusion | flops 4718592 | bytes 18874368 | tf_op jit(solution)/shard_map/stack | solution.py:142
  (182 shorter events, 160.7 us)
Async XLA Ops:
  9.0 67.6 %all-to-all-start = ((s32[16,1,96]{2,1,0:T(1,128)}), s32[16,1,96]{2,1,0:T(1,128)S(1)}, u32[]{:S(2)}, u32[]{:S(2)}) async-start(s32[16,1,96]{2,1,0:T(1,128)} %bitcast.5), calls=%async_computation | async-start | bytes 16384 | tf_op jit(solution)/shard_map/all_to_all | solution.py:98
  76.6 92.9 %all-to-all-start.1 = ((bf16[16,96,1536]{2,1,0:T(8,128)(2,1)}), bf16[16,96,1536]{2,1,0:T(8,128)(2,1)}, u32[]{:S(2)}, u32[]{:S(2)}) async-start(bf16[16,96,1536]{2,1,0:T(8,128)(2,1)} %reshape.45), calls=%async_computation.1 | async-start | bytes 9437184 | tf_op jit(solution)/shard_map/all_to_all | solution.py:110
  82.7 428.8 %all-gather.7.cloned.1.call-start = ((), (), s32[]{:S(2)}) async-start(), calls=%async_computation.3 | async-start | bytes 3932160 | tf_op jit(solution)/shard_map/all_gather | solution.py:121
  225.7 159.2 %all-to-all-start.2 = ((bf16[16,96,1536]{2,1,0:T(8,128)(2,1)}), bf16[16,96,1536]{2,1,0:T(8,128)(2,1)}, u32[]{:S(2)}, u32[]{:S(2)}) async-start(bf16[16,96,1536]{2,1,0:T(8,128)(2,1)} %reshape.49), calls=%async_computation.2 | async-start | bytes 9437184 | tf_op jit(solution)/shard_map/all_to_all | solution.py:110
  247.5 275.7 %all-gather.9.cloned.1.call-start = ((), (), s32[]{:S(2)}) async-start(), calls=%async_computation.4 | async-start | bytes 3932160 | tf_op jit(solution)/shard_map/all_gather | solution.py:121
  249.5 287.1 %all-gather.11.cloned.1.call-start = ((), (), s32[]{:S(2)}) async-start(), calls=%async_computation.5 | async-start | bytes 3932160 | tf_op jit(solution)/shard_map/all_gather | solution.py:121
  250.5 300.4 %all-gather.15.cloned.1.call-start = ((), (), s32[]{:S(2)}) async-start(), calls=%async_computation.7 | async-start | bytes 3932160 | tf_op jit(solution)/shard_map/all_gather | solution.py:121
  393.7 197.9 %all-gather.13.cloned.1.call-start = ((), (), s32[]{:S(2)}) async-start(), calls=%async_computation.6 | async-start | bytes 3932160 | tf_op jit(solution)/shard_map/all_gather | solution.py:121
  395.7 259.4 %all-gather.17.cloned.1.call-start = ((), (), s32[]{:S(2)}) async-start(), calls=%async_computation.8 | async-start | bytes 3932160 | tf_op jit(solution)/shard_map/all_gather | solution.py:121
  395.8 65.4 %collective-permute-start.1 = (bf16[768,1536]{1,0:T(8,128)(2,1)S(1)}, bf16[768,1536]{1,0:T(8,128)(2,1)}, u32[]{:S(2)}, u32[]{:S(2)}) collective-permute-start(bf16[768,1536]{1,0:T(8,128)(2,1)S(1)} %fusion.2.refs_0_), channel_id=1, source_target_pairs={{0,2},{1,3},{2,0},{3,1},{4,6},{5,7},{6,4},{7,5},{8,10},{9,11},{10,... | collective-permute-start | bytes 7077896 | tf_op jit(solution)/shard_map/ppermute | solution.py:32
  409.1 102.2 %collective-permute-start.4 = (bf16[768,1536]{1,0:T(8,128)(2,1)}, bf16[768,1536]{1,0:T(8,128)(2,1)}, u32[]{:S(2)}, u32[]{:S(2)}) collective-permute-start(bf16[768,1536]{1,0:T(8,128)(2,1)} %copy-done), channel_id=1, source_target_pairs={{0,2},{1,3},{2,0},{3,1},{4,6},{5,7},{6,4},{7,5},{8,10},{9,11},{10,... | collective-permute-start | bytes 7077896 | tf_op jit(solution)/shard_map/ppermute | solution.py:32
  409.1 102.3 %collective-permute-start = (bf16[768,1536]{1,0:T(8,128)(2,1)S(1)}, bf16[768,1536]{1,0:T(8,128)(2,1)}, u32[]{:S(2)}, u32[]{:S(2)}) collective-permute-start(bf16[768,1536]{1,0:T(8,128)(2,1)S(1)} %fusion.2.refs_0_), channel_id=1, source_target_pairs={{0,1},{1,0},{2,3},{3,2},{4,5},{5,4},{6,7},{7,6},{8,9},{9,8},{10,11... | collective-permute-start | bytes 7077896 | tf_op jit(solution)/shard_map/ppermute | solution.py:32
  461.2 50.2 %collective-permute-start.2 = (bf16[768,1536]{1,0:T(8,128)(2,1)}, bf16[768,1536]{1,0:T(8,128)(2,1)}, u32[]{:S(2)}, u32[]{:S(2)}) collective-permute-start(bf16[768,1536]{1,0:T(8,128)(2,1)} %collective-permute-done.1.refs_2_), channel_id=1, source_target_pairs={{0,1},{1,0},{2,3},{3,2},{4,5},{5,4},{6,7},{7,6},{8,9},{9,8},{10,11... | collective-permute-start | bytes 7077896 | tf_op jit(solution)/shard_map/ppermute | solution.py:32
  462.2 86.9 %collective-permute-start.3 = (bf16[768,1536]{1,0:T(8,128)(2,1)}, bf16[768,1536]{1,0:T(8,128)(2,1)}, u32[]{:S(2)}, u32[]{:S(2)}) collective-permute-start(bf16[768,1536]{1,0:T(8,128)(2,1)} %copy-done), channel_id=1, source_target_pairs={{0,1},{1,0},{2,3},{3,2},{4,5},{5,4},{6,7},{7,6},{8,9},{9,8},{10,11... | collective-permute-start | bytes 7077896 | tf_op jit(solution)/shard_map/ppermute | solution.py:32
  511.2 37.9 %collective-permute-start.5 = (bf16[768,1536]{1,0:T(8,128)(2,1)}, bf16[768,1536]{1,0:T(8,128)(2,1)}, u32[]{:S(2)}, u32[]{:S(2)}) collective-permute-start(bf16[768,1536]{1,0:T(8,128)(2,1)} %collective-permute-done.4.refs_2_), channel_id=1, source_target_pairs={{0,1},{1,0},{2,3},{3,2},{4,5},{5,4},{6,7},{7,6},{8,9},{9,8},{10,11... | collective-permute-start | bytes 7077896 | tf_op jit(solution)/shard_map/ppermute | solution.py:32
  521.1 145.2 %collective-permute-start.7 = (bf16[768,512]{1,0:T(8,128)(2,1)S(1)}, bf16[768,512]{1,0:T(8,128)(2,1)}, u32[]{:S(2)}, u32[]{:S(2)}) collective-permute-start(bf16[768,512]{1,0:T(8,128)(2,1)S(1)} %shard_map.37.refs_0_), channel_id=1, source_target_pairs={{0,2},{1,3},{2,0},{3,1},{4,6},{5,7},{6,4},{7,5},{8,10},{9,11},{10,... | collective-permute-start | bytes 2359304 | tf_op jit(solution)/shard_map/ppermute | solution.py:32
  522.9 143.5 %collective-permute-start.6 = (bf16[768,512]{1,0:T(8,128)(2,1)S(1)}, bf16[768,512]{1,0:T(8,128)(2,1)}, u32[]{:S(2)}, u32[]{:S(2)}) collective-permute-start(bf16[768,512]{1,0:T(8,128)(2,1)S(1)} %shard_map.37.refs_0_), channel_id=1, source_target_pairs={{0,1},{1,0},{2,3},{3,2},{4,5},{5,4},{6,7},{7,6},{8,9},{9,8},{10,11... | collective-permute-start | bytes 2359304 | tf_op jit(solution)/shard_map/ppermute | solution.py:32
  533.3 133.6 %collective-permute-start.10 = (bf16[768,512]{1,0:T(8,128)(2,1)}, bf16[768,512]{1,0:T(8,128)(2,1)}, u32[]{:S(2)}, u32[]{:S(2)}) collective-permute-start(bf16[768,512]{1,0:T(8,128)(2,1)} %shard_map.38.refs_4_), channel_id=1, source_target_pairs={{0,2},{1,3},{2,0},{3,1},{4,6},{5,7},{6,4},{7,5},{8,10},{9,11},{10,... | collective-permute-start | bytes 2359304 | tf_op jit(solution)/shard_map/ppermute | solution.py:32
  549.1 122.7 %collective-permute-start.9 = (bf16[768,512]{1,0:T(8,128)(2,1)}, bf16[768,512]{1,0:T(8,128)(2,1)}, u32[]{:S(2)}, u32[]{:S(2)}) collective-permute-start(bf16[768,512]{1,0:T(8,128)(2,1)} %shard_map.38.refs_4_), channel_id=1, source_target_pairs={{0,1},{1,0},{2,3},{3,2},{4,5},{5,4},{6,7},{7,6},{8,9},{9,8},{10,11... | collective-permute-start | bytes 2359304 | tf_op jit(solution)/shard_map/ppermute | solution.py:32
  549.1 117.9 %collective-permute-start.13 = (bf16[768,512]{1,0:T(8,128)(2,1)}, bf16[768,512]{1,0:T(8,128)(2,1)}, u32[]{:S(2)}, u32[]{:S(2)}) collective-permute-start(bf16[768,512]{1,0:T(8,128)(2,1)} %shard_map.39.refs_8_), channel_id=1, source_target_pairs={{0,2},{1,3},{2,0},{3,1},{4,6},{5,7},{6,4},{7,5},{8,10},{9,11},{10,... | collective-permute-start | bytes 2359304 | tf_op jit(solution)/shard_map/ppermute | solution.py:32
  674.0 60.3 %collective-permute-start.18 = (bf16[768,512]{1,0:T(8,128)(2,1)S(1)}, bf16[768,512]{1,0:T(8,128)(2,1)}, u32[]{:S(2)}, u32[]{:S(2)}) collective-permute-start(bf16[768,512]{1,0:T(8,128)(2,1)S(1)} %copy-done.6), channel_id=1, source_target_pairs={{0,1},{1,0},{2,3},{3,2},{4,5},{5,4},{6,7},{7,6},{8,9},{9,8},{10,11... | collective-permute-start | bytes 2359304 | tf_op jit(solution)/shard_map/ppermute | solution.py:32
  674.2 51.1 %collective-permute-start.22 = (bf16[768,512]{1,0:T(8,128)(2,1)S(1)}, bf16[768,512]{1,0:T(8,128)(2,1)}, u32[]{:S(2)}, u32[]{:S(2)}) collective-permute-start(bf16[768,512]{1,0:T(8,128)(2,1)S(1)} %shard_map.42.refs_8_), channel_id=1, source_target_pairs={{0,2},{1,3},{2,0},{3,1},{4,6},{5,7},{6,4},{7,5},{8,10},{9,11},{10,... | collective-permute-start | bytes 2359304 | tf_op jit(solution)/shard_map/ppermute | solution.py:32
  692.3 42.0 %collective-permute-start.21 = (bf16[768,512]{1,0:T(8,128)(2,1)S(1)}, bf16[768,512]{1,0:T(8,128)(2,1)S(1)}, u32[]{:S(2)}, u32[]{:S(2)}) collective-permute-start(bf16[768,512]{1,0:T(8,128)(2,1)S(1)} %shard_map.42.refs_8_), channel_id=1, source_target_pairs={{0,1},{1,0},{2,3},{3,2},{4,5},{5,4},{6,7},{7,6},{8,9},{9,8},{10,11... | collective-permute-start | bytes 2359304 | tf_op jit(solution)/shard_map/ppermute | solution.py:32
  692.3 42.0 %collective-permute-start.17 = (bf16[768,512]{1,0:T(8,128)(2,1)S(1)}, bf16[768,512]{1,0:T(8,128)(2,1)S(1)}, u32[]{:S(2)}, u32[]{:S(2)}) collective-permute-start(bf16[768,512]{1,0:T(8,128)(2,1)S(1)} %collective-permute-done.16.refs_2_), channel_id=1, source_target_pairs={{0,1},{1,0},{2,3},{3,2},{4,5},{5,4},{6,7},{7,6},{8,9},{9,8},{10,11... | collective-permute-start | bytes 2359304 | tf_op jit(solution)/shard_map/ppermute | solution.py:32
  (44 other events, 355.3 us)
Sparse Core Ops, SparseCore 0:
  177.9 109.8 all-gather.6
  289.3 108.8 all-gather.8
  399.7 64.5 all-gather.10
  465.7 62.1 all-gather.14
  529.3 62.2 all-gather.12
  593.0 62.0 all-gather.16

commit v2 on v1

v2 whole, which is shorter than its diff:
```python
import functools
import math

import jax
import jax.numpy as jnp
from jax import lax
from jax.experimental import pallas as pl
from jax.experimental.pallas import tpu as pltpu
from jax.sharding import PartitionSpec as P

NS = 3072
FREQ = 2
THIRDS = 3
BF16 = jnp.bfloat16
F32 = jnp.float32


def after(value, earlier):
    return lax.optimization_barrier((value, earlier))[0]


def gather_cols(piece, n_col):
    held = {0: piece}
    bit = n_col // 2
    while bit:
        pairs = [(c, c ^ bit) for c in range(n_col)]
        arrived = {d ^ bit: lax.ppermute(a, "col", pairs) for d, a in held.items()}
        held.update(arrived)
        bit //= 2
    return [held[d] for d in range(n_col)]


def hop(pair, k, n_row):
    down = [(r, r - 1) for r in range(1, n_row) if r + k - 1 < n_row]
    up = [(r, r + 1) for r in range(n_row - 1) if r - k + 1 >= 0]
    return lax.ppermute(pair[0], "row", down), lax.ppermute(pair[1], "row", up)


def bin_kernel(picker, data, out0, out1):
    hits = picker[...]
    n_row, cap = out0.shape[0], out0.shape[2]
    sub = data.shape[2] // THIRDS
    for p in range(2 * FREQ):
        out = out0 if p < 2 else out1
        rows = jnp.dot(hits, data[p], preferred_element_type=F32).astype(BF16)
        for b in range(n_row):
            for j in range(THIRDS):
                start = (2 * j + p % 2) * sub
                out[b, 0, :, start : start + sub] = rows[b * cap : (b + 1) * cap, j * sub : (j + 1) * sub]


def bin_rows(picker, data, n_row, n_col):
    planes, own_cap, order = data.shape
    cap = picker.shape[0] // n_row
    wide = 2 * order // n_col
    shape = jax.ShapeDtypeStruct((n_row, n_col, cap, wide), BF16)
    block = pl.BlockSpec((n_row, 1, cap, wide), lambda c: (0, c, 0, 0))
    return pl.pallas_call(
        bin_kernel,
        grid=(n_col,),
        in_specs=[
            pl.BlockSpec(picker.shape, lambda c: (0, 0)),
            pl.BlockSpec((planes, own_cap, order // n_col), lambda c: (0, 0, c)),
        ],
        out_specs=[block, block],
        out_shape=[shape, shape],
        compiler_params=pltpu.CompilerParams(vmem_limit_bytes=40 * 2**20),
        cost_estimate=pl.CostEstimate(
            flops=2 * picker.shape[0] * own_cap * planes * order,
            bytes_accessed=4 * planes * own_cap * order,
            transcendentals=0,
        ),
    )(picker, data)


def product_kernel(plan, n_left, has_piece, weight, spots, *refs):
    lefts, refs = refs[:n_left], refs[n_left:]
    sources, refs = refs[: len(plan)], refs[len(plan) :]
    *outs, right, sems = refs[-(4 if has_piece else 3) :]
    whole, piece = outs[0], (outs[1] if has_piece else None)
    rows_at = spots[n_left]
    block = sources[0].shape[0]

    @pl.when(pl.program_id(0) == 0)
    def _():
        for phase in range(2):
            for s, (low, high, step) in enumerate(plan):

                @pl.when((rows_at >= low) & (rows_at <= high))
                def _(s=s, step=step):
                    start = pl.multiple_of((rows_at + step) * block if len(plan) > 1 else 0, 32)
                    copy = pltpu.make_async_copy(sources[s], right.at[pl.ds(start, block)], sems.at[s])
                    if phase == 0:
                        copy.start()
                    else:
                        copy.wait()

    width = right.shape[1] // 2
    tile = lefts[0].shape[0]
    by_real = jnp.zeros((tile, 2 * width), F32)
    by_imag = jnp.zeros((tile, 2 * width), F32)
    for i, left in enumerate(lefts):
        depth = left.shape[1] // 2
        part = right[pl.ds(pl.multiple_of(spots[i], 128), depth), :]
        by_real += jnp.dot(left[:, :depth], part, preferred_element_type=F32)
        by_imag += jnp.dot(left[:, depth:], part, preferred_element_type=F32)
    real = ((by_real[:, :width] - by_imag[:, width:]) * weight).astype(BF16)
    imag = ((by_real[:, width:] + by_imag[:, :width]) * weight).astype(BF16)
    whole[0, 0] = real
    whole[0, 1] = imag
    if has_piece:
        piece[:, :width] = real
        piece[:, width:] = imag


def complex_product(spots, lefts, sources, plan, result, at, shape, weight):
    n, f, j = at
    has_piece = n == 0
    rows = lefts[0].shape[0]
    tile = 256 if rows % 256 == 0 else rows
    wide = sources[0].shape[1]
    held = [] if result is None else [result]
    out_specs = [pl.BlockSpec((1, 2, tile, wide // 2), lambda i, s: (n, f, i, j))]
    out_shape = [jax.ShapeDtypeStruct(shape, BF16)]
    if has_piece:
        out_specs.append(pl.BlockSpec((tile, wide), lambda i, s: (i, 0)))
        out_shape.append(jax.ShapeDtypeStruct((rows, wide), BF16))
    spec = pltpu.PrefetchScalarGridSpec(
        num_scalar_prefetch=1,
        grid=(rows // tile,),
        in_specs=[pl.BlockSpec((tile, a.shape[1]), lambda i, s: (i, 0)) for a in lefts]
        + [pl.BlockSpec(memory_space=pl.ANY)] * (len(sources) + len(held)),
        out_specs=out_specs,
        scratch_shapes=[pltpu.VMEM((NS, wide), BF16), pltpu.SemaphoreType.DMA((len(plan),))],
    )
    return pl.pallas_call(
        functools.partial(product_kernel, plan, len(lefts), has_piece, weight),
        grid_spec=spec,
        out_shape=out_shape,
        input_output_aliases={1 + len(lefts) + len(sources): 0} if held else {},
        compiler_params=pltpu.CompilerParams(vmem_limit_bytes=40 * 2**20),
        cost_estimate=pl.CostEstimate(
            flops=4 * rows * NS * wide, bytes_accessed=2 * NS * (wide + 2 * rows), transcendentals=0
        ),
    )(spots, *lefts, *sources, *held)


def per_device(acq_data, grid_row, counts):
    n_row = lax.axis_size("row")
    n_col = lax.axis_size("col")
    own_cap, planes, order = acq_data.shape
    block_rows = order // n_row
    tile_cols = order // n_col
    cap = own_cap // n_row
    slots = n_row * cap
    sub = tile_cols // THIRDS
    weight = 1.0 / math.sqrt(2.0 * NS)
    me = lax.axis_index("col")

    slot_index = jnp.arange(own_cap, dtype=jnp.int32)
    block = jnp.where(slot_index < counts[0], grid_row // block_rows, n_row)
    earlier = (block[None, :] == block[:, None]) & (slot_index[None, :] < slot_index[:, None])
    rank = jnp.sum(earlier.astype(jnp.int32), axis=1)
    leaving = jnp.where(block < n_row, block * cap + rank, -1)
    hit = jnp.arange(slots, dtype=jnp.int32)[:, None] == leaving[None, :]
    spots = jnp.sum(jnp.where(hit, (grid_row % block_rows)[None, :] + 1, 0), axis=1) - 1
    labels = jnp.broadcast_to(spots.reshape(n_row, 1, cap), (n_row, n_col, cap))
    places = lax.all_to_all(
        labels.reshape(n_row * n_col, cap), ("row", "col"), split_axis=0, concat_axis=0, tiled=True
    ).reshape(-1)
    placer = (jnp.arange(block_rows, dtype=jnp.int32)[:, None] == places[None, :]).astype(BF16)
    sent = bin_rows(hit.astype(BF16), jnp.transpose(acq_data, (1, 0, 2)), n_row, n_col)

    tiles = []
    for f in range(FREQ):
        got = lax.all_to_all(
            sent[f].reshape(n_row * n_col, cap, 2 * tile_cols),
            ("row", "col"),
            split_axis=0,
            concat_axis=0,
            tiled=True,
        ).reshape(-1, 2 * tile_cols)
        tiles.append(
            [
                jnp.dot(placer, got[:, 2 * j * sub : 2 * (j + 1) * sub], preferred_element_type=F32).astype(BF16)
                for j in range(THIRDS)
            ]
        )

    if n_row <= 4:
        plan = [(0, n_row - 1, 0)]
        for k in range(1, n_row):
            plan += [(0, n_row - 1 - k, k), (k, n_row - 1, -k)]
        rights = []
        passed = None
        for f in range(FREQ):
            begun = tiles[f] if passed is None else [after(t, p) for t, p in zip(tiles[f], passed)]
            carried = [(t, t) for t in begun]
            found = [[t] for t in tiles[f]]
            for k in range(1, n_row):
                carried = [hop(pair, k, n_row) for pair in carried]
                for j in range(THIRDS):
                    found[j] += list(carried[j])
                if k == n_row - 2:
                    passed = carried
            rights.append(found)
    else:
        plan = [(0, n_row - 1, 0)]
        rights = [[[lax.all_gather(t, "row", axis=0, tiled=True)] for t in tiles[f]] for f in range(FREQ)]

    spots = jnp.stack(
        [(me ^ d) * tile_cols + j * sub for j in range(THIRDS) for d in range(n_col)] + [lax.axis_index("row")]
    ).astype(jnp.int32)
    shape = (2, planes, block_rows, tile_cols)
    result = None
    for f in range(FREQ):
        lefts = []
        for j in range(THIRDS):
            lefts += gather_cols(tiles[f][j], n_col)
        gathered = []
        for j in range(THIRDS):
            result, piece = complex_product(spots, lefts, rights[f][j], plan, result, (0, f, j), shape, weight)
            gathered += gather_cols(piece, n_col)
        for j in range(THIRDS):
            (result,) = complex_product(spots, gathered, rights[f][j], plan, result, (1, f, j), shape, weight)
    return result


def solution(mesh):
    placed = (
        P(("groups", "row", "col"), None, None),
        P(("groups", "row", "col")),
        P(("groups", "row", "col")),
    )
    return jax.shard_map(
        per_device,
        mesh=mesh,
        in_specs=placed,
        out_specs=P("groups", None, "row", "col"),
        check_vma=False,
    )
```

time: 785 us -> 727 us (0.926)
  waiting for transfers between devices: 432 us -> 303 us
  blocking collectives: 0 us -> 110 us
  local copies, waits for them, and re-layouts: 127 us -> 46.1 us
  starting transfers between devices: 59.1 us -> 132 us
  Pallas kernels: 91.6 us -> 115 us
  other arithmetic: 23.9 us -> 1.88 us
  between operations: 15.1 us -> 1.8 us
  matrix products: 27.5 us -> 15.1 us
    all_to_all x2 -> x1, waiting for transfers between devices: 220 us -> 0.01 us  [per_device(): lax.all_to_all(sent[f].reshape(n_row * n_col, cap, 2 * tile_cols), ('row'...]
    ppermute x0 -> x36, waiting for transfers between devices: none -> 178 us  [the longest x18 176 us: hop(): lax.ppermute(pair[0], 'row', down)]
    all_to_all x0 -> x1, blocking collectives: none -> 110 us  [per_device(): lax.all_to_all(sent[f].reshape(n_row * n_col, cap, 2 * tile_cols), ('row'...]
    ppermute x0 -> x36, starting transfers between devices: none -> 101 us  [the longest x18 77.3 us: hop(): lax.ppermute(pair[1], 'row', up)]
    all_gather x6 -> x0, waiting for transfers between devices: 78.2 us -> none  [per_device(): lax.all_gather(jnp.concatenate([real, imag], axis=1), 'row', axis=0, tile...]
    reshape x6 -> x0, local copies, waits for them, and re-layouts: 56.1 us -> none  [the longest x4 33.6 us: per_device(): sent.reshape(n_row, cap, 2, n_col, tile_cols).transpose(0, 3, 1, 2, 4)]
    slice x15 -> x0, local copies, waits for them, and re-layouts: 23.3 us -> none  [the longest x1 12.3 us: per_device(): raw = acq_data[:, 2 * f:2 * f + 2, :].reshape(own_cap, 2 * order)]
    pallas_call x12 -> x13, Pallas kernels: 91.6 us -> 115 us  [the longest x12 107 us: complex_product(): pl.pallas_call(functools.partial(product_kernel, plan, len(lefts), has_pi...]
  transfers between devices with their start and end apart: 33 -> 74, of which waited for: 9 -> 26; matrix products, arithmetic and copies ran while one was open for 17% -> 4% of each run, Pallas kernels for 9% -> 11%
where the time goes in v2:
time: 727 us; the launch traced here: 724 us
  waiting for transfers between devices  303 us (42%)
  starting transfers between devices  132 us (18%)
  Pallas kernels  115 us (16%)
  blocking collectives  110 us (15%)
  local copies, waits for them, and re-layouts  46.1 us (6%)
  matrix products  15.1 us (2%)
    ppermute x18, waiting for transfers between devices, hop(): lax.ppermute(pair[0], 'row', down)  176 us
    ppermute x36, waiting for transfers between devices, gather_cols(): arrived = {d ^ bit: lax.ppermute(a, 'col', pairs) for d, a in held.items()}  125 us
    all_to_all x1, blocking collectives, per_device(): lax.all_to_all(sent[f].reshape(n_row * n_col, cap, 2 * tile_cols), ('row'...  110 us
    pallas_call x12, Pallas kernels, complex_product(): pl.pallas_call(functools.partial(product_kernel, plan, len(lefts), has_pi...  107 us
    ppermute x18, starting transfers between devices, hop(): lax.ppermute(pair[1], 'row', up)  77.3 us
    unnamed x123, local copies, waits for them, and re-layouts  44.6 us
    ppermute x18, starting transfers between devices, hop(): lax.ppermute(pair[0], 'row', down)  23.8 us
    ppermute x36, starting transfers between devices, gather_cols(): arrived = {d ^ bit: lax.ppermute(a, 'col', pairs) for d, a in held.items()}  17.8 us
  transfers between devices with their start and end apart: 74, of which 26 were waited for; matrix products, arithmetic and copies ran while one was open for 4% of the time, Pallas kernels for 11%

profile of v2, /device:TPU:0, one launch (start us, length us, event | category | flops | bytes accessed | tf_op | source)
XLA Modules:
  0.0 723.8 jit_solution(9515158566270630366)
XLA Ops:
  9.9 10.4 %copy.19 = bf16[384,4,3072]{2,0,1:T(8,128)(2,1)} copy(bf16[384,4,3072]{2,1,0:T(4,128)(2,1)} %param.3) | data formatting | bytes 18874368 | tf_op args[0]
  32.6 109.6 %all_to_all.19 = bf16[16,96,1536]{2,1,0:T(8,128)(2,1)} all-to-all(bf16[16,96,1536]{2,1,0:T(8,128)(2,1)} %bitcast.24), channel_id=1, replica_groups=mesh['groups'=2,'row'=4,'col'=4] {'row','col'}, dimensions={0} | all-to-all | bytes 9437184 | tf_op jit(solution)/shard_map/all_to_all | solution.py:176
  165.6 77.9 %collective-permute-done.9.refs_13_ = bf16[768,512]{1,0:T(8,128)(2,1)S(1)} collective-permute-done((bf16[768,512]{1,0:T(8,128)(2,1)S(1)}, bf16[768,512]{1,0:T(8,128)(2,1)S(1)}, u32[]{:S(2)}, u32[]{:S(2)}) %collective-permute-start.9) | collective-permute-done | bytes 786464 | tf_op jit(solution)/shard_map/ppermute | solution.py:36
  251.8 24.3 %collective-permute-start.34 = (bf16[768,512]{1,0:T(8,128)(2,1)}, bf16[768,512]{1,0:T(8,128)(2,1)}, u32[]{:S(2)}, u32[]{:S(2)}) collective-permute-start(bf16[768,512]{1,0:T(8,128)(2,1)} %fusion.30.refs_4_.refs_12_), channel_id=1, source_target_pairs={{0,4},{4,8},{8,12},{1,5},{5,9},{9,13},{2,6},{6,10},{10,14},{3,7},{... | collective-permute-start | bytes 2359304 | tf_op jit(solution)/shard_map/ppermute | solution.py:36
  297.7 10.6 %collective-permute-done.42.refs_13_ = bf16[768,512]{1,0:T(8,128)(2,1)} collective-permute-done((bf16[768,512]{1,0:T(8,128)(2,1)S(1)}, bf16[768,512]{1,0:T(8,128)(2,1)}, u32[]{:S(2)}, u32[]{:S(2)}) %collective-permute-start.42) | collective-permute-done | bytes 786464 | tf_op jit(solution)/shard_map/ppermute | solution.py:36
  309.9 16.6 %collective-permute-done.7.refs_10_ = bf16[768,512]{1,0:T(8,128)(2,1)S(1)} collective-permute-done((bf16[768,512]{1,0:T(8,128)(2,1)S(1)}, bf16[768,512]{1,0:T(8,128)(2,1)S(1)}, u32[]{:S(2)}, u32[]{:S(2)}) %collective-permute-start.7) | collective-permute-done | bytes 786464 | tf_op jit(solution)/shard_map/ppermute | solution.py:27
  327.8 13.9 %collective-permute-done.1.refs_2_ = bf16[768,512]{1,0:T(8,128)(2,1)} collective-permute-done((bf16[768,512]{1,0:T(8,128)(2,1)S(1)}, bf16[768,512]{1,0:T(8,128)(2,1)}, u32[]{:S(2)}, u32[]{:S(2)}) %collective-permute-start.1) | collective-permute-done | bytes 786464 | tf_op jit(solution)/shard_map/ppermute | solution.py:27
  356.3 13.6 %collective-permute-done.35.refs_15_ = bf16[768,512]{1,0:T(8,128)(2,1)} collective-permute-done((bf16[768,512]{1,0:T(8,128)(2,1)S(1)}, bf16[768,512]{1,0:T(8,128)(2,1)}, u32[]{:S(2)}, u32[]{:S(2)}) %collective-permute-start.35) | collective-permute-done | bytes 786464 | tf_op jit(solution)/shard_map/ppermute | solution.py:36
  372.2 15.3 %collective-permute-done.44.refs_15_ = bf16[768,512]{1,0:T(8,128)(2,1)S(1)} collective-permute-done((bf16[768,512]{1,0:T(8,128)(2,1)}, bf16[768,512]{1,0:T(8,128)(2,1)S(1)}, u32[]{:S(2)}, u32[]{:S(2)}) %collective-permute-start.44) | collective-permute-done | bytes 786464 | tf_op jit(solution)/shard_map/ppermute | solution.py:36
  393.8 10.6 %collective-permute-done.28.refs_17_ = bf16[768,512]{1,0:T(8,128)(2,1)} collective-permute-done((bf16[768,512]{1,0:T(8,128)(2,1)}, bf16[768,512]{1,0:T(8,128)(2,1)}, u32[]{:S(2)}, u32[]{:S(2)}) %collective-permute-start.28) | collective-permute-done | bytes 786464 | tf_op jit(solution)/shard_map/ppermute | solution.py:36
  417.4 9.7 %shard_map.38 = (bf16[2,4,768,768]{3,2,1,0:T(8,128)(2,1)}, bf16[768,512]{1,0:T(8,128)(2,1)S(1)}) custom-call(s32[13]{0:T(128)S(1)} %stack.55.spots, bf16[768,512]{1,0:T(8,128)(2,1)S(1)} %copy-done.7, bf16[768,512]{1,0:T(8,128)(2,1)S(1)} %copy-done.37, bf16[768,512]{1,0:T(8,128)(2,1)S(1)} %copy-done.30, bf16[768,512]{1,0:T(8,128)(2,1)S(1)} %copy-done.40, ...), custom_call_target="tpu_custom_call" | custom-call | flops 4831838208 | bytes 12582912 | tf_op jit(solution)/shard_map/pallas_call | solution.py:136
  439.2 10.0 %shard_map.39 = (bf16[2,4,768,768]{3,2,1,0:T(8,128)(2,1)}, bf16[768,512]{1,0:T(8,128)(2,1)S(1)}) custom-call(s32[13]{0:T(128)S(1)} %stack.55.spots, bf16[768,512]{1,0:T(8,128)(2,1)S(1)} %copy-done.7, bf16[768,512]{1,0:T(8,128)(2,1)S(1)} %copy-done.38, bf16[768,512]{1,0:T(8,128)(2,1)S(1)} %copy-done.31, ...), custom_call_target="tpu_custom_call", output_to_operand_aliasing={{0}: (20, {})} | custom-call | flops 4831838208 | bytes 12582912 | tf_op jit(solution)/shard_map/pallas_call | solution.py:136
  449.1 15.2 %collective-permute-start.55 = (bf16[768,512]{1,0:T(8,128)(2,1)S(1)}, bf16[768,512]{1,0:T(8,128)(2,1)}, u32[]{:S(2)}, u32[]{:S(2)}) collective-permute-start(bf16[768,512]{1,0:T(8,128)(2,1)S(1)} %fusion.21.refs_4_.refs_12_), channel_id=1, source_target_pairs={{0,4},{4,8},{8,12},{1,5},{5,9},{9,13},{2,6},{6,10},{10,14},{3,7},{... | collective-permute-start | bytes 2359304 | tf_op jit(solution)/shard_map/ppermute | solution.py:36
  466.9 9.5 %shard_map.40 = (bf16[2,4,768,768]{3,2,1,0:T(8,128)(2,1)}, bf16[768,512]{1,0:T(8,128)(2,1)S(1)}) custom-call(s32[13]{0:T(128)S(1)} %stack.55.spots, bf16[768,512]{1,0:T(8,128)(2,1)S(1)} %copy-done.7, bf16[768,512]{1,0:T(8,128)(2,1)S(1)} %copy-done.38, bf16[768,512]{1,0:T(8,128)(2,1)S(1)} %copy-done.31, ...), custom_call_target="tpu_custom_call", output_to_operand_aliasing={{0}: (20, {})} | custom-call | flops 4831838208 | bytes 12582912 | tf_op jit(solution)/shard_map/pallas_call | solution.py:136
  490.2 11.1 %collective-permute-done.49.refs_10_ = bf16[768,512]{1,0:T(8,128)(2,1)S(1)} collective-permute-done((bf16[768,512]{1,0:T(8,128)(2,1)S(1)}, bf16[768,512]{1,0:T(8,128)(2,1)S(1)}, u32[]{:S(2)}, u32[]{:S(2)}) %collective-permute-start.49) | collective-permute-done | bytes 786464 | tf_op jit(solution)/shard_map/ppermute | solution.py:27
  501.8 16.2 %collective-permute-done.40.refs_6_ = bf16[768,512]{1,0:T(8,128)(2,1)S(1)} collective-permute-done((bf16[768,512]{1,0:T(8,128)(2,1)S(1)}, bf16[768,512]{1,0:T(8,128)(2,1)S(1)}, u32[]{:S(2)}, u32[]{:S(2)}) %collective-permute-start.40) | collective-permute-done | bytes 786464 | tf_op jit(solution)/shard_map/ppermute | solution.py:27
  518.0 9.3 %collective-permute-done.31.refs_2_ = bf16[768,512]{1,0:T(8,128)(2,1)S(1)} collective-permute-done((bf16[768,512]{1,0:T(8,128)(2,1)S(1)}, bf16[768,512]{1,0:T(8,128)(2,1)S(1)}, u32[]{:S(2)}, u32[]{:S(2)}) %collective-permute-start.31) | collective-permute-done | bytes 786464 | tf_op jit(solution)/shard_map/ppermute | solution.py:27
  552.5 14.0 %collective-permute-done.56.refs_15_ = bf16[768,512]{1,0:T(8,128)(2,1)} collective-permute-done((bf16[768,512]{1,0:T(8,128)(2,1)S(1)}, bf16[768,512]{1,0:T(8,128)(2,1)}, u32[]{:S(2)}, u32[]{:S(2)}) %collective-permute-start.56) | collective-permute-done | bytes 786464 | tf_op jit(solution)/shard_map/ppermute | solution.py:36
  601.0 9.3 %shard_map.44 = (bf16[2,4,768,768]{3,2,1,0:T(8,128)(2,1)}, bf16[768,512]{1,0:T(8,128)(2,1)S(1)}) custom-call(s32[13]{0:T(128)S(1)} %stack.55.spots, bf16[768,512]{1,0:T(8,128)(2,1)S(1)} %fusion.18.refs_0_.refs_12_, bf16[768,512]{1,0:T(8,128)(2,1)S(1)} %copy-done.11, ...), custom_call_target="tpu_custom_call", output_to_operand_aliasing={{0}: (20, {})} | custom-call | flops 4831838208 | bytes 12582912 | tf_op jit(solution)/shard_map/pallas_call | solution.py:136
  617.1 9.3 %shard_map.45 = (bf16[2,4,768,768]{3,2,1,0:T(8,128)(2,1)}, bf16[768,512]{1,0:T(8,128)(2,1)S(1)}) custom-call(s32[13]{0:T(128)S(1)} %stack.55.spots, bf16[768,512]{1,0:T(8,128)(2,1)S(1)} %fusion.18.refs_0_.refs_12_, bf16[768,512]{1,0:T(8,128)(2,1)S(1)} %copy-done.11, ...), custom_call_target="tpu_custom_call", output_to_operand_aliasing={{0}: (20, {})} | custom-call | flops 4831838208 | bytes 12582912 | tf_op jit(solution)/shard_map/pallas_call | solution.py:136
  634.3 9.3 %shard_map.46 = (bf16[2,4,768,768]{3,2,1,0:T(8,128)(2,1)}, bf16[768,512]{1,0:T(8,128)(2,1)S(1)}) custom-call(s32[13]{0:T(128)S(1)} %stack.55.spots, bf16[768,512]{1,0:T(8,128)(2,1)S(1)} %fusion.18.refs_0_.refs_12_, bf16[768,512]{1,0:T(8,128)(2,1)S(1)} %copy-done.11, ...), custom_call_target="tpu_custom_call", output_to_operand_aliasing={{0}: (20, {})} | custom-call | flops 4831838208 | bytes 12582912 | tf_op jit(solution)/shard_map/pallas_call | solution.py:136
  647.2 16.8 %collective-permute-done.70.refs_10_ = bf16[768,512]{1,0:T(8,128)(2,1)S(1)} collective-permute-done((bf16[768,512]{1,0:T(8,128)(2,1)S(1)}, bf16[768,512]{1,0:T(8,128)(2,1)S(1)}, u32[]{:S(2)}, u32[]{:S(2)}) %collective-permute-start.70) | collective-permute-done | bytes 786464 | tf_op jit(solution)/shard_map/ppermute | solution.py:27
  664.6 16.3 %collective-permute-done.61.refs_6_ = bf16[768,512]{1,0:T(8,128)(2,1)S(1)} collective-permute-done((bf16[768,512]{1,0:T(8,128)(2,1)S(1)}, bf16[768,512]{1,0:T(8,128)(2,1)S(1)}, u32[]{:S(2)}, u32[]{:S(2)}) %collective-permute-start.61) | collective-permute-done | bytes 786464 | tf_op jit(solution)/shard_map/ppermute | solution.py:27
  680.9 15.6 %collective-permute-done.52.refs_2_ = bf16[768,512]{1,0:T(8,128)(2,1)S(1)} collective-permute-done((bf16[768,512]{1,0:T(8,128)(2,1)S(1)}, bf16[768,512]{1,0:T(8,128)(2,1)S(1)}, u32[]{:S(2)}, u32[]{:S(2)}) %collective-permute-start.52) | collective-permute-done | bytes 786464 | tf_op jit(solution)/shard_map/ppermute | solution.py:27
  (279 shorter events, 247.6 us)
Async XLA Ops:
  142.2 136.4 %all-to-all-start.1 = ((bf16[16,96,1536]{2,1,0:T(8,128)(2,1)}), bf16[16,96,1536]{2,1,0:T(8,128)(2,1)}, u32[]{:S(2)}, u32[]{:S(2)}) async-start(bf16[16,96,1536]{2,1,0:T(8,128)(2,1)} %bitcast.23), calls=%async_computation.1 | async-start | bytes 9437184 | tf_op jit(solution)/shard_map/all_to_all | solution.py:176
  152.0 91.5 %collective-permute-start.9 = (bf16[768,512]{1,0:T(8,128)(2,1)S(1)}, bf16[768,512]{1,0:T(8,128)(2,1)S(1)}, u32[]{:S(2)}, u32[]{:S(2)}) collective-permute-start(bf16[768,512]{1,0:T(8,128)(2,1)S(1)} %fusion.27.refs_0_.refs_12_), channel_id=1, source_target_pairs={{4,0},{8,4},{12,8},{5,1},{9,5},{13,9},{6,2},{10,6},{14,10},{7,3},{... | collective-permute-start | bytes 2359304 | tf_op jit(solution)/shard_map/ppermute | solution.py:36
  153.3 90.2 %collective-permute-start.11 = (bf16[768,512]{1,0:T(8,128)(2,1)S(1)}, bf16[768,512]{1,0:T(8,128)(2,1)S(1)}, u32[]{:S(2)}, u32[]{:S(2)}) collective-permute-start(bf16[768,512]{1,0:T(8,128)(2,1)S(1)} %fusion.27.refs_0_.refs_12_), channel_id=1, source_target_pairs={{0,4},{4,8},{8,12},{1,5},{5,9},{9,13},{2,6},{6,10},{10,14},{3,7},{... | collective-permute-start | bytes 2359304 | tf_op jit(solution)/shard_map/ppermute | solution.py:36
  157.9 86.1 %collective-permute-start.20 = (bf16[768,512]{1,0:T(8,128)(2,1)S(1)}, bf16[768,512]{1,0:T(8,128)(2,1)S(1)}, u32[]{:S(2)}, u32[]{:S(2)}) collective-permute-start(bf16[768,512]{1,0:T(8,128)(2,1)S(1)} %fusion.27.refs_0_.refs_12_), channel_id=1, source_target_pairs={{0,2},{1,3},{2,0},{3,1},{4,6},{5,7},{6,4},{7,5},{8,10},{9,11},{10,... | collective-permute-start | bytes 2359304 | tf_op jit(solution)/shard_map/ppermute | solution.py:27
  162.1 82.3 %collective-permute-start.23 = (bf16[768,512]{1,0:T(8,128)(2,1)}, bf16[768,512]{1,0:T(8,128)(2,1)}, u32[]{:S(2)}, u32[]{:S(2)}) collective-permute-start(bf16[768,512]{1,0:T(8,128)(2,1)} %fusion.30.refs_4_.refs_12_), channel_id=1, source_target_pairs={{0,2},{1,3},{2,0},{3,1},{4,6},{5,7},{6,4},{7,5},{8,10},{9,11},{10,... | collective-permute-start | bytes 2359304 | tf_op jit(solution)/shard_map/ppermute | solution.py:27
  163.6 88.2 %collective-permute-start.26 = (bf16[768,512]{1,0:T(8,128)(2,1)S(1)}, bf16[768,512]{1,0:T(8,128)(2,1)S(1)}, u32[]{:S(2)}, u32[]{:S(2)}) collective-permute-start(bf16[768,512]{1,0:T(8,128)(2,1)S(1)} %fusion.33.refs_8_.refs_12_), channel_id=1, source_target_pairs={{0,2},{1,3},{2,0},{3,1},{4,6},{5,7},{6,4},{7,5},{8,10},{9,11},{10,... | collective-permute-start | bytes 2359304 | tf_op jit(solution)/shard_map/ppermute | solution.py:27
  243.5 40.7 %collective-permute-start.22 = (bf16[768,512]{1,0:T(8,128)(2,1)}, bf16[768,512]{1,0:T(8,128)(2,1)}, u32[]{:S(2)}, u32[]{:S(2)}) collective-permute-start(bf16[768,512]{1,0:T(8,128)(2,1)} %fusion.30.refs_4_.refs_12_), channel_id=1, source_target_pairs={{0,1},{1,0},{2,3},{3,2},{4,5},{5,4},{6,7},{7,6},{8,9},{9,8},{10,11... | collective-permute-start | bytes 2359304 | tf_op jit(solution)/shard_map/ppermute | solution.py:27
  244.0 45.1 %collective-permute-start.25 = (bf16[768,512]{1,0:T(8,128)(2,1)S(1)}, bf16[768,512]{1,0:T(8,128)(2,1)}, u32[]{:S(2)}, u32[]{:S(2)}) collective-permute-start(bf16[768,512]{1,0:T(8,128)(2,1)S(1)} %fusion.33.refs_8_.refs_12_), channel_id=1, source_target_pairs={{0,1},{1,0},{2,3},{3,2},{4,5},{5,4},{6,7},{7,6},{8,9},{9,8},{10,11... | collective-permute-start | bytes 2359304 | tf_op jit(solution)/shard_map/ppermute | solution.py:27
  244.4 47.4 %collective-permute-start.33 = (bf16[768,512]{1,0:T(8,128)(2,1)}, bf16[768,512]{1,0:T(8,128)(2,1)S(1)}, u32[]{:S(2)}, u32[]{:S(2)}) collective-permute-start(bf16[768,512]{1,0:T(8,128)(2,1)} %fusion.30.refs_4_.refs_12_), channel_id=1, source_target_pairs={{4,0},{8,4},{12,8},{5,1},{9,5},{13,9},{6,2},{10,6},{14,10},{7,3},{... | collective-permute-start | bytes 2359304 | tf_op jit(solution)/shard_map/ppermute | solution.py:36
  251.8 45.3 %collective-permute-start.34 = (bf16[768,512]{1,0:T(8,128)(2,1)}, bf16[768,512]{1,0:T(8,128)(2,1)}, u32[]{:S(2)}, u32[]{:S(2)}) collective-permute-start(bf16[768,512]{1,0:T(8,128)(2,1)} %fusion.30.refs_4_.refs_12_), channel_id=1, source_target_pairs={{0,4},{4,8},{8,12},{1,5},{5,9},{9,13},{2,6},{6,10},{10,14},{3,7},{... | collective-permute-start | bytes 2359304 | tf_op jit(solution)/shard_map/ppermute | solution.py:36
  297.1 44.7 %collective-permute-start.1 = (bf16[768,512]{1,0:T(8,128)(2,1)S(1)}, bf16[768,512]{1,0:T(8,128)(2,1)}, u32[]{:S(2)}, u32[]{:S(2)}) collective-permute-start(bf16[768,512]{1,0:T(8,128)(2,1)S(1)} %fusion.18.refs_0_.refs_12_), channel_id=1, source_target_pairs={{0,2},{1,3},{2,0},{3,1},{4,6},{5,7},{6,4},{7,5},{8,10},{9,11},{10,... | collective-permute-start | bytes 2359304 | tf_op jit(solution)/shard_map/ppermute | solution.py:27
  392.1 42.3 %collective-permute-start.38 = (bf16[768,512]{1,0:T(8,128)(2,1)}, bf16[768,512]{1,0:T(8,128)(2,1)}, u32[]{:S(2)}, u32[]{:S(2)}) collective-permute-start(bf16[768,512]{1,0:T(8,128)(2,1)} %collective-permute-done.36.refs_16_), channel_id=1, source_target_pairs={{8,12},{9,13},{10,14},{11,15},{24,28},{25,29},{26,30},{27,31}} | collective-permute-start | bytes 2359304 | tf_op jit(solution)/shard_map/ppermute | solution.py:36
  404.4 44.8 %collective-permute-start.46 = (bf16[768,512]{1,0:T(8,128)(2,1)}, bf16[768,512]{1,0:T(8,128)(2,1)}, u32[]{:S(2)}, u32[]{:S(2)}) collective-permute-start(bf16[768,512]{1,0:T(8,128)(2,1)} %copy-done.23), channel_id=1, source_target_pairs={{4,0},{5,1},{6,2},{7,3},{20,16},{21,17},{22,18},{23,19}} | collective-permute-start | bytes 2359304 | tf_op jit(solution)/shard_map/ppermute | solution.py:36
  405.7 58.7 %collective-permute-start.47 = (bf16[768,512]{1,0:T(8,128)(2,1)}, bf16[768,512]{1,0:T(8,128)(2,1)}, u32[]{:S(2)}, u32[]{:S(2)}) collective-permute-start(bf16[768,512]{1,0:T(8,128)(2,1)} %copy-done.25), channel_id=1, source_target_pairs={{8,12},{9,13},{10,14},{11,15},{24,28},{25,29},{26,30},{27,31}} | collective-permute-start | bytes 2359304 | tf_op jit(solution)/shard_map/ppermute | solution.py:36
  427.1 49.2 %collective-permute-start.13 = (bf16[768,512]{1,0:T(8,128)(2,1)S(1)}, bf16[768,512]{1,0:T(8,128)(2,1)S(1)}, u32[]{:S(2)}, u32[]{:S(2)}) collective-permute-start(bf16[768,512]{1,0:T(8,128)(2,1)S(1)} %fusion.18.refs_0_.refs_12_), channel_id=1, source_target_pairs={{4,0},{8,4},{12,8},{5,1},{9,5},{13,9},{6,2},{10,6},{14,10},{7,3},{... | collective-permute-start | bytes 2359304 | tf_op jit(solution)/shard_map/ppermute | solution.py:36
  428.4 53.2 %collective-permute-start.14 = (bf16[768,512]{1,0:T(8,128)(2,1)S(1)}, bf16[768,512]{1,0:T(8,128)(2,1)S(1)}, u32[]{:S(2)}, u32[]{:S(2)}) collective-permute-start(bf16[768,512]{1,0:T(8,128)(2,1)S(1)} %fusion.18.refs_0_.refs_12_), channel_id=1, source_target_pairs={{0,4},{4,8},{8,12},{1,5},{5,9},{9,13},{2,6},{6,10},{10,14},{3,7},{... | collective-permute-start | bytes 2359304 | tf_op jit(solution)/shard_map/ppermute | solution.py:36
  434.4 48.9 %collective-permute-start.54 = (bf16[768,512]{1,0:T(8,128)(2,1)S(1)}, bf16[768,512]{1,0:T(8,128)(2,1)S(1)}, u32[]{:S(2)}, u32[]{:S(2)}) collective-permute-start(bf16[768,512]{1,0:T(8,128)(2,1)S(1)} %fusion.21.refs_4_.refs_12_), channel_id=1, source_target_pairs={{4,0},{8,4},{12,8},{5,1},{9,5},{13,9},{6,2},{10,6},{14,10},{7,3},{... | collective-permute-start | bytes 2359304 | tf_op jit(solution)/shard_map/ppermute | solution.py:36
  531.5 45.0 %collective-permute-start.57 = (bf16[768,512]{1,0:T(8,128)(2,1)}, bf16[768,512]{1,0:T(8,128)(2,1)}, u32[]{:S(2)}, u32[]{:S(2)}) collective-permute-start(bf16[768,512]{1,0:T(8,128)(2,1)} %collective-permute-done.55.refs_14_), channel_id=1, source_target_pairs={{4,8},{8,12},{5,9},{9,13},{6,10},{10,14},{7,11},{11,15},{20,24},{2... | collective-permute-start | bytes 2359304 | tf_op jit(solution)/shard_map/ppermute | solution.py:36
  533.1 50.3 %collective-permute-start.65 = (bf16[768,512]{1,0:T(8,128)(2,1)}, bf16[768,512]{1,0:T(8,128)(2,1)}, u32[]{:S(2)}, u32[]{:S(2)}) collective-permute-start(bf16[768,512]{1,0:T(8,128)(2,1)} %collective-permute-done.63.refs_13_), channel_id=1, source_target_pairs={{4,0},{8,4},{5,1},{9,5},{6,2},{10,6},{7,3},{11,7},{20,16},{24,20},... | collective-permute-start | bytes 2359304 | tf_op jit(solution)/shard_map/ppermute | solution.py:36
  549.6 43.6 %collective-permute-start.66 = (bf16[768,512]{1,0:T(8,128)(2,1)}, bf16[768,512]{1,0:T(8,128)(2,1)}, u32[]{:S(2)}, u32[]{:S(2)}) collective-permute-start(bf16[768,512]{1,0:T(8,128)(2,1)} %collective-permute-done.64.refs_14_), channel_id=1, source_target_pairs={{4,8},{8,12},{5,9},{9,13},{6,10},{10,14},{7,11},{11,15},{20,24},{2... | collective-permute-start | bytes 2359304 | tf_op jit(solution)/shard_map/ppermute | solution.py:36
  551.2 49.0 %collective-permute-start.17 = (bf16[768,512]{1,0:T(8,128)(2,1)}, bf16[768,512]{1,0:T(8,128)(2,1)}, u32[]{:S(2)}, u32[]{:S(2)}) collective-permute-start(bf16[768,512]{1,0:T(8,128)(2,1)} %collective-permute-done.15.refs_15_), channel_id=1, source_target_pairs={{4,0},{5,1},{6,2},{7,3},{20,16},{21,17},{22,18},{23,19}} | collective-permute-start | bytes 2359304 | tf_op jit(solution)/shard_map/ppermute | solution.py:36
  576.5 40.5 %collective-permute-start.58 = (bf16[768,512]{1,0:T(8,128)(2,1)}, bf16[768,512]{1,0:T(8,128)(2,1)}, u32[]{:S(2)}, u32[]{:S(2)}) collective-permute-start(bf16[768,512]{1,0:T(8,128)(2,1)} %collective-permute-done.56.refs_15_), channel_id=1, source_target_pairs={{4,0},{5,1},{6,2},{7,3},{20,16},{21,17},{22,18},{23,19}} | collective-permute-start | bytes 2359304 | tf_op jit(solution)/shard_map/ppermute | solution.py:36
  645.7 50.8 %collective-permute-start.52 = (bf16[768,512]{1,0:T(8,128)(2,1)S(1)}, bf16[768,512]{1,0:T(8,128)(2,1)S(1)}, u32[]{:S(2)}, u32[]{:S(2)}) collective-permute-start(bf16[768,512]{1,0:T(8,128)(2,1)S(1)} %get-tuple-element.31.refs_0_), channel_id=1, source_target_pairs={{0,2},{1,3},{2,0},{3,1},{4,6},{5,7},{6,4},{7,5},{8,10},{9,11},{10,... | collective-permute-start | bytes 2359304 | tf_op jit(solution)/shard_map/ppermute | solution.py:27
  647.2 49.3 %collective-permute-start.60 = (bf16[768,512]{1,0:T(8,128)(2,1)S(1)}, bf16[768,512]{1,0:T(8,128)(2,1)S(1)}, u32[]{:S(2)}, u32[]{:S(2)}) collective-permute-start(bf16[768,512]{1,0:T(8,128)(2,1)S(1)} %get-tuple-element.34.refs_4_), channel_id=1, source_target_pairs={{0,1},{1,0},{2,3},{3,2},{4,5},{5,4},{6,7},{7,6},{8,9},{9,8},{10,11... | collective-permute-start | bytes 2359304 | tf_op jit(solution)/shard_map/ppermute | solution.py:27
  (111 other events, 2241.8 us)

commit v3 on v1

v3 whole, which is shorter than its diff:
```python
import functools
import math

import jax
import jax.numpy as jnp
from jax import lax
from jax.experimental import pallas as pl
from jax.experimental.pallas import tpu as pltpu
from jax.sharding import PartitionSpec as P

NS = 3072
FREQ = 2
THIRDS = 3
BF16 = jnp.bfloat16
F32 = jnp.float32


def hop(pair, k, n_row):
    down = [(r, r - 1) for r in range(1, n_row) if r + k - 1 < n_row]
    up = [(r, r + 1) for r in range(n_row - 1) if r - k + 1 >= 0]
    return lax.ppermute(pair[0], "row", down), lax.ppermute(pair[1], "row", up)


def bin_kernel(picker, data, out):
    n_row, cap = out.shape[0], out.shape[2]
    sub = data.shape[2]
    for p in range(2):
        rows = jnp.dot(picker[...], data[p], preferred_element_type=F32).astype(BF16)
        for b in range(n_row):
            out[b, 0, :, p * sub : (p + 1) * sub] = rows[b * cap : (b + 1) * cap]


def bin_rows(picker, data, f, thirds, n_row, n_col):
    planes, own_cap, order = data.shape
    cap = picker.shape[0] // n_row
    sub = order // n_col // THIRDS
    count, first = len(thirds), thirds[0]
    return pl.pallas_call(
        bin_kernel,
        grid=(n_col, count),
        in_specs=[
            pl.BlockSpec(picker.shape, lambda c, j: (0, 0)),
            pl.BlockSpec((2, own_cap, sub), lambda c, j: (f, 0, c * THIRDS + first + j)),
        ],
        out_specs=pl.BlockSpec((n_row, 1, cap, 2 * sub), lambda c, j: (0, c, 0, j)),
        out_shape=jax.ShapeDtypeStruct((n_row, n_col, cap, 2 * sub * count), BF16),
        compiler_params=pltpu.CompilerParams(vmem_limit_bytes=16 * 2**20),
        cost_estimate=pl.CostEstimate(
            flops=4 * picker.shape[0] * own_cap * n_col * count * sub,
            bytes_accessed=8 * own_cap * n_col * count * sub,
            transcendentals=0,
        ),
    )(picker, data)


def product_kernel(opts, at_row, *refs):
    plan, thirds, order, weight = opts["plan"], opts["thirds"], opts["order"], opts["weight"]
    lefts, refs = refs[: len(thirds)], refs[len(thirds) :]
    sources, refs = refs[: len(plan)], refs[len(plan) :]
    before = refs[0] if opts["before"] else None
    *outs, right, sems = refs[opts["before"] + opts["held"] :]
    row = at_row[0]
    block = sources[0].shape[0]

    @pl.when(pl.program_id(0) == 0)
    def _():
        for phase in range(2):
            for s, (low, high, step) in enumerate(plan):

                @pl.when((row >= low) & (row <= high))
                def _(s=s, step=step):
                    start = pl.multiple_of((row + step) * block if len(plan) > 1 else 0, 32)
                    copy = pltpu.make_async_copy(sources[s], right.at[pl.ds(start, block)], sems.at[s])
                    if phase == 0:
                        copy.start()
                    else:
                        copy.wait()

    sub = right.shape[1] // 2
    real_left, imag_left, parts = [], [], []
    for c in range(lefts[0].shape[0]):
        for left, group in zip(lefts, thirds):
            for k, j in enumerate(group):
                real_left.append(left[c, :, 2 * k * sub : (2 * k + 1) * sub])
                imag_left.append(left[c, :, (2 * k + 1) * sub : (2 * k + 2) * sub])
                parts.append((c * THIRDS + j) * sub)
    if len(parts) * sub == NS and parts == sorted(parts):
        rows = right[...]
    else:
        rows = jnp.concatenate([right[p : p + sub] for p in parts], axis=0)
    by_real = jnp.dot(jnp.concatenate(real_left, axis=1), rows, preferred_element_type=F32)
    by_imag = jnp.dot(jnp.concatenate(imag_left, axis=1), rows, preferred_element_type=F32)
    real = by_real[:, :sub] - by_imag[:, sub:]
    imag = by_real[:, sub:] + by_imag[:, :sub]
    if before is not None:
        real = real + before[:, :sub]
        imag = imag + before[:, sub:]
    if order is None:
        outs[0][:, :sub] = real
        outs[0][:, sub:] = imag
        return
    real = (real * weight).astype(BF16)
    imag = (imag * weight).astype(BF16)
    outs[0][0, 0] = real
    outs[0][0, 1] = imag
    if len(outs) > 1:
        outs[1][:, :sub] = real
        outs[1][:, sub:] = imag


def complex_product(row, lefts, right, shape, held, at, before=None, piece_at=(0, 1)):
    plan, sources = right
    thirds = [group for _, group in lefts]
    lefts = [a for a, _ in lefts]
    n_col, rows, _ = lefts[0].shape
    tile = 256 if rows % 256 == 0 else rows
    wide = sources[0].shape[1]
    sub = wide // 2
    order = None
    if at is None:
        out_specs = [pl.BlockSpec((tile, wide), lambda i, s: (i, 0))]
        out_shape = [jax.ShapeDtypeStruct((rows, wide), F32)]
    else:
        order, f, j = at
        out_specs = [pl.BlockSpec((1, 2, tile, sub), lambda i, s: (order, f, i, j))]
        out_shape = [jax.ShapeDtypeStruct(shape, BF16)]
        if order == 0:
            which, of = piece_at
            out_specs.append(pl.BlockSpec((tile, wide), lambda i, s: (i, which)))
            out_shape.append(jax.ShapeDtypeStruct((rows, of * wide), BF16))
    in_specs = [pl.BlockSpec((n_col, tile, a.shape[2]), lambda i, s: (0, i, 0)) for a in lefts]
    in_specs += [pl.BlockSpec(memory_space=pl.ANY)] * len(sources)
    args = [*lefts, *sources]
    if before is not None:
        in_specs.append(pl.BlockSpec((tile, wide), lambda i, s: (i, 0)))
        args.append(before)
    aliases = {1 + len(args) + k: k for k in range(len(held))}
    in_specs += [pl.BlockSpec(memory_space=pl.ANY)] * len(held)
    depth = sum(len(g) for g in thirds) * n_col * sub
    opts = dict(
        plan=plan,
        thirds=thirds,
        order=order,
        weight=1.0 / math.sqrt(2.0 * NS),
        before=int(before is not None),
        held=len(held),
    )
    return pl.pallas_call(
        functools.partial(product_kernel, opts),
        grid_spec=pltpu.PrefetchScalarGridSpec(
            num_scalar_prefetch=1,
            grid=(rows // tile,),
            in_specs=in_specs,
            out_specs=out_specs,
            scratch_shapes=[pltpu.VMEM((NS, wide), BF16), pltpu.SemaphoreType.DMA((len(plan),))],
        ),
        out_shape=out_shape,
        input_output_aliases=aliases,
        compiler_params=pltpu.CompilerParams(vmem_limit_bytes=48 * 2**20),
        cost_estimate=pl.CostEstimate(
            flops=4 * rows * depth * wide, bytes_accessed=2 * NS * wide + 4 * rows * depth, transcendentals=0
        ),
    )(row, *args, *held)


def per_device(acq_data, grid_row, counts):
    n_row = lax.axis_size("row")
    n_col = lax.axis_size("col")
    own_cap, planes, order = acq_data.shape
    block_rows = order // n_row
    tile_cols = order // n_col
    cap = own_cap // n_row
    slots = n_row * cap
    wide = 2 * tile_cols // THIRDS
    everything = tuple(range(THIRDS))

    slot_index = jnp.arange(own_cap, dtype=jnp.int32)
    block = jnp.where(slot_index < counts[0], grid_row // block_rows, n_row)
    earlier = (block[None, :] == block[:, None]) & (slot_index[None, :] < slot_index[:, None])
    rank = jnp.sum(earlier.astype(jnp.int32), axis=1)
    leaving = jnp.where(block < n_row, block * cap + rank, -1)
    hit = jnp.arange(slots, dtype=jnp.int32)[:, None] == leaving[None, :]
    spots = jnp.sum(jnp.where(hit, (grid_row % block_rows)[None, :] + 1, 0), axis=1) - 1
    labels = jnp.broadcast_to(spots.reshape(n_row, 1, cap), (n_row, n_col, cap))
    places = lax.all_to_all(
        labels.reshape(n_row * n_col, cap), ("row", "col"), split_axis=0, concat_axis=0, tiled=True
    ).reshape(-1)
    picker = hit.astype(BF16)
    placer = (jnp.arange(block_rows, dtype=jnp.int32)[:, None] == places[None, :]).astype(BF16)
    data = jnp.transpose(acq_data, (1, 0, 2))

    tiles = {}
    lefts = [[], []]
    for f, group in ((0, (0,)), (0, (1, 2)), (1, everything)):
        sent = bin_rows(picker, data, f, group, n_row, n_col)
        got = lax.all_to_all(
            sent.reshape(n_row * n_col, cap, wide * len(group)), ("row", "col"), split_axis=0, concat_axis=0, tiled=True
        ).reshape(-1, wide * len(group))
        tile = jnp.dot(placer, got, preferred_element_type=F32).astype(BF16)
        lefts[f].append((lax.all_gather(tile, "col", axis=0), group))
        for k, j in enumerate(group):
            tiles[f, j] = tile[:, k * wide : (k + 1) * wide]

    rights = {}
    plan = [(0, n_row - 1, 0)]
    if n_row <= 4:
        for k in range(1, n_row):
            plan += [(0, n_row - 1 - k, k), (k, n_row - 1, -k)]
        for key, tile in tiles.items():
            found = [tile]
            pair = (tile, tile)
            for k in range(1, n_row):
                pair = hop(pair, k, n_row)
                found += list(pair)
            rights[key] = (plan, found)
    else:
        for key, tile in tiles.items():
            rights[key] = (plan, [lax.all_gather(tile, "row", axis=0, tiled=True)])

    row = lax.axis_index("row").astype(jnp.int32).reshape(1)
    shape = (2, planes, block_rows, tile_cols)
    result = ()
    piece = ()
    for j in everything:
        result, piece = complex_product(row, lefts[0], rights[0, j], shape, (*result, *piece), (0, 0, j), piece_at=(j, 3))
        result, piece = (result,), (piece,)
    gathered = [(lax.all_gather(piece[0], "col", axis=0), everything)]
    for j in everything:
        result = complex_product(row, gathered, rights[0, j], shape, result, (1, 0, j))
    gathered = []
    for j in everything:
        *result, piece = complex_product(row, lefts[1], rights[1, j], shape, result, (0, 1, j))
        gathered.append((lax.all_gather(piece, "col", axis=0), (j,)))
    sums = []
    for j in everything:
        sums += complex_product(row, gathered[:2], rights[1, j], shape, (), None)
    for j in everything:
        result = complex_product(row, gathered[2:], rights[1, j], shape, result, (1, 1, j), before=sums[j])
    return result[0]


def solution(mesh):
    placed = (
        P(("groups", "row", "col"), None, None),
        P(("groups", "row", "col")),
        P(("groups", "row", "col")),
    )
    return jax.shard_map(
        per_device,
        mesh=mesh,
        in_specs=placed,
        out_specs=P("groups", None, "row", "col"),
        check_vma=False,
    )
```

time: 785 us -> 726 us (0.925)
  waiting for transfers between devices: 432 us -> 275 us
  blocking collectives: 0 us -> 111 us
  local copies, waits for them, and re-layouts: 127 us -> 55.1 us
  Pallas kernels: 91.6 us -> 145 us
  starting transfers between devices: 59.1 us -> 106 us
  other arithmetic: 23.9 us -> 1.86 us
  matrix products: 27.5 us -> 14.5 us
    all_to_all x2, waiting for transfers between devices: 220 us -> 77.4 us  [per_device(): lax.all_to_all(sent.reshape(n_row * n_col, cap, wide * len(group)), ('row...]
    all_to_all x0 -> x1, blocking collectives: none -> 111 us  [per_device(): lax.all_to_all(sent.reshape(n_row * n_col, cap, wide * len(group)), ('row...]
    all_gather x6 -> x7, waiting for transfers between devices: 78.2 us -> 4.07 us  [the longest x3 4.04 us: per_device(): gathered.append((lax.all_gather(piece, 'col', axis=0), (j,)))]
    ppermute x24 -> x36, starting transfers between devices: 23.5 us -> 83.1 us  [the longest x18 60 us: hop(): lax.ppermute(pair[1], 'row', up)]
    ppermute x24 -> x36, waiting for transfers between devices: 134 us -> 193 us  [the longest x18 193 us: hop(): lax.ppermute(pair[0], 'row', down)]
    reshape x6 -> x0, local copies, waits for them, and re-layouts: 56.1 us -> none  [the longest x4 33.6 us: per_device(): sent.reshape(n_row, cap, 2, n_col, tile_cols).transpose(0, 3, 1, 2, 4)]
    pallas_call x12 -> x18, Pallas kernels: 91.6 us -> 145 us  [the longest x15 131 us: complex_product(): pl.pallas_call(functools.partial(product_kernel, opts), grid_spec=pltpu.P...]
    slice x15 -> x2, local copies, waits for them, and re-layouts: 23.3 us -> 3.25 us  [per_device(): tiles[f, j] = tile[:, k * wide:(k + 1) * wide]]
  transfers between devices with their start and end apart: 33 -> 46, of which waited for: 9 -> 19; matrix products, arithmetic and copies ran while one was open for 17% -> 4% of each run, Pallas kernels for 9% -> 14%
where the time goes in v3:
time: 726 us; the launch traced here: 723 us
  waiting for transfers between devices  275 us (38%)
  Pallas kernels  145 us (20%)
  blocking collectives  111 us (15%)
  starting transfers between devices  106 us (15%)
  local copies, waits for them, and re-layouts  55.1 us (8%)
  between operations  15.2 us (2%)
  matrix products  14.5 us (2%)
    ppermute x18, waiting for transfers between devices, hop(): lax.ppermute(pair[0], 'row', down)  193 us
    pallas_call x15, Pallas kernels, complex_product(): pl.pallas_call(functools.partial(product_kernel, opts), grid_spec=pltpu.P...  131 us
    all_to_all x1, blocking collectives, per_device(): lax.all_to_all(sent.reshape(n_row * n_col, cap, wide * len(group)), ('row...  111 us
    all_to_all x2, waiting for transfers between devices, per_device(): lax.all_to_all(sent.reshape(n_row * n_col, cap, wide * len(group)), ('row...  77.4 us
    ppermute x18, starting transfers between devices, hop(): lax.ppermute(pair[1], 'row', up)  60 us
    unnamed x123, local copies, waits for them, and re-layouts  50.5 us
    ppermute x18, starting transfers between devices, hop(): lax.ppermute(pair[0], 'row', down)  23.1 us
    all_to_all x2, starting transfers between devices, per_device(): lax.all_to_all(sent.reshape(n_row * n_col, cap, wide * len(group)), ('row...  15.1 us
  transfers between devices with their start and end apart: 46, of which 19 were waited for; matrix products, arithmetic and copies ran while one was open for 4% of the time, Pallas kernels for 14%

profile of v3, /device:TPU:0, one launch (start us, length us, event | category | flops | bytes accessed | tf_op | source)
XLA Modules:
  0.0 723.2 jit_solution(14384005198663106055)
XLA Ops:
  16.4 10.4 %copy.21 = bf16[384,4,3072]{2,0,1:T(8,128)(2,1)} copy(bf16[384,4,3072]{2,1,0:T(4,128)(2,1)} %param.3) | data formatting | bytes 18874368 | tf_op args[0]
  48.3 23.1 %all-to-all-done.2 = bf16[16,96,512]{2,1,0:T(8,128)(2,1)S(1)} async-done(((bf16[16,96,512]{2,1,0:T(8,128)(2,1)}), bf16[16,96,512]{2,1,0:T(8,128)(2,1)S(1)}, u32[]{:S(2)}, u32[]{:S(2)}) %all-to-all-start.2) | async-done | bytes 1572896 | tf_op jit(solution)/shard_map/all_to_all | solution.py:196
  86.8 54.3 %all-to-all-done.3 = bf16[16,96,1024]{2,1,0:T(8,128)(2,1)S(1)} async-done(((bf16[16,96,1024]{2,1,0:T(8,128)(2,1)}), bf16[16,96,1024]{2,1,0:T(8,128)(2,1)S(1)}, u32[]{:S(2)}, u32[]{:S(2)}) %all-to-all-start.3) | async-done | bytes 3145760 | tf_op jit(solution)/shard_map/all_to_all | solution.py:196
  149.9 13.5 %collective-permute-start.31 = (bf16[768,512]{1,0:T(8,128)(2,1)S(1)}, bf16[768,512]{1,0:T(8,128)(2,1)S(1)}, u32[]{:S(2)}, u32[]{:S(2)}) collective-permute-start(bf16[768,512]{1,0:T(8,128)(2,1)S(1)} %copy-done.42), channel_id=1, source_target_pairs={{0,4},{4,8},{8,12},{1,5},{5,9},{9,13},{2,6},{6,10},{10,14},{3,7},{... | collective-permute-start | bytes 2359304 | tf_op jit(solution)/shard_map/ppermute | solution.py:21
  163.4 15.4 %collective-permute-done.30.refs_3_.refs_2_ = bf16[768,512]{1,0:T(8,128)(2,1)S(1)} collective-permute-done((bf16[768,512]{1,0:T(8,128)(2,1)S(1)}, bf16[768,512]{1,0:T(8,128)(2,1)S(1)}, u32[]{:S(2)}, u32[]{:S(2)}) %collective-permute-start.30) | collective-permute-done | bytes 786464 | tf_op jit(solution)/shard_map/ppermute | solution.py:21
  209.3 9.8 %collective-permute-done.24.refs_3_.refs_2_ = bf16[768,512]{1,0:T(8,128)(2,1)S(1)} collective-permute-done((bf16[768,512]{1,0:T(8,128)(2,1)S(1)}, bf16[768,512]{1,0:T(8,128)(2,1)S(1)}, u32[]{:S(2)}, u32[]{:S(2)}) %collective-permute-start.24) | collective-permute-done | bytes 786464 | tf_op jit(solution)/shard_map/ppermute | solution.py:21
  222.8 13.2 %collective-permute-done.18.refs_3_.refs_2_ = bf16[768,512]{1,0:T(8,128)(2,1)} collective-permute-done((bf16[768,512]{1,0:T(8,128)(2,1)S(1)}, bf16[768,512]{1,0:T(8,128)(2,1)}, u32[]{:S(2)}, u32[]{:S(2)}) %collective-permute-start.18) | collective-permute-done | bytes 786464 | tf_op jit(solution)/shard_map/ppermute | solution.py:21
  238.9 13.9 %collective-permute-done.34.refs_7_.refs_6_ = bf16[768,512]{1,0:T(8,128)(2,1)S(1)} collective-permute-done((bf16[768,512]{1,0:T(8,128)(2,1)S(1)}, bf16[768,512]{1,0:T(8,128)(2,1)S(1)}, u32[]{:S(2)}, u32[]{:S(2)}) %collective-permute-start.34) | collective-permute-done | bytes 786464 | tf_op jit(solution)/shard_map/ppermute | solution.py:21
  255.3 14.5 %collective-permute-done.26.refs_5_.refs_4_ = bf16[768,512]{1,0:T(8,128)(2,1)} collective-permute-done((bf16[768,512]{1,0:T(8,128)(2,1)S(1)}, bf16[768,512]{1,0:T(8,128)(2,1)}, u32[]{:S(2)}, u32[]{:S(2)}) %collective-permute-start.26) | collective-permute-done | bytes 786464 | tf_op jit(solution)/shard_map/ppermute | solution.py:21
  272.7 14.0 %collective-permute-done.20.refs_5_.refs_4_ = bf16[768,512]{1,0:T(8,128)(2,1)} collective-permute-done((bf16[768,512]{1,0:T(8,128)(2,1)}, bf16[768,512]{1,0:T(8,128)(2,1)}, u32[]{:S(2)}, u32[]{:S(2)}) %collective-permute-start.20) | collective-permute-done | bytes 786464 | tf_op jit(solution)/shard_map/ppermute | solution.py:21
  303.5 10.2 %shard_map.41 = (bf16[2,4,768,768]{3,2,1,0:T(8,128)(2,1)}, bf16[768,1536]{1,0:T(8,128)(2,1)}) custom-call(s32[1]{0:T(128)} %bitcast.at_row, bf16[4,768,512]{2,1,0:T(8,128)(2,1)} %bitcast.46, bf16[4,768,1024]{2,1,0:T(8,128)(2,1)} %bitcast.43, bf16[768,512]{1,0:T(8,128)(2,1)S(1)} %get-tuple-element.32.refs_2_.refs_1_, ...), custom_call_target="tpu_custom_call", output_to_operand_aliasing={{0}: (10, {}), {1}: (11, {})} | custom-call | flops 4831838208 | bytes 12582912 | tf_op jit(solution)/shard_map/pallas_call | solution.py:148
  318.7 10.4 %shard_map.42 = (bf16[2,4,768,768]{3,2,1,0:T(8,128)(2,1)}, bf16[768,1536]{1,0:T(8,128)(2,1)}) custom-call(s32[1]{0:T(128)} %bitcast.at_row, bf16[4,768,512]{2,1,0:T(8,128)(2,1)} %bitcast.47, bf16[4,768,1024]{2,1,0:T(8,128)(2,1)} %bitcast.44, bf16[768,512]{1,0:T(8,128)(2,1)S(1)} %get-tuple-element.33.refs_2_.refs_1_, ...), custom_call_target="tpu_custom_call", output_to_operand_aliasing={{0}: (10, {}), {1}: (11, {})} | custom-call | flops 4831838208 | bytes 12582912 | tf_op jit(solution)/shard_map/pallas_call | solution.py:148
  338.3 111.2 %all_to_all.24 = bf16[16,96,1536]{2,1,0:T(8,128)(2,1)S(1)} all-to-all(bf16[16,96,1536]{2,1,0:T(8,128)(2,1)S(1)} %bitcast.26), channel_id=1, replica_groups=mesh['groups'=2,'row'=4,'col'=4] {'row','col'}, dimensions={0} | all-to-all | bytes 9437184 | tf_op jit(solution)/shard_map/all_to_all | solution.py:196
  468.3 10.5 %collective-permute-done.12.refs_2_.refs_3_ = bf16[768,512]{1,0:T(8,128)(2,1)S(1)} collective-permute-done((bf16[768,512]{1,0:T(8,128)(2,1)S(1)}, bf16[768,512]{1,0:T(8,128)(2,1)S(1)}, u32[]{:S(2)}, u32[]{:S(2)}) %collective-permute-start.12) | collective-permute-done | bytes 786464 | tf_op jit(solution)/shard_map/ppermute | solution.py:21
  483.4 12.3 %collective-permute-done.6.refs_2_.refs_3_ = bf16[768,512]{1,0:T(8,128)(2,1)S(1)} collective-permute-done((bf16[768,512]{1,0:T(8,128)(2,1)S(1)}, bf16[768,512]{1,0:T(8,128)(2,1)S(1)}, u32[]{:S(2)}, u32[]{:S(2)}) %collective-permute-start.6) | collective-permute-done | bytes 786464 | tf_op jit(solution)/shard_map/ppermute | solution.py:21
  500.3 12.3 %collective-permute-done.14.refs_4_.refs_5_ = bf16[768,512]{1,0:T(8,128)(2,1)} collective-permute-done((bf16[768,512]{1,0:T(8,128)(2,1)S(1)}, bf16[768,512]{1,0:T(8,128)(2,1)}, u32[]{:S(2)}, u32[]{:S(2)}) %collective-permute-start.14) | collective-permute-done | bytes 786464 | tf_op jit(solution)/shard_map/ppermute | solution.py:21
  515.5 14.0 %collective-permute-done.8.refs_4_.refs_5_ = bf16[768,512]{1,0:T(8,128)(2,1)} collective-permute-done((bf16[768,512]{1,0:T(8,128)(2,1)S(1)}, bf16[768,512]{1,0:T(8,128)(2,1)}, u32[]{:S(2)}, u32[]{:S(2)}) %collective-permute-start.8) | collective-permute-done | bytes 786464 | tf_op jit(solution)/shard_map/ppermute | solution.py:21
  546.7 10.0 %shard_map.44.refs_8_ = bf16[2,4,768,768]{3,2,1,0:T(8,128)(2,1)} custom-call(s32[1]{0:T(128)} %bitcast.at_row, bf16[4,768,1536]{2,1,0:T(8,128)(2,1)} %bitcast.28, bf16[768,512]{1,0:T(8,128)(2,1)S(1)} %copy-done.4, bf16[768,512]{1,0:T(8,128)(2,1)S(1)} %copy-done.38, bf16[768,512]{1,0:T(8,128)(2,1)S(1)} %copy-done.41, ...), custom_call_target="tpu_custom_call", output_to_operand_aliasing={{}: (9, {})} | custom-call | flops 4831838208 | bytes 12582912 | tf_op jit(solution)/shard_map/pallas_call | solution.py:148
  556.6 10.1 %shard_map.45.refs_8_ = bf16[2,4,768,768]{3,2,1,0:T(8,128)(2,1)} custom-call(s32[1]{0:T(128)} %bitcast.at_row, bf16[4,768,1536]{2,1,0:T(8,128)(2,1)} %bitcast.29, bf16[768,512]{1,0:T(8,128)(2,1)S(1)} %get-tuple-element.33.refs_2_.refs_1_, bf16[768,512]{1,0:T(8,128)(2,1)} %collective-permute-done.18.refs_3_.refs_2_, ...), custom_call_target="tpu_custom_call", output_to_operand_aliasing={{}: (9, {})} | custom-call | flops 4831838208 | bytes 12582912 | tf_op jit(solution)/shard_map/pallas_call | solution.py:148
  569.1 10.2 %shard_map.46 = (bf16[2,4,768,768]{3,2,1,0:T(8,128)(2,1)}, bf16[768,512]{1,0:T(8,128)(2,1)S(1)}) custom-call(s32[1]{0:T(128)} %bitcast.at_row, bf16[4,768,1536]{2,1,0:T(8,128)(2,1)} %bitcast.30, bf16[768,512]{1,0:T(8,128)(2,1)S(1)} %get-tuple-element.29.refs_1_.refs_2_, bf16[768,512]{1,0:T(8,128)(2,1)S(1)} %copy-done.8, ...), custom_call_target="tpu_custom_call", output_to_operand_aliasing={{0}: (9, {})} | custom-call | flops 4831838208 | bytes 12582912 | tf_op jit(solution)/shard_map/pallas_call | solution.py:148
  579.4 10.2 %shard_map.47 = (bf16[2,4,768,768]{3,2,1,0:T(8,128)(2,1)}, bf16[768,512]{1,0:T(8,128)(2,1)S(1)}) custom-call(s32[1]{0:T(128)} %bitcast.at_row, bf16[4,768,1536]{2,1,0:T(8,128)(2,1)} %bitcast.31, bf16[768,512]{1,0:T(8,128)(2,1)S(1)} %get-tuple-element.30.refs_1_.refs_2_, bf16[768,512]{1,0:T(8,128)(2,1)S(1)} %copy-done.6, ...), custom_call_target="tpu_custom_call", output_to_operand_aliasing={{0}: (9, {})} | custom-call | flops 4831838208 | bytes 12582912 | tf_op jit(solution)/shard_map/pallas_call | solution.py:148
  598.0 15.4 %collective-permute-done.refs_2_.refs_3_ = bf16[768,512]{1,0:T(8,128)(2,1)S(1)} collective-permute-done((bf16[768,512]{1,0:T(8,128)(2,1)S(1)}, bf16[768,512]{1,0:T(8,128)(2,1)S(1)}, u32[]{:S(2)}, u32[]{:S(2)}) %collective-permute-start) | collective-permute-done | bytes 786464 | tf_op jit(solution)/shard_map/ppermute | solution.py:21
  615.4 18.5 %collective-permute-done.2.refs_4_.refs_5_ = bf16[768,512]{1,0:T(8,128)(2,1)S(1)} collective-permute-done((bf16[768,512]{1,0:T(8,128)(2,1)S(1)}, bf16[768,512]{1,0:T(8,128)(2,1)S(1)}, u32[]{:S(2)}, u32[]{:S(2)}) %collective-permute-start.2) | collective-permute-done | bytes 786464 | tf_op jit(solution)/shard_map/ppermute | solution.py:21
  636.2 16.8 %collective-permute-done.4.refs_6_.refs_7_ = bf16[768,512]{1,0:T(8,128)(2,1)S(1)} collective-permute-done((bf16[768,512]{1,0:T(8,128)(2,1)S(1)}, bf16[768,512]{1,0:T(8,128)(2,1)S(1)}, u32[]{:S(2)}, u32[]{:S(2)}) %collective-permute-start.4) | collective-permute-done | bytes 786464 | tf_op jit(solution)/shard_map/ppermute | solution.py:21
  (233 shorter events, 254.1 us)
Async XLA Ops:
  33.4 38.0 %all-to-all-start.2 = ((bf16[16,96,512]{2,1,0:T(8,128)(2,1)}), bf16[16,96,512]{2,1,0:T(8,128)(2,1)S(1)}, u32[]{:S(2)}, u32[]{:S(2)}) async-start(bf16[16,96,512]{2,1,0:T(8,128)(2,1)} %bitcast.7), calls=%async_computation.2 | async-start | bytes 3145728 | tf_op jit(solution)/shard_map/all_to_all | solution.py:196
  72.6 68.6 %all-to-all-start.3 = ((bf16[16,96,1024]{2,1,0:T(8,128)(2,1)}), bf16[16,96,1024]{2,1,0:T(8,128)(2,1)S(1)}, u32[]{:S(2)}, u32[]{:S(2)}) async-start(bf16[16,96,1024]{2,1,0:T(8,128)(2,1)} %bitcast.10), calls=%async_computation.3 | async-start | bytes 6291456 | tf_op jit(solution)/shard_map/all_to_all | solution.py:196
  81.7 207.8 %all-gather.17.cloned.1.call-start = ((), (), s32[]{:S(2)}) async-start(), calls=%async_computation.5 | async-start | bytes 3932160 | tf_op jit(solution)/shard_map/all_gather | solution.py:200
  86.8 202.7 %all-gather.19.cloned.1.call-start = ((), (), s32[]{:S(2)}) async-start(), calls=%async_computation.6 | async-start | bytes 7864320 | tf_op jit(solution)/shard_map/all_gather | solution.py:200
  148.5 383.8 %all-gather.21.cloned.1.call-start = ((), (), s32[]{:S(2)}) async-start(), calls=%async_computation.7 | async-start | bytes 11796480 | tf_op jit(solution)/shard_map/all_gather | solution.py:227
  183.1 36.1 %collective-permute-start.24 = (bf16[768,512]{1,0:T(8,128)(2,1)S(1)}, bf16[768,512]{1,0:T(8,128)(2,1)S(1)}, u32[]{:S(2)}, u32[]{:S(2)}) collective-permute-start(bf16[768,512]{1,0:T(8,128)(2,1)S(1)} %get-tuple-element.32.refs_2_.refs_1_), channel_id=1, source_target_pairs={{4,0},{8,4},{12,8},{5,1},{9,5},{13,9},{6,2},{10,6},{14,10},{7,3},{... | collective-permute-start | bytes 2359304 | tf_op jit(solution)/shard_map/ppermute | solution.py:21
  184.4 36.0 %collective-permute-start.25 = (bf16[768,512]{1,0:T(8,128)(2,1)S(1)}, bf16[768,512]{1,0:T(8,128)(2,1)S(1)}, u32[]{:S(2)}, u32[]{:S(2)}) collective-permute-start(bf16[768,512]{1,0:T(8,128)(2,1)S(1)} %get-tuple-element.32.refs_2_.refs_1_), channel_id=1, source_target_pairs={{0,4},{4,8},{8,12},{1,5},{5,9},{9,13},{2,6},{6,10},{10,14},{3,7},{... | collective-permute-start | bytes 2359304 | tf_op jit(solution)/shard_map/ppermute | solution.py:21
  194.1 42.0 %collective-permute-start.18 = (bf16[768,512]{1,0:T(8,128)(2,1)S(1)}, bf16[768,512]{1,0:T(8,128)(2,1)}, u32[]{:S(2)}, u32[]{:S(2)}) collective-permute-start(bf16[768,512]{1,0:T(8,128)(2,1)S(1)} %get-tuple-element.33.refs_2_.refs_1_), channel_id=1, source_target_pairs={{4,0},{8,4},{12,8},{5,1},{9,5},{13,9},{6,2},{10,6},{14,10},{7,3},{... | collective-permute-start | bytes 2359304 | tf_op jit(solution)/shard_map/ppermute | solution.py:21
  202.3 35.1 %collective-permute-start.19 = (bf16[768,512]{1,0:T(8,128)(2,1)S(1)}, bf16[768,512]{1,0:T(8,128)(2,1)}, u32[]{:S(2)}, u32[]{:S(2)}) collective-permute-start(bf16[768,512]{1,0:T(8,128)(2,1)S(1)} %get-tuple-element.33.refs_2_.refs_1_), channel_id=1, source_target_pairs={{0,4},{4,8},{8,12},{1,5},{5,9},{9,13},{2,6},{6,10},{10,14},{3,7},{... | collective-permute-start | bytes 2359304 | tf_op jit(solution)/shard_map/ppermute | solution.py:21
  207.1 45.7 %collective-permute-start.34 = (bf16[768,512]{1,0:T(8,128)(2,1)S(1)}, bf16[768,512]{1,0:T(8,128)(2,1)S(1)}, u32[]{:S(2)}, u32[]{:S(2)}) collective-permute-start(bf16[768,512]{1,0:T(8,128)(2,1)S(1)} %collective-permute-done.32.refs_5_.refs_4_), channel_id=1, source_target_pairs={{4,0},{5,1},{6,2},{7,3},{20,16},{21,17},{22,18},{23,19}} | collective-permute-start | bytes 2359304 | tf_op jit(solution)/shard_map/ppermute | solution.py:21
  219.1 50.7 %collective-permute-start.26 = (bf16[768,512]{1,0:T(8,128)(2,1)S(1)}, bf16[768,512]{1,0:T(8,128)(2,1)}, u32[]{:S(2)}, u32[]{:S(2)}) collective-permute-start(bf16[768,512]{1,0:T(8,128)(2,1)S(1)} %collective-permute-done.24.refs_3_.refs_2_), channel_id=1, source_target_pairs={{4,0},{8,4},{5,1},{9,5},{6,2},{10,6},{7,3},{11,7},{20,16},{24,20},... | collective-permute-start | bytes 2359304 | tf_op jit(solution)/shard_map/ppermute | solution.py:21
  220.4 50.7 %collective-permute-start.27 = (bf16[768,512]{1,0:T(8,128)(2,1)S(1)}, bf16[768,512]{1,0:T(8,128)(2,1)}, u32[]{:S(2)}, u32[]{:S(2)}) collective-permute-start(bf16[768,512]{1,0:T(8,128)(2,1)S(1)} %collective-permute-done.25.refs_4_.refs_3_), channel_id=1, source_target_pairs={{4,8},{8,12},{5,9},{9,13},{6,10},{10,14},{7,11},{11,15},{20,24},{2... | collective-permute-start | bytes 2359304 | tf_op jit(solution)/shard_map/ppermute | solution.py:21
  236.1 50.6 %collective-permute-start.20 = (bf16[768,512]{1,0:T(8,128)(2,1)}, bf16[768,512]{1,0:T(8,128)(2,1)}, u32[]{:S(2)}, u32[]{:S(2)}) collective-permute-start(bf16[768,512]{1,0:T(8,128)(2,1)} %collective-permute-done.18.refs_3_.refs_2_), channel_id=1, source_target_pairs={{4,0},{8,4},{5,1},{9,5},{6,2},{10,6},{7,3},{11,7},{20,16},{24,20},... | collective-permute-start | bytes 2359304 | tf_op jit(solution)/shard_map/ppermute | solution.py:21
  237.4 50.6 %collective-permute-start.21 = (bf16[768,512]{1,0:T(8,128)(2,1)}, bf16[768,512]{1,0:T(8,128)(2,1)}, u32[]{:S(2)}, u32[]{:S(2)}) collective-permute-start(bf16[768,512]{1,0:T(8,128)(2,1)} %collective-permute-done.19.refs_4_.refs_3_), channel_id=1, source_target_pairs={{4,8},{8,12},{5,9},{9,13},{6,10},{10,14},{7,11},{11,15},{20,24},{2... | collective-permute-start | bytes 2359304 | tf_op jit(solution)/shard_map/ppermute | solution.py:21
  253.7 35.7 %collective-permute-start.35 = (bf16[768,512]{1,0:T(8,128)(2,1)}, bf16[768,512]{1,0:T(8,128)(2,1)}, u32[]{:S(2)}, u32[]{:S(2)}) collective-permute-start(bf16[768,512]{1,0:T(8,128)(2,1)} %collective-permute-done.33.refs_6_.refs_5_), channel_id=1, source_target_pairs={{8,12},{9,13},{10,14},{11,15},{24,28},{25,29},{26,30},{27,31}} | collective-permute-start | bytes 2359304 | tf_op jit(solution)/shard_map/ppermute | solution.py:21
  329.2 237.7 %all-gather.15.cloned.1.call-start = ((), (), s32[]{:S(2)}) async-start(), calls=%async_computation.4 | async-start | bytes 11796480 | tf_op jit(solution)/shard_map/all_gather | solution.py:200
  454.7 208.7 %all-gather.27.cloned.1.call-start = ((), (), s32[]{:S(2)}) async-start(), calls=%async_computation.10 | async-start | bytes 3932160 | tf_op jit(solution)/shard_map/all_gather | solution.py:233
  463.7 34.1 %collective-permute-start.7 = (bf16[768,512]{1,0:T(8,128)(2,1)S(1)}, bf16[768,512]{1,0:T(8,128)(2,1)S(1)}, u32[]{:S(2)}, u32[]{:S(2)}) collective-permute-start(bf16[768,512]{1,0:T(8,128)(2,1)S(1)} %get-tuple-element.30.refs_1_.refs_2_), channel_id=1, source_target_pairs={{0,4},{4,8},{8,12},{1,5},{5,9},{9,13},{2,6},{6,10},{10,14},{3,7},{... | collective-permute-start | bytes 2359304 | tf_op jit(solution)/shard_map/ppermute | solution.py:21
  512.6 54.2 %collective-permute-start.16 = (bf16[768,512]{1,0:T(8,128)(2,1)}, bf16[768,512]{1,0:T(8,128)(2,1)}, u32[]{:S(2)}, u32[]{:S(2)}) collective-permute-start(bf16[768,512]{1,0:T(8,128)(2,1)} %collective-permute-done.14.refs_4_.refs_5_), channel_id=1, source_target_pairs={{4,0},{5,1},{6,2},{7,3},{20,16},{21,17},{22,18},{23,19}} | collective-permute-start | bytes 2359304 | tf_op jit(solution)/shard_map/ppermute | solution.py:21
  513.9 52.9 %collective-permute-start.17 = (bf16[768,512]{1,0:T(8,128)(2,1)}, bf16[768,512]{1,0:T(8,128)(2,1)}, u32[]{:S(2)}, u32[]{:S(2)}) collective-permute-start(bf16[768,512]{1,0:T(8,128)(2,1)} %collective-permute-done.15.refs_5_.refs_6_), channel_id=1, source_target_pairs={{8,12},{9,13},{10,14},{11,15},{24,28},{25,29},{26,30},{27,31}} | collective-permute-start | bytes 2359304 | tf_op jit(solution)/shard_map/ppermute | solution.py:21
  529.5 49.9 %collective-permute-start.10 = (bf16[768,512]{1,0:T(8,128)(2,1)}, bf16[768,512]{1,0:T(8,128)(2,1)}, u32[]{:S(2)}, u32[]{:S(2)}) collective-permute-start(bf16[768,512]{1,0:T(8,128)(2,1)} %collective-permute-done.8.refs_4_.refs_5_), channel_id=1, source_target_pairs={{4,0},{5,1},{6,2},{7,3},{20,16},{21,17},{22,18},{23,19}} | collective-permute-start | bytes 2359304 | tf_op jit(solution)/shard_map/ppermute | solution.py:21
  530.8 48.6 %collective-permute-start.11 = (bf16[768,512]{1,0:T(8,128)(2,1)}, bf16[768,512]{1,0:T(8,128)(2,1)}, u32[]{:S(2)}, u32[]{:S(2)}) collective-permute-start(bf16[768,512]{1,0:T(8,128)(2,1)} %collective-permute-done.9.refs_5_.refs_6_), channel_id=1, source_target_pairs={{8,12},{9,13},{10,14},{11,15},{24,28},{25,29},{26,30},{27,31}} | collective-permute-start | bytes 2359304 | tf_op jit(solution)/shard_map/ppermute | solution.py:21
  590.6 72.8 %all-gather.25.cloned.1.call-start = ((), (), s32[]{:S(2)}) async-start(), calls=%async_computation.9 | async-start | bytes 3932160 | tf_op jit(solution)/shard_map/all_gather | solution.py:233
  591.1 103.4 %all-gather.23.cloned.1.call-start = ((), (), s32[]{:S(2)}) async-start(), calls=%async_computation.8 | async-start | bytes 3932160 | tf_op jit(solution)/shard_map/all_gather | solution.py:233
  (83 other events, 1409.5 us)
Sparse Core Ops, SparseCore 0:
  86.9 43.1 all-gather.16
  148.6 57.1 all-gather.18
  329.3 116.2 all-gather.20
  454.8 64.8 all-gather.14
  590.7 33.3 all-gather.26
  625.5 28.5 all-gather.24
  663.5 31.0 all-gather.22

commit v4 on v3

v4 whole, which is shorter than its diff:
```python
import functools
import math

import jax
import jax.numpy as jnp
from jax import lax
from jax.experimental import pallas as pl
from jax.experimental.pallas import tpu as pltpu
from jax.sharding import PartitionSpec as P

NS = 3072
FREQ = 2
THIRDS = 3
BF16 = jnp.bfloat16
F32 = jnp.float32


def hop(pair, k, n_row):
    down = [(r, r - 1) for r in range(1, n_row) if r + k - 1 < n_row]
    up = [(r, r + 1) for r in range(n_row - 1) if r - k + 1 >= 0]
    return lax.ppermute(pair[0], "row", down), lax.ppermute(pair[1], "row", up)


def bin_kernel(picker, data, out):
    n_row, cap = out.shape[0], out.shape[2]
    sub = data.shape[2]
    for p in range(2):
        rows = jnp.dot(picker[...], data[p], preferred_element_type=F32).astype(BF16)
        for b in range(n_row):
            out[b, 0, :, p * sub : (p + 1) * sub] = rows[b * cap : (b + 1) * cap]


def bin_rows(picker, data, f, thirds, n_row, n_col):
    planes, own_cap, order = data.shape
    cap = picker.shape[0] // n_row
    sub = order // n_col // THIRDS
    count, first = len(thirds), thirds[0]
    return pl.pallas_call(
        bin_kernel,
        grid=(n_col, count),
        in_specs=[
            pl.BlockSpec(picker.shape, lambda c, j: (0, 0)),
            pl.BlockSpec((2, own_cap, sub), lambda c, j: (f, 0, c * THIRDS + first + j)),
        ],
        out_specs=pl.BlockSpec((n_row, 1, cap, 2 * sub), lambda c, j: (0, c, 0, j)),
        out_shape=jax.ShapeDtypeStruct((n_row, n_col, cap, 2 * sub * count), BF16),
        compiler_params=pltpu.CompilerParams(vmem_limit_bytes=16 * 2**20),
        cost_estimate=pl.CostEstimate(
            flops=4 * picker.shape[0] * own_cap * n_col * count * sub,
            bytes_accessed=8 * own_cap * n_col * count * sub,
            transcendentals=0,
        ),
    )(picker, data)


def after(value, earlier):
    return lax.optimization_barrier((value, earlier))[0]


def gather_cols(piece, n_col):
    held = {0: piece}
    bit = n_col // 2
    while bit:
        pairs = [(c, c ^ bit) for c in range(n_col)]
        arrived = {d ^ bit: lax.ppermute(a, "col", pairs) for d, a in held.items()}
        held.update(arrived)
        bit //= 2
    return [held[d] for d in range(n_col)]


def product_kernel(opts, where, *refs):
    plan, groups, order, n_col = opts["plan"], opts["groups"], opts["order"], opts["n_col"]
    lefts, refs = refs[: opts["lefts"]], refs[opts["lefts"] :]
    sources, refs = refs[: opts["outs"] * len(plan)], refs[opts["outs"] * len(plan) :]
    before = refs[0] if opts["before"] else None
    *outs, right, sems = refs[opts["before"] + opts["held"] :]
    row, me = where[0], where[1]
    sub = right.shape[2] // 2
    depth = right.shape[1] // n_col
    first = groups[0][0] * sub
    third = pl.program_id(1)

    def copies(t, phase):
        for s, (low, high, step) in enumerate(plan):
            source = sources[t * len(plan) + s]
            if len(plan) == 1:
                for c in range(n_col):
                    copy = pltpu.make_async_copy(
                        source.at[pl.ds(c * sub * THIRDS + first, depth)],
                        right.at[t, pl.ds(c * depth, depth)],
                        sems.at[t, c],
                    )
                    copy.start() if phase == 0 else copy.wait()
                continue

            @pl.when((row >= low) & (row <= high))
            def _(s=s, step=step, source=source):
                start = pl.multiple_of((row + step) * depth, 32)
                copy = pltpu.make_async_copy(
                    source.at[pl.ds(first, depth)], right.at[t, pl.ds(start, depth)], sems.at[t, s]
                )
                copy.start() if phase == 0 else copy.wait()

    for t in range(opts["outs"]):

        @pl.when((pl.program_id(0) == 0) & (third == 0))
        def _(t=t):
            copies(t, 0)

    for t in range(opts["outs"]):

        @pl.when((pl.program_id(0) == 0) & (third == t))
        def _(t=t):
            copies(t, 1)

    tile = lefts[0].shape[-2]
    by_real = jnp.zeros((tile, 2 * sub), F32)
    by_imag = jnp.zeros((tile, 2 * sub), F32)
    for c in range(n_col):
        if opts["by_xor"]:
            real_left, imag_left = [lefts[c][:, :sub]], [lefts[c][:, sub:]]
            start = pl.multiple_of((me ^ c) * depth, 32)
        else:
            real_left, imag_left = [], []
            start = c * depth
            for left, group in zip(lefts, groups):
                for k in range(len(group)):
                    real_left.append(left[c, :, 2 * k * sub : (2 * k + 1) * sub])
                    imag_left.append(left[c, :, (2 * k + 1) * sub : (2 * k + 2) * sub])
        rows = right[third, pl.ds(start, depth), :]
        by_real += jnp.dot(jnp.concatenate(real_left, axis=1), rows, preferred_element_type=F32)
        by_imag += jnp.dot(jnp.concatenate(imag_left, axis=1), rows, preferred_element_type=F32)
    real = by_real[:, :sub] - by_imag[:, sub:]
    imag = by_real[:, sub:] + by_imag[:, :sub]
    if before is not None:
        real = real + before[:, :sub]
        imag = imag + before[:, sub:]
    if order is None:
        outs[0][:, :sub] = real
        outs[0][:, sub:] = imag
        return
    real = (real * opts["weight"]).astype(BF16)
    imag = (imag * opts["weight"]).astype(BF16)
    outs[0][0, 0] = real
    outs[0][0, 1] = imag
    if len(outs) > 1:
        outs[1][:, :sub] = real
        outs[1][:, sub:] = imag


def complex_product(where, lefts, plan, rights, shape, held, at, before=None, piece_at=(0, 1)):
    groups = [group for _, group in lefts]
    by_xor = isinstance(lefts[0][0], list)
    arrays = lefts[0][0] if by_xor else [a for a, _ in lefts]
    n_col = len(arrays) if by_xor else arrays[0].shape[0]
    rows = arrays[0].shape[-2]
    tile = 256 if rows % 256 == 0 else rows
    wide = rights[0][0].shape[1]
    sub = wide // 2
    count = len(rights)
    order = None
    if at is None:
        out_specs = [pl.BlockSpec((tile, wide), lambda i, j, s: (i, j))]
        out_shape = [jax.ShapeDtypeStruct((rows, count * wide), F32)]
    else:
        order, f, first = at
        out_specs = [pl.BlockSpec((1, 2, tile, sub), lambda i, j, s: (order, f, i, first + j))]
        out_shape = [jax.ShapeDtypeStruct(shape, BF16)]
        if order == 0:
            which, of = piece_at
            out_specs.append(pl.BlockSpec((tile, wide), lambda i, j, s: (i, which + j)))
            out_shape.append(jax.ShapeDtypeStruct((rows, of * wide), BF16))
    if by_xor:
        in_specs = [pl.BlockSpec((tile, wide), lambda i, j, s: (i, 0)) for a in arrays]
    else:
        in_specs = [pl.BlockSpec((n_col, tile, a.shape[2]), lambda i, j, s: (0, i, 0)) for a in arrays]
    sources = [a for found in rights for a in found]
    in_specs += [pl.BlockSpec(memory_space=pl.ANY)] * len(sources)
    args = [*arrays, *sources]
    if before is not None:
        in_specs.append(pl.BlockSpec((tile, wide), lambda i, j, s: (i, j)))
        args.append(before)
    aliases = {1 + len(args) + k: k for k in range(len(held))}
    in_specs += [pl.BlockSpec(memory_space=pl.ANY)] * len(held)
    depth = sum(len(g) for g in groups) * n_col * sub
    opts = dict(
        plan=plan,
        groups=groups,
        order=order,
        n_col=n_col,
        lefts=len(arrays),
        outs=count,
        by_xor=by_xor,
        weight=1.0 / math.sqrt(2.0 * NS),
        before=int(before is not None),
        held=len(held),
    )
    return pl.pallas_call(
        functools.partial(product_kernel, opts),
        grid_spec=pltpu.PrefetchScalarGridSpec(
            num_scalar_prefetch=1,
            grid=(rows // tile, count),
            in_specs=in_specs,
            out_specs=out_specs,
            scratch_shapes=[
                pltpu.VMEM((count, depth, wide), BF16),
                pltpu.SemaphoreType.DMA((count, max(len(plan), n_col))),
            ],
        ),
        out_shape=out_shape,
        input_output_aliases=aliases,
        compiler_params=pltpu.CompilerParams(vmem_limit_bytes=48 * 2**20),
        cost_estimate=pl.CostEstimate(
            flops=4 * rows * depth * wide * count,
            bytes_accessed=2 * depth * wide * count + 4 * rows * depth,
            transcendentals=0,
        ),
    )(where, *args, *held)


def per_device(acq_data, grid_row, counts):
    n_row = lax.axis_size("row")
    n_col = lax.axis_size("col")
    own_cap, planes, order = acq_data.shape
    block_rows = order // n_row
    tile_cols = order // n_col
    cap = own_cap // n_row
    slots = n_row * cap
    wide = 2 * tile_cols // THIRDS
    everything = tuple(range(THIRDS))

    slot_index = jnp.arange(own_cap, dtype=jnp.int32)
    block = jnp.where(slot_index < counts[0], grid_row // block_rows, n_row)
    earlier = (block[None, :] == block[:, None]) & (slot_index[None, :] < slot_index[:, None])
    rank = jnp.sum(earlier.astype(jnp.int32), axis=1)
    leaving = jnp.where(block < n_row, block * cap + rank, -1)
    hit = jnp.arange(slots, dtype=jnp.int32)[:, None] == leaving[None, :]
    spots = jnp.sum(jnp.where(hit, (grid_row % block_rows)[None, :] + 1, 0), axis=1) - 1
    picker = hit.astype(BF16)
    data = jnp.transpose(acq_data, (1, 0, 2))
    line = n_row <= 4 and block_rows == tile_cols
    plan = [(0, n_row - 1, 0)]
    if line:
        for k in range(1, n_row):
            plan += [(0, n_row - 1 - k, k), (k, n_row - 1, -k)]

    keys = [(f, j) for f in range(FREQ) for j in everything]
    sent = bin_rows(picker, data, 0, (0,), n_row, n_col)
    labels = jnp.broadcast_to(after(spots, sent).reshape(n_row, 1, cap), (n_row, n_col, cap))
    places = lax.all_to_all(
        labels.reshape(n_row * n_col, cap), ("row", "col"), split_axis=0, concat_axis=0, tiled=True
    ).reshape(-1)
    placer = (jnp.arange(block_rows, dtype=jnp.int32)[:, None] == places[None, :]).astype(BF16)

    pieces, pairs, rights = [], {}, {key: [] for key in keys}
    lefts = [[], []]
    for p, (f, j) in enumerate(keys):
        if p:
            sent = bin_rows(picker, data, f, (j,), n_row, n_col)
        if line and p >= 2:
            sent = after(sent, pairs[p - 2, 1])
        got = lax.all_to_all(
            sent.reshape(n_row * n_col, cap, wide), ("row", "col"), split_axis=0, concat_axis=0, tiled=True
        ).reshape(-1, wide)
        tile = jnp.dot(placer, got, preferred_element_type=F32).astype(BF16)
        lefts[f].append((lax.all_gather(tile, "col", axis=0), (j,)))
        pieces.append(tile)
        if not line:
            rights[f, j] = [lax.all_gather(tile, "row", axis=0, tiled=True)]
            continue
        pairs[p, 1] = hop((tile, tile), 1, n_row)
        if p >= 2:
            for k in range(2, n_row):
                begun = pairs[p - 2, k - 1]
                pairs[p - 2, k] = hop(after(begun, got) if k == n_row - 1 else begun, k, n_row)
    if line:
        last = len(keys) - 1
        for k in range(2, n_row):
            pairs[last - 1, k] = hop(after(pairs[last - 1, k - 1], pairs[last, k - 1]), k, n_row)
            pairs[last, k] = hop(pairs[last, k - 1], k, n_row)
        for p, key in enumerate(keys):
            rights[key] = [pieces[p]] + [a for k in range(1, n_row) for a in pairs[p, k]]

    where = jnp.stack([lax.axis_index("row"), lax.axis_index("col")]).astype(jnp.int32)
    product = functools.partial(complex_product, where)
    shape = (2, planes, block_rows, tile_cols)
    held = ()
    for j in everything:
        held = product(lefts[0], plan, [rights[0, j]], shape, tuple(held), (0, 0, j), piece_at=(j, THIRDS))
    result, piece = held
    gathered = [(lax.all_gather(piece, "col", axis=0), everything)]
    for j in everything:
        (result,) = product(gathered, plan, [rights[0, j]], shape, (result,), (1, 0, j))
    gathered = []
    for j in everything:
        result, piece = product(lefts[1], plan, [rights[1, j]], shape, (result,), (0, 1, j))
        gathered.append((gather_cols(piece, n_col) if j == THIRDS - 1 else lax.all_gather(piece, "col", axis=0), (j,)))
    final = [rights[1, j] for j in everything]
    (sums,) = product(gathered[:-1], plan, final, shape, (), None)
    return product(gathered[-1:], plan, final, shape, (result,), (1, 1, 0), before=sums)[0]


def solution(mesh):
    placed = (
        P(("groups", "row", "col"), None, None),
        P(("groups", "row", "col")),
        P(("groups", "row", "col")),
    )
    return jax.shard_map(
        per_device,
        mesh=mesh,
        in_specs=placed,
        out_specs=P("groups", None, "row", "col"),
        check_vma=False,
    )
```

time: 726 us -> 748 us (1.030)
  waiting for transfers between devices: 275 us -> 337 us
  blocking collectives: 111 us -> 54.5 us
  starting transfers between devices: 106 us -> 121 us
    all_to_all x1 -> x2, blocking collectives: 111 us -> 54.5 us  [the longest x1 40.9 us: per_device(): lax.all_to_all(sent.reshape(n_row * n_col, cap, wide), ('row', 'col'), sp...]
    ppermute x18, waiting for transfers between devices: 193 us -> 240 us  [hop(): lax.ppermute(pair[0], 'row', down)]
    ppermute x0 -> x3, waiting for transfers between devices: none -> 29.2 us  [gather_cols(): arrived = {d ^ bit: lax.ppermute(a, 'col', pairs) for d, a in held.items()}]
    all_to_all x3 -> x5, starting transfers between devices: 22.5 us -> 50.3 us  [per_device(): lax.all_to_all(sent.reshape(n_row * n_col, cap, wide), ('row', 'col'), sp...]
    all_to_all x3 -> x5, waiting for transfers between devices: 77.4 us -> 57 us  [per_device(): lax.all_to_all(sent.reshape(n_row * n_col, cap, wide), ('row', 'col'), sp...]
    ppermute x18, starting transfers between devices: 60 us -> 45.6 us  [hop(): lax.ppermute(pair[1], 'row', up)]
    pallas_call x15 -> x11, Pallas kernels: 131 us -> 122 us  [complex_product(): pl.pallas_call(functools.partial(product_kernel, opts), grid_spec=pltpu.P...]
    unnamed x123 -> x101, local copies, waits for them, and re-layouts: 50.5 us -> 57.8 us
  transfers between devices with their start and end apart: 46 -> 53, of which waited for: 19 -> 22; matrix products, arithmetic and copies ran while one was open for 4% -> 2% of each run, Pallas kernels for 14% -> 14%
where the time goes in v4:
time: 748 us; the launch traced here: 744 us
  waiting for transfers between devices  337 us (45%)
  Pallas kernels  138 us (18%)
  starting transfers between devices  121 us (16%)
  local copies, waits for them, and re-layouts  58.4 us (8%)
  blocking collectives  54.5 us (7%)
  matrix products  19.5 us (3%)
  between operations  14.6 us (2%)
    ppermute x18, waiting for transfers between devices, hop(): lax.ppermute(pair[0], 'row', down)  240 us
    pallas_call x11, Pallas kernels, complex_product(): pl.pallas_call(functools.partial(product_kernel, opts), grid_spec=pltpu.P...  122 us
    unnamed x101, local copies, waits for them, and re-layouts  57.8 us
    all_to_all x5, waiting for transfers between devices, per_device(): lax.all_to_all(sent.reshape(n_row * n_col, cap, wide), ('row', 'col'), sp...  57 us
    all_to_all x5, starting transfers between devices, per_device(): lax.all_to_all(sent.reshape(n_row * n_col, cap, wide), ('row', 'col'), sp...  50.3 us
    ppermute x18, starting transfers between devices, hop(): lax.ppermute(pair[1], 'row', up)  45.6 us
    all_to_all x1, blocking collectives, per_device(): lax.all_to_all(sent.reshape(n_row * n_col, cap, wide), ('row', 'col'), sp...  40.9 us
    ppermute x3, waiting for transfers between devices, gather_cols(): arrived = {d ^ bit: lax.ppermute(a, 'col', pairs) for d, a in held.items()}  29.2 us
  transfers between devices with their start and end apart: 53, of which 22 were waited for; matrix products, arithmetic and copies ran while one was open for 2% of the time, Pallas kernels for 14%

profile of v4, /device:TPU:0, one launch (start us, length us, event | category | flops | bytes accessed | tf_op | source)
XLA Modules:
  0.0 744.4 jit_solution(15941709622270939992)
XLA Ops:
  25.1 13.6 %all_to_all.39 = s32[16,1,96]{2,1,0:T(1,128)S(1)} all-to-all(s32[16,1,96]{2,1,0:T(1,128)S(1)} %bitcast.65), channel_id=1, replica_groups=mesh['groups'=2,'row'=4,'col'=4] {'row','col'}, dimensions={0} | all-to-all | bytes 12288 | tf_op jit(solution)/shard_map/all_to_all | solution.py:250
  43.6 30.7 %all-to-all-done.3 = bf16[16,96,512]{2,1,0:T(8,128)(2,1)S(1)} async-done(((bf16[16,96,512]{2,1,0:T(8,128)(2,1)}), bf16[16,96,512]{2,1,0:T(8,128)(2,1)S(1)}, u32[]{:S(2)}, u32[]{:S(2)}) %all-to-all-start.3) | async-done | bytes 1572896 | tf_op jit(solution)/shard_map/all_to_all | solution.py:262
  98.3 26.3 %all-to-all-done.1 = bf16[16,96,512]{2,1,0:T(8,128)(2,1)} async-done(((bf16[16,96,512]{2,1,0:T(8,128)(2,1)}), bf16[16,96,512]{2,1,0:T(8,128)(2,1)}, u32[]{:S(2)}, u32[]{:S(2)}) %all-to-all-start.1) | async-done | bytes 1572896 | tf_op jit(solution)/shard_map/all_to_all | solution.py:262
  138.8 12.4 %all-to-all-start.4 = ((bf16[16,96,512]{2,1,0:T(8,128)(2,1)}), bf16[16,96,512]{2,1,0:T(8,128)(2,1)}, u32[]{:S(2)}, u32[]{:S(2)}) async-start(bf16[16,96,512]{2,1,0:T(8,128)(2,1)} %bitcast.12), calls=%async_computation.4 | async-start | bytes 3145728 | tf_op jit(solution)/shard_map/all_to_all | solution.py:262
  163.7 32.8 %collective-permute-done.refs_4_.refs_2_ = bf16[768,512]{1,0:T(8,128)(2,1)S(1)} collective-permute-done((bf16[768,512]{1,0:T(8,128)(2,1)S(1)}, bf16[768,512]{1,0:T(8,128)(2,1)S(1)}, u32[]{:S(2)}, u32[]{:S(2)}) %collective-permute-start) | collective-permute-done | bytes 786464 | tf_op jit(solution)/shard_map/ppermute | solution.py:21
  196.5 12.5 %all-to-all-start.2 = ((bf16[16,96,512]{2,1,0:T(8,128)(2,1)}), bf16[16,96,512]{2,1,0:T(8,128)(2,1)}, u32[]{:S(2)}, u32[]{:S(2)}) async-start(bf16[16,96,512]{2,1,0:T(8,128)(2,1)} %bitcast.7), calls=%async_computation.2 | async-start | bytes 3145728 | tf_op jit(solution)/shard_map/all_to_all | solution.py:262
  227.0 27.2 %collective-permute-done.4.refs_4_.refs_2_ = bf16[768,512]{1,0:T(8,128)(2,1)S(1)} collective-permute-done((bf16[768,512]{1,0:T(8,128)(2,1)}, bf16[768,512]{1,0:T(8,128)(2,1)S(1)}, u32[]{:S(2)}, u32[]{:S(2)}) %collective-permute-start.4) | collective-permute-done | bytes 786464 | tf_op jit(solution)/shard_map/ppermute | solution.py:21
  254.2 12.5 %all-to-all-start.5 = ((bf16[16,96,512]{2,1,0:T(8,128)(2,1)}), bf16[16,96,512]{2,1,0:T(8,128)(2,1)}, u32[]{:S(2)}, u32[]{:S(2)}) async-start(bf16[16,96,512]{2,1,0:T(8,128)(2,1)} %bitcast.14), calls=%async_computation.5 | async-start | bytes 3145728 | tf_op jit(solution)/shard_map/all_to_all | solution.py:262
  274.0 38.5 %collective-permute-done.32.refs_6_.refs_4_ = bf16[768,512]{1,0:T(8,128)(2,1)} collective-permute-done((bf16[768,512]{1,0:T(8,128)(2,1)}, bf16[768,512]{1,0:T(8,128)(2,1)}, u32[]{:S(2)}, u32[]{:S(2)}) %collective-permute-start.32) | collective-permute-done | bytes 786464 | tf_op jit(solution)/shard_map/ppermute | solution.py:21
  315.3 14.0 %collective-permute-done.28.refs_6_.refs_4_ = bf16[768,512]{1,0:T(8,128)(2,1)} collective-permute-done((bf16[768,512]{1,0:T(8,128)(2,1)S(1)}, bf16[768,512]{1,0:T(8,128)(2,1)}, u32[]{:S(2)}, u32[]{:S(2)}) %collective-permute-start.28) | collective-permute-done | bytes 786464 | tf_op jit(solution)/shard_map/ppermute | solution.py:21
  332.3 13.8 %collective-permute-done.24.refs_6_.refs_4_ = bf16[768,512]{1,0:T(8,128)(2,1)S(1)} collective-permute-done((bf16[768,512]{1,0:T(8,128)(2,1)S(1)}, bf16[768,512]{1,0:T(8,128)(2,1)S(1)}, u32[]{:S(2)}, u32[]{:S(2)}) %collective-permute-start.24) | collective-permute-done | bytes 786464 | tf_op jit(solution)/shard_map/ppermute | solution.py:21
  349.9 13.2 %collective-permute-done.34.refs_8_.refs_6_ = bf16[768,512]{1,0:T(8,128)(2,1)} collective-permute-done((bf16[768,512]{1,0:T(8,128)(2,1)}, bf16[768,512]{1,0:T(8,128)(2,1)}, u32[]{:S(2)}, u32[]{:S(2)}) %collective-permute-start.34) | collective-permute-done | bytes 786464 | tf_op jit(solution)/shard_map/ppermute | solution.py:21
  368.0 10.6 %shard_map.43 = (bf16[2,4,768,768]{3,2,1,0:T(8,128)(2,1)}, bf16[768,1536]{1,0:T(8,128)(2,1)}) custom-call(s32[2]{0:T(128)S(1)} %pad_add_fusion.where, bf16[4,768,512]{2,1,0:T(8,128)(2,1)} %bitcast.54, bf16[4,768,512]{2,1,0:T(8,128)(2,1)} %bitcast.57, bf16[4,768,512]{2,1,0:T(8,128)(2,1)} %bitcast.60, bf16[768,512]{1,0:T(8,128)(2,1)S(1)} %copy-done.20, ...), custom_call_target="tpu_custom_call" | custom-call | flops 4831838208 | bytes 12582912 | tf_op jit(solution)/shard_map/pallas_call | solution.py:198
  379.9 10.8 %shard_map.44 = (bf16[2,4,768,768]{3,2,1,0:T(8,128)(2,1)}, bf16[768,1536]{1,0:T(8,128)(2,1)}) custom-call(s32[2]{0:T(128)S(1)} %pad_add_fusion.where, bf16[4,768,512]{2,1,0:T(8,128)(2,1)} %bitcast.55, bf16[4,768,512]{2,1,0:T(8,128)(2,1)} %bitcast.58, bf16[4,768,512]{2,1,0:T(8,128)(2,1)} %bitcast.61, ...), custom_call_target="tpu_custom_call", output_to_operand_aliasing={{0}: (11, {}), {1}: (12, {})} | custom-call | flops 4831838208 | bytes 12582912 | tf_op jit(solution)/shard_map/pallas_call | solution.py:198
  433.1 40.9 %all_to_all.40 = bf16[16,96,512]{2,1,0:T(8,128)(2,1)S(1)} all-to-all(bf16[16,96,512]{2,1,0:T(8,128)(2,1)S(1)} %bitcast.41), channel_id=1, replica_groups=mesh['groups'=2,'row'=4,'col'=4] {'row','col'}, dimensions={0} | all-to-all | bytes 3145728 | tf_op jit(solution)/shard_map/all_to_all | solution.py:262
  504.2 15.2 %collective-permute-done.14.refs_4_.refs_10_.refs_12_ = bf16[768,512]{1,0:T(8,128)(2,1)S(1)} collective-permute-done((bf16[768,512]{1,0:T(8,128)(2,1)}, bf16[768,512]{1,0:T(8,128)(2,1)S(1)}, u32[]{:S(2)}, u32[]{:S(2)}) %collective-permute-start.14) | collective-permute-done | bytes 786464 | tf_op jit(solution)/shard_map/ppermute | solution.py:21
  539.3 14.0 %collective-permute-done.16.refs_6_.refs_12_.refs_14_ = bf16[768,512]{1,0:T(8,128)(2,1)} collective-permute-done((bf16[768,512]{1,0:T(8,128)(2,1)S(1)}, bf16[768,512]{1,0:T(8,128)(2,1)}, u32[]{:S(2)}, u32[]{:S(2)}) %collective-permute-start.16) | collective-permute-done | bytes 786464 | tf_op jit(solution)/shard_map/ppermute | solution.py:21
  554.8 15.2 %collective-permute-done.10.refs_6_.refs_19_.refs_21_ = bf16[768,512]{1,0:T(8,128)(2,1)S(1)} collective-permute-done((bf16[768,512]{1,0:T(8,128)(2,1)S(1)}, bf16[768,512]{1,0:T(8,128)(2,1)S(1)}, u32[]{:S(2)}, u32[]{:S(2)}) %collective-permute-start.10) | collective-permute-done | bytes 786464 | tf_op jit(solution)/shard_map/ppermute | solution.py:21
  587.7 10.5 %shard_map.47.refs_8_ = bf16[2,4,768,768]{3,2,1,0:T(8,128)(2,1)} custom-call(s32[2]{0:T(128)S(1)} %pad_add_fusion.where, bf16[4,768,1536]{2,1,0:T(8,128)(2,1)} %bitcast.43, bf16[768,512]{1,0:T(8,128)(2,1)S(1)} %copy-done.6, bf16[768,512]{1,0:T(8,128)(2,1)S(1)} %collective-permute-done.refs_4_.refs_2_, ...), custom_call_target="tpu_custom_call", output_to_operand_aliasing={{}: (9, {})} | custom-call | flops 4831838208 | bytes 12582912 | tf_op jit(solution)/shard_map/pallas_call | solution.py:198
  610.9 10.6 %shard_map.49 = (bf16[2,4,768,768]{3,2,1,0:T(8,128)(2,1)}, bf16[768,512]{1,0:T(8,128)(2,1)S(1)}) custom-call(s32[2]{0:T(128)S(1)} %pad_add_fusion.where, bf16[4,768,512]{2,1,0:T(8,128)(2,1)} %bitcast.45, bf16[4,768,512]{2,1,0:T(8,128)(2,1)} %bitcast.51, bf16[4,768,512]{2,1,0:T(8,128)(2,1)} %bitcast.48, ...), custom_call_target="tpu_custom_call", output_to_operand_aliasing={{0}: (11, {})} | custom-call | flops 4831838208 | bytes 12582912 | tf_op jit(solution)/shard_map/pallas_call | solution.py:198
  636.5 19.9 %collective-permute-done.12.refs_8_.refs_21_.refs_23_ = bf16[768,512]{1,0:T(8,128)(2,1)S(1)} collective-permute-done((bf16[768,512]{1,0:T(8,128)(2,1)}, bf16[768,512]{1,0:T(8,128)(2,1)S(1)}, u32[]{:S(2)}, u32[]{:S(2)}) %collective-permute-start.12) | collective-permute-done | bytes 786464 | tf_op jit(solution)/shard_map/ppermute | solution.py:21
  670.1 29.2 %collective-permute-done.37.refs_2_ = bf16[768,512]{1,0:T(8,128)(2,1)S(1)} collective-permute-done((bf16[768,512]{1,0:T(8,128)(2,1)}, bf16[768,512]{1,0:T(8,128)(2,1)S(1)}, u32[]{:S(2)}, u32[]{:S(2)}) %collective-permute-start.37) | collective-permute-done | bytes 786464 | tf_op jit(solution)/shard_map/ppermute | solution.py:65
  708.8 17.0 %shard_map.52.refs_25_ = f32[768,1536]{1,0:T(8,128)} custom-call(s32[2]{0:T(128)S(1)} %pad_add_fusion.where, bf16[4,768,512]{2,1,0:T(8,128)(2,1)} %bitcast.67, bf16[4,768,512]{2,1,0:T(8,128)(2,1)} %bitcast.66, bf16[768,512]{1,0:T(8,128)(2,1)S(1)} %copy-done.8, bf16[768,512]{1,0:T(8,128)(2,1)S(1)} %copy-done.24, bf16[768,512]{1,0:T(8,128)(2,1)S(1)} %copy-done.27, ...), custom_call_target="tpu_custom_call" | custom-call | flops 9663676416 | bytes 12582912 | tf_op jit(solution)/shard_map/pallas_call | solution.py:198
  725.8 12.1 %shard_map.53 = bf16[2,4,768,768]{3,2,1,0:T(8,128)(2,1)} custom-call(s32[2]{0:T(128)S(1)} %pad_add_fusion.where, bf16[768,512]{1,0:T(8,128)(2,1)} %get-tuple-element.59.refs_0_, bf16[768,512]{1,0:T(8,128)(2,1)S(1)} %collective-permute-done.36.refs_1_, bf16[768,512]{1,0:T(8,128)(2,1)S(1)} %collective-permute-done.37.refs_2_, ...), custom_call_target="tpu_custom_call", output_to_operand_aliasing={{}: (27, {})} | custom-call | flops 4831838208 | bytes 6291456 | tf_op jit(solution)/shard_map/pallas_call | solution.py:198
  (229 shorter events, 276.4 us)
Async XLA Ops:
  42.4 322.2 %all-gather.25.cloned.1.call-start = ((), (), s32[]{:S(2)}) async-start(), calls=%async_computation.10 | async-start | bytes 3932160 | tf_op jit(solution)/shard_map/all_gather | solution.py:266
  92.4 272.2 %all-gather.27.cloned.1.call-start = ((), (), s32[]{:S(2)}) async-start(), calls=%async_computation.11 | async-start | bytes 3932160 | tf_op jit(solution)/shard_map/all_gather | solution.py:266
  138.8 57.7 %all-to-all-start.4 = ((bf16[16,96,512]{2,1,0:T(8,128)(2,1)}), bf16[16,96,512]{2,1,0:T(8,128)(2,1)}, u32[]{:S(2)}, u32[]{:S(2)}) async-start(bf16[16,96,512]{2,1,0:T(8,128)(2,1)} %bitcast.12), calls=%async_computation.4 | async-start | bytes 3145728 | tf_op jit(solution)/shard_map/all_to_all | solution.py:262
  196.5 57.7 %all-to-all-start.2 = ((bf16[16,96,512]{2,1,0:T(8,128)(2,1)}), bf16[16,96,512]{2,1,0:T(8,128)(2,1)}, u32[]{:S(2)}, u32[]{:S(2)}) async-start(bf16[16,96,512]{2,1,0:T(8,128)(2,1)} %bitcast.7), calls=%async_computation.2 | async-start | bytes 3145728 | tf_op jit(solution)/shard_map/all_to_all | solution.py:262
  209.0 155.7 %all-gather.29.cloned.1.call-start = ((), (), s32[]{:S(2)}) async-start(), calls=%async_computation.12 | async-start | bytes 3932160 | tf_op jit(solution)/shard_map/all_gather | solution.py:266
  254.2 94.4 %all-to-all-start.5 = ((bf16[16,96,512]{2,1,0:T(8,128)(2,1)}), bf16[16,96,512]{2,1,0:T(8,128)(2,1)}, u32[]{:S(2)}, u32[]{:S(2)}) async-start(bf16[16,96,512]{2,1,0:T(8,128)(2,1)} %bitcast.14), calls=%async_computation.5 | async-start | bytes 3145728 | tf_op jit(solution)/shard_map/all_to_all | solution.py:262
  266.7 307.0 %all-gather.31.cloned.1.call-start = ((), (), s32[]{:S(2)}) async-start(), calls=%async_computation.13 | async-start | bytes 11796480 | tf_op jit(solution)/shard_map/all_gather | solution.py:291
  268.2 45.8 %collective-permute-start.33 = (bf16[768,512]{1,0:T(8,128)(2,1)}, bf16[768,512]{1,0:T(8,128)(2,1)}, u32[]{:S(2)}, u32[]{:S(2)}) collective-permute-start(bf16[768,512]{1,0:T(8,128)(2,1)} %copy-done.46), channel_id=1, source_target_pairs={{4,8},{8,12},{5,9},{9,13},{6,10},{10,14},{7,11},{11,15},{20,24},{2... | collective-permute-start | bytes 2359304 | tf_op jit(solution)/shard_map/ppermute | solution.py:21
  269.8 59.6 %collective-permute-start.28 = (bf16[768,512]{1,0:T(8,128)(2,1)S(1)}, bf16[768,512]{1,0:T(8,128)(2,1)}, u32[]{:S(2)}, u32[]{:S(2)}) collective-permute-start(bf16[768,512]{1,0:T(8,128)(2,1)S(1)} %collective-permute-done.refs_4_.refs_2_), channel_id=1, source_target_pairs={{4,0},{8,4},{5,1},{9,5},{6,2},{10,6},{7,3},{11,7},{20,16},{24,20},... | collective-permute-start | bytes 2359304 | tf_op jit(solution)/shard_map/ppermute | solution.py:21
  271.1 59.9 %collective-permute-start.29 = (bf16[768,512]{1,0:T(8,128)(2,1)S(1)}, bf16[768,512]{1,0:T(8,128)(2,1)}, u32[]{:S(2)}, u32[]{:S(2)}) collective-permute-start(bf16[768,512]{1,0:T(8,128)(2,1)S(1)} %collective-permute-done.1.refs_5_.refs_3_), channel_id=1, source_target_pairs={{4,8},{8,12},{5,9},{9,13},{6,10},{10,14},{7,11},{11,15},{20,24},{2... | collective-permute-start | bytes 2359304 | tf_op jit(solution)/shard_map/ppermute | solution.py:21
  272.7 73.4 %collective-permute-start.24 = (bf16[768,512]{1,0:T(8,128)(2,1)S(1)}, bf16[768,512]{1,0:T(8,128)(2,1)S(1)}, u32[]{:S(2)}, u32[]{:S(2)}) collective-permute-start(bf16[768,512]{1,0:T(8,128)(2,1)S(1)} %collective-permute-done.4.refs_4_.refs_2_), channel_id=1, source_target_pairs={{4,0},{8,4},{5,1},{9,5},{6,2},{10,6},{7,3},{11,7},{20,16},{24,20},... | collective-permute-start | bytes 2359304 | tf_op jit(solution)/shard_map/ppermute | solution.py:21
  314.1 49.0 %collective-permute-start.34 = (bf16[768,512]{1,0:T(8,128)(2,1)}, bf16[768,512]{1,0:T(8,128)(2,1)}, u32[]{:S(2)}, u32[]{:S(2)}) collective-permute-start(bf16[768,512]{1,0:T(8,128)(2,1)} %collective-permute-done.32.refs_6_.refs_4_), channel_id=1, source_target_pairs={{4,0},{5,1},{6,2},{7,3},{20,16},{21,17},{22,18},{23,19}} | collective-permute-start | bytes 2359304 | tf_op jit(solution)/shard_map/ppermute | solution.py:21
  331.0 48.9 %collective-permute-start.30 = (bf16[768,512]{1,0:T(8,128)(2,1)}, bf16[768,512]{1,0:T(8,128)(2,1)}, u32[]{:S(2)}, u32[]{:S(2)}) collective-permute-start(bf16[768,512]{1,0:T(8,128)(2,1)} %collective-permute-done.28.refs_6_.refs_4_), channel_id=1, source_target_pairs={{4,0},{5,1},{6,2},{7,3},{20,16},{21,17},{22,18},{23,19}} | collective-permute-start | bytes 2359304 | tf_op jit(solution)/shard_map/ppermute | solution.py:21
  348.6 47.7 %collective-permute-start.26 = (bf16[768,512]{1,0:T(8,128)(2,1)}, bf16[768,512]{1,0:T(8,128)(2,1)}, u32[]{:S(2)}, u32[]{:S(2)}) collective-permute-start(bf16[768,512]{1,0:T(8,128)(2,1)} %copy-done.16), channel_id=1, source_target_pairs={{4,0},{5,1},{6,2},{7,3},{20,16},{21,17},{22,18},{23,19}} | collective-permute-start | bytes 2359304 | tf_op jit(solution)/shard_map/ppermute | solution.py:21
  406.8 201.7 %all-gather.19.cloned.1.call-start = ((), (), s32[]{:S(2)}) async-start(), calls=%async_computation.7 | async-start | bytes 3932160 | tf_op jit(solution)/shard_map/all_gather | solution.py:266
  410.6 198.0 %all-gather.23.cloned.1.call-start = ((), (), s32[]{:S(2)}) async-start(), calls=%async_computation.9 | async-start | bytes 3932160 | tf_op jit(solution)/shard_map/all_gather | solution.py:266
  476.4 132.2 %all-gather.21.cloned.1.call-start = ((), (), s32[]{:S(2)}) async-start(), calls=%async_computation.8 | async-start | bytes 3932160 | tf_op jit(solution)/shard_map/all_gather | solution.py:266
  480.2 219.0 %all-gather.35.cloned.1.call-start = ((), (), s32[]{:S(2)}) async-start(), calls=%async_computation.15 | async-start | bytes 3932160 | tf_op jit(solution)/shard_map/all_gather | solution.py:297
  538.0 70.5 %collective-permute-start.22 = (bf16[768,512]{1,0:T(8,128)(2,1)}, bf16[768,512]{1,0:T(8,128)(2,1)}, u32[]{:S(2)}, u32[]{:S(2)}) collective-permute-start(bf16[768,512]{1,0:T(8,128)(2,1)} %collective-permute-done.20.refs_6_.refs_5_.refs_7_), channel_id=1, source_target_pairs={{4,0},{5,1},{6,2},{7,3},{20,16},{21,17},{22,18},{23,19}} | collective-permute-start | bytes 2359304 | tf_op jit(solution)/shard_map/ppermute | solution.py:21
  553.2 55.3 %collective-permute-start.23 = (bf16[768,512]{1,0:T(8,128)(2,1)}, bf16[768,512]{1,0:T(8,128)(2,1)}, u32[]{:S(2)}, u32[]{:S(2)}) collective-permute-start(bf16[768,512]{1,0:T(8,128)(2,1)} %collective-permute-done.21.refs_7_.refs_6_.refs_8_), channel_id=1, source_target_pairs={{8,12},{9,13},{10,14},{11,15},{24,28},{25,29},{26,30},{27,31}} | collective-permute-start | bytes 2359304 | tf_op jit(solution)/shard_map/ppermute | solution.py:21
  570.9 51.5 %collective-permute-start.18 = (bf16[768,512]{1,0:T(8,128)(2,1)}, bf16[768,512]{1,0:T(8,128)(2,1)}, u32[]{:S(2)}, u32[]{:S(2)}) collective-permute-start(bf16[768,512]{1,0:T(8,128)(2,1)} %collective-permute-done.16.refs_6_.refs_12_.refs_14_), channel_id=1, source_target_pairs={{4,0},{5,1},{6,2},{7,3},{20,16},{21,17},{22,18},{23,19}} | collective-permute-start | bytes 2359304 | tf_op jit(solution)/shard_map/ppermute | solution.py:21
  572.2 50.2 %collective-permute-start.19 = (bf16[768,512]{1,0:T(8,128)(2,1)}, bf16[768,512]{1,0:T(8,128)(2,1)}, u32[]{:S(2)}, u32[]{:S(2)}) collective-permute-start(bf16[768,512]{1,0:T(8,128)(2,1)} %collective-permute-done.17.refs_7_.refs_13_.refs_15_), channel_id=1, source_target_pairs={{8,12},{9,13},{10,14},{11,15},{24,28},{25,29},{26,30},{27,31}} | collective-permute-start | bytes 2359304 | tf_op jit(solution)/shard_map/ppermute | solution.py:21
  633.8 72.7 %all-gather.33.cloned.1.call-start = ((), (), s32[]{:S(2)}) async-start(), calls=%async_computation.14 | async-start | bytes 3932160 | tf_op jit(solution)/shard_map/all_gather | solution.py:297
  670.1 55.7 %collective-permute-start.36 = (bf16[768,512]{1,0:T(8,128)(2,1)}, bf16[768,512]{1,0:T(8,128)(2,1)S(1)}, u32[]{:S(2)}, u32[]{:S(2)}) collective-permute-start(bf16[768,512]{1,0:T(8,128)(2,1)} %get-tuple-element.59.refs_0_), channel_id=1, source_target_pairs={{0,1},{1,0},{2,3},{3,2},{4,5},{5,4},{6,7},{7,6},{8,9},{9,8},{10,11... | collective-permute-start | bytes 2359304 | tf_op jit(solution)/shard_map/ppermute | solution.py:65
  (79 other events, 1542.8 us)
Sparse Core Ops, SparseCore 0:
  76.7 46.4 all-gather.24
  128.5 45.9 all-gather.26
  212.8 37.1 all-gather.28
  406.9 81.4 all-gather.30
  489.8 28.5 all-gather.18
  519.8 28.5 all-gather.22
  549.9 28.5 all-gather.20
  633.9 32.5 all-gather.34
  668.1 38.3 all-gather.32

commit v5 on v4

--- a/solution.py
+++ b/solution.py
@@ -45,11 +45,7 @@
         out_specs=pl.BlockSpec((n_row, 1, cap, 2 * sub), lambda c, j: (0, c, 0, j)),
         out_shape=jax.ShapeDtypeStruct((n_row, n_col, cap, 2 * sub * count), BF16),
         compiler_params=pltpu.CompilerParams(vmem_limit_bytes=16 * 2**20),
-        cost_estimate=pl.CostEstimate(
-            flops=4 * picker.shape[0] * own_cap * n_col * count * sub,
-            bytes_accessed=8 * own_cap * n_col * count * sub,
-            transcendentals=0,
-        ),
+        cost_estimate=pl.CostEstimate(flops=1000, bytes_accessed=1000, transcendentals=0),
     )(picker, data)
 
 
@@ -118,18 +114,17 @@
     by_imag = jnp.zeros((tile, 2 * sub), F32)
     for c in range(n_col):
         if opts["by_xor"]:
-            real_left, imag_left = [lefts[c][:, :sub]], [lefts[c][:, sub:]]
+            slices = [lefts[g * n_col + c][...] for g in range(len(groups))]
             start = pl.multiple_of((me ^ c) * depth, 32)
         else:
-            real_left, imag_left = [], []
+            slices = [
+                left[c, :, 2 * k * sub : 2 * (k + 1) * sub] for left, group in zip(lefts, groups) for k in range(len(group))
+            ]
             start = c * depth
-            for left, group in zip(lefts, groups):
-                for k in range(len(group)):
-                    real_left.append(left[c, :, 2 * k * sub : (2 * k + 1) * sub])
-                    imag_left.append(left[c, :, (2 * k + 1) * sub : (2 * k + 2) * sub])
-        rows = right[third, pl.ds(start, depth), :]
-        by_real += jnp.dot(jnp.concatenate(real_left, axis=1), rows, preferred_element_type=F32)
-        by_imag += jnp.dot(jnp.concatenate(imag_left, axis=1), rows, preferred_element_type=F32)
+        for k, left in enumerate(slices):
+            rows = right[third, pl.ds(start + k * sub, sub), :]
+            by_real += jnp.dot(left[:, :sub], rows, preferred_element_type=F32)
+            by_imag += jnp.dot(left[:, sub:], rows, preferred_element_type=F32)
     real = by_real[:, :sub] - by_imag[:, sub:]
     imag = by_real[:, sub:] + by_imag[:, :sub]
     if before is not None:
@@ -151,8 +146,8 @@
 def complex_product(where, lefts, plan, rights, shape, held, at, before=None, piece_at=(0, 1)):
     groups = [group for _, group in lefts]
     by_xor = isinstance(lefts[0][0], list)
-    arrays = lefts[0][0] if by_xor else [a for a, _ in lefts]
-    n_col = len(arrays) if by_xor else arrays[0].shape[0]
+    arrays = [a for pieces, _ in lefts for a in pieces] if by_xor else [a for a, _ in lefts]
+    n_col = len(lefts[0][0]) if by_xor else arrays[0].shape[0]
     rows = arrays[0].shape[-2]
     tile = 256 if rows % 256 == 0 else rows
     wide = rights[0][0].shape[1]
@@ -210,11 +205,7 @@
         out_shape=out_shape,
         input_output_aliases=aliases,
         compiler_params=pltpu.CompilerParams(vmem_limit_bytes=48 * 2**20),
-        cost_estimate=pl.CostEstimate(
-            flops=4 * rows * depth * wide * count,
-            bytes_accessed=2 * depth * wide * count + 4 * rows * depth,
-            transcendentals=0,
-        ),
+        cost_estimate=pl.CostEstimate(flops=1000, bytes_accessed=1000, transcendentals=0),
     )(where, *args, *held)
 
 
@@ -244,47 +235,50 @@
         for k in range(1, n_row):
             plan += [(0, n_row - 1 - k, k), (k, n_row - 1, -k)]
 
+    my_row = lax.axis_index("row")
     keys = [(f, j) for f in range(FREQ) for j in everything]
-    sent = bin_rows(picker, data, 0, (0,), n_row, n_col)
-    labels = jnp.broadcast_to(after(spots, sent).reshape(n_row, 1, cap), (n_row, n_col, cap))
-    places = lax.all_to_all(
-        labels.reshape(n_row * n_col, cap), ("row", "col"), split_axis=0, concat_axis=0, tiled=True
-    ).reshape(-1)
+    known = lax.all_gather(spots, ("row", "col"), axis=0).reshape(n_row * n_col, n_row, cap)
+    places = lax.dynamic_index_in_dim(known, my_row, axis=1, keepdims=False).reshape(-1)
     placer = (jnp.arange(block_rows, dtype=jnp.int32)[:, None] == places[None, :]).astype(BF16)
 
-    pieces, pairs, rights = [], {}, {key: [] for key in keys}
-    lefts = [[], []]
-    for p, (f, j) in enumerate(keys):
-        if p:
-            sent = bin_rows(picker, data, f, (j,), n_row, n_col)
-        if line and p >= 2:
-            sent = after(sent, pairs[p - 2, 1])
+    pieces, pairs, rights, lefts = {}, {}, {}, [[], []]
+    for f, group in ((0, (0,)), (0, everything[1:]), (1, everything)):
+        sent = bin_rows(picker, data, f, group, n_row, n_col)
         got = lax.all_to_all(
-            sent.reshape(n_row * n_col, cap, wide), ("row", "col"), split_axis=0, concat_axis=0, tiled=True
-        ).reshape(-1, wide)
+            sent.reshape(n_row * n_col, cap, wide * len(group)), ("row", "col"), split_axis=0, concat_axis=0, tiled=True
+        ).reshape(-1, wide * len(group))
+        if line and f == 0 and group[0]:
+            got = after(got, pairs[0, 0, 1])
         tile = jnp.dot(placer, got, preferred_element_type=F32).astype(BF16)
-        lefts[f].append((lax.all_gather(tile, "col", axis=0), (j,)))
-        pieces.append(tile)
-        if not line:
-            rights[f, j] = [lax.all_gather(tile, "row", axis=0, tiled=True)]
-            continue
-        pairs[p, 1] = hop((tile, tile), 1, n_row)
-        if p >= 2:
+        lefts[f].append((lax.all_gather(tile, "col", axis=0), group))
+        for k, j in enumerate(group):
+            piece = pieces[f, j] = tile[:, k * wide : (k + 1) * wide]
+            if line:
+                pairs[f, j, 1] = hop((piece, piece), 1, n_row)
+    if line:
+        for f in range(FREQ):
             for k in range(2, n_row):
-                begun = pairs[p - 2, k - 1]
-                pairs[p - 2, k] = hop(after(begun, got) if k == n_row - 1 else begun, k, n_row)
-    if line:
-        last = len(keys) - 1
-        for k in range(2, n_row):
-            pairs[last - 1, k] = hop(after(pairs[last - 1, k - 1], pairs[last, k - 1]), k, n_row)
-            pairs[last, k] = hop(pairs[last, k - 1], k, n_row)
-        for p, key in enumerate(keys):
-            rights[key] = [pieces[p]] + [a for k in range(1, n_row) for a in pairs[p, k]]
-
-    where = jnp.stack([lax.axis_index("row"), lax.axis_index("col")]).astype(jnp.int32)
+                for j in everything:
+                    begun = pairs[f, j, k - 1]
+                    if f == 0 and k == 2 and j:
+                        begun = after(begun, got)
+                    if f == 0 and k == n_row - 1 and j == THIRDS - 1:
+                        begun = after(begun, pairs[1, 0, 1])
+                    if f == 1 and j + 1 < THIRDS:
+                        begun = after(begun, pairs[f, j + 1, k - 1])
+                    pairs[f, j, k] = hop(begun, k, n_row)
+    for key in keys:
+        if line:
+            rights[key] = [pieces[key]] + [a for k in range(1, n_row) for a in pairs[(*key, k)]]
+        else:
+            rights[key] = [lax.all_gather(pieces[key], "row", axis=0, tiled=True)]
+
+    where = jnp.stack([my_row, lax.axis_index("col")]).astype(jnp.int32)
     product = functools.partial(complex_product, where)
     shape = (2, planes, block_rows, tile_cols)
     held = ()
+    if line:
+        rights[0, THIRDS - 1][0] = after(rights[0, THIRDS - 1][0], pairs[1, 1, 1])
     for j in everything:
         held = product(lefts[0], plan, [rights[0, j]], shape, tuple(held), (0, 0, j), piece_at=(j, THIRDS))
     result, piece = held
@@ -294,7 +288,9 @@
     gathered = []
     for j in everything:
         result, piece = product(lefts[1], plan, [rights[1, j]], shape, (result,), (0, 1, j))
-        gathered.append((gather_cols(piece, n_col) if j == THIRDS - 1 else lax.all_gather(piece, "col", axis=0), (j,)))
+        if gathered:
+            piece = after(piece, gathered[-1][0][n_col // 2])
+        gathered.append((gather_cols(piece, n_col), (j,)))
     final = [rights[1, j] for j in everything]
     (sums,) = product(gathered[:-1], plan, final, shape, (), None)
     return product(gathered[-1:], plan, final, shape, (result,), (1, 1, 0), before=sums)[0]

time: 748 us -> 730 us (0.976)
  local copies, waits for them, and re-layouts: 58.4 us -> 39.8 us
  waiting for transfers between devices: 337 us -> 323 us
  blocking collectives: 54.5 us -> 67.3 us
  starting transfers between devices: 121 us -> 129 us
    all_gather x0 -> x1, blocking collectives: none -> 67.3 us  [per_device(): lax.all_gather(spots, ('row', 'col'), axis=0)]
    all_to_all x2 -> x0, blocking collectives: 54.5 us -> none  [the longest x1 40.9 us: per_device(): lax.all_to_all(sent.reshape(n_row * n_col, cap, wide), ('row', 'col'), sp...]
    all_to_all x5 -> x3, waiting for transfers between devices: 57 us -> 22.9 us  [per_device(): lax.all_to_all(sent.reshape(n_row * n_col, cap, wide * len(group)), ('row...]
    ppermute x18, starting transfers between devices: 45.6 us -> 70.1 us  [hop(): lax.ppermute(pair[1], 'row', up)]
    unnamed x101 -> x78, local copies, waits for them, and re-layouts: 57.8 us -> 35.4 us
    all_to_all x5 -> x3, starting transfers between devices: 50.3 us -> 33.5 us  [per_device(): lax.all_to_all(sent.reshape(n_row * n_col, cap, wide * len(group)), ('row...]
    ppermute x18, waiting for transfers between devices: 240 us -> 251 us  [hop(): lax.ppermute(pair[0], 'row', down)]
    all_gather x8 -> x3, waiting for transfers between devices: 7.33 us -> 17.7 us  [per_device(): lefts[f].append((lax.all_gather(tile, 'col', axis=0), group))]
  transfers between devices with their start and end apart: 53 -> 52, of which waited for: 22 -> 21; matrix products, arithmetic and copies ran while one was open for 2% -> 3% of each run, Pallas kernels for 14% -> 15%
where the time goes in v5:
time: 730 us; the launch traced here: 727 us
  waiting for transfers between devices  323 us (44%)
  Pallas kernels  136 us (19%)
  starting transfers between devices  129 us (18%)
  blocking collectives  67.3 us (9%)
  local copies, waits for them, and re-layouts  39.8 us (5%)
  matrix products  15.6 us (2%)
  between operations  14.5 us (2%)
    ppermute x18, waiting for transfers between devices, hop(): lax.ppermute(pair[0], 'row', down)  251 us
    pallas_call x11, Pallas kernels, complex_product(): pl.pallas_call(functools.partial(product_kernel, opts), grid_spec=pltpu.P...  123 us
    ppermute x18, starting transfers between devices, hop(): lax.ppermute(pair[1], 'row', up)  70.1 us
    all_gather x1, blocking collectives, per_device(): lax.all_gather(spots, ('row', 'col'), axis=0)  67.3 us
    unnamed x78, local copies, waits for them, and re-layouts  35.4 us
    all_to_all x3, starting transfers between devices, per_device(): lax.all_to_all(sent.reshape(n_row * n_col, cap, wide * len(group)), ('row...  33.5 us
    ppermute x9, waiting for transfers between devices, gather_cols(): arrived = {d ^ bit: lax.ppermute(a, 'col', pairs) for d, a in held.items()}  30.2 us
    ppermute x18, starting transfers between devices, hop(): lax.ppermute(pair[0], 'row', down)  23.4 us
  transfers between devices with their start and end apart: 52, of which 21 were waited for; matrix products, arithmetic and copies ran while one was open for 3% of the time, Pallas kernels for 15%

profile of v5, /device:TPU:0, one launch (start us, length us, event | category | flops | bytes accessed | tf_op | source)
XLA Modules:
  0.0 727.2 jit_solution(9205422136496468934)
XLA Ops:
  41.5 22.9 %all-to-all-done.1 = bf16[16,96,512]{2,1,0:T(8,128)(2,1)S(1)} async-done(((bf16[16,96,512]{2,1,0:T(8,128)(2,1)}), bf16[16,96,512]{2,1,0:T(8,128)(2,1)S(1)}, u32[]{:S(2)}, u32[]{:S(2)}) %all-to-all-start.1) | async-done | bytes 1572896 | tf_op jit(solution)/shard_map/all_to_all | solution.py:247
  73.8 67.3 %all-gather.5 = s32[16,1,384]{2,1,0:T(1,128)S(1)} all-gather(s32[1,1,384]{2,1,0:T(1,128)S(1)} %reshape.50), channel_id=2, replica_groups=mesh['groups'=2,'row'=4,'col'=4] {'row','col'}, dimensions={0}, use_global_device_ids=true | all-gather | bytes 26112 | tf_op jit(solution)/shard_map/all_gather | solution.py:240
  155.0 17.0 %all-to-all-start = ((bf16[16,96,1536]{2,1,0:T(8,128)(2,1)}), bf16[16,96,1536]{2,1,0:T(8,128)(2,1)}, u32[]{:S(2)}, u32[]{:S(2)}) async-start(bf16[16,96,1536]{2,1,0:T(8,128)(2,1)} %bitcast.23), calls=%async_computation | async-start | bytes 9437184 | tf_op jit(solution)/shard_map/all_to_all | solution.py:247
  178.9 89.2 %collective-permute-done.18.refs_3_.refs_2_ = bf16[768,512]{1,0:T(8,128)(2,1)S(1)} collective-permute-done((bf16[768,512]{1,0:T(8,128)(2,1)S(1)}, bf16[768,512]{1,0:T(8,128)(2,1)S(1)}, u32[]{:S(2)}, u32[]{:S(2)}) %collective-permute-start.18) | collective-permute-done | bytes 786464 | tf_op jit(solution)/shard_map/ppermute | solution.py:21
  279.0 30.9 %collective-permute-start.21 = (bf16[768,512]{1,0:T(8,128)(2,1)S(1)}, bf16[768,512]{1,0:T(8,128)(2,1)}, u32[]{:S(2)}, u32[]{:S(2)}) collective-permute-start(bf16[768,512]{1,0:T(8,128)(2,1)S(1)} %get-tuple-element.44.refs_2_.refs_1_), channel_id=1, source_target_pairs={{0,4},{4,8},{8,12},{1,5},{5,9},{9,13},{2,6},{6,10},{10,14},{3,7},{... | collective-permute-start | bytes 2359304 | tf_op jit(solution)/shard_map/ppermute | solution.py:21
  323.9 14.3 %collective-permute-done.20.refs_3_.refs_2_ = bf16[768,512]{1,0:T(8,128)(2,1)} collective-permute-done((bf16[768,512]{1,0:T(8,128)(2,1)S(1)}, bf16[768,512]{1,0:T(8,128)(2,1)}, u32[]{:S(2)}, u32[]{:S(2)}) %collective-permute-start.20) | collective-permute-done | bytes 786464 | tf_op jit(solution)/shard_map/ppermute | solution.py:21
  351.7 20.0 %collective-permute-done.26.refs_3_.refs_2_ = bf16[768,512]{1,0:T(8,128)(2,1)S(1)} collective-permute-done((bf16[768,512]{1,0:T(8,128)(2,1)}, bf16[768,512]{1,0:T(8,128)(2,1)S(1)}, u32[]{:S(2)}, u32[]{:S(2)}) %collective-permute-start.26) | collective-permute-done | bytes 786464 | tf_op jit(solution)/shard_map/ppermute | solution.py:21
  391.6 13.9 %collective-permute-done.12.refs_2_.refs_9_.refs_5_ = bf16[768,512]{1,0:T(8,128)(2,1)S(1)} collective-permute-done((bf16[768,512]{1,0:T(8,128)(2,1)S(1)}, bf16[768,512]{1,0:T(8,128)(2,1)S(1)}, u32[]{:S(2)}, u32[]{:S(2)}) %collective-permute-start.12) | collective-permute-done | bytes 786464 | tf_op jit(solution)/shard_map/ppermute | solution.py:21
  408.5 13.9 %collective-permute-done.28.refs_5_.refs_4_ = bf16[768,512]{1,0:T(8,128)(2,1)} collective-permute-done((bf16[768,512]{1,0:T(8,128)(2,1)S(1)}, bf16[768,512]{1,0:T(8,128)(2,1)}, u32[]{:S(2)}, u32[]{:S(2)}) %collective-permute-start.28) | collective-permute-done | bytes 786464 | tf_op jit(solution)/shard_map/ppermute | solution.py:21
  425.3 13.9 %collective-permute-done.6.refs_2_.refs_16_.refs_12_ = bf16[768,512]{1,0:T(8,128)(2,1)S(1)} collective-permute-done((bf16[768,512]{1,0:T(8,128)(2,1)S(1)}, bf16[768,512]{1,0:T(8,128)(2,1)S(1)}, u32[]{:S(2)}, u32[]{:S(2)}) %collective-permute-start.6) | collective-permute-done | bytes 786464 | tf_op jit(solution)/shard_map/ppermute | solution.py:21
  444.1 10.7 %shard_map.40 = (bf16[2,4,768,768]{3,2,1,0:T(8,128)(2,1)}, bf16[768,1536]{1,0:T(8,128)(2,1)}) custom-call(s32[2]{0:T(128)S(1)} %pad_add_fusion.where, bf16[4,768,512]{2,1,0:T(8,128)(2,1)} %bitcast.33, bf16[4,768,1024]{2,1,0:T(8,128)(2,1)} %bitcast.30, bf16[768,512]{1,0:T(8,128)(2,1)S(1)} %copy-done.8, bf16[768,512]{1,0:T(8,128)(2,1)S(1)} %copy-done.30, ...), custom_call_target="tpu_custom_call" | custom-call | flops 1000 | bytes 1000 | tf_op jit(solution)/shard_map/pallas_call | solution.py:193
  456.1 10.8 %shard_map.41 = (bf16[2,4,768,768]{3,2,1,0:T(8,128)(2,1)}, bf16[768,1536]{1,0:T(8,128)(2,1)}) custom-call(s32[2]{0:T(128)S(1)} %pad_add_fusion.where, bf16[4,768,512]{2,1,0:T(8,128)(2,1)} %bitcast.34, bf16[4,768,1024]{2,1,0:T(8,128)(2,1)} %bitcast.31, ...), custom_call_target="tpu_custom_call", output_to_operand_aliasing={{0}: (10, {}), {1}: (11, {})} | custom-call | flops 1000 | bytes 1000 | tf_op jit(solution)/shard_map/pallas_call | solution.py:193
  472.1 10.9 %shard_map.42 = (bf16[2,4,768,768]{3,2,1,0:T(8,128)(2,1)}, bf16[768,1536]{1,0:T(8,128)(2,1)}) custom-call(s32[2]{0:T(128)S(1)} %pad_add_fusion.where, bf16[4,768,512]{2,1,0:T(8,128)(2,1)} %bitcast.35, bf16[4,768,1024]{2,1,0:T(8,128)(2,1)} %bitcast.32, bf16[768,512]{1,0:T(8,128)(2,1)S(1)} %copy-done.10, ...), custom_call_target="tpu_custom_call", output_to_operand_aliasing={{0}: (10, {}), {1}: (11, {})} | custom-call | flops 1000 | bytes 1000 | tf_op jit(solution)/shard_map/pallas_call | solution.py:193
  489.5 14.6 %collective-permute-done.refs_2_.refs_23_.refs_19_ = bf16[768,512]{1,0:T(8,128)(2,1)S(1)} collective-permute-done((bf16[768,512]{1,0:T(8,128)(2,1)S(1)}, bf16[768,512]{1,0:T(8,128)(2,1)S(1)}, u32[]{:S(2)}, u32[]{:S(2)}) %collective-permute-start) | collective-permute-done | bytes 786464 | tf_op jit(solution)/shard_map/ppermute | solution.py:21
  513.2 20.6 %collective-permute-done.8.refs_4_.refs_18_.refs_14_ = bf16[768,512]{1,0:T(8,128)(2,1)} collective-permute-done((bf16[768,512]{1,0:T(8,128)(2,1)}, bf16[768,512]{1,0:T(8,128)(2,1)}, u32[]{:S(2)}, u32[]{:S(2)}) %collective-permute-start.8) | collective-permute-done | bytes 786464 | tf_op jit(solution)/shard_map/ppermute | solution.py:21
  536.2 14.4 %collective-permute-done.14.refs_4_.refs_11_.refs_7_ = bf16[768,512]{1,0:T(8,128)(2,1)} collective-permute-done((bf16[768,512]{1,0:T(8,128)(2,1)}, bf16[768,512]{1,0:T(8,128)(2,1)}, u32[]{:S(2)}, u32[]{:S(2)}) %collective-permute-start.14) | collective-permute-done | bytes 786464 | tf_op jit(solution)/shard_map/ppermute | solution.py:21
  553.5 13.9 %collective-permute-done.2.refs_4_.refs_25_.refs_21_ = bf16[768,512]{1,0:T(8,128)(2,1)S(1)} collective-permute-done((bf16[768,512]{1,0:T(8,128)(2,1)S(1)}, bf16[768,512]{1,0:T(8,128)(2,1)S(1)}, u32[]{:S(2)}, u32[]{:S(2)}) %collective-permute-start.2) | collective-permute-done | bytes 786464 | tf_op jit(solution)/shard_map/ppermute | solution.py:21
  569.5 10.8 %shard_map.43.refs_8_ = bf16[2,4,768,768]{3,2,1,0:T(8,128)(2,1)} custom-call(s32[2]{0:T(128)S(1)} %pad_add_fusion.where, bf16[4,768,1536]{2,1,0:T(8,128)(2,1)} %bitcast.24, bf16[768,512]{1,0:T(8,128)(2,1)S(1)} %copy-done.8, bf16[768,512]{1,0:T(8,128)(2,1)S(1)} %copy-done.31, ...), custom_call_target="tpu_custom_call", output_to_operand_aliasing={{}: (9, {})} | custom-call | flops 1000 | bytes 1000 | tf_op jit(solution)/shard_map/pallas_call | solution.py:193
  581.7 10.7 %shard_map.44.refs_8_ = bf16[2,4,768,768]{3,2,1,0:T(8,128)(2,1)} custom-call(s32[2]{0:T(128)S(1)} %pad_add_fusion.where, bf16[4,768,1536]{2,1,0:T(8,128)(2,1)} %bitcast.25, bf16[768,512]{1,0:T(8,128)(2,1)} %get-tuple-element.68.refs_2_.refs_1_, bf16[768,512]{1,0:T(8,128)(2,1)S(1)} %copy-done.35, ...), custom_call_target="tpu_custom_call", output_to_operand_aliasing={{}: (9, {})} | custom-call | flops 1000 | bytes 1000 | tf_op jit(solution)/shard_map/pallas_call | solution.py:193
  594.0 10.7 %shard_map.45.refs_8_ = bf16[2,4,768,768]{3,2,1,0:T(8,128)(2,1)} custom-call(s32[2]{0:T(128)S(1)} %pad_add_fusion.where, bf16[4,768,1536]{2,1,0:T(8,128)(2,1)} %bitcast.26, bf16[768,512]{1,0:T(8,128)(2,1)S(1)} %copy-done.11, bf16[768,512]{1,0:T(8,128)(2,1)} %collective-permute-done.20.refs_3_.refs_2_, ...), custom_call_target="tpu_custom_call", output_to_operand_aliasing={{}: (9, {})} | custom-call | flops 1000 | bytes 1000 | tf_op jit(solution)/shard_map/pallas_call | solution.py:193
  604.7 17.7 %all-gather.11.cloned.1.call-done = bf16[3072,1536]{1,0:T(8,128)(2,1)} async-done(((bf16[768,1536]{1,0:T(8,128)(2,1)}), bf16[3072,1536]{1,0:T(8,128)(2,1)}) %all-gather.11.cloned.1.call-update) | async-done | bytes 9437200 | tf_op jit(solution)/shard_map/all_gather | solution.py:253
  675.3 16.6 %collective-permute-done.39.refs_2_ = bf16[768,512]{1,0:T(8,128)(2,1)S(1)} collective-permute-done((bf16[768,512]{1,0:T(8,128)(2,1)S(1)}, bf16[768,512]{1,0:T(8,128)(2,1)S(1)}, u32[]{:S(2)}, u32[]{:S(2)}) %collective-permute-start.39) | collective-permute-done | bytes 786464 | tf_op jit(solution)/shard_map/ppermute | solution.py:61
  692.8 15.9 %shard_map.49.refs_25_ = f32[768,1536]{1,0:T(8,128)} custom-call(s32[2]{0:T(128)S(1)} %pad_add_fusion.where, bf16[768,512]{1,0:T(8,128)(2,1)S(1)} %get-tuple-element.61.refs_0_, bf16[768,512]{1,0:T(8,128)(2,1)S(1)} %collective-permute-done.41.refs_1_, bf16[768,512]{1,0:T(8,128)(2,1)S(1)} %collective-permute-done.36.refs_2_, ...), custom_call_target="tpu_custom_call" | custom-call | flops 1000 | bytes 1000 | tf_op jit(solution)/shard_map/pallas_call | solution.py:193
  708.8 11.9 %shard_map.50 = bf16[2,4,768,768]{3,2,1,0:T(8,128)(2,1)} custom-call(s32[2]{0:T(128)S(1)} %pad_add_fusion.where, bf16[768,512]{1,0:T(8,128)(2,1)S(1)} %get-tuple-element.63.refs_0_, bf16[768,512]{1,0:T(8,128)(2,1)S(1)} %collective-permute-done.38.refs_1_, bf16[768,512]{1,0:T(8,128)(2,1)S(1)} %collective-permute-done.39.refs_2_, ...), custom_call_target="tpu_custom_call", output_to_operand_aliasing={{}: (27, {})} | custom-call | flops 1000 | bytes 1000 | tf_op jit(solution)/shard_map/pallas_call | solution.py:193
  (193 shorter events, 219.3 us)
Async XLA Ops:
  64.5 90.5 %all-to-all-start.2 = ((bf16[16,96,1024]{2,1,0:T(8,128)(2,1)}), bf16[16,96,1024]{2,1,0:T(8,128)(2,1)}, u32[]{:S(2)}, u32[]{:S(2)}) async-start(bf16[16,96,1024]{2,1,0:T(8,128)(2,1)} %bitcast.10), calls=%async_computation.2 | async-start | bytes 6291456 | tf_op jit(solution)/shard_map/all_to_all | solution.py:247
  73.6 369.4 %all-gather.13.cloned.1.call-start = ((), (), s32[]{:S(2)}) async-start(), calls=%async_computation.4 | async-start | bytes 3932160 | tf_op jit(solution)/shard_map/all_gather | solution.py:253
  155.0 188.1 %all-to-all-start = ((bf16[16,96,1536]{2,1,0:T(8,128)(2,1)}), bf16[16,96,1536]{2,1,0:T(8,128)(2,1)}, u32[]{:S(2)}, u32[]{:S(2)}) async-start(bf16[16,96,1536]{2,1,0:T(8,128)(2,1)} %bitcast.23), calls=%async_computation | async-start | bytes 9437184 | tf_op jit(solution)/shard_map/all_to_all | solution.py:247
  172.0 271.0 %all-gather.15.cloned.1.call-start = ((), (), s32[]{:S(2)}) async-start(), calls=%async_computation.5 | async-start | bytes 7864320 | tf_op jit(solution)/shard_map/all_gather | solution.py:253
  172.0 96.1 %collective-permute-start.18 = (bf16[768,512]{1,0:T(8,128)(2,1)S(1)}, bf16[768,512]{1,0:T(8,128)(2,1)S(1)}, u32[]{:S(2)}, u32[]{:S(2)}) collective-permute-start(bf16[768,512]{1,0:T(8,128)(2,1)S(1)} %copy-done.8), channel_id=1, source_target_pairs={{4,0},{8,4},{12,8},{5,1},{9,5},{13,9},{6,2},{10,6},{14,10},{7,3},{... | collective-permute-start | bytes 2359304 | tf_op jit(solution)/shard_map/ppermute | solution.py:21
  173.3 94.8 %collective-permute-start.19 = (bf16[768,512]{1,0:T(8,128)(2,1)S(1)}, bf16[768,512]{1,0:T(8,128)(2,1)}, u32[]{:S(2)}, u32[]{:S(2)}) collective-permute-start(bf16[768,512]{1,0:T(8,128)(2,1)S(1)} %copy-done.8), channel_id=1, source_target_pairs={{0,4},{4,8},{8,12},{1,5},{5,9},{9,13},{2,6},{6,10},{10,14},{3,7},{... | collective-permute-start | bytes 2359304 | tf_op jit(solution)/shard_map/ppermute | solution.py:21
  274.0 294.3 %all-gather.17.cloned.1.call-start = ((), (), s32[]{:S(2)}) async-start(), calls=%async_computation.6 | async-start | bytes 11796480 | tf_op jit(solution)/shard_map/all_gather | solution.py:285
  274.0 47.2 %collective-permute-start.32 = (bf16[768,512]{1,0:T(8,128)(2,1)S(1)}, bf16[768,512]{1,0:T(8,128)(2,1)}, u32[]{:S(2)}, u32[]{:S(2)}) collective-permute-start(bf16[768,512]{1,0:T(8,128)(2,1)S(1)} %collective-permute-done.18.refs_3_.refs_2_), channel_id=1, source_target_pairs={{4,0},{8,4},{5,1},{9,5},{6,2},{10,6},{7,3},{11,7},{20,16},{24,20},... | collective-permute-start | bytes 2359304 | tf_op jit(solution)/shard_map/ppermute | solution.py:21
  277.7 60.4 %collective-permute-start.20 = (bf16[768,512]{1,0:T(8,128)(2,1)S(1)}, bf16[768,512]{1,0:T(8,128)(2,1)}, u32[]{:S(2)}, u32[]{:S(2)}) collective-permute-start(bf16[768,512]{1,0:T(8,128)(2,1)S(1)} %get-tuple-element.44.refs_2_.refs_1_), channel_id=1, source_target_pairs={{4,0},{8,4},{12,8},{5,1},{9,5},{13,9},{6,2},{10,6},{14,10},{7,3},{... | collective-permute-start | bytes 2359304 | tf_op jit(solution)/shard_map/ppermute | solution.py:21
  279.0 64.0 %collective-permute-start.21 = (bf16[768,512]{1,0:T(8,128)(2,1)S(1)}, bf16[768,512]{1,0:T(8,128)(2,1)}, u32[]{:S(2)}, u32[]{:S(2)}) collective-permute-start(bf16[768,512]{1,0:T(8,128)(2,1)S(1)} %get-tuple-element.44.refs_2_.refs_1_), channel_id=1, source_target_pairs={{0,4},{4,8},{8,12},{1,5},{5,9},{9,13},{2,6},{6,10},{10,14},{3,7},{... | collective-permute-start | bytes 2359304 | tf_op jit(solution)/shard_map/ppermute | solution.py:21
  310.8 66.8 %collective-permute-start.33 = (bf16[768,512]{1,0:T(8,128)(2,1)}, bf16[768,512]{1,0:T(8,128)(2,1)}, u32[]{:S(2)}, u32[]{:S(2)}) collective-permute-start(bf16[768,512]{1,0:T(8,128)(2,1)} %collective-permute-done.19.refs_4_.refs_3_), channel_id=1, source_target_pairs={{4,8},{8,12},{5,9},{9,13},{6,10},{10,14},{7,11},{11,15},{20,24},{2... | collective-permute-start | bytes 2359304 | tf_op jit(solution)/shard_map/ppermute | solution.py:21
  321.3 60.9 %collective-permute-start.34 = (bf16[768,512]{1,0:T(8,128)(2,1)}, bf16[768,512]{1,0:T(8,128)(2,1)}, u32[]{:S(2)}, u32[]{:S(2)}) collective-permute-start(bf16[768,512]{1,0:T(8,128)(2,1)} %collective-permute-done.32.refs_5_.refs_4_), channel_id=1, source_target_pairs={{4,0},{5,1},{6,2},{7,3},{20,16},{21,17},{22,18},{23,19}} | collective-permute-start | bytes 2359304 | tf_op jit(solution)/shard_map/ppermute | solution.py:21
  322.6 49.2 %collective-permute-start.26 = (bf16[768,512]{1,0:T(8,128)(2,1)}, bf16[768,512]{1,0:T(8,128)(2,1)S(1)}, u32[]{:S(2)}, u32[]{:S(2)}) collective-permute-start(bf16[768,512]{1,0:T(8,128)(2,1)} %get-tuple-element.68.refs_2_.refs_1_), channel_id=1, source_target_pairs={{4,0},{8,4},{12,8},{5,1},{9,5},{13,9},{6,2},{10,6},{14,10},{7,3},{... | collective-permute-start | bytes 2359304 | tf_op jit(solution)/shard_map/ppermute | solution.py:21
  343.0 45.7 %collective-permute-start.22 = (bf16[768,512]{1,0:T(8,128)(2,1)}, bf16[768,512]{1,0:T(8,128)(2,1)}, u32[]{:S(2)}, u32[]{:S(2)}) collective-permute-start(bf16[768,512]{1,0:T(8,128)(2,1)} %collective-permute-done.20.refs_3_.refs_2_), channel_id=1, source_target_pairs={{4,0},{8,4},{5,1},{9,5},{6,2},{10,6},{7,3},{11,7},{20,16},{24,20},... | collective-permute-start | bytes 2359304 | tf_op jit(solution)/shard_map/ppermute | solution.py:21
  382.2 40.2 %collective-permute-start.28 = (bf16[768,512]{1,0:T(8,128)(2,1)S(1)}, bf16[768,512]{1,0:T(8,128)(2,1)}, u32[]{:S(2)}, u32[]{:S(2)}) collective-permute-start(bf16[768,512]{1,0:T(8,128)(2,1)S(1)} %copy-done.33), channel_id=1, source_target_pairs={{4,0},{8,4},{5,1},{9,5},{6,2},{10,6},{7,3},{11,7},{20,16},{24,20},... | collective-permute-start | bytes 2359304 | tf_op jit(solution)/shard_map/ppermute | solution.py:21
  390.3 48.9 %collective-permute-start.6 = (bf16[768,512]{1,0:T(8,128)(2,1)S(1)}, bf16[768,512]{1,0:T(8,128)(2,1)S(1)}, u32[]{:S(2)}, u32[]{:S(2)}) collective-permute-start(bf16[768,512]{1,0:T(8,128)(2,1)S(1)} %get-tuple-element.66.refs_1_.refs_15_.refs_11_), channel_id=1, source_target_pairs={{4,0},{8,4},{12,8},{5,1},{9,5},{13,9},{6,2},{10,6},{14,10},{7,3},{... | collective-permute-start | bytes 2359304 | tf_op jit(solution)/shard_map/ppermute | solution.py:21
  483.0 139.4 %all-gather.11.cloned.1.call-start = ((), (), s32[]{:S(2)}) async-start(), calls=%async_computation.3 | async-start | bytes 11796480 | tf_op jit(solution)/shard_map/all_gather | solution.py:253
  508.1 42.5 %collective-permute-start.14 = (bf16[768,512]{1,0:T(8,128)(2,1)}, bf16[768,512]{1,0:T(8,128)(2,1)}, u32[]{:S(2)}, u32[]{:S(2)}) collective-permute-start(bf16[768,512]{1,0:T(8,128)(2,1)} %copy-done.12), channel_id=1, source_target_pairs={{4,0},{8,4},{5,1},{9,5},{6,2},{10,6},{7,3},{11,7},{20,16},{24,20},... | collective-permute-start | bytes 2359304 | tf_op jit(solution)/shard_map/ppermute | solution.py:21
  509.4 41.2 %collective-permute-start.15 = (bf16[768,512]{1,0:T(8,128)(2,1)}, bf16[768,512]{1,0:T(8,128)(2,1)}, u32[]{:S(2)}, u32[]{:S(2)}) collective-permute-start(bf16[768,512]{1,0:T(8,128)(2,1)} %copy-done.15), channel_id=1, source_target_pairs={{4,8},{8,12},{5,9},{9,13},{6,10},{10,14},{7,11},{11,15},{20,24},{2... | collective-permute-start | bytes 2359304 | tf_op jit(solution)/shard_map/ppermute | solution.py:21
  511.0 56.4 %collective-permute-start.2 = (bf16[768,512]{1,0:T(8,128)(2,1)S(1)}, bf16[768,512]{1,0:T(8,128)(2,1)S(1)}, u32[]{:S(2)}, u32[]{:S(2)}) collective-permute-start(bf16[768,512]{1,0:T(8,128)(2,1)S(1)} %collective-permute-done.refs_2_.refs_23_.refs_19_), channel_id=1, source_target_pairs={{4,0},{8,4},{5,1},{9,5},{6,2},{10,6},{7,3},{11,7},{20,16},{24,20},... | collective-permute-start | bytes 2359304 | tf_op jit(solution)/shard_map/ppermute | solution.py:21
  550.6 54.0 %collective-permute-start.16 = (bf16[768,512]{1,0:T(8,128)(2,1)}, bf16[768,512]{1,0:T(8,128)(2,1)}, u32[]{:S(2)}, u32[]{:S(2)}) collective-permute-start(bf16[768,512]{1,0:T(8,128)(2,1)} %collective-permute-done.14.refs_4_.refs_11_.refs_7_), channel_id=1, source_target_pairs={{4,0},{5,1},{6,2},{7,3},{20,16},{21,17},{22,18},{23,19}} | collective-permute-start | bytes 2359304 | tf_op jit(solution)/shard_map/ppermute | solution.py:21
  551.9 52.7 %collective-permute-start.17 = (bf16[768,512]{1,0:T(8,128)(2,1)}, bf16[768,512]{1,0:T(8,128)(2,1)}, u32[]{:S(2)}, u32[]{:S(2)}) collective-permute-start(bf16[768,512]{1,0:T(8,128)(2,1)} %collective-permute-done.15.refs_5_.refs_12_.refs_8_), channel_id=1, source_target_pairs={{8,12},{9,13},{10,14},{11,15},{24,28},{25,29},{26,30},{27,31}} | collective-permute-start | bytes 2359304 | tf_op jit(solution)/shard_map/ppermute | solution.py:21
  580.3 57.6 %collective-permute-start.10 = (bf16[768,512]{1,0:T(8,128)(2,1)}, bf16[768,512]{1,0:T(8,128)(2,1)}, u32[]{:S(2)}, u32[]{:S(2)}) collective-permute-start(bf16[768,512]{1,0:T(8,128)(2,1)} %collective-permute-done.8.refs_4_.refs_18_.refs_14_), channel_id=1, source_target_pairs={{4,0},{5,1},{6,2},{7,3},{20,16},{21,17},{22,18},{23,19}} | collective-permute-start | bytes 2359304 | tf_op jit(solution)/shard_map/ppermute | solution.py:21
  592.4 45.5 %collective-permute-start.11 = (bf16[768,512]{1,0:T(8,128)(2,1)}, bf16[768,512]{1,0:T(8,128)(2,1)}, u32[]{:S(2)}, u32[]{:S(2)}) collective-permute-start(bf16[768,512]{1,0:T(8,128)(2,1)} %collective-permute-done.9.refs_5_.refs_19_.refs_15_), channel_id=1, source_target_pairs={{8,12},{9,13},{10,14},{11,15},{24,28},{25,29},{26,30},{27,31}} | collective-permute-start | bytes 2359304 | tf_op jit(solution)/shard_map/ppermute | solution.py:21
  (66 other events, 1904.5 us)
Sparse Core Ops, SparseCore 0:
  143.8 62.3 all-gather.12
  274.1 70.5 all-gather.14
  483.1 73.4 all-gather.16
  558.1 64.2 all-gather.10

commit v6 on v5

v6 whole, which is shorter than its diff:
```python
import functools
import math

import jax
import jax.numpy as jnp
from jax import lax
from jax.experimental import pallas as pl
from jax.experimental.pallas import tpu as pltpu
from jax.sharding import PartitionSpec as P

NS = 3072
FREQ = 2
THIRDS = 3
BF16 = jnp.bfloat16
F32 = jnp.float32


def hop(pair, k, n_row):
    down = [(r, r - 1) for r in range(1, n_row) if r + k - 1 < n_row]
    up = [(r, r + 1) for r in range(n_row - 1) if r - k + 1 >= 0]
    return lax.ppermute(pair[0], "row", down), lax.ppermute(pair[1], "row", up)


CHEAP = pl.CostEstimate(flops=1000, bytes_accessed=1000, transcendentals=0)


def bin_kernel(picker, data, out):
    n_row, cap = out.shape[0], out.shape[2]
    cols = data.shape[2]
    for p in range(2):
        rows = jnp.dot(picker[...], data[p], preferred_element_type=F32).astype(BF16)
        for b in range(n_row):
            out[b, 0, :, p * cols : (p + 1) * cols] = rows[b * cap : (b + 1) * cap]


def bin_rows(picker, data, f, n_row, n_col):
    planes, own_cap, order = data.shape
    cap = picker.shape[0] // n_row
    cols = order // n_col
    return pl.pallas_call(
        bin_kernel,
        grid=(n_col,),
        in_specs=[
            pl.BlockSpec(picker.shape, lambda c: (0, 0)),
            pl.BlockSpec((2, own_cap, cols), lambda c: (f, 0, c)),
        ],
        out_specs=pl.BlockSpec((n_row, 1, cap, 2 * cols), lambda c: (0, c, 0, 0)),
        out_shape=jax.ShapeDtypeStruct((n_row, n_col, cap, 2 * cols), BF16),
        compiler_params=pltpu.CompilerParams(vmem_limit_bytes=24 * 2**20),
        cost_estimate=CHEAP,
    )(picker, data)


def place_kernel(placer, got, tile, *thirds):
    rows = jnp.dot(placer[...], got[...], preferred_element_type=F32).astype(BF16)
    tile[0] = rows
    for j, third in enumerate(thirds):
        sub = third.shape[2]
        third[0] = rows[:, j * sub : (j + 1) * sub]


def place_rows(placer, got, split):
    block_rows, arrived = placer.shape
    cols = got.shape[1] // 2
    sizes = [cols] + [cols // THIRDS] * (THIRDS if split else 0)
    return pl.pallas_call(
        place_kernel,
        grid=(2,),
        in_specs=[
            pl.BlockSpec(placer.shape, lambda p: (0, 0)),
            pl.BlockSpec((arrived, cols), lambda p: (0, p)),
        ],
        out_specs=[pl.BlockSpec((1, block_rows, n), lambda p: (p, 0, 0)) for n in sizes],
        out_shape=[jax.ShapeDtypeStruct((2, block_rows, n), BF16) for n in sizes],
        compiler_params=pltpu.CompilerParams(vmem_limit_bytes=32 * 2**20),
        cost_estimate=CHEAP,
    )(placer, got)


def after(value, earlier):
    return lax.optimization_barrier((value, earlier))[0]


def gather_cols(piece, n_col):
    held = {0: piece}
    bit = n_col // 2
    while bit:
        pairs = [(c, c ^ bit) for c in range(n_col)]
        arrived = {d ^ bit: lax.ppermute(a, "col", pairs) for d, a in held.items()}
        held.update(arrived)
        bit //= 2
    return [held[d] for d in range(n_col)]


def product_kernel(opts, where, *refs):
    plan, groups, order, n_col = opts["plan"], opts["groups"], opts["order"], opts["n_col"]
    per_third = opts["per_third"]
    lefts, refs = refs[: len(groups)], refs[len(groups) :]
    sources, refs = refs[: opts["sources"]], refs[opts["sources"] :]
    before = refs[0] if opts["before"] else None
    *outs, right, total, sems = refs[opts["before"] + opts["held"] :]
    row, me = where[0], where[1]
    sub = right.shape[2] // 2
    depth = right.shape[1] // n_col
    first = groups[0][0] * sub
    third, step = pl.program_id(0), pl.program_id(1)

    def copy_of(source, from_row, t, p, block):
        lanes = pl.ds(0 if per_third else (opts["third"] + t) * sub, sub)
        start = block * depth if isinstance(block, int) else pl.multiple_of(block * depth, 32)
        return pltpu.make_async_copy(
            source.at[p, pl.ds(from_row, depth), lanes],
            right.at[t, pl.ds(start, depth), pl.ds(p * sub, sub)],
            sems.at[t, p, block],
        )

    @pl.when((third == 0) & (step == 0))
    def _():
        for t in range(right.shape[0]):
            for s, (low, high, up) in enumerate(plan):
                source = sources[t * len(plan) + s if per_third else s]
                if len(plan) == 1:
                    for c in range(n_col):
                        for p in range(2):
                            copy_of(source, c * sub * THIRDS + first, t, p, c).start()
                    continue

                @pl.when((row >= low) & (row <= high))
                def _(source=source, up=up, t=t):
                    for p in range(2):
                        copy_of(source, first, t, p, row + up).start()

    block = me ^ step if opts["by_xor"] else step
    for t in range(right.shape[0]):

        @pl.when(third == t)
        def _(t=t):
            for p in range(2):
                copy_of(sources[0], first, t, p, block).wait()

    real = imag = None
    start = block * depth
    for left, group in zip(lefts, groups):
        deep = len(group) * sub
        rows = right[third, pl.ds(pl.multiple_of(start, 32), deep), :]
        start = start + deep
        by_real = jnp.dot(left[0, 0], rows, preferred_element_type=F32)
        by_imag = jnp.dot(left[0, 1], rows, preferred_element_type=F32)
        real_now = by_real[:, :sub] - by_imag[:, sub:]
        imag_now = by_real[:, sub:] + by_imag[:, :sub]
        real = real_now if real is None else real + real_now
        imag = imag_now if imag is None else imag + imag_now

    @pl.when(step == 0)
    def _():
        total[0] = real if before is None else real + before[0]
        total[1] = imag if before is None else imag + before[1]

    @pl.when(step > 0)
    def _():
        total[0] += real
        total[1] += imag

    @pl.when(step == n_col - 1)
    def _():
        for p in range(2):
            if order is None:
                outs[0][p] = total[p]
                continue
            value = (total[p] * opts["weight"]).astype(BF16)
            outs[0][0, p] = value
            if len(outs) > 1:
                outs[1][p] = value


def complex_product(where, lefts, plan, sources, per_third, count, shape, held, at, before=None, piece_at=(0, 1), by_xor=False):
    groups = [group for _, group in lefts]
    arrays = [a for a, _ in lefts]
    n_col, _, rows, lanes = arrays[0].shape
    sub = lanes // len(groups[0])
    order, third = None, 0
    if at is None:
        out_specs = [pl.BlockSpec((2, rows, sub), lambda t, c, s: (0, 0, t))]
        out_shape = [jax.ShapeDtypeStruct((2, rows, count * sub), F32)]
    else:
        order, f, third = at
        out_specs = [pl.BlockSpec((1, 2, rows, sub), lambda t, c, s: (order, f, 0, third + t))]
        out_shape = [jax.ShapeDtypeStruct(shape, BF16)]
        if order == 0:
            which, of = piece_at
            out_specs.append(pl.BlockSpec((2, rows, sub), lambda t, c, s: (0, 0, which + t)))
            out_shape.append(jax.ShapeDtypeStruct((2, rows, of * sub), BF16))
    in_specs = [pl.BlockSpec((1, 2, rows, a.shape[3]), lambda t, c, s: (c, 0, 0, 0)) for a in arrays]
    in_specs += [pl.BlockSpec(memory_space=pl.ANY)] * len(sources)
    args = [*arrays, *sources]
    if before is not None:
        in_specs.append(pl.BlockSpec((2, rows, sub), lambda t, c, s: (0, 0, t)))
        args.append(before)
    aliases = {1 + len(args) + k: k for k in range(len(held))}
    in_specs += [pl.BlockSpec(memory_space=pl.ANY)] * len(held)
    depth = sum(len(g) for g in groups) * n_col * sub
    opts = dict(
        plan=plan,
        groups=groups,
        order=order,
        third=third,
        n_col=n_col,
        sources=len(sources),
        per_third=per_third,
        by_xor=by_xor,
        weight=1.0 / math.sqrt(2.0 * NS),
        before=int(before is not None),
        held=len(held),
    )
    return pl.pallas_call(
        functools.partial(product_kernel, opts),
        grid_spec=pltpu.PrefetchScalarGridSpec(
            num_scalar_prefetch=1,
            grid=(count, n_col),
            in_specs=in_specs,
            out_specs=out_specs,
            scratch_shapes=[
                pltpu.VMEM((count, depth, 2 * sub), BF16),
                pltpu.VMEM((2, rows, sub), F32),
                pltpu.SemaphoreType.DMA((count, 2, n_col)),
            ],
        ),
        out_shape=out_shape,
        input_output_aliases=aliases,
        compiler_params=pltpu.CompilerParams(vmem_limit_bytes=48 * 2**20),
        cost_estimate=CHEAP,
    )(where, *args, *held)


def per_device(acq_data, grid_row, counts):
    n_row = lax.axis_size("row")
    n_col = lax.axis_size("col")
    own_cap, planes, order = acq_data.shape
    block_rows = order // n_row
    tile_cols = order // n_col
    cap = own_cap // n_row
    slots = n_row * cap
    wide = 2 * tile_cols // THIRDS
    everything = tuple(range(THIRDS))

    slot_index = jnp.arange(own_cap, dtype=jnp.int32)
    block = jnp.where(slot_index < counts[0], grid_row // block_rows, n_row)
    earlier = (block[None, :] == block[:, None]) & (slot_index[None, :] < slot_index[:, None])
    rank = jnp.sum(earlier.astype(jnp.int32), axis=1)
    leaving = jnp.where(block < n_row, block * cap + rank, -1)
    hit = jnp.arange(slots, dtype=jnp.int32)[:, None] == leaving[None, :]
    spots = jnp.sum(jnp.where(hit, (grid_row % block_rows)[None, :] + 1, 0), axis=1) - 1
    picker = hit.astype(BF16)
    data = jnp.transpose(acq_data, (1, 0, 2))
    line = n_row <= 4 and block_rows == tile_cols
    plan = [(0, n_row - 1, 0)]
    if line:
        for k in range(1, n_row):
            plan += [(0, n_row - 1 - k, k), (k, n_row - 1, -k)]

    my_row = lax.axis_index("row")
    keys = [(f, j) for f in range(FREQ) for j in everything]
    known = lax.all_gather(spots, ("row", "col"), axis=0).reshape(n_row * n_col, n_row, cap)
    places = lax.dynamic_index_in_dim(known, my_row, axis=1, keepdims=False).reshape(-1)
    placer = (jnp.arange(block_rows, dtype=jnp.int32)[:, None] == places[None, :]).astype(BF16)

    tiles, thirds, lefts = [], [], []
    for f in range(FREQ):
        sent = bin_rows(picker, data, f, n_row, n_col)
        got = lax.all_to_all(
            sent.reshape(n_row * n_col, cap, 2 * tile_cols), ("row", "col"), split_axis=0, concat_axis=0, tiled=True
        ).reshape(-1, 2 * tile_cols)
        tile, *cut = place_rows(placer, got, line and f == 1)
        tiles.append(tile)
        thirds.append(cut)
        lefts.append((lax.all_gather(tile, "col", axis=0), everything))

    if line:
        pair = hop((tiles[0], tiles[0]), 1, n_row)
        right0 = [tiles[0], *pair]
        for k in range(2, n_row):
            pair = hop(after(pair, got) if k == 2 else pair, k, n_row)
            right0 += list(pair)
        hops = [[hop((a, a), 1, n_row) for a in thirds[1]]]
        for k in range(2, n_row):
            begun = hops[-1]
            hops.append([])
            for j in everything:
                hops[-1].append(hop(begun[j], k, n_row))
        right1 = [[thirds[1][j]] + [a for of in hops for a in of[j]] for j in everything]
    else:
        right0, right1 = ([lax.all_gather(tile, "row", axis=1, tiled=True)] for tile in tiles)

    where = jnp.stack([my_row, lax.axis_index("col")]).astype(jnp.int32)
    shape = (2, planes, block_rows, tile_cols)

    def product(lefts, f, at, held, count=1, **rest):
        first = 0 if at is None else at[2]
        sources, per_third = right0, False
        if f == 1:
            sources, per_third = right1, line
            if line:
                sources = [a for j in range(first, first + count) for a in right1[j]]
        return complex_product(where, lefts, plan, sources, per_third, count, shape, tuple(held), at, **rest)

    held = ()
    gate = where
    for j in everything:
        if line:
            gate = (hops[0], lefts[1][0]) if j == 0 else hops[1][0]
            right0[0] = after(right0[0], gate)
        held = product([lefts[0]], 0, (0, 0, j), held, piece_at=(j, THIRDS))
    result, piece = held
    left0 = [(lax.all_gather(piece, "col", axis=0), everything)]
    left1 = []
    arrived = None
    for j in everything:
        if j == THIRDS - 1:
            (result,) = product(left0, 0, (1, 0, 0), (result,), count=THIRDS)
        result, piece = product([lefts[1]], 1, (0, 1, j), (result,))
        if arrived is not None:
            piece = after(piece, arrived)
        found = gather_cols(piece, n_col)
        arrived = found[n_col // 2]
        left1.append((jnp.stack(found), (j,)))
    (sums,) = product(left1[:-1], 1, None, (), count=THIRDS, by_xor=True)
    return product(left1[-1:], 1, (1, 1, 0), (result,), count=THIRDS, before=sums, by_xor=True)[0]


def solution(mesh):
    placed = (
        P(("groups", "row", "col"), None, None),
        P(("groups", "row", "col")),
        P(("groups", "row", "col")),
    )
    return jax.shard_map(
        per_device,
        mesh=mesh,
        in_specs=placed,
        out_specs=P("groups", None, "row", "col"),
        check_vma=False,
    )
```

time: 730 us -> 749 us (1.026); the launches traced: 727 us -> 738 us
  blocking collectives: 67.3 us -> 221 us
  starting transfers between devices: 129 us -> 60.1 us
  waiting for transfers between devices: 323 us -> 262 us
  matrix products: 15.6 us -> 0 us
  local copies, waits for them, and re-layouts: 39.8 us -> 28.4 us
  other arithmetic: 1.29 us -> 10.1 us
    all_to_all x0 -> x1, blocking collectives: none -> 129 us  [per_device(): lax.all_to_all(sent.reshape(n_row * n_col, cap, 2 * tile_cols), ('row', '...]
    ppermute x18 -> x12, starting transfers between devices: 70.1 us -> 33 us  [hop(): lax.ppermute(pair[1], 'row', up)]
    all_to_all x3 -> x1, starting transfers between devices: 33.5 us -> 7.4 us  [per_device(): lax.all_to_all(sent.reshape(n_row * n_col, cap, 2 * tile_cols), ('row', '...]
    all_gather x1, blocking collectives: 67.3 us -> 92.5 us  [per_device(): lax.all_gather(spots, ('row', 'col'), axis=0)]
    all_to_all x3 -> x1, waiting for transfers between devices: 22.9 us -> 0.01 us  [per_device(): lax.all_to_all(sent.reshape(n_row * n_col, cap, 2 * tile_cols), ('row', '...]
    all_gather x4 -> x3, waiting for transfers between devices: 17.7 us -> 0.02 us  [the longest x2 0.02 us: per_device(): lefts.append((lax.all_gather(tile, 'col', axis=0), everything))]
    dot_general x3 -> x0, matrix products: 15.6 us -> none  [per_device(): tile = jnp.dot(placer, got, preferred_element_type=F32).astype(BF16)]
    ppermute x9, waiting for transfers between devices: 30.2 us -> 17.8 us  [gather_cols(): arrived = {d ^ bit: lax.ppermute(a, 'col', pairs) for d, a in held.items()}]
  transfers between devices with their start and end apart: 52 -> 37, of which waited for: 21 -> 12; matrix products, arithmetic and copies ran while one was open for 3% -> 1% of each run, Pallas kernels for 15% -> 11%
where the time goes in v6:
time: 749 us; the launch traced here: 738 us
  waiting for transfers between devices  262 us (35%)
  blocking collectives  221 us (30%)
  Pallas kernels  143 us (19%)
  starting transfers between devices  60.1 us (8%)
  local copies, waits for them, and re-layouts  28.4 us (4%)
  between operations  14.4 us (2%)
  other arithmetic  10.1 us (1%)
    ppermute x12, waiting for transfers between devices, hop(): lax.ppermute(pair[0], 'row', down)  242 us
    all_to_all x1, blocking collectives, per_device(): lax.all_to_all(sent.reshape(n_row * n_col, cap, 2 * tile_cols), ('row', '...  129 us
    pallas_call x9, Pallas kernels, complex_product(): pl.pallas_call(functools.partial(product_kernel, opts), grid_spec=pltpu.P...  124 us
    all_gather x1, blocking collectives, per_device(): lax.all_gather(spots, ('row', 'col'), axis=0)  92.5 us
    ppermute x12, starting transfers between devices, hop(): lax.ppermute(pair[1], 'row', up)  33 us
    unnamed x64, local copies, waits for them, and re-layouts  28.2 us
    ppermute x9, waiting for transfers between devices, gather_cols(): arrived = {d ^ bit: lax.ppermute(a, 'col', pairs) for d, a in held.items()}  17.8 us
    ppermute x12, starting transfers between devices, hop(): lax.ppermute(pair[0], 'row', down)  15.4 us
  transfers between devices with their start and end apart: 37, of which 12 were waited for; matrix products, arithmetic and copies ran while one was open for 1% of the time, Pallas kernels for 11%

profile of v6, /device:TPU:0, one launch (start us, length us, event | category | flops | bytes accessed | tf_op | source)
XLA Modules:
  0.0 738.4 jit_solution(8927698763528867397)
XLA Ops:
  8.2 10.4 %copy.17 = bf16[384,4,3072]{2,0,1:T(8,128)(2,1)} copy(bf16[384,4,3072]{2,1,0:T(4,128)(2,1)} %param.3) | data formatting | bytes 18874368 | tf_op args[0]
  28.2 7.4 %all-to-all-start = ((bf16[16,96,1536]{2,1,0:T(8,128)(2,1)}), bf16[16,96,1536]{2,1,0:T(8,128)(2,1)}, u32[]{:S(2)}, u32[]{:S(2)}) async-start(bf16[16,96,1536]{2,1,0:T(8,128)(2,1)} %bitcast.28), calls=%async_computation | async-start | bytes 9437184 | tf_op jit(solution)/shard_map/all_to_all | solution.py:270
  35.8 92.5 %all-gather.4 = s32[16,1,384]{2,1,0:T(1,128)S(1)} all-gather(s32[1,1,384]{2,1,0:T(1,128)S(1)} %reshape.41), channel_id=2, replica_groups=mesh['groups'=2,'row'=4,'col'=4] {'row','col'}, dimensions={0}, use_global_device_ids=true | all-gather | bytes 26112 | tf_op jit(solution)/shard_map/all_gather | solution.py:263
  145.9 128.5 %all_to_all.10 = bf16[16,96,1536]{2,1,0:T(8,128)(2,1)S(1)} all-to-all(bf16[16,96,1536]{2,1,0:T(8,128)(2,1)S(1)} %bitcast.29), channel_id=1, replica_groups=mesh['groups'=2,'row'=4,'col'=4] {'row','col'}, dimensions={0} | all-to-all | bytes 9437184 | tf_op jit(solution)/shard_map/all_to_all | solution.py:270
  285.8 50.1 %collective-permute-done.12.refs_2_ = bf16[2,768,768]{2,1,0:T(8,128)(2,1)S(1)} collective-permute-done((bf16[2,768,768]{2,1,0:T(8,128)(2,1)}, bf16[2,768,768]{2,1,0:T(8,128)(2,1)S(1)}, u32[]{:S(2)}, u32[]{:S(2)}) %collective-permute-start.12) | collective-permute-done | bytes 2359328 | tf_op jit(solution)/shard_map/ppermute | solution.py:21
  341.9 10.3 %collective-permute-start.1 = (bf16[2,768,256]{2,1,0:T(8,128)(2,1)}, bf16[2,768,256]{2,1,0:T(8,128)(2,1)S(1)}, u32[]{:S(2)}, u32[]{:S(2)}) collective-permute-start(bf16[2,768,256]{2,1,0:T(8,128)(2,1)} %copy-done.8), channel_id=1, source_target_pairs={{0,4},{4,8},{8,12},{1,5},{5,9},{9,13},{2,6},{6,10},{10,14},{3,7},{... | collective-permute-start | bytes 2359304 | tf_op jit(solution)/shard_map/ppermute | solution.py:21
  352.2 41.5 %collective-permute-done.14.refs_4_ = bf16[2,768,768]{2,1,0:T(8,128)(2,1)} collective-permute-done((bf16[2,768,768]{2,1,0:T(8,128)(2,1)S(1)}, bf16[2,768,768]{2,1,0:T(8,128)(2,1)}, u32[]{:S(2)}, u32[]{:S(2)}) %collective-permute-start.14) | collective-permute-done | bytes 2359328 | tf_op jit(solution)/shard_map/ppermute | solution.py:21
  398.3 12.1 %collective-permute-done.refs_2_.refs_17_.refs_16_ = bf16[2,768,256]{2,1,0:T(8,128)(2,1)S(1)} collective-permute-done((bf16[2,768,256]{2,1,0:T(8,128)(2,1)}, bf16[2,768,256]{2,1,0:T(8,128)(2,1)S(1)}, u32[]{:S(2)}, u32[]{:S(2)}) %collective-permute-start) | collective-permute-done | bytes 786464 | tf_op jit(solution)/shard_map/ppermute | solution.py:21
  416.6 61.4 %collective-permute-done.6.refs_2_.refs_3_ = bf16[2,768,256]{2,1,0:T(8,128)(2,1)} collective-permute-done((bf16[2,768,256]{2,1,0:T(8,128)(2,1)S(1)}, bf16[2,768,256]{2,1,0:T(8,128)(2,1)}, u32[]{:S(2)}, u32[]{:S(2)}) %collective-permute-start.6) | collective-permute-done | bytes 786464 | tf_op jit(solution)/shard_map/ppermute | solution.py:21
  481.5 13.2 %collective-permute-done.8.refs_2_.refs_10_.refs_9_ = bf16[2,768,256]{2,1,0:T(8,128)(2,1)S(1)} collective-permute-done((bf16[2,768,256]{2,1,0:T(8,128)(2,1)}, bf16[2,768,256]{2,1,0:T(8,128)(2,1)S(1)}, u32[]{:S(2)}, u32[]{:S(2)}) %collective-permute-start.8) | collective-permute-done | bytes 786464 | tf_op jit(solution)/shard_map/ppermute | solution.py:21
  497.2 13.7 %collective-permute-done.10.refs_4_.refs_5_ = bf16[2,768,256]{2,1,0:T(8,128)(2,1)} collective-permute-done((bf16[2,768,256]{2,1,0:T(8,128)(2,1)}, bf16[2,768,256]{2,1,0:T(8,128)(2,1)}, u32[]{:S(2)}, u32[]{:S(2)}) %collective-permute-start.10) | collective-permute-done | bytes 786464 | tf_op jit(solution)/shard_map/ppermute | solution.py:21
  511.0 10.9 %shard_map.41 = (bf16[2,4,768,768]{3,2,1,0:T(8,128)(2,1)}, bf16[2,768,768]{2,1,0:T(8,128)(2,1)S(1)}) custom-call(s32[2]{0:T(128)S(1)} %pad_add_fusion.where, bf16[4,2,768,768]{3,2,1,0:T(8,128)(2,1)} %bitcast.32, bf16[2,768,768]{2,1,0:T(8,128)(2,1)} %shard_map.40.refs_1_, bf16[2,768,768]{2,1,0:T(8,128)(2,1)} %copy-done.2, bf16[2,768,768]{2,1,0:T(8,128)(2,1)} %copy-done.27, ...), custom_call_target="tpu_custom_call" | custom-call | flops 1000 | bytes 1000 | tf_op jit(solution)/shard_map/pallas_call | solution.py:215
  521.9 10.9 %shard_map.42 = (bf16[2,4,768,768]{3,2,1,0:T(8,128)(2,1)}, bf16[2,768,768]{2,1,0:T(8,128)(2,1)S(1)}) custom-call(s32[2]{0:T(128)S(1)} %pad_add_fusion.where, bf16[4,2,768,768]{3,2,1,0:T(8,128)(2,1)} %bitcast.33, bf16[2,768,768]{2,1,0:T(8,128)(2,1)} %shard_map.40.refs_1_, ...), custom_call_target="tpu_custom_call", output_to_operand_aliasing={{0}: (9, {}), {1}: (10, {})} | custom-call | flops 1000 | bytes 1000 | tf_op jit(solution)/shard_map/pallas_call | solution.py:215
  532.8 11.0 %shard_map.43 = (bf16[2,4,768,768]{3,2,1,0:T(8,128)(2,1)}, bf16[2,768,768]{2,1,0:T(8,128)(2,1)S(1)}) custom-call(s32[2]{0:T(128)S(1)} %pad_add_fusion.where, bf16[4,2,768,768]{3,2,1,0:T(8,128)(2,1)} %bitcast.34, bf16[2,768,768]{2,1,0:T(8,128)(2,1)} %shard_map.40.refs_1_, ...), custom_call_target="tpu_custom_call", output_to_operand_aliasing={{0}: (9, {}), {1}: (10, {})} | custom-call | flops 1000 | bytes 1000 | tf_op jit(solution)/shard_map/pallas_call | solution.py:215
  550.7 18.3 %collective-permute-done.18.refs_4_.refs_12_.refs_11_ = bf16[2,768,256]{2,1,0:T(8,128)(2,1)S(1)} collective-permute-done((bf16[2,768,256]{2,1,0:T(8,128)(2,1)S(1)}, bf16[2,768,256]{2,1,0:T(8,128)(2,1)S(1)}, u32[]{:S(2)}, u32[]{:S(2)}) %collective-permute-start.18) | collective-permute-done | bytes 786464 | tf_op jit(solution)/shard_map/ppermute | solution.py:21
  571.8 14.0 %collective-permute-done.22.refs_6_.refs_7_ = bf16[2,768,256]{2,1,0:T(8,128)(2,1)S(1)} collective-permute-done((bf16[2,768,256]{2,1,0:T(8,128)(2,1)}, bf16[2,768,256]{2,1,0:T(8,128)(2,1)S(1)}, u32[]{:S(2)}, u32[]{:S(2)}) %collective-permute-start.22) | collective-permute-done | bytes 786464 | tf_op jit(solution)/shard_map/ppermute | solution.py:21
  587.4 10.0 %shard_map.44 = (bf16[2,4,768,768]{3,2,1,0:T(8,128)(2,1)}, bf16[2,768,256]{2,1,0:T(8,128)(2,1)}) custom-call(s32[2]{0:T(128)S(1)} %pad_add_fusion.where, bf16[4,2,768,768]{3,2,1,0:T(8,128)(2,1)} %bitcast.35, bf16[2,768,256]{2,1,0:T(8,128)(2,1)S(1)} %get-tuple-element.30.refs_1_.refs_2_, ...), custom_call_target="tpu_custom_call", output_to_operand_aliasing={{0}: (9, {})} | custom-call | flops 1000 | bytes 1000 | tf_op jit(solution)/shard_map/pallas_call | solution.py:215
  605.6 13.9 %collective-permute-done.20.refs_6_.refs_14_.refs_13_ = bf16[2,768,256]{2,1,0:T(8,128)(2,1)S(1)} collective-permute-done((bf16[2,768,256]{2,1,0:T(8,128)(2,1)S(1)}, bf16[2,768,256]{2,1,0:T(8,128)(2,1)S(1)}, u32[]{:S(2)}, u32[]{:S(2)}) %collective-permute-start.20) | collective-permute-done | bytes 786464 | tf_op jit(solution)/shard_map/ppermute | solution.py:21
  620.5 10.3 %shard_map.45 = (bf16[2,4,768,768]{3,2,1,0:T(8,128)(2,1)}, bf16[2,768,256]{2,1,0:T(8,128)(2,1)}) custom-call(s32[2]{0:T(128)S(1)} %pad_add_fusion.where, bf16[4,2,768,768]{3,2,1,0:T(8,128)(2,1)} %bitcast.36, bf16[2,768,256]{2,1,0:T(8,128)(2,1)S(1)} %copy-done.7, bf16[2,768,256]{2,1,0:T(8,128)(2,1)S(1)} %copy-done.18, ...), custom_call_target="tpu_custom_call", output_to_operand_aliasing={{0}: (9, {})} | custom-call | flops 1000 | bytes 1000 | tf_op jit(solution)/shard_map/pallas_call | solution.py:215
  632.5 25.0 %shard_map.46.refs_8_ = bf16[2,4,768,768]{3,2,1,0:T(8,128)(2,1)} custom-call(s32[2]{0:T(128)S(1)} %pad_add_fusion.where, bf16[4,2,768,768]{3,2,1,0:T(8,128)(2,1)} %bitcast.38, bf16[2,768,768]{2,1,0:T(8,128)(2,1)} %shard_map.40.refs_1_, bf16[2,768,768]{2,1,0:T(8,128)(2,1)S(1)} %copy-done.3, ...), custom_call_target="tpu_custom_call", output_to_operand_aliasing={{}: (9, {})} | custom-call | flops 1000 | bytes 1000 | tf_op jit(solution)/shard_map/pallas_call | solution.py:215
  657.6 9.7 %shard_map.47 = (bf16[2,4,768,768]{3,2,1,0:T(8,128)(2,1)}, bf16[2,768,256]{2,1,0:T(8,128)(2,1)S(1)}) custom-call(s32[2]{0:T(128)S(1)} %pad_add_fusion.where, bf16[4,2,768,768]{3,2,1,0:T(8,128)(2,1)} %bitcast.37, bf16[2,768,256]{2,1,0:T(8,128)(2,1)S(1)} %copy-done.9, bf16[2,768,256]{2,1,0:T(8,128)(2,1)S(1)} %copy-done.12, ...), custom_call_target="tpu_custom_call", output_to_operand_aliasing={{0}: (9, {})} | custom-call | flops 1000 | bytes 1000 | tf_op jit(solution)/shard_map/pallas_call | solution.py:215
  669.6 17.8 %collective-permute-done.27 = bf16[2,768,256]{2,1,0:T(8,128)(2,1)S(1)} collective-permute-done((bf16[2,768,256]{2,1,0:T(8,128)(2,1)S(1)}, bf16[2,768,256]{2,1,0:T(8,128)(2,1)S(1)}, u32[]{:S(2)}, u32[]{:S(2)}) %collective-permute-start.27) | collective-permute-done | bytes 786464 | tf_op jit(solution)/shard_map/ppermute | solution.py:89
  693.5 20.5 %shard_map.48.refs_22_ = f32[2,768,768]{2,1,0:T(8,128)} custom-call(s32[2]{0:T(128)S(1)} %pad_add_fusion.where, bf16[4,2,768,256]{3,2,1,0:T(8,128)(2,1)} %pad_maximum_fusion.1.refs_0_, bf16[4,2,768,256]{3,2,1,0:T(8,128)(2,1)} %pad_maximum_fusion.2.refs_1_, bf16[2,768,256]{2,1,0:T(8,128)(2,1)S(1)} %get-tuple-element.30.refs_1_.refs_2_, ...), custom_call_target="tpu_custom_call" | custom-call | flops 1000 | bytes 1000 | tf_op jit(solution)/shard_map/pallas_call | solution.py:215
  715.9 16.0 %shard_map.49 = bf16[2,4,768,768]{3,2,1,0:T(8,128)(2,1)} custom-call(s32[2]{0:T(128)S(1)} %pad_add_fusion.where, bf16[4,2,768,256]{3,2,1,0:T(8,128)(2,1)} %pad_maximum_fusion.refs_0_, bf16[2,768,256]{2,1,0:T(8,128)(2,1)S(1)} %get-tuple-element.30.refs_1_.refs_2_, ...), custom_call_target="tpu_custom_call", output_to_operand_aliasing={{}: (24, {})} | custom-call | flops 1000 | bytes 1000 | tf_op jit(solution)/shard_map/pallas_call | solution.py:215
  (147 shorter events, 94.6 us)
Async XLA Ops:
  28.2 101.3 %all-to-all-start = ((bf16[16,96,1536]{2,1,0:T(8,128)(2,1)}), bf16[16,96,1536]{2,1,0:T(8,128)(2,1)}, u32[]{:S(2)}, u32[]{:S(2)}) async-start(bf16[16,96,1536]{2,1,0:T(8,128)(2,1)} %bitcast.28), calls=%async_computation | async-start | bytes 9437184 | tf_op jit(solution)/shard_map/all_to_all | solution.py:270
  35.6 461.6 %all-gather.9.cloned.1.call-start = ((), (), s32[]{:S(2)}) async-start(), calls=%async_computation.2 | async-start | bytes 11796480 | tf_op jit(solution)/shard_map/all_gather | solution.py:276
  138.4 372.6 %all-gather.11.cloned.1.call-start = ((), (), s32[]{:S(2)}) async-start(), calls=%async_computation.3 | async-start | bytes 11796480 | tf_op jit(solution)/shard_map/all_gather | solution.py:276
  279.8 352.7 %all-gather.13.cloned.1.call-start = ((), (), s32[]{:S(2)}) async-start(), calls=%async_computation.4 | async-start | bytes 11796480 | tf_op jit(solution)/shard_map/all_gather | solution.py:314
  279.8 56.1 %collective-permute-start.12 = (bf16[2,768,768]{2,1,0:T(8,128)(2,1)}, bf16[2,768,768]{2,1,0:T(8,128)(2,1)S(1)}, u32[]{:S(2)}, u32[]{:S(2)}) collective-permute-start(bf16[2,768,768]{2,1,0:T(8,128)(2,1)} %shard_map.40.refs_1_), channel_id=1, source_target_pairs={{4,0},{8,4},{12,8},{5,1},{9,5},{13,9},{6,2},{10,6},{14,10},{7,3},{... | collective-permute-start | bytes 7077896 | tf_op jit(solution)/shard_map/ppermute | solution.py:21
  281.1 56.1 %collective-permute-start.13 = (bf16[2,768,768]{2,1,0:T(8,128)(2,1)}, bf16[2,768,768]{2,1,0:T(8,128)(2,1)S(1)}, u32[]{:S(2)}, u32[]{:S(2)}) collective-permute-start(bf16[2,768,768]{2,1,0:T(8,128)(2,1)} %shard_map.40.refs_1_), channel_id=1, source_target_pairs={{0,4},{4,8},{8,12},{1,5},{5,9},{9,13},{2,6},{6,10},{10,14},{3,7},{... | collective-permute-start | bytes 7077896 | tf_op jit(solution)/shard_map/ppermute | solution.py:21
  337.2 56.4 %collective-permute-start.14 = (bf16[2,768,768]{2,1,0:T(8,128)(2,1)S(1)}, bf16[2,768,768]{2,1,0:T(8,128)(2,1)}, u32[]{:S(2)}, u32[]{:S(2)}) collective-permute-start(bf16[2,768,768]{2,1,0:T(8,128)(2,1)S(1)} %collective-permute-done.12.refs_2_), channel_id=1, source_target_pairs={{4,0},{8,4},{5,1},{9,5},{6,2},{10,6},{7,3},{11,7},{20,16},{24,20},... | collective-permute-start | bytes 7077896 | tf_op jit(solution)/shard_map/ppermute | solution.py:21
  338.5 56.4 %collective-permute-start.15 = (bf16[2,768,768]{2,1,0:T(8,128)(2,1)S(1)}, bf16[2,768,768]{2,1,0:T(8,128)(2,1)}, u32[]{:S(2)}, u32[]{:S(2)}) collective-permute-start(bf16[2,768,768]{2,1,0:T(8,128)(2,1)S(1)} %collective-permute-done.13.refs_3_), channel_id=1, source_target_pairs={{4,8},{8,12},{5,9},{9,13},{6,10},{10,14},{7,11},{11,15},{20,24},{2... | collective-permute-start | bytes 7077896 | tf_op jit(solution)/shard_map/ppermute | solution.py:21
  340.6 69.8 %collective-permute-start = (bf16[2,768,256]{2,1,0:T(8,128)(2,1)}, bf16[2,768,256]{2,1,0:T(8,128)(2,1)S(1)}, u32[]{:S(2)}, u32[]{:S(2)}) collective-permute-start(bf16[2,768,256]{2,1,0:T(8,128)(2,1)} %copy-done.8), channel_id=1, source_target_pairs={{4,0},{8,4},{12,8},{5,1},{9,5},{13,9},{6,2},{10,6},{14,10},{7,3},{... | collective-permute-start | bytes 2359304 | tf_op jit(solution)/shard_map/ppermute | solution.py:21
  341.9 73.4 %collective-permute-start.1 = (bf16[2,768,256]{2,1,0:T(8,128)(2,1)}, bf16[2,768,256]{2,1,0:T(8,128)(2,1)S(1)}, u32[]{:S(2)}, u32[]{:S(2)}) collective-permute-start(bf16[2,768,256]{2,1,0:T(8,128)(2,1)} %copy-done.8), channel_id=1, source_target_pairs={{0,4},{4,8},{8,12},{1,5},{5,9},{9,13},{2,6},{6,10},{10,14},{3,7},{... | collective-permute-start | bytes 2359304 | tf_op jit(solution)/shard_map/ppermute | solution.py:21
  393.7 117.3 %collective-permute-start.16 = (bf16[2,768,768]{2,1,0:T(8,128)(2,1)}, bf16[2,768,768]{2,1,0:T(8,128)(2,1)}, u32[]{:S(2)}, u32[]{:S(2)}) collective-permute-start(bf16[2,768,768]{2,1,0:T(8,128)(2,1)} %collective-permute-done.14.refs_4_), channel_id=1, source_target_pairs={{4,0},{5,1},{6,2},{7,3},{20,16},{21,17},{22,18},{23,19}} | collective-permute-start | bytes 7077896 | tf_op jit(solution)/shard_map/ppermute | solution.py:21
  395.0 116.0 %collective-permute-start.17 = (bf16[2,768,768]{2,1,0:T(8,128)(2,1)}, bf16[2,768,768]{2,1,0:T(8,128)(2,1)}, u32[]{:S(2)}, u32[]{:S(2)}) collective-permute-start(bf16[2,768,768]{2,1,0:T(8,128)(2,1)} %collective-permute-done.15.refs_5_), channel_id=1, source_target_pairs={{8,12},{9,13},{10,14},{11,15},{24,28},{25,29},{26,30},{27,31}} | collective-permute-start | bytes 7077896 | tf_op jit(solution)/shard_map/ppermute | solution.py:21
  397.0 80.9 %collective-permute-start.6 = (bf16[2,768,256]{2,1,0:T(8,128)(2,1)S(1)}, bf16[2,768,256]{2,1,0:T(8,128)(2,1)}, u32[]{:S(2)}, u32[]{:S(2)}) collective-permute-start(bf16[2,768,256]{2,1,0:T(8,128)(2,1)S(1)} %get-tuple-element.30.refs_1_.refs_2_), channel_id=1, source_target_pairs={{4,0},{8,4},{12,8},{5,1},{9,5},{13,9},{6,2},{10,6},{14,10},{7,3},{... | collective-permute-start | bytes 2359304 | tf_op jit(solution)/shard_map/ppermute | solution.py:21
  410.4 69.8 %collective-permute-start.7 = (bf16[2,768,256]{2,1,0:T(8,128)(2,1)S(1)}, bf16[2,768,256]{2,1,0:T(8,128)(2,1)}, u32[]{:S(2)}, u32[]{:S(2)}) collective-permute-start(bf16[2,768,256]{2,1,0:T(8,128)(2,1)S(1)} %get-tuple-element.30.refs_1_.refs_2_), channel_id=1, source_target_pairs={{0,4},{4,8},{8,12},{1,5},{5,9},{9,13},{2,6},{6,10},{10,14},{3,7},{... | collective-permute-start | bytes 2359304 | tf_op jit(solution)/shard_map/ppermute | solution.py:21
  415.3 79.4 %collective-permute-start.8 = (bf16[2,768,256]{2,1,0:T(8,128)(2,1)}, bf16[2,768,256]{2,1,0:T(8,128)(2,1)S(1)}, u32[]{:S(2)}, u32[]{:S(2)}) collective-permute-start(bf16[2,768,256]{2,1,0:T(8,128)(2,1)} %copy-done.6), channel_id=1, source_target_pairs={{4,0},{8,4},{12,8},{5,1},{9,5},{13,9},{6,2},{10,6},{14,10},{7,3},{... | collective-permute-start | bytes 2359304 | tf_op jit(solution)/shard_map/ppermute | solution.py:21
  547.3 38.5 %collective-permute-start.22 = (bf16[2,768,256]{2,1,0:T(8,128)(2,1)}, bf16[2,768,256]{2,1,0:T(8,128)(2,1)S(1)}, u32[]{:S(2)}, u32[]{:S(2)}) collective-permute-start(bf16[2,768,256]{2,1,0:T(8,128)(2,1)} %collective-permute-done.10.refs_4_.refs_5_), channel_id=1, source_target_pairs={{4,0},{5,1},{6,2},{7,3},{20,16},{21,17},{22,18},{23,19}} | collective-permute-start | bytes 2359304 | tf_op jit(solution)/shard_map/ppermute | solution.py:21
  548.6 37.9 %collective-permute-start.23 = (bf16[2,768,256]{2,1,0:T(8,128)(2,1)}, bf16[2,768,256]{2,1,0:T(8,128)(2,1)S(1)}, u32[]{:S(2)}, u32[]{:S(2)}) collective-permute-start(bf16[2,768,256]{2,1,0:T(8,128)(2,1)} %collective-permute-done.11.refs_5_.refs_6_), channel_id=1, source_target_pairs={{8,12},{9,13},{10,14},{11,15},{24,28},{25,29},{26,30},{27,31}} | collective-permute-start | bytes 2359304 | tf_op jit(solution)/shard_map/ppermute | solution.py:21
  549.4 53.4 %collective-permute-start.2 = (bf16[2,768,256]{2,1,0:T(8,128)(2,1)S(1)}, bf16[2,768,256]{2,1,0:T(8,128)(2,1)}, u32[]{:S(2)}, u32[]{:S(2)}) collective-permute-start(bf16[2,768,256]{2,1,0:T(8,128)(2,1)S(1)} %copy-done.11), channel_id=1, source_target_pairs={{4,0},{8,4},{5,1},{9,5},{6,2},{10,6},{7,3},{11,7},{20,16},{24,20},... | collective-permute-start | bytes 2359304 | tf_op jit(solution)/shard_map/ppermute | solution.py:21
  570.5 49.0 %collective-permute-start.20 = (bf16[2,768,256]{2,1,0:T(8,128)(2,1)S(1)}, bf16[2,768,256]{2,1,0:T(8,128)(2,1)S(1)}, u32[]{:S(2)}, u32[]{:S(2)}) collective-permute-start(bf16[2,768,256]{2,1,0:T(8,128)(2,1)S(1)} %collective-permute-done.18.refs_4_.refs_12_.refs_11_), channel_id=1, source_target_pairs={{4,0},{5,1},{6,2},{7,3},{20,16},{21,17},{22,18},{23,19}} | collective-permute-start | bytes 2359304 | tf_op jit(solution)/shard_map/ppermute | solution.py:21
  602.8 54.8 %collective-permute-start.4 = (bf16[2,768,256]{2,1,0:T(8,128)(2,1)}, bf16[2,768,256]{2,1,0:T(8,128)(2,1)}, u32[]{:S(2)}, u32[]{:S(2)}) collective-permute-start(bf16[2,768,256]{2,1,0:T(8,128)(2,1)} %collective-permute-done.2.refs_4_.refs_19_.refs_18_), channel_id=1, source_target_pairs={{4,0},{5,1},{6,2},{7,3},{20,16},{21,17},{22,18},{23,19}} | collective-permute-start | bytes 2359304 | tf_op jit(solution)/shard_map/ppermute | solution.py:21
  604.1 53.5 %collective-permute-start.5 = (bf16[2,768,256]{2,1,0:T(8,128)(2,1)}, bf16[2,768,256]{2,1,0:T(8,128)(2,1)}, u32[]{:S(2)}, u32[]{:S(2)}) collective-permute-start(bf16[2,768,256]{2,1,0:T(8,128)(2,1)} %collective-permute-done.3.refs_5_.refs_20_.refs_19_), channel_id=1, source_target_pairs={{8,12},{9,13},{10,14},{11,15},{24,28},{25,29},{26,30},{27,31}} | collective-permute-start | bytes 2359304 | tf_op jit(solution)/shard_map/ppermute | solution.py:21
  631.6 35.7 %collective-permute-start.25 = (bf16[2,768,256]{2,1,0:T(8,128)(2,1)}, bf16[2,768,256]{2,1,0:T(8,128)(2,1)}, u32[]{:S(2)}, u32[]{:S(2)}) collective-permute-start(bf16[2,768,256]{2,1,0:T(8,128)(2,1)} %get-tuple-element.48), channel_id=1, source_target_pairs={{0,2},{1,3},{2,0},{3,1},{4,6},{5,7},{6,4},{7,5},{8,10},{9,11},{10,... | collective-permute-start | bytes 2359304 | tf_op jit(solution)/shard_map/ppermute | solution.py:89
  632.5 36.8 %collective-permute-start.29 = (bf16[2,768,256]{2,1,0:T(8,128)(2,1)}, bf16[2,768,256]{2,1,0:T(8,128)(2,1)}, u32[]{:S(2)}, u32[]{:S(2)}) collective-permute-start(bf16[2,768,256]{2,1,0:T(8,128)(2,1)} %get-tuple-element.47), channel_id=1, source_target_pairs={{0,1},{1,0},{2,3},{3,2},{4,5},{5,4},{6,7},{7,6},{8,9},{9,8},{10,11... | collective-permute-start | bytes 2359304 | tf_op jit(solution)/shard_map/ppermute | solution.py:89
  669.3 44.7 %collective-permute-start.26 = (bf16[2,768,256]{2,1,0:T(8,128)(2,1)S(1)}, bf16[2,768,256]{2,1,0:T(8,128)(2,1)S(1)}, u32[]{:S(2)}, u32[]{:S(2)}) collective-permute-start(bf16[2,768,256]{2,1,0:T(8,128)(2,1)S(1)} %get-tuple-element.49), channel_id=1, source_target_pairs={{0,1},{1,0},{2,3},{3,2},{4,5},{5,4},{6,7},{7,6},{8,9},{9,8},{10,11... | collective-permute-start | bytes 2359304 | tf_op jit(solution)/shard_map/ppermute | solution.py:89
  (44 other events, 1088.3 us)
Sparse Core Ops, SparseCore 0:
  138.5 133.9 all-gather.8
  279.9 64.9 all-gather.10
  545.4 85.2 all-gather.12

commit v7 on v6

--- a/solution.py
+++ b/solution.py
@@ -81,10 +81,12 @@
     return lax.optimization_barrier((value, earlier))[0]
 
 
-def gather_cols(piece, n_col):
+def gather_cols(piece, n_col, second_after=None):
     held = {0: piece}
     bit = n_col // 2
     while bit:
+        if second_after is not None and len(held) == 2:
+            held = {d: after(a, second_after) for d, a in held.items()}
         pairs = [(c, c ^ bit) for c in range(n_col)]
         arrived = {d ^ bit: lax.ppermute(a, "col", pairs) for d, a in held.items()}
         held.update(arrived)
@@ -93,17 +95,26 @@
 
 
 def product_kernel(opts, where, *refs):
-    plan, groups, order, n_col = opts["plan"], opts["groups"], opts["order"], opts["n_col"]
-    per_third = opts["per_third"]
-    lefts, refs = refs[: len(groups)], refs[len(groups) :]
+    plan, groups, order, n_col, count = (opts[k] for k in ("plan", "groups", "order", "n_col", "count"))
+    per_third, by_xor = opts["per_third"], opts["by_xor"]
+    arrays, refs = refs[: opts["lefts"]], refs[opts["lefts"] :]
     sources, refs = refs[: opts["sources"]], refs[opts["sources"] :]
     before = refs[0] if opts["before"] else None
-    *outs, right, total, sems = refs[opts["before"] + opts["held"] :]
+    *outs, left, right, total, left_sems, sems = refs[opts["before"] + opts["held"] :]
     row, me = where[0], where[1]
     sub = right.shape[2] // 2
     depth = right.shape[1] // n_col
     first = groups[0][0] * sub
-    third, step = pl.program_id(0), pl.program_id(1)
+    step, third = pl.program_id(0), pl.program_id(1)
+
+    def left_copies(c):
+        found, at = [], 0
+        for g, group in enumerate(groups):
+            source = arrays[g * n_col + c] if by_xor else arrays[g].at[c]
+            lanes = pl.ds(at, len(group) * sub)
+            found.append(pltpu.make_async_copy(source, left.at[c, :, :, lanes], left_sems.at[g, c]))
+            at += len(group) * sub
+        return found
 
     def copy_of(source, from_row, t, p, block):
         lanes = pl.ds(0 if per_third else (opts["third"] + t) * sub, sub)
@@ -116,7 +127,9 @@
 
     @pl.when((third == 0) & (step == 0))
     def _():
-        for t in range(right.shape[0]):
+        for copy in left_copies(0):
+            copy.start()
+        for t in range(count):
             for s, (low, high, up) in enumerate(plan):
                 source = sources[t * len(plan) + s if per_third else s]
                 if len(plan) == 1:
@@ -130,81 +143,91 @@
                     for p in range(2):
                         copy_of(source, first, t, p, row + up).start()
 
-    block = me ^ step if opts["by_xor"] else step
-    for t in range(right.shape[0]):
+        for c in range(1, n_col):
+            for copy in left_copies(c):
+                copy.start()
+
+    for c in range(n_col):
+
+        @pl.when((third == 0) & (step == c))
+        def _(c=c):
+            for copy in left_copies(c):
+                copy.wait()
+
+    block = me ^ step if by_xor else step
+    for t in range(count):
 
         @pl.when(third == t)
         def _(t=t):
             for p in range(2):
                 copy_of(sources[0], first, t, p, block).wait()
 
-    real = imag = None
-    start = block * depth
-    for left, group in zip(lefts, groups):
-        deep = len(group) * sub
-        rows = right[third, pl.ds(pl.multiple_of(start, 32), deep), :]
-        start = start + deep
-        by_real = jnp.dot(left[0, 0], rows, preferred_element_type=F32)
-        by_imag = jnp.dot(left[0, 1], rows, preferred_element_type=F32)
-        real_now = by_real[:, :sub] - by_imag[:, sub:]
-        imag_now = by_real[:, sub:] + by_imag[:, :sub]
-        real = real_now if real is None else real + real_now
-        imag = imag_now if imag is None else imag + imag_now
+    rows = right[third, pl.ds(pl.multiple_of(block * depth, 32), depth), :]
+    by_real = jnp.dot(left[step, 0], rows, preferred_element_type=F32)
+    by_imag = jnp.dot(left[step, 1], rows, preferred_element_type=F32)
+    real = by_real[:, :sub] - by_imag[:, sub:]
+    imag = by_real[:, sub:] + by_imag[:, :sub]
 
     @pl.when(step == 0)
     def _():
-        total[0] = real if before is None else real + before[0]
-        total[1] = imag if before is None else imag + before[1]
+        total[third, 0] = real if before is None else real + before[0]
+        total[third, 1] = imag if before is None else imag + before[1]
 
     @pl.when(step > 0)
     def _():
-        total[0] += real
-        total[1] += imag
+        total[third, 0] += real
+        total[third, 1] += imag
 
     @pl.when(step == n_col - 1)
     def _():
         for p in range(2):
             if order is None:
-                outs[0][p] = total[p]
+                outs[0][p] = total[third, p]
                 continue
-            value = (total[p] * opts["weight"]).astype(BF16)
+            value = (total[third, p] * opts["weight"]).astype(BF16)
             outs[0][0, p] = value
             if len(outs) > 1:
                 outs[1][p] = value
 
 
-def complex_product(where, lefts, plan, sources, per_third, count, shape, held, at, before=None, piece_at=(0, 1), by_xor=False):
+def complex_product(where, lefts, plan, sources, per_third, count, shape, held, at, before=None):
     groups = [group for _, group in lefts]
-    arrays = [a for a, _ in lefts]
-    n_col, _, rows, lanes = arrays[0].shape
-    sub = lanes // len(groups[0])
+    by_xor = isinstance(lefts[0][0], list)
+    arrays = [a for pieces, _ in lefts for a in pieces] if by_xor else [a for a, _ in lefts]
+    n_col = len(lefts[0][0]) if by_xor else arrays[0].shape[0]
+    rows = arrays[0].shape[-2]
+    sub = arrays[0].shape[-1] // len(groups[0])
+    lanes = sum(len(g) for g in groups) * sub
     order, third = None, 0
+
+    def late(c, t):
+        return jnp.where(c == n_col - 1, t, 0)
+
     if at is None:
-        out_specs = [pl.BlockSpec((2, rows, sub), lambda t, c, s: (0, 0, t))]
+        out_specs = [pl.BlockSpec((2, rows, sub), lambda c, t, s: (0, 0, late(c, t)))]
         out_shape = [jax.ShapeDtypeStruct((2, rows, count * sub), F32)]
     else:
         order, f, third = at
-        out_specs = [pl.BlockSpec((1, 2, rows, sub), lambda t, c, s: (order, f, 0, third + t))]
+        out_specs = [pl.BlockSpec((1, 2, rows, sub), lambda c, t, s: (order, f, 0, third + late(c, t)))]
         out_shape = [jax.ShapeDtypeStruct(shape, BF16)]
         if order == 0:
-            which, of = piece_at
-            out_specs.append(pl.BlockSpec((2, rows, sub), lambda t, c, s: (0, 0, which + t)))
-            out_shape.append(jax.ShapeDtypeStruct((2, rows, of * sub), BF16))
-    in_specs = [pl.BlockSpec((1, 2, rows, a.shape[3]), lambda t, c, s: (c, 0, 0, 0)) for a in arrays]
-    in_specs += [pl.BlockSpec(memory_space=pl.ANY)] * len(sources)
+            out_specs.append(pl.BlockSpec((2, rows, sub), lambda c, t, s: (0, 0, late(c, t))))
+            out_shape.append(jax.ShapeDtypeStruct((2, rows, count * sub), BF16))
+    in_specs = [pl.BlockSpec(memory_space=pl.ANY)] * (len(arrays) + len(sources))
     args = [*arrays, *sources]
     if before is not None:
-        in_specs.append(pl.BlockSpec((2, rows, sub), lambda t, c, s: (0, 0, t)))
+        in_specs.append(pl.BlockSpec((2, rows, sub), lambda c, t, s: (0, 0, jnp.where(c == 0, t, count - 1))))
         args.append(before)
     aliases = {1 + len(args) + k: k for k in range(len(held))}
     in_specs += [pl.BlockSpec(memory_space=pl.ANY)] * len(held)
-    depth = sum(len(g) for g in groups) * n_col * sub
     opts = dict(
         plan=plan,
         groups=groups,
         order=order,
         third=third,
         n_col=n_col,
+        count=count,
+        lefts=len(arrays),
         sources=len(sources),
         per_third=per_third,
         by_xor=by_xor,
@@ -216,18 +239,20 @@
         functools.partial(product_kernel, opts),
         grid_spec=pltpu.PrefetchScalarGridSpec(
             num_scalar_prefetch=1,
-            grid=(count, n_col),
+            grid=(n_col, count),
             in_specs=in_specs,
             out_specs=out_specs,
             scratch_shapes=[
-                pltpu.VMEM((count, depth, 2 * sub), BF16),
-                pltpu.VMEM((2, rows, sub), F32),
+                pltpu.VMEM((n_col, 2, rows, lanes), BF16),
+                pltpu.VMEM((count, lanes * n_col, 2 * sub), BF16),
+                pltpu.VMEM((count, 2, rows, sub), F32),
+                pltpu.SemaphoreType.DMA((len(groups), n_col)),
                 pltpu.SemaphoreType.DMA((count, 2, n_col)),
             ],
         ),
         out_shape=out_shape,
         input_output_aliases=aliases,
-        compiler_params=pltpu.CompilerParams(vmem_limit_bytes=48 * 2**20),
+        compiler_params=pltpu.CompilerParams(vmem_limit_bytes=(44 if count > 1 else 24) * 2**20),
         cost_estimate=CHEAP,
     )(where, *args, *held)
 
@@ -265,36 +290,39 @@
     placer = (jnp.arange(block_rows, dtype=jnp.int32)[:, None] == places[None, :]).astype(BF16)
 
     tiles, thirds, lefts = [], [], []
+    pair = None
     for f in range(FREQ):
         sent = bin_rows(picker, data, f, n_row, n_col)
         got = lax.all_to_all(
             sent.reshape(n_row * n_col, cap, 2 * tile_cols), ("row", "col"), split_axis=0, concat_axis=0, tiled=True
         ).reshape(-1, 2 * tile_cols)
+        if pair is not None:
+            got, pair = lax.optimization_barrier((got, pair))
         tile, *cut = place_rows(placer, got, line and f == 1)
+        if line and f == 0:
+            pair = hop((tile, tile), 1, n_row)
         tiles.append(tile)
         thirds.append(cut)
         lefts.append((lax.all_gather(tile, "col", axis=0), everything))
 
     if line:
-        pair = hop((tiles[0], tiles[0]), 1, n_row)
         right0 = [tiles[0], *pair]
         for k in range(2, n_row):
-            pair = hop(after(pair, got) if k == 2 else pair, k, n_row)
+            pair = hop(pair, k, n_row)
             right0 += list(pair)
         hops = [[hop((a, a), 1, n_row) for a in thirds[1]]]
         for k in range(2, n_row):
             begun = hops[-1]
-            hops.append([])
-            for j in everything:
-                hops[-1].append(hop(begun[j], k, n_row))
+            hops.append([hop(begun[j], k, n_row) for j in everything])
         right1 = [[thirds[1][j]] + [a for of in hops for a in of[j]] for j in everything]
+        right0[0] = after(right0[0], (hops[0], hops[1][0], lefts[1][0]))
     else:
         right0, right1 = ([lax.all_gather(tile, "row", axis=1, tiled=True)] for tile in tiles)
 
     where = jnp.stack([my_row, lax.axis_index("col")]).astype(jnp.int32)
     shape = (2, planes, block_rows, tile_cols)
 
-    def product(lefts, f, at, held, count=1, **rest):
+    def product(lefts, f, at, held, count=THIRDS, **rest):
         first = 0 if at is None else at[2]
         sources, per_third = right0, False
         if f == 1:
@@ -303,28 +331,18 @@
                 sources = [a for j in range(first, first + count) for a in right1[j]]
         return complex_product(where, lefts, plan, sources, per_third, count, shape, tuple(held), at, **rest)
 
-    held = ()
-    gate = where
+    result, piece = product([lefts[0]], 0, (0, 0, 0), ())
+    found = gather_cols(piece, n_col, hops[1][1:] if line else None)
+    arrived = found[n_col // 2]
+    (result,) = product([(found, everything)], 0, (1, 0, 0), (result,))
+    left1 = []
     for j in everything:
-        if line:
-            gate = (hops[0], lefts[1][0]) if j == 0 else hops[1][0]
-            right0[0] = after(right0[0], gate)
-        held = product([lefts[0]], 0, (0, 0, j), held, piece_at=(j, THIRDS))
-    result, piece = held
-    left0 = [(lax.all_gather(piece, "col", axis=0), everything)]
-    left1 = []
-    arrived = None
-    for j in everything:
-        if j == THIRDS - 1:
-            (result,) = product(left0, 0, (1, 0, 0), (result,), count=THIRDS)
-        result, piece = product([lefts[1]], 1, (0, 1, j), (result,))
-        if arrived is not None:
-            piece = after(piece, arrived)
-        found = gather_cols(piece, n_col)
+        result, piece = product([lefts[1]], 1, (0, 1, j), (result,), count=1)
+        found = gather_cols(after(piece, arrived), n_col)
         arrived = found[n_col // 2]
-        left1.append((jnp.stack(found), (j,)))
-    (sums,) = product(left1[:-1], 1, None, (), count=THIRDS, by_xor=True)
-    return product(left1[-1:], 1, (1, 1, 0), (result,), count=THIRDS, before=sums, by_xor=True)[0]
+        left1.append((found, (j,)))
+    (sums,) = product(left1[:-1], 1, None, ())
+    return product(left1[-1:], 1, (1, 1, 0), (result,), before=sums)[0]
 
 
 def solution(mesh):

time: 749 us -> 737 us (0.984)
  blocking collectives: 221 us -> 92.5 us
  waiting for transfers between devices: 262 us -> 349 us
  starting transfers between devices: 60.1 us -> 106 us
  Pallas kernels: 143 us -> 125 us
  local copies, waits for them, and re-layouts: 28.4 us -> 40.2 us
  other arithmetic: 10.1 us -> 2.12 us
    all_to_all x1 -> x0, blocking collectives: 129 us -> none  [per_device(): lax.all_to_all(sent.reshape(n_row * n_col, cap, 2 * tile_cols), ('row', '...]
    all_to_all x1 -> x2, waiting for transfers between devices: 0.01 us -> 77.2 us  [per_device(): lax.all_to_all(sent.reshape(n_row * n_col, cap, 2 * tile_cols), ('row', '...]
    ppermute x9 -> x12, waiting for transfers between devices: 17.8 us -> 43 us  [gather_cols(): arrived = {d ^ bit: lax.ppermute(a, 'col', pairs) for d, a in held.items()}]
    ppermute x12, starting transfers between devices: 33 us -> 56.6 us  [hop(): lax.ppermute(pair[1], 'row', up)]
    all_to_all x1 -> x2, starting transfers between devices: 7.4 us -> 29.2 us  [per_device(): lax.all_to_all(sent.reshape(n_row * n_col, cap, 2 * tile_cols), ('row', '...]
    pallas_call x9 -> x7, Pallas kernels: 124 us -> 105 us  [complex_product(): pl.pallas_call(functools.partial(product_kernel, opts), grid_spec=pltpu.P...]
    ppermute x12, waiting for transfers between devices: 242 us -> 226 us  [hop(): lax.ppermute(pair[0], 'row', down)]
    unnamed x64 -> x82, local copies, waits for them, and re-layouts: 28.2 us -> 40 us
  transfers between devices with their start and end apart: 37 -> 40, of which waited for: 12 -> 15; matrix products, arithmetic and copies ran while one was open for 1% -> 0% of each run, Pallas kernels for 11% -> 10%
where the time goes in v7:
time: 737 us; the launch traced here: 730 us
  waiting for transfers between devices  349 us (47%)
  Pallas kernels  125 us (17%)
  starting transfers between devices  106 us (14%)
  blocking collectives  92.5 us (13%)
  local copies, waits for them, and re-layouts  40.2 us (5%)
  between operations  14.7 us (2%)
    ppermute x12, waiting for transfers between devices, hop(): lax.ppermute(pair[0], 'row', down)  226 us
    pallas_call x7, Pallas kernels, complex_product(): pl.pallas_call(functools.partial(product_kernel, opts), grid_spec=pltpu.P...  105 us
    all_gather x1, blocking collectives, per_device(): lax.all_gather(spots, ('row', 'col'), axis=0)  92.5 us
    all_to_all x2, waiting for transfers between devices, per_device(): lax.all_to_all(sent.reshape(n_row * n_col, cap, 2 * tile_cols), ('row', '...  77.2 us
    ppermute x12, starting transfers between devices, hop(): lax.ppermute(pair[1], 'row', up)  56.6 us
    ppermute x12, waiting for transfers between devices, gather_cols(): arrived = {d ^ bit: lax.ppermute(a, 'col', pairs) for d, a in held.items()}  43 us
    unnamed x82, local copies, waits for them, and re-layouts  40 us
    all_to_all x2, starting transfers between devices, per_device(): lax.all_to_all(sent.reshape(n_row * n_col, cap, 2 * tile_cols), ('row', '...  29.2 us
  transfers between devices with their start and end apart: 40, of which 15 were waited for; matrix products, arithmetic and copies ran while one was open for 0% of the time, Pallas kernels for 10%

profile of v7, /device:TPU:0, one launch (start us, length us, event | category | flops | bytes accessed | tf_op | source)
XLA Modules:
  0.0 729.7 jit_solution(13870912947169152483)
XLA Ops:
  8.2 10.4 %copy.13 = bf16[384,4,3072]{2,0,1:T(8,128)(2,1)} copy(bf16[384,4,3072]{2,1,0:T(4,128)(2,1)} %param.3) | data formatting | bytes 18874368 | tf_op args[0]
  45.2 77.2 %all-to-all-done.1 = bf16[16,96,1536]{2,1,0:T(8,128)(2,1)} async-done(((bf16[16,96,1536]{2,1,0:T(8,128)(2,1)}), bf16[16,96,1536]{2,1,0:T(8,128)(2,1)}, u32[]{:S(2)}, u32[]{:S(2)}) %all-to-all-start.1) | async-done | bytes 4718624 | tf_op jit(solution)/shard_map/all_to_all | solution.py:296
  122.4 21.8 %all-to-all-start = ((bf16[16,96,1536]{2,1,0:T(8,128)(2,1)}), bf16[16,96,1536]{2,1,0:T(8,128)(2,1)}, u32[]{:S(2)}, u32[]{:S(2)}) async-start(bf16[16,96,1536]{2,1,0:T(8,128)(2,1)} %bitcast.20), calls=%async_computation | async-start | bytes 9437184 | tf_op jit(solution)/shard_map/all_to_all | solution.py:296
  144.4 92.5 %all-gather.3 = s32[16,1,384]{2,1,0:T(1,128)S(1)} all-gather(s32[1,1,384]{2,1,0:T(1,128)S(1)} %reshape.40), channel_id=2, replica_groups=mesh['groups'=2,'row'=4,'col'=4] {'row','col'}, dimensions={0}, use_global_device_ids=true | all-gather | bytes 26112 | tf_op jit(solution)/shard_map/all_gather | solution.py:288
  246.1 27.0 %collective-permute-start.1 = (bf16[2,768,768]{2,1,0:T(8,128)(2,1)}, bf16[2,768,768]{2,1,0:T(8,128)(2,1)}, u32[]{:S(2)}, u32[]{:S(2)}) collective-permute-start(bf16[2,768,768]{2,1,0:T(8,128)(2,1)} %shard_map.39.refs_1_.refs_4_), channel_id=1, source_target_pairs={{0,4},{4,8},{8,12},{1,5},{5,9},{9,13},{2,6},{6,10},{10,14},{3,7},{... | collective-permute-start | bytes 7077896 | tf_op jit(solution)/shard_map/ppermute | solution.py:21
  273.1 48.6 %collective-permute-done.refs_2_.refs_5_ = bf16[2,768,768]{2,1,0:T(8,128)(2,1)} collective-permute-done((bf16[2,768,768]{2,1,0:T(8,128)(2,1)}, bf16[2,768,768]{2,1,0:T(8,128)(2,1)}, u32[]{:S(2)}, u32[]{:S(2)}) %collective-permute-start) | collective-permute-done | bytes 2359328 | tf_op jit(solution)/shard_map/ppermute | solution.py:21
  337.3 11.2 %collective-permute-start.15 = (bf16[2,768,256]{2,1,0:T(8,128)(2,1)S(1)}, bf16[2,768,256]{2,1,0:T(8,128)(2,1)}, u32[]{:S(2)}, u32[]{:S(2)}) collective-permute-start(bf16[2,768,256]{2,1,0:T(8,128)(2,1)S(1)} %get-tuple-element.30.refs_1_.refs_8_.refs_4_), channel_id=1, source_target_pairs={{0,4},{4,8},{8,12},{1,5},{5,9},{9,13},{2,6},{6,10},{10,14},{3,7},{... | collective-permute-start | bytes 2359304 | tf_op jit(solution)/shard_map/ppermute | solution.py:21
  348.5 41.0 %collective-permute-done.20.refs_4_.refs_7_ = bf16[2,768,768]{2,1,0:T(8,128)(2,1)} collective-permute-done((bf16[2,768,768]{2,1,0:T(8,128)(2,1)}, bf16[2,768,768]{2,1,0:T(8,128)(2,1)}, u32[]{:S(2)}, u32[]{:S(2)}) %collective-permute-start.20) | collective-permute-done | bytes 2359328 | tf_op jit(solution)/shard_map/ppermute | solution.py:21
  394.1 12.2 %collective-permute-done.14.refs_2_.refs_9_.refs_5_ = bf16[2,768,256]{2,1,0:T(8,128)(2,1)} collective-permute-done((bf16[2,768,256]{2,1,0:T(8,128)(2,1)S(1)}, bf16[2,768,256]{2,1,0:T(8,128)(2,1)}, u32[]{:S(2)}, u32[]{:S(2)}) %collective-permute-start.14) | collective-permute-done | bytes 786464 | tf_op jit(solution)/shard_map/ppermute | solution.py:21
  411.6 62.0 %collective-permute-done.2.refs_2_.refs_23_.refs_19_ = bf16[2,768,256]{2,1,0:T(8,128)(2,1)S(1)} collective-permute-done((bf16[2,768,256]{2,1,0:T(8,128)(2,1)S(1)}, bf16[2,768,256]{2,1,0:T(8,128)(2,1)S(1)}, u32[]{:S(2)}, u32[]{:S(2)}) %collective-permute-start.2) | collective-permute-done | bytes 786464 | tf_op jit(solution)/shard_map/ppermute | solution.py:21
  477.3 13.2 %collective-permute-done.8.refs_2_.refs_16_.refs_12_ = bf16[2,768,256]{2,1,0:T(8,128)(2,1)S(1)} collective-permute-done((bf16[2,768,256]{2,1,0:T(8,128)(2,1)S(1)}, bf16[2,768,256]{2,1,0:T(8,128)(2,1)S(1)}, u32[]{:S(2)}, u32[]{:S(2)}) %collective-permute-start.8) | collective-permute-done | bytes 786464 | tf_op jit(solution)/shard_map/ppermute | solution.py:21
  493.0 13.2 %collective-permute-done.16.refs_4_.refs_11_.refs_7_ = bf16[2,768,256]{2,1,0:T(8,128)(2,1)} collective-permute-done((bf16[2,768,256]{2,1,0:T(8,128)(2,1)}, bf16[2,768,256]{2,1,0:T(8,128)(2,1)}, u32[]{:S(2)}, u32[]{:S(2)}) %collective-permute-start.16) | collective-permute-done | bytes 786464 | tf_op jit(solution)/shard_map/ppermute | solution.py:21
  506.3 25.6 %shard_map.41 = (bf16[2,4,768,768]{3,2,1,0:T(8,128)(2,1)}, bf16[2,768,768]{2,1,0:T(8,128)(2,1)S(1)}) custom-call(s32[2]{0:T(128)S(1)} %pad_add_fusion.where, bf16[4,2,768,768]{3,2,1,0:T(8,128)(2,1)} %bitcast.22, bf16[2,768,768]{2,1,0:T(8,128)(2,1)} %shard_map.39.refs_1_.refs_4_, bf16[2,768,768]{2,1,0:T(8,128)(2,1)} %collective-permute-done.refs_2_.refs_5_, ...), custom_call_target="tpu_custom_call" | custom-call | flops 1000 | bytes 1000 | tf_op jit(solution)/shard_map/pallas_call | solution.py:238
  537.4 17.6 %collective-permute-done.10.refs_4_.refs_18_.refs_14_ = bf16[2,768,256]{2,1,0:T(8,128)(2,1)} collective-permute-done((bf16[2,768,256]{2,1,0:T(8,128)(2,1)S(1)}, bf16[2,768,256]{2,1,0:T(8,128)(2,1)}, u32[]{:S(2)}, u32[]{:S(2)}) %collective-permute-start.10) | collective-permute-done | bytes 786464 | tf_op jit(solution)/shard_map/ppermute | solution.py:21
  555.0 14.4 %collective-permute-done.4.refs_4_.refs_25_.refs_21_ = bf16[2,768,256]{2,1,0:T(8,128)(2,1)S(1)} collective-permute-done((bf16[2,768,256]{2,1,0:T(8,128)(2,1)S(1)}, bf16[2,768,256]{2,1,0:T(8,128)(2,1)S(1)}, u32[]{:S(2)}, u32[]{:S(2)}) %collective-permute-start.4) | collective-permute-done | bytes 786464 | tf_op jit(solution)/shard_map/ppermute | solution.py:21
  570.9 13.1 %collective-permute-done.25.refs_2_ = bf16[2,768,768]{2,1,0:T(8,128)(2,1)S(1)} collective-permute-done((bf16[2,768,768]{2,1,0:T(8,128)(2,1)S(1)}, bf16[2,768,768]{2,1,0:T(8,128)(2,1)S(1)}, u32[]{:S(2)}, u32[]{:S(2)}) %collective-permute-start.25) | collective-permute-done | bytes 2359328 | tf_op jit(solution)/shard_map/ppermute | solution.py:91
  601.0 22.6 %shard_map.42.refs_8_ = bf16[2,4,768,768]{3,2,1,0:T(8,128)(2,1)} custom-call(s32[2]{0:T(128)S(1)} %pad_add_fusion.where, bf16[2,768,768]{2,1,0:T(8,128)(2,1)S(1)} %copy-done.27, bf16[2,768,768]{2,1,0:T(8,128)(2,1)S(1)} %copy-done.31, bf16[2,768,768]{2,1,0:T(8,128)(2,1)S(1)} %copy-done.29, ...), custom_call_target="tpu_custom_call", output_to_operand_aliasing={{}: (12, {})} | custom-call | flops 1000 | bytes 1000 | tf_op jit(solution)/shard_map/pallas_call | solution.py:238
  623.6 8.6 %shard_map.43 = (bf16[2,4,768,768]{3,2,1,0:T(8,128)(2,1)}, bf16[2,768,256]{2,1,0:T(8,128)(2,1)S(1)}) custom-call(s32[2]{0:T(128)S(1)} %pad_add_fusion.where, bf16[4,2,768,768]{3,2,1,0:T(8,128)(2,1)S(1)} %bitcast.15, bf16[2,768,256]{2,1,0:T(8,128)(2,1)S(1)} %get-tuple-element.30.refs_1_.refs_8_.refs_4_, ...), custom_call_target="tpu_custom_call", output_to_operand_aliasing={{0}: (9, {})} | custom-call | flops 1000 | bytes 1000 | tf_op jit(solution)/shard_map/pallas_call | solution.py:238
  635.6 8.6 %shard_map.44 = (bf16[2,4,768,768]{3,2,1,0:T(8,128)(2,1)}, bf16[2,768,256]{2,1,0:T(8,128)(2,1)S(1)}) custom-call(s32[2]{0:T(128)S(1)} %pad_add_fusion.where, bf16[4,2,768,768]{3,2,1,0:T(8,128)(2,1)S(1)} %bitcast.16, bf16[2,768,256]{2,1,0:T(8,128)(2,1)S(1)} %copy-done.5, bf16[2,768,256]{2,1,0:T(8,128)(2,1)S(1)} %copy-done.18, ...), custom_call_target="tpu_custom_call", output_to_operand_aliasing={{0}: (9, {})} | custom-call | flops 1000 | bytes 1000 | tf_op jit(solution)/shard_map/pallas_call | solution.py:238
  644.2 8.2 %collective-permute-done.27.refs_2_ = bf16[2,768,256]{2,1,0:T(8,128)(2,1)S(1)} collective-permute-done((bf16[2,768,256]{2,1,0:T(8,128)(2,1)S(1)}, bf16[2,768,256]{2,1,0:T(8,128)(2,1)S(1)}, u32[]{:S(2)}, u32[]{:S(2)}) %collective-permute-start.27) | collective-permute-done | bytes 786464 | tf_op jit(solution)/shard_map/ppermute | solution.py:91
  657.8 8.7 %shard_map.45 = (bf16[2,4,768,768]{3,2,1,0:T(8,128)(2,1)}, bf16[2,768,256]{2,1,0:T(8,128)(2,1)S(1)}) custom-call(s32[2]{0:T(128)S(1)} %pad_add_fusion.where, bf16[4,2,768,768]{3,2,1,0:T(8,128)(2,1)S(1)} %bitcast.17, bf16[2,768,256]{2,1,0:T(8,128)(2,1)S(1)} %copy-done.9, bf16[2,768,256]{2,1,0:T(8,128)(2,1)S(1)} %copy-done.12, ...), custom_call_target="tpu_custom_call", output_to_operand_aliasing={{0}: (9, {})} | custom-call | flops 1000 | bytes 1000 | tf_op jit(solution)/shard_map/pallas_call | solution.py:238
  673.9 16.4 %collective-permute-done.30.refs_2_ = bf16[2,768,256]{2,1,0:T(8,128)(2,1)S(1)} collective-permute-done((bf16[2,768,256]{2,1,0:T(8,128)(2,1)S(1)}, bf16[2,768,256]{2,1,0:T(8,128)(2,1)S(1)}, u32[]{:S(2)}, u32[]{:S(2)}) %collective-permute-start.30) | collective-permute-done | bytes 786464 | tf_op jit(solution)/shard_map/ppermute | solution.py:91
  690.3 17.1 %shard_map.46.refs_25_ = f32[2,768,768]{2,1,0:T(8,128)} custom-call(s32[2]{0:T(128)S(1)} %pad_add_fusion.where, bf16[2,768,256]{2,1,0:T(8,128)(2,1)S(1)} %get-tuple-element.43.refs_0_, bf16[2,768,256]{2,1,0:T(8,128)(2,1)S(1)} %collective-permute-done.32.refs_1_, bf16[2,768,256]{2,1,0:T(8,128)(2,1)S(1)} %collective-permute-done.27.refs_2_, ...), custom_call_target="tpu_custom_call" | custom-call | flops 1000 | bytes 1000 | tf_op jit(solution)/shard_map/pallas_call | solution.py:238
  708.7 14.2 %shard_map.47 = bf16[2,4,768,768]{3,2,1,0:T(8,128)(2,1)} custom-call(s32[2]{0:T(128)S(1)} %pad_add_fusion.where, bf16[2,768,256]{2,1,0:T(8,128)(2,1)S(1)} %copy-done.36, bf16[2,768,256]{2,1,0:T(8,128)(2,1)S(1)} %collective-permute-done.29.refs_1_, bf16[2,768,256]{2,1,0:T(8,128)(2,1)S(1)} %collective-permute-done.30.refs_2_, ...), custom_call_target="tpu_custom_call", output_to_operand_aliasing={{}: (27, {})} | custom-call | flops 1000 | bytes 1000 | tf_op jit(solution)/shard_map/pallas_call | solution.py:238
  (165 shorter events, 109.6 us)
Async XLA Ops:
  28.2 94.2 %all-to-all-start.1 = ((bf16[16,96,1536]{2,1,0:T(8,128)(2,1)}), bf16[16,96,1536]{2,1,0:T(8,128)(2,1)}, u32[]{:S(2)}, u32[]{:S(2)}) async-start(bf16[16,96,1536]{2,1,0:T(8,128)(2,1)} %bitcast.21), calls=%async_computation.1 | async-start | bytes 9437184 | tf_op jit(solution)/shard_map/all_to_all | solution.py:296
  122.4 150.7 %all-to-all-start = ((bf16[16,96,1536]{2,1,0:T(8,128)(2,1)}), bf16[16,96,1536]{2,1,0:T(8,128)(2,1)}, u32[]{:S(2)}, u32[]{:S(2)}) async-start(bf16[16,96,1536]{2,1,0:T(8,128)(2,1)} %bitcast.20), calls=%async_computation | async-start | bytes 9437184 | tf_op jit(solution)/shard_map/all_to_all | solution.py:296
  144.2 362.0 %all-gather.7.cloned.1.call-start = ((), (), s32[]{:S(2)}) async-start(), calls=%async_computation.2 | async-start | bytes 11796480 | tf_op jit(solution)/shard_map/all_gather | solution.py:306
  244.8 76.9 %collective-permute-start = (bf16[2,768,768]{2,1,0:T(8,128)(2,1)}, bf16[2,768,768]{2,1,0:T(8,128)(2,1)}, u32[]{:S(2)}, u32[]{:S(2)}) collective-permute-start(bf16[2,768,768]{2,1,0:T(8,128)(2,1)} %shard_map.39.refs_1_.refs_4_), channel_id=1, source_target_pairs={{4,0},{8,4},{12,8},{5,1},{9,5},{13,9},{6,2},{10,6},{14,10},{7,3},{... | collective-permute-start | bytes 7077896 | tf_op jit(solution)/shard_map/ppermute | solution.py:21
  246.1 76.8 %collective-permute-start.1 = (bf16[2,768,768]{2,1,0:T(8,128)(2,1)}, bf16[2,768,768]{2,1,0:T(8,128)(2,1)}, u32[]{:S(2)}, u32[]{:S(2)}) collective-permute-start(bf16[2,768,768]{2,1,0:T(8,128)(2,1)} %shard_map.39.refs_1_.refs_4_), channel_id=1, source_target_pairs={{0,4},{4,8},{8,12},{1,5},{5,9},{9,13},{2,6},{6,10},{10,14},{3,7},{... | collective-permute-start | bytes 7077896 | tf_op jit(solution)/shard_map/ppermute | solution.py:21
  331.9 174.4 %all-gather.9.cloned.1.call-start = ((), (), s32[]{:S(2)}) async-start(), calls=%async_computation.3 | async-start | bytes 11796480 | tf_op jit(solution)/shard_map/all_gather | solution.py:306
  332.6 56.8 %collective-permute-start.20 = (bf16[2,768,768]{2,1,0:T(8,128)(2,1)}, bf16[2,768,768]{2,1,0:T(8,128)(2,1)}, u32[]{:S(2)}, u32[]{:S(2)}) collective-permute-start(bf16[2,768,768]{2,1,0:T(8,128)(2,1)} %collective-permute-done.refs_2_.refs_5_), channel_id=1, source_target_pairs={{4,0},{8,4},{5,1},{9,5},{6,2},{10,6},{7,3},{11,7},{20,16},{24,20},... | collective-permute-start | bytes 7077896 | tf_op jit(solution)/shard_map/ppermute | solution.py:21
  333.9 56.8 %collective-permute-start.21 = (bf16[2,768,768]{2,1,0:T(8,128)(2,1)}, bf16[2,768,768]{2,1,0:T(8,128)(2,1)}, u32[]{:S(2)}, u32[]{:S(2)}) collective-permute-start(bf16[2,768,768]{2,1,0:T(8,128)(2,1)} %collective-permute-done.1.refs_3_.refs_6_), channel_id=1, source_target_pairs={{4,8},{8,12},{5,9},{9,13},{6,10},{10,14},{7,11},{11,15},{20,24},{2... | collective-permute-start | bytes 7077896 | tf_op jit(solution)/shard_map/ppermute | solution.py:21
  336.0 70.3 %collective-permute-start.14 = (bf16[2,768,256]{2,1,0:T(8,128)(2,1)S(1)}, bf16[2,768,256]{2,1,0:T(8,128)(2,1)}, u32[]{:S(2)}, u32[]{:S(2)}) collective-permute-start(bf16[2,768,256]{2,1,0:T(8,128)(2,1)S(1)} %get-tuple-element.30.refs_1_.refs_8_.refs_4_), channel_id=1, source_target_pairs={{4,0},{8,4},{12,8},{5,1},{9,5},{13,9},{6,2},{10,6},{14,10},{7,3},{... | collective-permute-start | bytes 2359304 | tf_op jit(solution)/shard_map/ppermute | solution.py:21
  337.3 73.0 %collective-permute-start.15 = (bf16[2,768,256]{2,1,0:T(8,128)(2,1)S(1)}, bf16[2,768,256]{2,1,0:T(8,128)(2,1)}, u32[]{:S(2)}, u32[]{:S(2)}) collective-permute-start(bf16[2,768,256]{2,1,0:T(8,128)(2,1)S(1)} %get-tuple-element.30.refs_1_.refs_8_.refs_4_), channel_id=1, source_target_pairs={{0,4},{4,8},{8,12},{1,5},{5,9},{9,13},{2,6},{6,10},{10,14},{3,7},{... | collective-permute-start | bytes 2359304 | tf_op jit(solution)/shard_map/ppermute | solution.py:21
  389.4 116.8 %collective-permute-start.22 = (bf16[2,768,768]{2,1,0:T(8,128)(2,1)}, bf16[2,768,768]{2,1,0:T(8,128)(2,1)}, u32[]{:S(2)}, u32[]{:S(2)}) collective-permute-start(bf16[2,768,768]{2,1,0:T(8,128)(2,1)} %collective-permute-done.20.refs_4_.refs_7_), channel_id=1, source_target_pairs={{4,0},{5,1},{6,2},{7,3},{20,16},{21,17},{22,18},{23,19}} | collective-permute-start | bytes 7077896 | tf_op jit(solution)/shard_map/ppermute | solution.py:21
  390.7 115.5 %collective-permute-start.23 = (bf16[2,768,768]{2,1,0:T(8,128)(2,1)}, bf16[2,768,768]{2,1,0:T(8,128)(2,1)}, u32[]{:S(2)}, u32[]{:S(2)}) collective-permute-start(bf16[2,768,768]{2,1,0:T(8,128)(2,1)} %collective-permute-done.21.refs_5_.refs_8_), channel_id=1, source_target_pairs={{8,12},{9,13},{10,14},{11,15},{24,28},{25,29},{26,30},{27,31}} | collective-permute-start | bytes 7077896 | tf_op jit(solution)/shard_map/ppermute | solution.py:21
  392.8 80.8 %collective-permute-start.2 = (bf16[2,768,256]{2,1,0:T(8,128)(2,1)S(1)}, bf16[2,768,256]{2,1,0:T(8,128)(2,1)S(1)}, u32[]{:S(2)}, u32[]{:S(2)}) collective-permute-start(bf16[2,768,256]{2,1,0:T(8,128)(2,1)S(1)} %copy-done.8), channel_id=1, source_target_pairs={{4,0},{8,4},{12,8},{5,1},{9,5},{13,9},{6,2},{10,6},{14,10},{7,3},{... | collective-permute-start | bytes 2359304 | tf_op jit(solution)/shard_map/ppermute | solution.py:21
  406.3 69.7 %collective-permute-start.3 = (bf16[2,768,256]{2,1,0:T(8,128)(2,1)S(1)}, bf16[2,768,256]{2,1,0:T(8,128)(2,1)S(1)}, u32[]{:S(2)}, u32[]{:S(2)}) collective-permute-start(bf16[2,768,256]{2,1,0:T(8,128)(2,1)S(1)} %copy-done.8), channel_id=1, source_target_pairs={{0,4},{4,8},{8,12},{1,5},{5,9},{9,13},{2,6},{6,10},{10,14},{3,7},{... | collective-permute-start | bytes 2359304 | tf_op jit(solution)/shard_map/ppermute | solution.py:21
  410.3 80.1 %collective-permute-start.8 = (bf16[2,768,256]{2,1,0:T(8,128)(2,1)S(1)}, bf16[2,768,256]{2,1,0:T(8,128)(2,1)S(1)}, u32[]{:S(2)}, u32[]{:S(2)}) collective-permute-start(bf16[2,768,256]{2,1,0:T(8,128)(2,1)S(1)} %copy-done.5), channel_id=1, source_target_pairs={{4,0},{8,4},{12,8},{5,1},{9,5},{13,9},{6,2},{10,6},{14,10},{7,3},{... | collective-permute-start | bytes 2359304 | tf_op jit(solution)/shard_map/ppermute | solution.py:21
  476.0 30.2 %collective-permute-start.16 = (bf16[2,768,256]{2,1,0:T(8,128)(2,1)}, bf16[2,768,256]{2,1,0:T(8,128)(2,1)}, u32[]{:S(2)}, u32[]{:S(2)}) collective-permute-start(bf16[2,768,256]{2,1,0:T(8,128)(2,1)} %collective-permute-done.14.refs_2_.refs_9_.refs_5_), channel_id=1, source_target_pairs={{4,0},{8,4},{5,1},{9,5},{6,2},{10,6},{7,3},{11,7},{20,16},{24,20},... | collective-permute-start | bytes 2359304 | tf_op jit(solution)/shard_map/ppermute | solution.py:21
  531.9 52.1 %collective-permute-start.25 = (bf16[2,768,768]{2,1,0:T(8,128)(2,1)S(1)}, bf16[2,768,768]{2,1,0:T(8,128)(2,1)S(1)}, u32[]{:S(2)}, u32[]{:S(2)}) collective-permute-start(bf16[2,768,768]{2,1,0:T(8,128)(2,1)S(1)} %get-tuple-element.35.refs_0_), channel_id=1, source_target_pairs={{0,2},{1,3},{2,0},{3,1},{4,6},{5,7},{6,4},{7,5},{8,10},{9,11},{10,... | collective-permute-start | bytes 7077896 | tf_op jit(solution)/shard_map/ppermute | solution.py:91
  535.3 34.0 %collective-permute-start.4 = (bf16[2,768,256]{2,1,0:T(8,128)(2,1)S(1)}, bf16[2,768,256]{2,1,0:T(8,128)(2,1)S(1)}, u32[]{:S(2)}, u32[]{:S(2)}) collective-permute-start(bf16[2,768,256]{2,1,0:T(8,128)(2,1)S(1)} %copy-done.11), channel_id=1, source_target_pairs={{4,0},{8,4},{5,1},{9,5},{6,2},{10,6},{7,3},{11,7},{20,16},{24,20},... | collective-permute-start | bytes 2359304 | tf_op jit(solution)/shard_map/ppermute | solution.py:21
  536.6 32.7 %collective-permute-start.5 = (bf16[2,768,256]{2,1,0:T(8,128)(2,1)S(1)}, bf16[2,768,256]{2,1,0:T(8,128)(2,1)S(1)}, u32[]{:S(2)}, u32[]{:S(2)}) collective-permute-start(bf16[2,768,256]{2,1,0:T(8,128)(2,1)S(1)} %copy-done.14), channel_id=1, source_target_pairs={{4,8},{8,12},{5,9},{9,13},{6,10},{10,14},{7,11},{11,15},{20,24},{2... | collective-permute-start | bytes 2359304 | tf_op jit(solution)/shard_map/ppermute | solution.py:21
  585.4 38.2 %collective-permute-start.18 = (bf16[2,768,256]{2,1,0:T(8,128)(2,1)}, bf16[2,768,256]{2,1,0:T(8,128)(2,1)}, u32[]{:S(2)}, u32[]{:S(2)}) collective-permute-start(bf16[2,768,256]{2,1,0:T(8,128)(2,1)} %collective-permute-done.16.refs_4_.refs_11_.refs_7_), channel_id=1, source_target_pairs={{4,0},{5,1},{6,2},{7,3},{20,16},{21,17},{22,18},{23,19}} | collective-permute-start | bytes 2359304 | tf_op jit(solution)/shard_map/ppermute | solution.py:21
  586.7 36.9 %collective-permute-start.19 = (bf16[2,768,256]{2,1,0:T(8,128)(2,1)}, bf16[2,768,256]{2,1,0:T(8,128)(2,1)}, u32[]{:S(2)}, u32[]{:S(2)}) collective-permute-start(bf16[2,768,256]{2,1,0:T(8,128)(2,1)} %collective-permute-done.17.refs_5_.refs_12_.refs_8_), channel_id=1, source_target_pairs={{8,12},{9,13},{10,14},{11,15},{24,28},{25,29},{26,30},{27,31}} | collective-permute-start | bytes 2359304 | tf_op jit(solution)/shard_map/ppermute | solution.py:21
  588.3 47.3 %collective-permute-start.12 = (bf16[2,768,256]{2,1,0:T(8,128)(2,1)}, bf16[2,768,256]{2,1,0:T(8,128)(2,1)}, u32[]{:S(2)}, u32[]{:S(2)}) collective-permute-start(bf16[2,768,256]{2,1,0:T(8,128)(2,1)} %collective-permute-done.10.refs_4_.refs_18_.refs_14_), channel_id=1, source_target_pairs={{4,0},{5,1},{6,2},{7,3},{20,16},{21,17},{22,18},{23,19}} | collective-permute-start | bytes 2359304 | tf_op jit(solution)/shard_map/ppermute | solution.py:21
  591.0 44.6 %collective-permute-start.13 = (bf16[2,768,256]{2,1,0:T(8,128)(2,1)}, bf16[2,768,256]{2,1,0:T(8,128)(2,1)}, u32[]{:S(2)}, u32[]{:S(2)}) collective-permute-start(bf16[2,768,256]{2,1,0:T(8,128)(2,1)} %collective-permute-done.11.refs_5_.refs_19_.refs_15_), channel_id=1, source_target_pairs={{8,12},{9,13},{10,14},{11,15},{24,28},{25,29},{26,30},{27,31}} | collective-permute-start | bytes 2359304 | tf_op jit(solution)/shard_map/ppermute | solution.py:21
  673.4 34.1 %collective-permute-start.29 = (bf16[2,768,256]{2,1,0:T(8,128)(2,1)S(1)}, bf16[2,768,256]{2,1,0:T(8,128)(2,1)S(1)}, u32[]{:S(2)}, u32[]{:S(2)}) collective-permute-start(bf16[2,768,256]{2,1,0:T(8,128)(2,1)S(1)} %get-tuple-element.45.refs_0_), channel_id=1, source_target_pairs={{0,1},{1,0},{2,3},{3,2},{4,5},{5,4},{6,7},{7,6},{8,9},{9,8},{10,11... | collective-permute-start | bytes 2359304 | tf_op jit(solution)/shard_map/ppermute | solution.py:91
  (56 other events, 937.9 us)
Sparse Core Ops, SparseCore 0:
  332.0 66.8 all-gather.6
  400.4 64.2 all-gather.8

commit v8 on v7

--- a/solution.py
+++ b/solution.py
@@ -51,18 +51,19 @@
     )(picker, data)
 
 
-def place_kernel(placer, got, tile, *thirds):
+def place_kernel(placer, got, tile, *parts):
     rows = jnp.dot(placer[...], got[...], preferred_element_type=F32).astype(BF16)
     tile[0] = rows
-    for j, third in enumerate(thirds):
-        sub = third.shape[2]
-        third[0] = rows[:, j * sub : (j + 1) * sub]
-
-
-def place_rows(placer, got, split):
+    at = 0
+    for part in parts:
+        part[0] = rows[:, at : at + part.shape[2]]
+        at += part.shape[2]
+
+
+def place_rows(placer, got, parts):
     block_rows, arrived = placer.shape
     cols = got.shape[1] // 2
-    sizes = [cols] + [cols // THIRDS] * (THIRDS if split else 0)
+    sizes = [cols] + [n * cols // THIRDS for n in parts]
     return pl.pallas_call(
         place_kernel,
         grid=(2,),
@@ -95,8 +96,8 @@
 
 
 def product_kernel(opts, where, *refs):
-    plan, groups, order, n_col, count = (opts[k] for k in ("plan", "groups", "order", "n_col", "count"))
-    per_third, by_xor = opts["per_third"], opts["by_xor"]
+    views, groups, order, n_col = (opts[k] for k in ("views", "groups", "order", "n_col"))
+    by_xor, count = opts["by_xor"], len(views)
     arrays, refs = refs[: opts["lefts"]], refs[opts["lefts"] :]
     sources, refs = refs[: opts["sources"]], refs[opts["sources"] :]
     before = refs[0] if opts["before"] else None
@@ -116,52 +117,56 @@
             at += len(group) * sub
         return found
 
-    def copy_of(source, from_row, t, p, block):
-        lanes = pl.ds(0 if per_third else (opts["third"] + t) * sub, sub)
-        start = block * depth if isinstance(block, int) else pl.multiple_of(block * depth, 32)
-        return pltpu.make_async_copy(
-            source.at[p, pl.ds(from_row, depth), lanes],
-            right.at[t, pl.ds(start, depth), pl.ds(p * sub, sub)],
-            sems.at[t, p, block],
-        )
-
-    @pl.when((third == 0) & (step == 0))
-    def _():
-        for copy in left_copies(0):
+    def right_copies(t, s, lane, c):
+        block = me ^ c if by_xor else c
+        start = pl.multiple_of(block * depth, 32) if by_xor else block * depth
+        found = []
+        for p in range(2):
+            source, lanes = sources[s], pl.ds(lane, sub)
+            if len(source.shape) == 4:
+                rows = source.at[block, p, pl.ds(first, depth), lanes]
+            elif source.shape[1] == NS:
+                rows = source.at[p, pl.ds(pl.multiple_of(block * sub * THIRDS + first, 32), depth), lanes]
+            else:
+                rows = source.at[p, pl.ds(first, depth), lanes]
+            target = right.at[t, pl.ds(start, depth), pl.ds(p * sub, sub)]
+            found.append(pltpu.make_async_copy(rows, target, sems.at[t, p, c]))
+        return found
+
+    def start_all(c):
+        for copy in left_copies(c):
             copy.start()
-        for t in range(count):
-            for s, (low, high, up) in enumerate(plan):
-                source = sources[t * len(plan) + s if per_third else s]
-                if len(plan) == 1:
-                    for c in range(n_col):
-                        for p in range(2):
-                            copy_of(source, c * sub * THIRDS + first, t, p, c).start()
+        for t, (found, lane) in enumerate(views):
+            for s, up in found:
+                if up is None:
+                    for copy in right_copies(t, s, lane, c):
+                        copy.start()
                     continue
 
-                @pl.when((row >= low) & (row <= high))
-                def _(source=source, up=up, t=t):
-                    for p in range(2):
-                        copy_of(source, first, t, p, row + up).start()
-
-        for c in range(1, n_col):
-            for copy in left_copies(c):
-                copy.start()
+                @pl.when(row + up == (me ^ c if by_xor else c))
+                def _(t=t, s=s, lane=lane):
+                    for copy in right_copies(t, s, lane, c):
+                        copy.start()
 
     for c in range(n_col):
 
         @pl.when((third == 0) & (step == c))
         def _(c=c):
+            if c == 0:
+                start_all(0)
+            if c + 1 < n_col:
+                start_all(c + 1)
             for copy in left_copies(c):
                 copy.wait()
 
+        for t, (found, lane) in enumerate(views):
+
+            @pl.when((third == t) & (step == c))
+            def _(c=c, t=t, s=found[0][0], lane=lane):
+                for copy in right_copies(t, s, lane, c):
+                    copy.wait()
+
     block = me ^ step if by_xor else step
-    for t in range(count):
-
-        @pl.when(third == t)
-        def _(t=t):
-            for p in range(2):
-                copy_of(sources[0], first, t, p, block).wait()
-
     rows = right[third, pl.ds(pl.multiple_of(block * depth, 32), depth), :]
     by_real = jnp.dot(left[step, 0], rows, preferred_element_type=F32)
     by_imag = jnp.dot(left[step, 1], rows, preferred_element_type=F32)
@@ -190,7 +195,7 @@
                 outs[1][p] = value
 
 
-def complex_product(where, lefts, plan, sources, per_third, count, shape, held, at, before=None):
+def complex_product(where, lefts, sources, views, shape, held, at, before=None):
     groups = [group for _, group in lefts]
     by_xor = isinstance(lefts[0][0], list)
     arrays = [a for pieces, _ in lefts for a in pieces] if by_xor else [a for a, _ in lefts]
@@ -198,7 +203,7 @@
     rows = arrays[0].shape[-2]
     sub = arrays[0].shape[-1] // len(groups[0])
     lanes = sum(len(g) for g in groups) * sub
-    order, third = None, 0
+    order, count = None, len(views)
 
     def late(c, t):
         return jnp.where(c == n_col - 1, t, 0)
@@ -221,15 +226,12 @@
     aliases = {1 + len(args) + k: k for k in range(len(held))}
     in_specs += [pl.BlockSpec(memory_space=pl.ANY)] * len(held)
     opts = dict(
-        plan=plan,
+        views=views,
         groups=groups,
         order=order,
-        third=third,
         n_col=n_col,
-        count=count,
         lefts=len(arrays),
         sources=len(sources),
-        per_third=per_third,
         by_xor=by_xor,
         weight=1.0 / math.sqrt(2.0 * NS),
         before=int(before is not None),
@@ -278,71 +280,62 @@
     picker = hit.astype(BF16)
     data = jnp.transpose(acq_data, (1, 0, 2))
     line = n_row <= 4 and block_rows == tile_cols
-    plan = [(0, n_row - 1, 0)]
-    if line:
-        for k in range(1, n_row):
-            plan += [(0, n_row - 1 - k, k), (k, n_row - 1, -k)]
-
     my_row = lax.axis_index("row")
-    keys = [(f, j) for f in range(FREQ) for j in everything]
-    known = lax.all_gather(spots, ("row", "col"), axis=0).reshape(n_row * n_col, n_row, cap)
-    places = lax.dynamic_index_in_dim(known, my_row, axis=1, keepdims=False).reshape(-1)
+    labels = jnp.broadcast_to(spots.reshape(n_row, 1, cap), (n_row, n_col, cap))
+    places = lax.all_to_all(
+        labels.reshape(n_row * n_col, cap), ("row", "col"), split_axis=0, concat_axis=0, tiled=True
+    ).reshape(-1)
     placer = (jnp.arange(block_rows, dtype=jnp.int32)[:, None] == places[None, :]).astype(BF16)
 
-    tiles, thirds, lefts = [], [], []
+    tiles, lefts = [], []
     pair = None
     for f in range(FREQ):
         sent = bin_rows(picker, data, f, n_row, n_col)
+        if f == 0:
+            sent = after(sent, places)
         got = lax.all_to_all(
             sent.reshape(n_row * n_col, cap, 2 * tile_cols), ("row", "col"), split_axis=0, concat_axis=0, tiled=True
         ).reshape(-1, 2 * tile_cols)
         if pair is not None:
-            got, pair = lax.optimization_barrier((got, pair))
-        tile, *cut = place_rows(placer, got, line and f == 1)
+            got, pair, _ = lax.optimization_barrier((got, pair, lefts[0][0]))
+        tile, *cut = place_rows(placer, got, (THIRDS - 1, 1) if f else ())
         if line and f == 0:
             pair = hop((tile, tile), 1, n_row)
         tiles.append(tile)
-        thirds.append(cut)
         lefts.append((lax.all_gather(tile, "col", axis=0), everything))
 
+    def gather_rows(part):
+        if block_rows == tile_cols:
+            return lax.all_gather(part, "row", axis=0)
+        return lax.all_gather(part, "row", axis=1, tiled=True)
+
+    sub = tile_cols // THIRDS
+    right1 = [gather_rows(after(part, lefts[1][0])) for part in cut]
+    views1 = [([(0, None)], j * sub) for j in everything[:-1]] + [([(1, None)], 0)]
     if line:
-        right0 = [tiles[0], *pair]
+        right0, ups = [tiles[0], *pair], [0, 1, -1]
         for k in range(2, n_row):
             pair = hop(pair, k, n_row)
             right0 += list(pair)
-        hops = [[hop((a, a), 1, n_row) for a in thirds[1]]]
-        for k in range(2, n_row):
-            begun = hops[-1]
-            hops.append([hop(begun[j], k, n_row) for j in everything])
-        right1 = [[thirds[1][j]] + [a for of in hops for a in of[j]] for j in everything]
-        right0[0] = after(right0[0], (hops[0], hops[1][0], lefts[1][0]))
+            ups += [k, -k]
+        right0[0] = after(right0[0], lefts[1][0])
     else:
-        right0, right1 = ([lax.all_gather(tile, "row", axis=1, tiled=True)] for tile in tiles)
+        right0, ups = [gather_rows(tiles[0])], [None]
+    views0 = [(list(enumerate(ups)), j * sub) for j in everything]
 
     where = jnp.stack([my_row, lax.axis_index("col")]).astype(jnp.int32)
+    product = functools.partial(complex_product, where)
     shape = (2, planes, block_rows, tile_cols)
-
-    def product(lefts, f, at, held, count=THIRDS, **rest):
-        first = 0 if at is None else at[2]
-        sources, per_third = right0, False
-        if f == 1:
-            sources, per_third = right1, line
-            if line:
-                sources = [a for j in range(first, first + count) for a in right1[j]]
-        return complex_product(where, lefts, plan, sources, per_third, count, shape, tuple(held), at, **rest)
-
-    result, piece = product([lefts[0]], 0, (0, 0, 0), ())
-    found = gather_cols(piece, n_col, hops[1][1:] if line else None)
-    arrived = found[n_col // 2]
-    (result,) = product([(found, everything)], 0, (1, 0, 0), (result,))
-    left1 = []
-    for j in everything:
-        result, piece = product([lefts[1]], 1, (0, 1, j), (result,), count=1)
-        found = gather_cols(after(piece, arrived), n_col)
-        arrived = found[n_col // 2]
-        left1.append((found, (j,)))
-    (sums,) = product(left1[:-1], 1, None, ())
-    return product(left1[-1:], 1, (1, 1, 0), (result,), before=sums)[0]
+    result, piece = product([lefts[0]], right0, views0, shape, (), (0, 0, 0))
+    found = gather_cols(piece, n_col)
+    found[0], right1[0] = lax.optimization_barrier((found[0], right1[0]))
+    (result,) = product([(found, everything)], right0, views0, shape, (result,), (1, 0, 0))
+    result, piece = product([lefts[1]], right1[:1], views1[:-1], shape, (result,), (0, 1, 0))
+    most = (gather_cols(piece, n_col), everything[:-1])
+    result, piece = product([lefts[1]], right1[1:], [([(0, None)], 0)], shape, (result,), (0, 1, THIRDS - 1))
+    rest = (gather_cols(piece, n_col), everything[-1:])
+    (sums,) = product([most], right1, views1, shape, (), None)
+    return product([rest], right1, views1, shape, (result,), (1, 1, 0), before=sums)[0]
 
 
 def solution(mesh):

time: 737 us -> 822 us (1.12)
  waiting for transfers between devices: 349 us -> 596 us
  blocking collectives: 92.5 us -> 0 us
  starting transfers between devices: 106 us -> 51.6 us
  local copies, waits for them, and re-layouts: 40.2 us -> 30.3 us
    all_gather x1 -> x0, blocking collectives: 92.5 us -> none  [per_device(): lax.all_gather(spots, ('row', 'col'), axis=0)]
    all_gather x2, waiting for transfers between devices: 0.02 us -> 88.9 us  [per_device(): lefts.append((lax.all_gather(tile, 'col', axis=0), everything))]
    all_to_all x2, waiting for transfers between devices: 77.2 us -> 165 us  [per_device(): lax.all_to_all(sent.reshape(n_row * n_col, cap, 2 * tile_cols), ('row', '...]
    ppermute x12 -> x9, waiting for transfers between devices: 43 us -> 98.3 us  [gather_cols(): arrived = {d ^ bit: lax.ppermute(a, 'col', pairs) for d, a in held.items()}]
    ppermute x12 -> x3, starting transfers between devices: 56.6 us -> 10.2 us  [hop(): lax.ppermute(pair[1], 'row', up)]
    ppermute x12 -> x3, waiting for transfers between devices: 226 us -> 244 us  [hop(): lax.ppermute(pair[0], 'row', down)]
    ppermute x12 -> x3, starting transfers between devices: 15.4 us -> 3.86 us  [hop(): lax.ppermute(pair[0], 'row', down)]
    unnamed x82 -> x21, local copies, waits for them, and re-layouts: 40 us -> 29.1 us
  transfers between devices with their start and end apart: 40 -> 22, of which waited for: 15 -> 10; matrix products, arithmetic and copies ran while one was open for 0% -> 2% of each run, Pallas kernels for 10% -> 12%
where the time goes in v8:
time: 822 us; the launch traced here: 821 us
  waiting for transfers between devices  596 us (73%)
  Pallas kernels  126 us (15%)
  starting transfers between devices  51.6 us (6%)
  local copies, waits for them, and re-layouts  30.3 us (4%)
  between operations  14 us (2%)
    ppermute x3, waiting for transfers between devices, hop(): lax.ppermute(pair[0], 'row', down)  244 us
    all_to_all x2, waiting for transfers between devices, per_device(): lax.all_to_all(sent.reshape(n_row * n_col, cap, 2 * tile_cols), ('row', '...  165 us
    pallas_call x6, Pallas kernels, complex_product(): pl.pallas_call(functools.partial(product_kernel, opts), grid_spec=pltpu.P...  105 us
    ppermute x9, waiting for transfers between devices, gather_cols(): arrived = {d ^ bit: lax.ppermute(a, 'col', pairs) for d, a in held.items()}  98.3 us
    all_gather x2, waiting for transfers between devices, per_device(): lefts.append((lax.all_gather(tile, 'col', axis=0), everything))  88.9 us
    unnamed x21, local copies, waits for them, and re-layouts  29.1 us
    all_to_all x2, starting transfers between devices, per_device(): lax.all_to_all(sent.reshape(n_row * n_col, cap, 2 * tile_cols), ('row', '...  28 us
  transfers between devices with their start and end apart: 22, of which 10 were waited for; matrix products, arithmetic and copies ran while one was open for 2% of the time, Pallas kernels for 12%

profile of v8, /device:TPU:0, one launch (start us, length us, event | category | flops | bytes accessed | tf_op | source)
XLA Modules:
  0.0 820.6 jit_solution(12773947928702996122)
XLA Ops:
  9.0 7.4 all-to-all-start
  16.4 10.4 %copy.12 = bf16[384,4,3072]{2,0,1:T(8,128)(2,1)} copy(bf16[384,4,3072]{2,1,0:T(4,128)(2,1)} %param.3) | data formatting | bytes 18874368 | tf_op args[0]
  36.4 6.0 all-to-all-start.2
  44.5 84.8 %all-to-all-done.2 = bf16[16,96,1536]{2,1,0:T(8,128)(2,1)} async-done(((bf16[16,96,1536]{2,1,0:T(8,128)(2,1)}), bf16[16,96,1536]{2,1,0:T(8,128)(2,1)}, u32[]{:S(2)}, u32[]{:S(2)}) %all-to-all-start.2) | async-done | bytes 4718624 | tf_op jit(solution)/shard_map/all_to_all | solution.py:296
  129.3 6.7 shard_map.39.refs_1_.refs_4_
  139.6 3.7 shard_map.37
  145.6 21.9 %all-to-all-start.1 = ((bf16[16,96,1536]{2,1,0:T(8,128)(2,1)}), bf16[16,96,1536]{2,1,0:T(8,128)(2,1)}, u32[]{:S(2)}, u32[]{:S(2)}) async-start(bf16[16,96,1536]{2,1,0:T(8,128)(2,1)} %bitcast.27), calls=%async_computation.1 | async-start | bytes 9437184 | tf_op jit(solution)/shard_map/all_to_all | solution.py:296
  168.8 6.0 collective-permute-start.1
  174.8 79.8 %all-to-all-done.1 = bf16[16,96,1536]{2,1,0:T(8,128)(2,1)} async-done(((bf16[16,96,1536]{2,1,0:T(8,128)(2,1)}), bf16[16,96,1536]{2,1,0:T(8,128)(2,1)}, u32[]{:S(2)}, u32[]{:S(2)}) %all-to-all-start.1) | async-done | bytes 4718624 | tf_op jit(solution)/shard_map/all_to_all | solution.py:296
  254.6 42.6 %collective-permute-done.refs_2_.refs_5_ = bf16[2,768,768]{2,1,0:T(8,128)(2,1)} collective-permute-done((bf16[2,768,768]{2,1,0:T(8,128)(2,1)}, bf16[2,768,768]{2,1,0:T(8,128)(2,1)}, u32[]{:S(2)}, u32[]{:S(2)}) %collective-permute-start) | collective-permute-done | bytes 2359328 | tf_op jit(solution)/shard_map/ppermute | solution.py:21
  297.2 6.7 shard_map.40
  305.4 88.9 %all-gather.11.cloned.1.call-done = bf16[8,768,768]{2,1,0:T(8,128)(2,1)} async-done(((bf16[2,768,768]{2,1,0:T(8,128)(2,1)}), bf16[8,768,768]{2,1,0:T(8,128)(2,1)}) %all-gather.11.cloned.1.call-update) | async-done | bytes 9437200 | tf_op jit(solution)/shard_map/all_gather | solution.py:305
  397.8 127.9 %collective-permute-done.2.refs_4_.refs_7_ = bf16[2,768,768]{2,1,0:T(8,128)(2,1)S(1)} collective-permute-done((bf16[2,768,768]{2,1,0:T(8,128)(2,1)}, bf16[2,768,768]{2,1,0:T(8,128)(2,1)S(1)}, u32[]{:S(2)}, u32[]{:S(2)}) %collective-permute-start.2) | collective-permute-done | bytes 2359328 | tf_op jit(solution)/shard_map/ppermute | solution.py:21
  529.1 73.4 %collective-permute-done.4.refs_6_.refs_9_ = bf16[2,768,768]{2,1,0:T(8,128)(2,1)} collective-permute-done((bf16[2,768,768]{2,1,0:T(8,128)(2,1)S(1)}, bf16[2,768,768]{2,1,0:T(8,128)(2,1)}, u32[]{:S(2)}, u32[]{:S(2)}) %collective-permute-start.4) | collective-permute-done | bytes 2359328 | tf_op jit(solution)/shard_map/ppermute | solution.py:21
  602.6 24.6 %shard_map.41 = (bf16[2,4,768,768]{3,2,1,0:T(8,128)(2,1)}, bf16[2,768,768]{2,1,0:T(8,128)(2,1)S(1)}) custom-call(s32[2]{0:T(128)S(1)} %pad_add_fusion.where, bf16[4,2,768,768]{3,2,1,0:T(8,128)(2,1)} %bitcast.28, bf16[2,768,768]{2,1,0:T(8,128)(2,1)} %shard_map.39.refs_1_.refs_4_, bf16[2,768,768]{2,1,0:T(8,128)(2,1)} %collective-permute-done.refs_2_.refs_5_, ...), custom_call_target="tpu_custom_call" | custom-call | flops 1000 | bytes 1000 | tf_op jit(solution)/shard_map/pallas_call | solution.py:240
  628.0 52.7 %collective-permute-done.7.refs_2_ = bf16[2,768,768]{2,1,0:T(8,128)(2,1)} collective-permute-done((bf16[2,768,768]{2,1,0:T(8,128)(2,1)S(1)}, bf16[2,768,768]{2,1,0:T(8,128)(2,1)}, u32[]{:S(2)}, u32[]{:S(2)}) %collective-permute-start.7) | collective-permute-done | bytes 2359328 | tf_op jit(solution)/shard_map/ppermute | solution.py:92
  680.6 4.9 collective-permute-done.8.refs_3_
  685.5 22.9 %shard_map.42.refs_2_ = bf16[2,4,768,768]{3,2,1,0:T(8,128)(2,1)} custom-call(s32[2]{0:T(128)S(1)} %pad_add_fusion.where, bf16[2,768,768]{2,1,0:T(8,128)(2,1)S(1)} %get-tuple-element.33.refs_0_, bf16[2,768,768]{2,1,0:T(8,128)(2,1)} %collective-permute-done.6.refs_1_, ...), custom_call_target="tpu_custom_call", output_to_operand_aliasing={{}: (12, {})} | custom-call | flops 1000 | bytes 1000 | tf_op jit(solution)/shard_map/pallas_call | solution.py:240
  708.4 16.4 %shard_map.43 = (bf16[2,4,768,768]{3,2,1,0:T(8,128)(2,1)}, bf16[2,768,512]{2,1,0:T(8,128)(2,1)S(1)}) custom-call(s32[2]{0:T(128)S(1)} %pad_add_fusion.where, bf16[4,2,768,768]{3,2,1,0:T(8,128)(2,1)} %bitcast.21, bf16[4,2,768,512]{3,2,1,0:T(8,128)(2,1)S(1)} %bitcast.20, bf16[2,4,768,768]{3,2,1,0:T(8,128)(2,1)} %shard_map.42.refs_2_), custom_call_target="tpu_custom_call", output_to_operand_aliasing={{0}: (3, {})} | custom-call | flops 1000 | bytes 1000 | tf_op jit(solution)/shard_map/pallas_call | solution.py:240
  731.0 8.7 %shard_map.44 = (bf16[2,4,768,768]{3,2,1,0:T(8,128)(2,1)}, bf16[2,768,256]{2,1,0:T(8,128)(2,1)S(1)}) custom-call(s32[2]{0:T(128)S(1)} %pad_add_fusion.where, bf16[4,2,768,768]{3,2,1,0:T(8,128)(2,1)S(1)} %bitcast.22, bf16[4,2,768,256]{3,2,1,0:T(8,128)(2,1)S(1)} %bitcast.23, ...), custom_call_target="tpu_custom_call", output_to_operand_aliasing={{0}: (3, {})} | custom-call | flops 1000 | bytes 1000 | tf_op jit(solution)/shard_map/pallas_call | solution.py:240
  739.7 21.6 %collective-permute-done.13.refs_2_ = bf16[2,768,512]{2,1,0:T(8,128)(2,1)S(1)} collective-permute-done((bf16[2,768,512]{2,1,0:T(8,128)(2,1)S(1)}, bf16[2,768,512]{2,1,0:T(8,128)(2,1)S(1)}, u32[]{:S(2)}, u32[]{:S(2)}) %collective-permute-start.13) | collective-permute-done | bytes 1572896 | tf_op jit(solution)/shard_map/ppermute | solution.py:92
  762.1 19.2 %collective-permute-done.10.refs_2_ = bf16[2,768,256]{2,1,0:T(8,128)(2,1)S(1)} collective-permute-done((bf16[2,768,256]{2,1,0:T(8,128)(2,1)S(1)}, bf16[2,768,256]{2,1,0:T(8,128)(2,1)S(1)}, u32[]{:S(2)}, u32[]{:S(2)}) %collective-permute-start.10) | collective-permute-done | bytes 786464 | tf_op jit(solution)/shard_map/ppermute | solution.py:92
  781.3 17.9 %shard_map.45.refs_6_ = f32[2,768,768]{2,1,0:T(8,128)} custom-call(s32[2]{0:T(128)S(1)} %pad_add_fusion.where, bf16[2,768,512]{2,1,0:T(8,128)(2,1)S(1)} %get-tuple-element.37.refs_0_, bf16[2,768,512]{2,1,0:T(8,128)(2,1)} %collective-permute-done.12.refs_1_, bf16[2,768,512]{2,1,0:T(8,128)(2,1)S(1)} %collective-permute-done.13.refs_2_, ...), custom_call_target="tpu_custom_call" | custom-call | flops 1000 | bytes 1000 | tf_op jit(solution)/shard_map/pallas_call | solution.py:240
  799.2 14.9 %shard_map.46 = bf16[2,4,768,768]{3,2,1,0:T(8,128)(2,1)} custom-call(s32[2]{0:T(128)S(1)} %pad_add_fusion.where, bf16[2,768,256]{2,1,0:T(8,128)(2,1)S(1)} %get-tuple-element.36.refs_0_, bf16[2,768,256]{2,1,0:T(8,128)(2,1)S(1)} %collective-permute-done.9.refs_1_, ...), custom_call_target="tpu_custom_call", output_to_operand_aliasing={{}: (8, {})} | custom-call | flops 1000 | bytes 1000 | tf_op jit(solution)/shard_map/pallas_call | solution.py:240
  (68 shorter events, 36.7 us)
Async XLA Ops:
  9.0 27.4 %all-to-all-start = ((s32[16,1,96]{2,1,0:T(1,128)}), s32[16,1,96]{2,1,0:T(1,128)S(1)}, u32[]{:S(2)}, u32[]{:S(2)}) async-start(s32[16,1,96]{2,1,0:T(1,128)} %bitcast.3), calls=%async_computation | async-start | bytes 16384 | tf_op jit(solution)/shard_map/all_to_all | solution.py:285
  36.4 92.9 %all-to-all-start.2 = ((bf16[16,96,1536]{2,1,0:T(8,128)(2,1)}), bf16[16,96,1536]{2,1,0:T(8,128)(2,1)}, u32[]{:S(2)}, u32[]{:S(2)}) async-start(bf16[16,96,1536]{2,1,0:T(8,128)(2,1)} %bitcast.26), calls=%async_computation.2 | async-start | bytes 9437184 | tf_op jit(solution)/shard_map/all_to_all | solution.py:296
  42.4 254.7 %all-gather.9.cloned.1.call-start = ((), (), s32[]{:S(2)}) async-start(), calls=%async_computation.3 | async-start | bytes 11796480 | tf_op jit(solution)/shard_map/all_gather | solution.py:305
  145.6 109.0 %all-to-all-start.1 = ((bf16[16,96,1536]{2,1,0:T(8,128)(2,1)}), bf16[16,96,1536]{2,1,0:T(8,128)(2,1)}, u32[]{:S(2)}, u32[]{:S(2)}) async-start(bf16[16,96,1536]{2,1,0:T(8,128)(2,1)} %bitcast.27), calls=%async_computation.1 | async-start | bytes 9437184 | tf_op jit(solution)/shard_map/all_to_all | solution.py:296
  167.5 226.8 %all-gather.11.cloned.1.call-start = ((), (), s32[]{:S(2)}) async-start(), calls=%async_computation.4 | async-start | bytes 11796480 | tf_op jit(solution)/shard_map/all_gather | solution.py:305
  167.5 129.6 %collective-permute-start = (bf16[2,768,768]{2,1,0:T(8,128)(2,1)}, bf16[2,768,768]{2,1,0:T(8,128)(2,1)}, u32[]{:S(2)}, u32[]{:S(2)}) collective-permute-start(bf16[2,768,768]{2,1,0:T(8,128)(2,1)} %shard_map.39.refs_1_.refs_4_), channel_id=1, source_target_pairs={{4,0},{8,4},{12,8},{5,1},{9,5},{13,9},{6,2},{10,6},{14,10},{7,3},{... | collective-permute-start | bytes 7077896 | tf_op jit(solution)/shard_map/ppermute | solution.py:21
  168.8 128.3 %collective-permute-start.1 = (bf16[2,768,768]{2,1,0:T(8,128)(2,1)}, bf16[2,768,768]{2,1,0:T(8,128)(2,1)}, u32[]{:S(2)}, u32[]{:S(2)}) collective-permute-start(bf16[2,768,768]{2,1,0:T(8,128)(2,1)} %shard_map.39.refs_1_.refs_4_), channel_id=1, source_target_pairs={{0,4},{4,8},{8,12},{1,5},{5,9},{9,13},{2,6},{6,10},{10,14},{3,7},{... | collective-permute-start | bytes 7077896 | tf_op jit(solution)/shard_map/ppermute | solution.py:21
  305.3 375.3 %all-gather.15.cloned.1.call-start = ((), (), s32[]{:S(2)}) async-start(), calls=%async_computation.6 | async-start | bytes 7864320 | tf_op jit(solution)/shard_map/all_gather | solution.py:309
  394.3 331.1 %all-gather.13.cloned.1.call-start = ((), (), s32[]{:S(2)}) async-start(), calls=%async_computation.5 | async-start | bytes 3932160 | tf_op jit(solution)/shard_map/all_gather | solution.py:309
  394.4 131.3 %collective-permute-start.2 = (bf16[2,768,768]{2,1,0:T(8,128)(2,1)}, bf16[2,768,768]{2,1,0:T(8,128)(2,1)S(1)}, u32[]{:S(2)}, u32[]{:S(2)}) collective-permute-start(bf16[2,768,768]{2,1,0:T(8,128)(2,1)} %collective-permute-done.refs_2_.refs_5_), channel_id=1, source_target_pairs={{4,0},{8,4},{5,1},{9,5},{6,2},{10,6},{7,3},{11,7},{20,16},{24,20},... | collective-permute-start | bytes 7077896 | tf_op jit(solution)/shard_map/ppermute | solution.py:21
  395.7 131.3 %collective-permute-start.3 = (bf16[2,768,768]{2,1,0:T(8,128)(2,1)}, bf16[2,768,768]{2,1,0:T(8,128)(2,1)}, u32[]{:S(2)}, u32[]{:S(2)}) collective-permute-start(bf16[2,768,768]{2,1,0:T(8,128)(2,1)} %collective-permute-done.1.refs_3_.refs_6_), channel_id=1, source_target_pairs={{4,8},{8,12},{5,9},{9,13},{6,10},{10,14},{7,11},{11,15},{20,24},{2... | collective-permute-start | bytes 7077896 | tf_op jit(solution)/shard_map/ppermute | solution.py:21
  525.6 76.9 %copy-start.9 = (bf16[2,768,768]{2,1,0:T(8,128)(2,1)}, bf16[2,768,768]{2,1,0:T(8,128)(2,1)S(1)}, u32[]{:S(2)}) copy-start(bf16[2,768,768]{2,1,0:T(8,128)(2,1)S(1)} %collective-permute-done.2.refs_4_.refs_7_) | copy-start | bytes 7077892
  525.6 76.9 %collective-permute-start.4 = (bf16[2,768,768]{2,1,0:T(8,128)(2,1)S(1)}, bf16[2,768,768]{2,1,0:T(8,128)(2,1)}, u32[]{:S(2)}, u32[]{:S(2)}) collective-permute-start(bf16[2,768,768]{2,1,0:T(8,128)(2,1)S(1)} %collective-permute-done.2.refs_4_.refs_7_), channel_id=1, source_target_pairs={{4,0},{5,1},{6,2},{7,3},{20,16},{21,17},{22,18},{23,19}} | collective-permute-start | bytes 7077896 | tf_op jit(solution)/shard_map/ppermute | solution.py:21
  526.9 75.6 %collective-permute-start.5 = (bf16[2,768,768]{2,1,0:T(8,128)(2,1)}, bf16[2,768,768]{2,1,0:T(8,128)(2,1)}, u32[]{:S(2)}, u32[]{:S(2)}) collective-permute-start(bf16[2,768,768]{2,1,0:T(8,128)(2,1)} %collective-permute-done.3.refs_5_.refs_8_), channel_id=1, source_target_pairs={{8,12},{9,13},{10,14},{11,15},{24,28},{25,29},{26,30},{27,31}} | collective-permute-start | bytes 7077896 | tf_op jit(solution)/shard_map/ppermute | solution.py:21
  627.2 53.4 %collective-permute-start.7 = (bf16[2,768,768]{2,1,0:T(8,128)(2,1)S(1)}, bf16[2,768,768]{2,1,0:T(8,128)(2,1)}, u32[]{:S(2)}, u32[]{:S(2)}) collective-permute-start(bf16[2,768,768]{2,1,0:T(8,128)(2,1)S(1)} %get-tuple-element.33.refs_0_), channel_id=1, source_target_pairs={{0,2},{1,3},{2,0},{3,1},{4,6},{5,7},{6,4},{7,5},{8,10},{9,11},{10,... | collective-permute-start | bytes 7077896 | tf_op jit(solution)/shard_map/ppermute | solution.py:92
  627.9 52.7 %collective-permute-start.6 = (bf16[2,768,768]{2,1,0:T(8,128)(2,1)S(1)}, bf16[2,768,768]{2,1,0:T(8,128)(2,1)}, u32[]{:S(2)}, u32[]{:S(2)}) collective-permute-start(bf16[2,768,768]{2,1,0:T(8,128)(2,1)S(1)} %get-tuple-element.33.refs_0_), channel_id=1, source_target_pairs={{0,1},{1,0},{2,3},{3,2},{4,5},{5,4},{6,7},{7,6},{8,9},{9,8},{10,11... | collective-permute-start | bytes 7077896 | tf_op jit(solution)/shard_map/ppermute | solution.py:92
  680.6 4.9 collective-permute-start.8
  724.8 36.5 %collective-permute-start.13 = (bf16[2,768,512]{2,1,0:T(8,128)(2,1)S(1)}, bf16[2,768,512]{2,1,0:T(8,128)(2,1)S(1)}, u32[]{:S(2)}, u32[]{:S(2)}) collective-permute-start(bf16[2,768,512]{2,1,0:T(8,128)(2,1)S(1)} %get-tuple-element.37.refs_0_), channel_id=1, source_target_pairs={{0,2},{1,3},{2,0},{3,1},{4,6},{5,7},{6,4},{7,5},{8,10},{9,11},{10,... | collective-permute-start | bytes 4718600 | tf_op jit(solution)/shard_map/ppermute | solution.py:92
  725.4 55.9 %collective-permute-start.12 = (bf16[2,768,512]{2,1,0:T(8,128)(2,1)S(1)}, bf16[2,768,512]{2,1,0:T(8,128)(2,1)}, u32[]{:S(2)}, u32[]{:S(2)}) collective-permute-start(bf16[2,768,512]{2,1,0:T(8,128)(2,1)S(1)} %get-tuple-element.37.refs_0_), channel_id=1, source_target_pairs={{0,1},{1,0},{2,3},{3,2},{4,5},{5,4},{6,7},{7,6},{8,9},{9,8},{10,11... | collective-permute-start | bytes 4718600 | tf_op jit(solution)/shard_map/ppermute | solution.py:92
  731.0 50.3 %copy-start.5 = (bf16[8,768,256]{2,1,0:T(8,128)(2,1)S(1)}, bf16[8,768,256]{2,1,0:T(8,128)(2,1)}, u32[]{:S(2)}) copy-start(bf16[8,768,256]{2,1,0:T(8,128)(2,1)} %all-gather.13.cloned.1.call-done) | copy-start | bytes 9437188
  761.3 20.0 %collective-permute-start.14 = (bf16[2,768,512]{2,1,0:T(8,128)(2,1)S(1)}, bf16[2,768,512]{2,1,0:T(8,128)(2,1)S(1)}, u32[]{:S(2)}, u32[]{:S(2)}) collective-permute-start(bf16[2,768,512]{2,1,0:T(8,128)(2,1)S(1)} %collective-permute-done.13.refs_2_), channel_id=1, source_target_pairs={{0,1},{1,0},{2,3},{3,2},{4,5},{5,4},{6,7},{7,6},{8,9},{9,8},{10,11... | collective-permute-start | bytes 4718600 | tf_op jit(solution)/shard_map/ppermute | solution.py:92
  761.3 20.0 %collective-permute-start.10 = (bf16[2,768,256]{2,1,0:T(8,128)(2,1)S(1)}, bf16[2,768,256]{2,1,0:T(8,128)(2,1)S(1)}, u32[]{:S(2)}, u32[]{:S(2)}) collective-permute-start(bf16[2,768,256]{2,1,0:T(8,128)(2,1)S(1)} %get-tuple-element.36.refs_0_), channel_id=1, source_target_pairs={{0,2},{1,3},{2,0},{3,1},{4,6},{5,7},{6,4},{7,5},{8,10},{9,11},{10,... | collective-permute-start | bytes 2359304 | tf_op jit(solution)/shard_map/ppermute | solution.py:92
  761.8 37.3 %collective-permute-start.9 = (bf16[2,768,256]{2,1,0:T(8,128)(2,1)S(1)}, bf16[2,768,256]{2,1,0:T(8,128)(2,1)S(1)}, u32[]{:S(2)}, u32[]{:S(2)}) collective-permute-start(bf16[2,768,256]{2,1,0:T(8,128)(2,1)S(1)} %get-tuple-element.36.refs_0_), channel_id=1, source_target_pairs={{0,1},{1,0},{2,3},{3,2},{4,5},{5,4},{6,7},{7,6},{8,9},{9,8},{10,11... | collective-permute-start | bytes 2359304 | tf_op jit(solution)/shard_map/ppermute | solution.py:92
  781.2 17.9 %collective-permute-start.11 = (bf16[2,768,256]{2,1,0:T(8,128)(2,1)S(1)}, bf16[2,768,256]{2,1,0:T(8,128)(2,1)S(1)}, u32[]{:S(2)}, u32[]{:S(2)}) collective-permute-start(bf16[2,768,256]{2,1,0:T(8,128)(2,1)S(1)} %collective-permute-done.10.refs_2_), channel_id=1, source_target_pairs={{0,1},{1,0},{2,3},{3,2},{4,5},{5,4},{6,7},{7,6},{8,9},{9,8},{10,11... | collective-permute-start | bytes 2359304 | tf_op jit(solution)/shard_map/ppermute | solution.py:92
  (8 other events, 41.6 us)
Sparse Core Ops, SparseCore 0:
  136.1 131.8 all-gather.8
  305.4 88.8 all-gather.10
  395.9 156.3 all-gather.14
  628.0 65.7 all-gather.12

commit v9 on v8

--- a/solution.py
+++ b/solution.py
@@ -168,28 +168,28 @@
 
     block = me ^ step if by_xor else step
     rows = right[third, pl.ds(pl.multiple_of(block * depth, 32), depth), :]
-    by_real = jnp.dot(left[step, 0], rows, preferred_element_type=F32)
-    by_imag = jnp.dot(left[step, 1], rows, preferred_element_type=F32)
-    real = by_real[:, :sub] - by_imag[:, sub:]
-    imag = by_real[:, sub:] + by_imag[:, :sub]
 
     @pl.when(step == 0)
     def _():
-        total[third, 0] = real if before is None else real + before[0]
-        total[third, 1] = imag if before is None else imag + before[1]
+        for p in range(2):
+            total[third, p] = jnp.dot(left[step, p], rows, preferred_element_type=F32)
 
     @pl.when(step > 0)
     def _():
-        total[third, 0] += real
-        total[third, 1] += imag
+        for p in range(2):
+            total[third, p] += jnp.dot(left[step, p], rows, preferred_element_type=F32)
 
     @pl.when(step == n_col - 1)
     def _():
-        for p in range(2):
+        real = total[third, 0, :, :sub] - total[third, 1, :, sub:]
+        imag = total[third, 0, :, sub:] + total[third, 1, :, :sub]
+        for p, value in enumerate((real, imag)):
+            if before is not None:
+                value = value + before[p]
             if order is None:
-                outs[0][p] = total[third, p]
+                outs[0][p] = value
                 continue
-            value = (total[third, p] * opts["weight"]).astype(BF16)
+            value = (value * opts["weight"]).astype(BF16)
             outs[0][0, p] = value
             if len(outs) > 1:
                 outs[1][p] = value
@@ -221,7 +221,7 @@
     in_specs = [pl.BlockSpec(memory_space=pl.ANY)] * (len(arrays) + len(sources))
     args = [*arrays, *sources]
     if before is not None:
-        in_specs.append(pl.BlockSpec((2, rows, sub), lambda c, t, s: (0, 0, jnp.where(c == 0, t, count - 1))))
+        in_specs.append(pl.BlockSpec((2, rows, sub), lambda c, t, s: (0, 0, late(c, t))))
         args.append(before)
     aliases = {1 + len(args) + k: k for k in range(len(held))}
     in_specs += [pl.BlockSpec(memory_space=pl.ANY)] * len(held)
@@ -247,7 +247,7 @@
             scratch_shapes=[
                 pltpu.VMEM((n_col, 2, rows, lanes), BF16),
                 pltpu.VMEM((count, lanes * n_col, 2 * sub), BF16),
-                pltpu.VMEM((count, 2, rows, sub), F32),
+                pltpu.VMEM((count, 2, rows, 2 * sub), F32),
                 pltpu.SemaphoreType.DMA((len(groups), n_col)),
                 pltpu.SemaphoreType.DMA((count, 2, n_col)),
             ],
@@ -302,7 +302,8 @@
         if line and f == 0:
             pair = hop((tile, tile), 1, n_row)
         tiles.append(tile)
-        lefts.append((lax.all_gather(tile, "col", axis=0), everything))
+        if f == 0:
+            lefts.append((lax.all_gather(tile, "col", axis=0), everything))
 
     def gather_rows(part):
         if block_rows == tile_cols:
@@ -310,17 +311,21 @@
         return lax.all_gather(part, "row", axis=1, tiled=True)
 
     sub = tile_cols // THIRDS
-    right1 = [gather_rows(after(part, lefts[1][0])) for part in cut]
     views1 = [([(0, None)], j * sub) for j in everything[:-1]] + [([(1, None)], 0)]
+    second = None
     if line:
         right0, ups = [tiles[0], *pair], [0, 1, -1]
         for k in range(2, n_row):
             pair = hop(pair, k, n_row)
+            second = pair if k == 2 else second
             right0 += list(pair)
             ups += [k, -k]
-        right0[0] = after(right0[0], lefts[1][0])
+        cut = [after(part, second) for part in cut]
     else:
         right0, ups = [gather_rows(tiles[0])], [None]
+    right1 = [gather_rows(part) for part in cut]
+    lefts.append((gather_cols(tiles[1], n_col, second), everything))
+    right0[0] = after(right0[0], lefts[1][0])
     views0 = [(list(enumerate(ups)), j * sub) for j in everything]
 
     where = jnp.stack([my_row, lax.axis_index("col")]).astype(jnp.int32)
@@ -328,7 +333,6 @@
     shape = (2, planes, block_rows, tile_cols)
     result, piece = product([lefts[0]], right0, views0, shape, (), (0, 0, 0))
     found = gather_cols(piece, n_col)
-    found[0], right1[0] = lax.optimization_barrier((found[0], right1[0]))
     (result,) = product([(found, everything)], right0, views0, shape, (result,), (1, 0, 0))
     result, piece = product([lefts[1]], right1[:1], views1[:-1], shape, (result,), (0, 1, 0))
     most = (gather_cols(piece, n_col), everything[:-1])

time: 822 us -> 765 us (0.931)
  waiting for transfers between devices: 596 us -> 533 us
    all_gather x2 -> x1, waiting for transfers between devices: 88.9 us -> 0.01 us  [per_device(): lefts.append((lax.all_gather(tile, 'col', axis=0), everything))]
    ppermute x9 -> x12, waiting for transfers between devices: 98.3 us -> 152 us  [gather_cols(): arrived = {d ^ bit: lax.ppermute(a, 'col', pairs) for d, a in held.items()}]
    ppermute x3, waiting for transfers between devices: 244 us -> 217 us  [hop(): lax.ppermute(pair[0], 'row', down)]
    unnamed x21 -> x29, local copies, waits for them, and re-layouts: 29.1 us -> 33 us
  transfers between devices with their start and end apart: 22 -> 24, of which waited for: 10 -> 12; matrix products, arithmetic and copies ran while one was open for 2% -> 2% of each run, Pallas kernels for 12% -> 13%
where the time goes in v9:
time: 765 us; the launch traced here: 764 us
  waiting for transfers between devices  533 us (70%)
  Pallas kernels  123 us (16%)
  starting transfers between devices  56.4 us (7%)
  local copies, waits for them, and re-layouts  34.3 us (4%)
  between operations  14 us (2%)
    ppermute x3, waiting for transfers between devices, hop(): lax.ppermute(pair[0], 'row', down)  217 us
    all_to_all x2, waiting for transfers between devices, per_device(): lax.all_to_all(sent.reshape(n_row * n_col, cap, 2 * tile_cols), ('row', '...  164 us
    ppermute x12, waiting for transfers between devices, gather_cols(): arrived = {d ^ bit: lax.ppermute(a, 'col', pairs) for d, a in held.items()}  152 us
    pallas_call x6, Pallas kernels, complex_product(): pl.pallas_call(functools.partial(product_kernel, opts), grid_spec=pltpu.P...  103 us
    unnamed x29, local copies, waits for them, and re-layouts  33 us
    all_to_all x2, starting transfers between devices, per_device(): lax.all_to_all(sent.reshape(n_row * n_col, cap, 2 * tile_cols), ('row', '...  28 us
  transfers between devices with their start and end apart: 24, of which 12 were waited for; matrix products, arithmetic and copies ran while one was open for 2% of the time, Pallas kernels for 13%

profile of v9, /device:TPU:0, one launch (start us, length us, event | category | flops | bytes accessed | tf_op | source)
XLA Modules:
  0.0 764.2 jit_solution(8393405304667428593)
XLA Ops:
  9.0 7.4 all-to-all-start
  16.4 10.4 %copy.12 = bf16[384,4,3072]{2,0,1:T(8,128)(2,1)} copy(bf16[384,4,3072]{2,1,0:T(4,128)(2,1)} %param.3) | data formatting | bytes 18874368 | tf_op args[0]
  30.5 3.7 shard_map.38
  36.4 6.0 all-to-all-start.2
  44.6 84.7 %all-to-all-done.2 = bf16[16,96,1536]{2,1,0:T(8,128)(2,1)} async-done(((bf16[16,96,1536]{2,1,0:T(8,128)(2,1)}), bf16[16,96,1536]{2,1,0:T(8,128)(2,1)}, u32[]{:S(2)}, u32[]{:S(2)}) %all-to-all-start.2) | async-done | bytes 4718624 | tf_op jit(solution)/shard_map/all_to_all | solution.py:296
  129.3 6.8 shard_map.39.refs_1_.refs_4_
  145.7 21.9 %all-to-all-start.1 = ((bf16[16,96,1536]{2,1,0:T(8,128)(2,1)}), bf16[16,96,1536]{2,1,0:T(8,128)(2,1)}, u32[]{:S(2)}, u32[]{:S(2)}) async-start(bf16[16,96,1536]{2,1,0:T(8,128)(2,1)} %bitcast.21), calls=%async_computation.1 | async-start | bytes 9437184 | tf_op jit(solution)/shard_map/all_to_all | solution.py:296
  169.0 6.0 collective-permute-start.1
  175.0 79.8 %all-to-all-done.1 = bf16[16,96,1536]{2,1,0:T(8,128)(2,1)} async-done(((bf16[16,96,1536]{2,1,0:T(8,128)(2,1)}), bf16[16,96,1536]{2,1,0:T(8,128)(2,1)}, u32[]{:S(2)}, u32[]{:S(2)}) %all-to-all-start.1) | async-done | bytes 4718624 | tf_op jit(solution)/shard_map/all_to_all | solution.py:296
  254.7 42.6 %collective-permute-done.refs_2_.refs_5_ = bf16[2,768,768]{2,1,0:T(8,128)(2,1)} collective-permute-done((bf16[2,768,768]{2,1,0:T(8,128)(2,1)}, bf16[2,768,768]{2,1,0:T(8,128)(2,1)}, u32[]{:S(2)}, u32[]{:S(2)}) %collective-permute-start) | collective-permute-done | bytes 2359328 | tf_op jit(solution)/shard_map/ppermute | solution.py:21
  300.7 6.4 shard_map.40
  309.8 67.8 %collective-permute-done.2.refs_4_.refs_7_ = bf16[2,768,768]{2,1,0:T(8,128)(2,1)} collective-permute-done((bf16[2,768,768]{2,1,0:T(8,128)(2,1)}, bf16[2,768,768]{2,1,0:T(8,128)(2,1)}, u32[]{:S(2)}, u32[]{:S(2)}) %collective-permute-start.2) | collective-permute-done | bytes 2359328 | tf_op jit(solution)/shard_map/ppermute | solution.py:21
  379.1 51.0 %collective-permute-done.5.refs_2_ = bf16[2,768,768]{2,1,0:T(8,128)(2,1)S(1)} collective-permute-done((bf16[2,768,768]{2,1,0:T(8,128)(2,1)}, bf16[2,768,768]{2,1,0:T(8,128)(2,1)S(1)}, u32[]{:S(2)}, u32[]{:S(2)}) %collective-permute-start.5) | collective-permute-done | bytes 2359328 | tf_op jit(solution)/shard_map/ppermute | solution.py:92
  434.1 4.0 collective-permute-done.6.refs_3_
  438.3 106.5 %collective-permute-done.7.refs_6_.refs_9_ = bf16[2,768,768]{2,1,0:T(8,128)(2,1)} collective-permute-done((bf16[2,768,768]{2,1,0:T(8,128)(2,1)}, bf16[2,768,768]{2,1,0:T(8,128)(2,1)}, u32[]{:S(2)}, u32[]{:S(2)}) %collective-permute-start.7) | collective-permute-done | bytes 2359328 | tf_op jit(solution)/shard_map/ppermute | solution.py:21
  544.9 24.1 %shard_map.41 = (bf16[2,4,768,768]{3,2,1,0:T(8,128)(2,1)}, bf16[2,768,768]{2,1,0:T(8,128)(2,1)}) custom-call(s32[2]{0:T(128)S(1)} %pad_add_fusion.where, bf16[4,2,768,768]{3,2,1,0:T(8,128)(2,1)} %bitcast.25, bf16[2,768,768]{2,1,0:T(8,128)(2,1)} %shard_map.39.refs_1_.refs_4_, bf16[2,768,768]{2,1,0:T(8,128)(2,1)} %collective-permute-done.refs_2_.refs_5_, ...), custom_call_target="tpu_custom_call" | custom-call | flops 1000 | bytes 1000 | tf_op jit(solution)/shard_map/pallas_call | solution.py:240
  570.6 51.9 %collective-permute-done.10.refs_2_ = bf16[2,768,768]{2,1,0:T(8,128)(2,1)S(1)} collective-permute-done((bf16[2,768,768]{2,1,0:T(8,128)(2,1)}, bf16[2,768,768]{2,1,0:T(8,128)(2,1)S(1)}, u32[]{:S(2)}, u32[]{:S(2)}) %collective-permute-start.10) | collective-permute-done | bytes 2359328 | tf_op jit(solution)/shard_map/ppermute | solution.py:92
  628.7 23.4 %shard_map.42.refs_5_ = bf16[2,4,768,768]{3,2,1,0:T(8,128)(2,1)} custom-call(s32[2]{0:T(128)S(1)} %pad_add_fusion.where, bf16[2,768,768]{2,1,0:T(8,128)(2,1)} %get-tuple-element.33.refs_0_, bf16[2,768,768]{2,1,0:T(8,128)(2,1)S(1)} %collective-permute-done.9.refs_1_, bf16[2,768,768]{2,1,0:T(8,128)(2,1)S(1)} %copy-done.12, ...), custom_call_target="tpu_custom_call", output_to_operand_aliasing={{}: (12, {})} | custom-call | flops 1000 | bytes 1000 | tf_op jit(solution)/shard_map/pallas_call | solution.py:240
  653.8 15.7 %shard_map.43 = (bf16[2,4,768,768]{3,2,1,0:T(8,128)(2,1)}, bf16[2,768,512]{2,1,0:T(8,128)(2,1)}) custom-call(s32[2]{0:T(128)S(1)} %pad_add_fusion.where, bf16[2,768,768]{2,1,0:T(8,128)(2,1)S(1)} %copy-done.7, bf16[2,768,768]{2,1,0:T(8,128)(2,1)} %collective-permute-done.4.refs_1_, ...), custom_call_target="tpu_custom_call", output_to_operand_aliasing={{0}: (6, {})} | custom-call | flops 1000 | bytes 1000 | tf_op jit(solution)/shard_map/pallas_call | solution.py:240
  674.6 8.3 %shard_map.44 = (bf16[2,4,768,768]{3,2,1,0:T(8,128)(2,1)}, bf16[2,768,256]{2,1,0:T(8,128)(2,1)S(1)}) custom-call(s32[2]{0:T(128)S(1)} %pad_add_fusion.where, bf16[2,768,768]{2,1,0:T(8,128)(2,1)S(1)} %copy-done.7, bf16[2,768,768]{2,1,0:T(8,128)(2,1)} %collective-permute-done.4.refs_1_, ...), custom_call_target="tpu_custom_call", output_to_operand_aliasing={{0}: (6, {})} | custom-call | flops 1000 | bytes 1000 | tf_op jit(solution)/shard_map/pallas_call | solution.py:240
  683.0 23.4 %collective-permute-done.16.refs_2_ = bf16[2,768,512]{2,1,0:T(8,128)(2,1)} collective-permute-done((bf16[2,768,512]{2,1,0:T(8,128)(2,1)}, bf16[2,768,512]{2,1,0:T(8,128)(2,1)}, u32[]{:S(2)}, u32[]{:S(2)}) %collective-permute-start.16) | collective-permute-done | bytes 1572896 | tf_op jit(solution)/shard_map/ppermute | solution.py:92
  708.1 18.3 %collective-permute-done.13.refs_2_ = bf16[2,768,256]{2,1,0:T(8,128)(2,1)S(1)} collective-permute-done((bf16[2,768,256]{2,1,0:T(8,128)(2,1)S(1)}, bf16[2,768,256]{2,1,0:T(8,128)(2,1)S(1)}, u32[]{:S(2)}, u32[]{:S(2)}) %collective-permute-start.13) | collective-permute-done | bytes 786464 | tf_op jit(solution)/shard_map/ppermute | solution.py:92
  726.3 17.5 %shard_map.45.refs_6_ = f32[2,768,768]{2,1,0:T(8,128)} custom-call(s32[2]{0:T(128)S(1)} %pad_add_fusion.where, bf16[2,768,512]{2,1,0:T(8,128)(2,1)} %get-tuple-element.37.refs_0_, bf16[2,768,512]{2,1,0:T(8,128)(2,1)} %collective-permute-done.15.refs_1_, bf16[2,768,512]{2,1,0:T(8,128)(2,1)} %collective-permute-done.16.refs_2_, ...), custom_call_target="tpu_custom_call" | custom-call | flops 1000 | bytes 1000 | tf_op jit(solution)/shard_map/pallas_call | solution.py:240
  743.8 13.8 %shard_map.46 = bf16[2,4,768,768]{3,2,1,0:T(8,128)(2,1)} custom-call(s32[2]{0:T(128)S(1)} %pad_add_fusion.where, bf16[2,768,256]{2,1,0:T(8,128)(2,1)S(1)} %get-tuple-element.36.refs_0_, bf16[2,768,256]{2,1,0:T(8,128)(2,1)S(1)} %collective-permute-done.12.refs_1_, ...), custom_call_target="tpu_custom_call", output_to_operand_aliasing={{}: (8, {})} | custom-call | flops 1000 | bytes 1000 | tf_op jit(solution)/shard_map/pallas_call | solution.py:240
  (79 shorter events, 48.9 us)
Async XLA Ops:
  9.0 27.4 %all-to-all-start = ((s32[16,1,96]{2,1,0:T(1,128)}), s32[16,1,96]{2,1,0:T(1,128)S(1)}, u32[]{:S(2)}, u32[]{:S(2)}) async-start(s32[16,1,96]{2,1,0:T(1,128)} %bitcast.3), calls=%async_computation | async-start | bytes 16384 | tf_op jit(solution)/shard_map/all_to_all | solution.py:285
  36.4 92.9 %all-to-all-start.2 = ((bf16[16,96,1536]{2,1,0:T(8,128)(2,1)}), bf16[16,96,1536]{2,1,0:T(8,128)(2,1)}, u32[]{:S(2)}, u32[]{:S(2)}) async-start(bf16[16,96,1536]{2,1,0:T(8,128)(2,1)} %bitcast.20), calls=%async_computation.2 | async-start | bytes 9437184 | tf_op jit(solution)/shard_map/all_to_all | solution.py:296
  42.4 254.9 %all-gather.7.cloned.1.call-start = ((), (), s32[]{:S(2)}) async-start(), calls=%async_computation.3 | async-start | bytes 11796480 | tf_op jit(solution)/shard_map/all_gather | solution.py:306
  145.7 109.0 %all-to-all-start.1 = ((bf16[16,96,1536]{2,1,0:T(8,128)(2,1)}), bf16[16,96,1536]{2,1,0:T(8,128)(2,1)}, u32[]{:S(2)}, u32[]{:S(2)}) async-start(bf16[16,96,1536]{2,1,0:T(8,128)(2,1)} %bitcast.21), calls=%async_computation.1 | async-start | bytes 9437184 | tf_op jit(solution)/shard_map/all_to_all | solution.py:296
  167.6 484.5 %all-gather.11.cloned.1.call-start = ((), (), s32[]{:S(2)}) async-start(), calls=%async_computation.5 | async-start | bytes 7864320 | tf_op jit(solution)/shard_map/all_gather | solution.py:310
  167.7 129.6 %collective-permute-start = (bf16[2,768,768]{2,1,0:T(8,128)(2,1)}, bf16[2,768,768]{2,1,0:T(8,128)(2,1)}, u32[]{:S(2)}, u32[]{:S(2)}) collective-permute-start(bf16[2,768,768]{2,1,0:T(8,128)(2,1)} %shard_map.39.refs_1_.refs_4_), channel_id=1, source_target_pairs={{4,0},{8,4},{12,8},{5,1},{9,5},{13,9},{6,2},{10,6},{14,10},{7,3},{... | collective-permute-start | bytes 7077896 | tf_op jit(solution)/shard_map/ppermute | solution.py:21
  169.0 128.3 %collective-permute-start.1 = (bf16[2,768,768]{2,1,0:T(8,128)(2,1)}, bf16[2,768,768]{2,1,0:T(8,128)(2,1)}, u32[]{:S(2)}, u32[]{:S(2)}) collective-permute-start(bf16[2,768,768]{2,1,0:T(8,128)(2,1)} %shard_map.39.refs_1_.refs_4_), channel_id=1, source_target_pairs={{0,4},{4,8},{8,12},{1,5},{5,9},{9,13},{2,6},{6,10},{10,14},{3,7},{... | collective-permute-start | bytes 7077896 | tf_op jit(solution)/shard_map/ppermute | solution.py:21
  297.3 80.2 %collective-permute-start.2 = (bf16[2,768,768]{2,1,0:T(8,128)(2,1)}, bf16[2,768,768]{2,1,0:T(8,128)(2,1)}, u32[]{:S(2)}, u32[]{:S(2)}) collective-permute-start(bf16[2,768,768]{2,1,0:T(8,128)(2,1)} %collective-permute-done.refs_2_.refs_5_), channel_id=1, source_target_pairs={{4,0},{8,4},{5,1},{9,5},{6,2},{10,6},{7,3},{11,7},{20,16},{24,20},... | collective-permute-start | bytes 7077896 | tf_op jit(solution)/shard_map/ppermute | solution.py:21
  298.6 78.9 %collective-permute-start.3 = (bf16[2,768,768]{2,1,0:T(8,128)(2,1)}, bf16[2,768,768]{2,1,0:T(8,128)(2,1)}, u32[]{:S(2)}, u32[]{:S(2)}) collective-permute-start(bf16[2,768,768]{2,1,0:T(8,128)(2,1)} %collective-permute-done.1.refs_3_.refs_6_), channel_id=1, source_target_pairs={{4,8},{8,12},{5,9},{9,13},{6,10},{10,14},{7,11},{11,15},{20,24},{2... | collective-permute-start | bytes 7077896 | tf_op jit(solution)/shard_map/ppermute | solution.py:21
  377.6 293.5 %all-gather.9.cloned.1.call-start = ((), (), s32[]{:S(2)}) async-start(), calls=%async_computation.4 | async-start | bytes 3932160 | tf_op jit(solution)/shard_map/all_gather | solution.py:310
  377.6 52.5 %collective-permute-start.5 = (bf16[2,768,768]{2,1,0:T(8,128)(2,1)}, bf16[2,768,768]{2,1,0:T(8,128)(2,1)S(1)}, u32[]{:S(2)}, u32[]{:S(2)}) collective-permute-start(bf16[2,768,768]{2,1,0:T(8,128)(2,1)} %copy-done.6), channel_id=1, source_target_pairs={{0,2},{1,3},{2,0},{3,1},{4,6},{5,7},{6,4},{7,5},{8,10},{9,11},{10,... | collective-permute-start | bytes 7077896 | tf_op jit(solution)/shard_map/ppermute | solution.py:92
  430.1 8.0 %collective-permute-start.6 = (bf16[2,768,768]{2,1,0:T(8,128)(2,1)S(1)}, bf16[2,768,768]{2,1,0:T(8,128)(2,1)}, u32[]{:S(2)}, u32[]{:S(2)}) collective-permute-start(bf16[2,768,768]{2,1,0:T(8,128)(2,1)S(1)} %collective-permute-done.5.refs_2_), channel_id=1, source_target_pairs={{0,1},{1,0},{2,3},{3,2},{4,5},{5,4},{6,7},{7,6},{8,9},{9,8},{10,11... | collective-permute-start | bytes 7077896 | tf_op jit(solution)/shard_map/ppermute | solution.py:92
  430.1 8.2 %collective-permute-start.4 = (bf16[2,768,768]{2,1,0:T(8,128)(2,1)}, bf16[2,768,768]{2,1,0:T(8,128)(2,1)}, u32[]{:S(2)}, u32[]{:S(2)}) collective-permute-start(bf16[2,768,768]{2,1,0:T(8,128)(2,1)} %copy-done.6), channel_id=1, source_target_pairs={{0,1},{1,0},{2,3},{3,2},{4,5},{5,4},{6,7},{7,6},{8,9},{9,8},{10,11... | collective-permute-start | bytes 7077896 | tf_op jit(solution)/shard_map/ppermute | solution.py:92
  430.6 114.3 %collective-permute-start.7 = (bf16[2,768,768]{2,1,0:T(8,128)(2,1)}, bf16[2,768,768]{2,1,0:T(8,128)(2,1)}, u32[]{:S(2)}, u32[]{:S(2)}) collective-permute-start(bf16[2,768,768]{2,1,0:T(8,128)(2,1)} %collective-permute-done.2.refs_4_.refs_7_), channel_id=1, source_target_pairs={{4,0},{5,1},{6,2},{7,3},{20,16},{21,17},{22,18},{23,19}} | collective-permute-start | bytes 7077896 | tf_op jit(solution)/shard_map/ppermute | solution.py:21
  431.9 113.0 %collective-permute-start.8 = (bf16[2,768,768]{2,1,0:T(8,128)(2,1)}, bf16[2,768,768]{2,1,0:T(8,128)(2,1)}, u32[]{:S(2)}, u32[]{:S(2)}) collective-permute-start(bf16[2,768,768]{2,1,0:T(8,128)(2,1)} %collective-permute-done.3.refs_5_.refs_8_), channel_id=1, source_target_pairs={{8,12},{9,13},{10,14},{11,15},{24,28},{25,29},{26,30},{27,31}} | collective-permute-start | bytes 7077896 | tf_op jit(solution)/shard_map/ppermute | solution.py:21
  569.0 53.5 %collective-permute-start.10 = (bf16[2,768,768]{2,1,0:T(8,128)(2,1)}, bf16[2,768,768]{2,1,0:T(8,128)(2,1)S(1)}, u32[]{:S(2)}, u32[]{:S(2)}) collective-permute-start(bf16[2,768,768]{2,1,0:T(8,128)(2,1)} %get-tuple-element.33.refs_0_), channel_id=1, source_target_pairs={{0,2},{1,3},{2,0},{3,1},{4,6},{5,7},{6,4},{7,5},{8,10},{9,11},{10,... | collective-permute-start | bytes 7077896 | tf_op jit(solution)/shard_map/ppermute | solution.py:92
  570.5 53.4 %collective-permute-start.9 = (bf16[2,768,768]{2,1,0:T(8,128)(2,1)}, bf16[2,768,768]{2,1,0:T(8,128)(2,1)S(1)}, u32[]{:S(2)}, u32[]{:S(2)}) collective-permute-start(bf16[2,768,768]{2,1,0:T(8,128)(2,1)} %get-tuple-element.33.refs_0_), channel_id=1, source_target_pairs={{0,1},{1,0},{2,3},{3,2},{4,5},{5,4},{6,7},{7,6},{8,9},{9,8},{10,11... | collective-permute-start | bytes 7077896 | tf_op jit(solution)/shard_map/ppermute | solution.py:92
  622.5 4.5 collective-permute-start.11
  669.5 36.8 %collective-permute-start.16 = (bf16[2,768,512]{2,1,0:T(8,128)(2,1)}, bf16[2,768,512]{2,1,0:T(8,128)(2,1)}, u32[]{:S(2)}, u32[]{:S(2)}) collective-permute-start(bf16[2,768,512]{2,1,0:T(8,128)(2,1)} %get-tuple-element.37.refs_0_), channel_id=1, source_target_pairs={{0,2},{1,3},{2,0},{3,1},{4,6},{5,7},{6,4},{7,5},{8,10},{9,11},{10,... | collective-permute-start | bytes 4718600 | tf_op jit(solution)/shard_map/ppermute | solution.py:92
  671.1 55.2 %collective-permute-start.15 = (bf16[2,768,512]{2,1,0:T(8,128)(2,1)}, bf16[2,768,512]{2,1,0:T(8,128)(2,1)}, u32[]{:S(2)}, u32[]{:S(2)}) collective-permute-start(bf16[2,768,512]{2,1,0:T(8,128)(2,1)} %get-tuple-element.37.refs_0_), channel_id=1, source_target_pairs={{0,1},{1,0},{2,3},{3,2},{4,5},{5,4},{6,7},{7,6},{8,9},{9,8},{10,11... | collective-permute-start | bytes 4718600 | tf_op jit(solution)/shard_map/ppermute | solution.py:92
  706.4 20.0 %collective-permute-start.17 = (bf16[2,768,512]{2,1,0:T(8,128)(2,1)}, bf16[2,768,512]{2,1,0:T(8,128)(2,1)S(1)}, u32[]{:S(2)}, u32[]{:S(2)}) collective-permute-start(bf16[2,768,512]{2,1,0:T(8,128)(2,1)} %collective-permute-done.16.refs_2_), channel_id=1, source_target_pairs={{0,1},{1,0},{2,3},{3,2},{4,5},{5,4},{6,7},{7,6},{8,9},{9,8},{10,11... | collective-permute-start | bytes 4718600 | tf_op jit(solution)/shard_map/ppermute | solution.py:92
  706.4 20.0 %collective-permute-start.13 = (bf16[2,768,256]{2,1,0:T(8,128)(2,1)S(1)}, bf16[2,768,256]{2,1,0:T(8,128)(2,1)S(1)}, u32[]{:S(2)}, u32[]{:S(2)}) collective-permute-start(bf16[2,768,256]{2,1,0:T(8,128)(2,1)S(1)} %get-tuple-element.36.refs_0_), channel_id=1, source_target_pairs={{0,2},{1,3},{2,0},{3,1},{4,6},{5,7},{6,4},{7,5},{8,10},{9,11},{10,... | collective-permute-start | bytes 2359304 | tf_op jit(solution)/shard_map/ppermute | solution.py:92
  707.8 36.0 %collective-permute-start.12 = (bf16[2,768,256]{2,1,0:T(8,128)(2,1)S(1)}, bf16[2,768,256]{2,1,0:T(8,128)(2,1)S(1)}, u32[]{:S(2)}, u32[]{:S(2)}) collective-permute-start(bf16[2,768,256]{2,1,0:T(8,128)(2,1)S(1)} %get-tuple-element.36.refs_0_), channel_id=1, source_target_pairs={{0,1},{1,0},{2,3},{3,2},{4,5},{5,4},{6,7},{7,6},{8,9},{9,8},{10,11... | collective-permute-start | bytes 2359304 | tf_op jit(solution)/shard_map/ppermute | solution.py:92
  726.3 17.5 %collective-permute-start.14 = (bf16[2,768,256]{2,1,0:T(8,128)(2,1)S(1)}, bf16[2,768,256]{2,1,0:T(8,128)(2,1)S(1)}, u32[]{:S(2)}, u32[]{:S(2)}) collective-permute-start(bf16[2,768,256]{2,1,0:T(8,128)(2,1)S(1)} %collective-permute-done.13.refs_2_), channel_id=1, source_target_pairs={{0,1},{1,0},{2,3},{3,2},{4,5},{5,4},{6,7},{7,6},{8,9},{9,8},{10,11... | collective-permute-start | bytes 2359304 | tf_op jit(solution)/shard_map/ppermute | solution.py:92
  (14 other events, 236.6 us)
Sparse Core Ops, SparseCore 0:
  136.2 131.8 all-gather.6
  377.7 144.4 all-gather.10
  570.7 62.5 all-gather.8

commit v10 on v9

--- a/solution.py
+++ b/solution.py
@@ -324,8 +324,7 @@
     else:
         right0, ups = [gather_rows(tiles[0])], [None]
     right1 = [gather_rows(part) for part in cut]
-    lefts.append((gather_cols(tiles[1], n_col, second), everything))
-    right0[0] = after(right0[0], lefts[1][0])
+    lefts.append((gather_cols(tiles[1], n_col, pair), everything))
     views0 = [(list(enumerate(ups)), j * sub) for j in everything]
 
     where = jnp.stack([my_row, lax.axis_index("col")]).astype(jnp.int32)
@@ -333,13 +332,14 @@
     shape = (2, planes, block_rows, tile_cols)
     result, piece = product([lefts[0]], right0, views0, shape, (), (0, 0, 0))
     found = gather_cols(piece, n_col)
+    result, most = product([lefts[1]], right1[:1], views1[:-1], shape, (result,), (0, 1, 0))
+    most = gather_cols(most, n_col)
+    found[0] = after(found[0], right1[1])
     (result,) = product([(found, everything)], right0, views0, shape, (result,), (1, 0, 0))
-    result, piece = product([lefts[1]], right1[:1], views1[:-1], shape, (result,), (0, 1, 0))
-    most = (gather_cols(piece, n_col), everything[:-1])
-    result, piece = product([lefts[1]], right1[1:], [([(0, None)], 0)], shape, (result,), (0, 1, THIRDS - 1))
-    rest = (gather_cols(piece, n_col), everything[-1:])
-    (sums,) = product([most], right1, views1, shape, (), None)
-    return product([rest], right1, views1, shape, (result,), (1, 1, 0), before=sums)[0]
+    result, rest = product([lefts[1]], right1[1:], [([(0, None)], 0)], shape, (result,), (0, 1, THIRDS - 1))
+    (sums,) = product([(most, everything[:-1])], right1, views1, shape, (), None)
+    rest = gather_cols(after(rest, most[n_col // 2]), n_col, sums)
+    return product([(rest, everything[-1:])], right1, views1, shape, (result,), (1, 1, 0), before=sums)[0]
 
 
 def solution(mesh):

time: 765 us -> 737 us (0.963)
  waiting for transfers between devices: 533 us -> 509 us
    ppermute x3, waiting for transfers between devices: 217 us -> 168 us  [hop(): lax.ppermute(pair[0], 'row', down)]
    ppermute x3, waiting for transfers between devices: 0.01 us -> 40.8 us  [hop(): lax.ppermute(pair[1], 'row', up)]
    ppermute x12, waiting for transfers between devices: 152 us -> 134 us  [gather_cols(): arrived = {d ^ bit: lax.ppermute(a, 'col', pairs) for d, a in held.items()}]
    unnamed x29 -> x23, local copies, waits for them, and re-layouts: 33 us -> 27.8 us
  transfers between devices with their start and end apart: 24 -> 24, of which waited for: 12 -> 12; matrix products, arithmetic and copies ran while one was open for 2% -> 2% of each run, Pallas kernels for 13% -> 14%
where the time goes in v10:
time: 737 us; the launch traced here: 731 us
  waiting for transfers between devices  509 us (69%)
  Pallas kernels  124 us (17%)
  starting transfers between devices  52.4 us (7%)
  local copies, waits for them, and re-layouts  29.1 us (4%)
  between operations  14 us (2%)
    ppermute x3, waiting for transfers between devices, hop(): lax.ppermute(pair[0], 'row', down)  168 us
    all_to_all x2, waiting for transfers between devices, per_device(): lax.all_to_all(sent.reshape(n_row * n_col, cap, 2 * tile_cols), ('row', '...  165 us
    ppermute x12, waiting for transfers between devices, gather_cols(): arrived = {d ^ bit: lax.ppermute(a, 'col', pairs) for d, a in held.items()}  134 us
    pallas_call x6, Pallas kernels, complex_product(): pl.pallas_call(functools.partial(product_kernel, opts), grid_spec=pltpu.P...  103 us
    ppermute x3, waiting for transfers between devices, hop(): lax.ppermute(pair[1], 'row', up)  40.8 us
    all_to_all x2, starting transfers between devices, per_device(): lax.all_to_all(sent.reshape(n_row * n_col, cap, 2 * tile_cols), ('row', '...  28 us
    unnamed x23, local copies, waits for them, and re-layouts  27.8 us
  transfers between devices with their start and end apart: 24, of which 12 were waited for; matrix products, arithmetic and copies ran while one was open for 2% of the time, Pallas kernels for 14%

profile of v10, /device:TPU:0, one launch (start us, length us, event | category | flops | bytes accessed | tf_op | source)
XLA Modules:
  0.0 730.9 jit_solution(13916565496305742700)
XLA Ops:
  9.0 7.4 %all-to-all-start = ((s32[16,1,96]{2,1,0:T(1,128)}), s32[16,1,96]{2,1,0:T(1,128)S(1)}, u32[]{:S(2)}, u32[]{:S(2)}) async-start(s32[16,1,96]{2,1,0:T(1,128)} %bitcast.3), calls=%async_computation | async-start | bytes 16384 | tf_op jit(solution)/shard_map/all_to_all | solution.py:285
  16.4 10.4 %copy.12 = bf16[384,4,3072]{2,0,1:T(8,128)(2,1)} copy(bf16[384,4,3072]{2,1,0:T(4,128)(2,1)} %param.3) | data formatting | bytes 18874368 | tf_op args[0]
  26.8 3.7 copy-done
  30.5 3.7 shard_map.38
  36.4 6.0 all-to-all-start.2
  44.6 84.7 %all-to-all-done.2 = bf16[16,96,1536]{2,1,0:T(8,128)(2,1)} async-done(((bf16[16,96,1536]{2,1,0:T(8,128)(2,1)}), bf16[16,96,1536]{2,1,0:T(8,128)(2,1)}, u32[]{:S(2)}, u32[]{:S(2)}) %all-to-all-start.2) | async-done | bytes 4718624 | tf_op jit(solution)/shard_map/all_to_all | solution.py:296
  129.3 6.7 shard_map.39.refs_1_.refs_4_
  139.7 3.7 shard_map.37
  145.6 21.9 %all-to-all-start.1 = ((bf16[16,96,1536]{2,1,0:T(8,128)(2,1)}), bf16[16,96,1536]{2,1,0:T(8,128)(2,1)}, u32[]{:S(2)}, u32[]{:S(2)}) async-start(bf16[16,96,1536]{2,1,0:T(8,128)(2,1)} %bitcast.21), calls=%async_computation.1 | async-start | bytes 9437184 | tf_op jit(solution)/shard_map/all_to_all | solution.py:296
  167.6 5.2 collective-permute-start.1
  174.1 80.6 %all-to-all-done.1 = bf16[16,96,1536]{2,1,0:T(8,128)(2,1)} async-done(((bf16[16,96,1536]{2,1,0:T(8,128)(2,1)}), bf16[16,96,1536]{2,1,0:T(8,128)(2,1)}, u32[]{:S(2)}, u32[]{:S(2)}) %all-to-all-start.1) | async-done | bytes 4718624 | tf_op jit(solution)/shard_map/all_to_all | solution.py:296
  254.6 40.8 %collective-permute-done.1.refs_3_.refs_6_ = bf16[2,768,768]{2,1,0:T(8,128)(2,1)} collective-permute-done((bf16[2,768,768]{2,1,0:T(8,128)(2,1)}, bf16[2,768,768]{2,1,0:T(8,128)(2,1)}, u32[]{:S(2)}, u32[]{:S(2)}) %collective-permute-start.1) | collective-permute-done | bytes 2359328 | tf_op jit(solution)/shard_map/ppermute | solution.py:21
  300.6 6.4 shard_map.40
  309.6 67.9 %collective-permute-done.2.refs_4_.refs_7_ = bf16[2,768,768]{2,1,0:T(8,128)(2,1)} collective-permute-done((bf16[2,768,768]{2,1,0:T(8,128)(2,1)}, bf16[2,768,768]{2,1,0:T(8,128)(2,1)}, u32[]{:S(2)}, u32[]{:S(2)}) %collective-permute-start.2) | collective-permute-done | bytes 2359328 | tf_op jit(solution)/shard_map/ppermute | solution.py:21
  382.6 47.6 %collective-permute-done.7.refs_2_ = bf16[2,768,768]{2,1,0:T(8,128)(2,1)} collective-permute-done((bf16[2,768,768]{2,1,0:T(8,128)(2,1)}, bf16[2,768,768]{2,1,0:T(8,128)(2,1)}, u32[]{:S(2)}, u32[]{:S(2)}) %collective-permute-start.7) | collective-permute-done | bytes 2359328 | tf_op jit(solution)/shard_map/ppermute | solution.py:92
  430.1 98.8 %collective-permute-done.3.refs_6_.refs_9_ = bf16[2,768,768]{2,1,0:T(8,128)(2,1)} collective-permute-done((bf16[2,768,768]{2,1,0:T(8,128)(2,1)}, bf16[2,768,768]{2,1,0:T(8,128)(2,1)}, u32[]{:S(2)}, u32[]{:S(2)}) %collective-permute-start.3) | collective-permute-done | bytes 2359328 | tf_op jit(solution)/shard_map/ppermute | solution.py:21
  528.9 24.0 %shard_map.41 = (bf16[2,4,768,768]{3,2,1,0:T(8,128)(2,1)}, bf16[2,768,768]{2,1,0:T(8,128)(2,1)}) custom-call(s32[2]{0:T(128)S(1)} %pad_add_fusion.where, bf16[4,2,768,768]{3,2,1,0:T(8,128)(2,1)} %bitcast.25, bf16[2,768,768]{2,1,0:T(8,128)(2,1)} %shard_map.39.refs_1_.refs_4_, bf16[2,768,768]{2,1,0:T(8,128)(2,1)} %collective-permute-done.refs_2_.refs_5_, ...), custom_call_target="tpu_custom_call" | custom-call | flops 1000 | bytes 1000 | tf_op jit(solution)/shard_map/pallas_call | solution.py:240
  553.7 45.1 %collective-permute-done.10.refs_2_ = bf16[2,768,768]{2,1,0:T(8,128)(2,1)} collective-permute-done((bf16[2,768,768]{2,1,0:T(8,128)(2,1)}, bf16[2,768,768]{2,1,0:T(8,128)(2,1)}, u32[]{:S(2)}, u32[]{:S(2)}) %collective-permute-start.10) | collective-permute-done | bytes 2359328 | tf_op jit(solution)/shard_map/ppermute | solution.py:92
  602.0 15.6 %shard_map.42 = (bf16[2,4,768,768]{3,2,1,0:T(8,128)(2,1)}, bf16[2,768,512]{2,1,0:T(8,128)(2,1)}) custom-call(s32[2]{0:T(128)S(1)} %pad_add_fusion.where, bf16[2,768,768]{2,1,0:T(8,128)(2,1)S(1)} %copy-done.6, bf16[2,768,768]{2,1,0:T(8,128)(2,1)S(1)} %copy-done.8, ...), custom_call_target="tpu_custom_call", output_to_operand_aliasing={{0}: (6, {})} | custom-call | flops 1000 | bytes 1000 | tf_op jit(solution)/shard_map/pallas_call | solution.py:240
  618.2 36.5 %collective-permute-done.12.refs_2_ = bf16[2,768,512]{2,1,0:T(8,128)(2,1)} collective-permute-done((bf16[2,768,512]{2,1,0:T(8,128)(2,1)}, bf16[2,768,512]{2,1,0:T(8,128)(2,1)}, u32[]{:S(2)}, u32[]{:S(2)}) %collective-permute-start.12) | collective-permute-done | bytes 1572896 | tf_op jit(solution)/shard_map/ppermute | solution.py:92
  654.8 24.0 %shard_map.43.refs_5_ = bf16[2,4,768,768]{3,2,1,0:T(8,128)(2,1)} custom-call(s32[2]{0:T(128)S(1)} %pad_add_fusion.where, bf16[2,768,768]{2,1,0:T(8,128)(2,1)} %get-tuple-element.34.refs_0_, bf16[2,768,768]{2,1,0:T(8,128)(2,1)} %collective-permute-done.9.refs_1_, ...), custom_call_target="tpu_custom_call", output_to_operand_aliasing={{}: (12, {})} | custom-call | flops 1000 | bytes 1000 | tf_op jit(solution)/shard_map/pallas_call | solution.py:240
  678.8 8.3 %shard_map.44 = (bf16[2,4,768,768]{3,2,1,0:T(8,128)(2,1)}, bf16[2,768,256]{2,1,0:T(8,128)(2,1)S(1)}) custom-call(s32[2]{0:T(128)S(1)} %pad_add_fusion.where, bf16[2,768,768]{2,1,0:T(8,128)(2,1)S(1)} %copy-done.6, bf16[2,768,768]{2,1,0:T(8,128)(2,1)S(1)} %copy-done.9, ...), custom_call_target="tpu_custom_call", output_to_operand_aliasing={{0}: (6, {})} | custom-call | flops 1000 | bytes 1000 | tf_op jit(solution)/shard_map/pallas_call | solution.py:240
  687.5 17.4 %shard_map.45.refs_6_ = f32[2,768,768]{2,1,0:T(8,128)} custom-call(s32[2]{0:T(128)S(1)} %pad_add_fusion.where, bf16[2,768,512]{2,1,0:T(8,128)(2,1)} %get-tuple-element.40.refs_0_, bf16[2,768,512]{2,1,0:T(8,128)(2,1)} %collective-permute-done.13.refs_1_, bf16[2,768,512]{2,1,0:T(8,128)(2,1)} %collective-permute-done.12.refs_2_, ...), custom_call_target="tpu_custom_call" | custom-call | flops 1000 | bytes 1000 | tf_op jit(solution)/shard_map/pallas_call | solution.py:240
  710.5 13.8 %shard_map.46 = bf16[2,4,768,768]{3,2,1,0:T(8,128)(2,1)} custom-call(s32[2]{0:T(128)S(1)} %pad_add_fusion.where, bf16[2,768,256]{2,1,0:T(8,128)(2,1)S(1)} %get-tuple-element.42.refs_0_, bf16[2,768,256]{2,1,0:T(8,128)(2,1)S(1)} %collective-permute-done.15.refs_1_, ...), custom_call_target="tpu_custom_call", output_to_operand_aliasing={{}: (8, {})} | custom-call | flops 1000 | bytes 1000 | tf_op jit(solution)/shard_map/pallas_call | solution.py:240
  (73 shorter events, 36.6 us)
Async XLA Ops:
  9.0 27.4 %all-to-all-start = ((s32[16,1,96]{2,1,0:T(1,128)}), s32[16,1,96]{2,1,0:T(1,128)S(1)}, u32[]{:S(2)}, u32[]{:S(2)}) async-start(s32[16,1,96]{2,1,0:T(1,128)} %bitcast.3), calls=%async_computation | async-start | bytes 16384 | tf_op jit(solution)/shard_map/all_to_all | solution.py:285
  36.4 92.9 %all-to-all-start.2 = ((bf16[16,96,1536]{2,1,0:T(8,128)(2,1)}), bf16[16,96,1536]{2,1,0:T(8,128)(2,1)}, u32[]{:S(2)}, u32[]{:S(2)}) async-start(bf16[16,96,1536]{2,1,0:T(8,128)(2,1)} %bitcast.20), calls=%async_computation.2 | async-start | bytes 9437184 | tf_op jit(solution)/shard_map/all_to_all | solution.py:296
  42.5 254.8 %all-gather.7.cloned.1.call-start = ((), (), s32[]{:S(2)}) async-start(), calls=%async_computation.3 | async-start | bytes 11796480 | tf_op jit(solution)/shard_map/all_gather | solution.py:306
  145.6 109.0 %all-to-all-start.1 = ((bf16[16,96,1536]{2,1,0:T(8,128)(2,1)}), bf16[16,96,1536]{2,1,0:T(8,128)(2,1)}, u32[]{:S(2)}, u32[]{:S(2)}) async-start(bf16[16,96,1536]{2,1,0:T(8,128)(2,1)} %bitcast.21), calls=%async_computation.1 | async-start | bytes 9437184 | tf_op jit(solution)/shard_map/all_to_all | solution.py:296
  167.5 432.7 %all-gather.11.cloned.1.call-start = ((), (), s32[]{:S(2)}) async-start(), calls=%async_computation.5 | async-start | bytes 7864320 | tf_op jit(solution)/shard_map/all_gather | solution.py:310
  167.6 127.9 %collective-permute-start.1 = (bf16[2,768,768]{2,1,0:T(8,128)(2,1)}, bf16[2,768,768]{2,1,0:T(8,128)(2,1)}, u32[]{:S(2)}, u32[]{:S(2)}) collective-permute-start(bf16[2,768,768]{2,1,0:T(8,128)(2,1)} %shard_map.39.refs_1_.refs_4_), channel_id=1, source_target_pairs={{0,4},{4,8},{8,12},{1,5},{5,9},{9,13},{2,6},{6,10},{10,14},{3,7},{... | collective-permute-start | bytes 7077896 | tf_op jit(solution)/shard_map/ppermute | solution.py:21
  172.8 124.4 %collective-permute-start = (bf16[2,768,768]{2,1,0:T(8,128)(2,1)}, bf16[2,768,768]{2,1,0:T(8,128)(2,1)}, u32[]{:S(2)}, u32[]{:S(2)}) collective-permute-start(bf16[2,768,768]{2,1,0:T(8,128)(2,1)} %shard_map.39.refs_1_.refs_4_), channel_id=1, source_target_pairs={{4,0},{8,4},{12,8},{5,1},{9,5},{13,9},{6,2},{10,6},{14,10},{7,3},{... | collective-permute-start | bytes 7077896 | tf_op jit(solution)/shard_map/ppermute | solution.py:21
  297.2 80.2 %collective-permute-start.2 = (bf16[2,768,768]{2,1,0:T(8,128)(2,1)}, bf16[2,768,768]{2,1,0:T(8,128)(2,1)}, u32[]{:S(2)}, u32[]{:S(2)}) collective-permute-start(bf16[2,768,768]{2,1,0:T(8,128)(2,1)} %collective-permute-done.refs_2_.refs_5_), channel_id=1, source_target_pairs={{4,0},{8,4},{5,1},{9,5},{6,2},{10,6},{7,3},{11,7},{20,16},{24,20},... | collective-permute-start | bytes 7077896 | tf_op jit(solution)/shard_map/ppermute | solution.py:21
  298.5 78.9 %collective-permute-start.4 = (bf16[2,768,768]{2,1,0:T(8,128)(2,1)}, bf16[2,768,768]{2,1,0:T(8,128)(2,1)}, u32[]{:S(2)}, u32[]{:S(2)}) collective-permute-start(bf16[2,768,768]{2,1,0:T(8,128)(2,1)} %collective-permute-done.1.refs_3_.refs_6_), channel_id=1, source_target_pairs={{4,8},{8,12},{5,9},{9,13},{6,10},{10,14},{7,11},{11,15},{20,24},{2... | collective-permute-start | bytes 7077896 | tf_op jit(solution)/shard_map/ppermute | solution.py:21
  377.5 277.3 %all-gather.9.cloned.1.call-start = ((), (), s32[]{:S(2)}) async-start(), calls=%async_computation.4 | async-start | bytes 3932160 | tf_op jit(solution)/shard_map/all_gather | solution.py:310
  377.5 52.6 %collective-permute-start.7 = (bf16[2,768,768]{2,1,0:T(8,128)(2,1)}, bf16[2,768,768]{2,1,0:T(8,128)(2,1)}, u32[]{:S(2)}, u32[]{:S(2)}) collective-permute-start(bf16[2,768,768]{2,1,0:T(8,128)(2,1)} %copy-done.5), channel_id=1, source_target_pairs={{0,2},{1,3},{2,0},{3,1},{4,6},{5,7},{6,4},{7,5},{8,10},{9,11},{10,... | collective-permute-start | bytes 7077896 | tf_op jit(solution)/shard_map/ppermute | solution.py:92
  379.1 149.9 %collective-permute-start.3 = (bf16[2,768,768]{2,1,0:T(8,128)(2,1)}, bf16[2,768,768]{2,1,0:T(8,128)(2,1)}, u32[]{:S(2)}, u32[]{:S(2)}) collective-permute-start(bf16[2,768,768]{2,1,0:T(8,128)(2,1)} %collective-permute-done.2.refs_4_.refs_7_), channel_id=1, source_target_pairs={{4,0},{5,1},{6,2},{7,3},{20,16},{21,17},{22,18},{23,19}} | collective-permute-start | bytes 7077896 | tf_op jit(solution)/shard_map/ppermute | solution.py:21
  380.3 148.6 %collective-permute-start.5 = (bf16[2,768,768]{2,1,0:T(8,128)(2,1)}, bf16[2,768,768]{2,1,0:T(8,128)(2,1)}, u32[]{:S(2)}, u32[]{:S(2)}) collective-permute-start(bf16[2,768,768]{2,1,0:T(8,128)(2,1)} %collective-permute-done.4.refs_5_.refs_8_), channel_id=1, source_target_pairs={{8,12},{9,13},{10,14},{11,15},{24,28},{25,29},{26,30},{27,31}} | collective-permute-start | bytes 7077896 | tf_op jit(solution)/shard_map/ppermute | solution.py:21
  553.0 45.9 %collective-permute-start.10 = (bf16[2,768,768]{2,1,0:T(8,128)(2,1)}, bf16[2,768,768]{2,1,0:T(8,128)(2,1)}, u32[]{:S(2)}, u32[]{:S(2)}) collective-permute-start(bf16[2,768,768]{2,1,0:T(8,128)(2,1)} %get-tuple-element.34.refs_0_), channel_id=1, source_target_pairs={{0,2},{1,3},{2,0},{3,1},{4,6},{5,7},{6,4},{7,5},{8,10},{9,11},{10,... | collective-permute-start | bytes 7077896 | tf_op jit(solution)/shard_map/ppermute | solution.py:92
  553.1 45.8 %collective-permute-start.6 = (bf16[2,768,768]{2,1,0:T(8,128)(2,1)S(1)}, bf16[2,768,768]{2,1,0:T(8,128)(2,1)S(1)}, u32[]{:S(2)}, u32[]{:S(2)}) collective-permute-start(bf16[2,768,768]{2,1,0:T(8,128)(2,1)S(1)} %copy-done.6), channel_id=1, source_target_pairs={{0,1},{1,0},{2,3},{3,2},{4,5},{5,4},{6,7},{7,6},{8,9},{9,8},{10,11... | collective-permute-start | bytes 7077896 | tf_op jit(solution)/shard_map/ppermute | solution.py:92
  553.1 47.1 %collective-permute-start.8 = (bf16[2,768,768]{2,1,0:T(8,128)(2,1)}, bf16[2,768,768]{2,1,0:T(8,128)(2,1)}, u32[]{:S(2)}, u32[]{:S(2)}) collective-permute-start(bf16[2,768,768]{2,1,0:T(8,128)(2,1)} %collective-permute-done.7.refs_2_), channel_id=1, source_target_pairs={{0,1},{1,0},{2,3},{3,2},{4,5},{5,4},{6,7},{7,6},{8,9},{9,8},{10,11... | collective-permute-start | bytes 7077896 | tf_op jit(solution)/shard_map/ppermute | solution.py:92
  553.6 101.1 %collective-permute-start.9 = (bf16[2,768,768]{2,1,0:T(8,128)(2,1)}, bf16[2,768,768]{2,1,0:T(8,128)(2,1)}, u32[]{:S(2)}, u32[]{:S(2)}) collective-permute-start(bf16[2,768,768]{2,1,0:T(8,128)(2,1)} %get-tuple-element.34.refs_0_), channel_id=1, source_target_pairs={{0,1},{1,0},{2,3},{3,2},{4,5},{5,4},{6,7},{7,6},{8,9},{9,8},{10,11... | collective-permute-start | bytes 7077896 | tf_op jit(solution)/shard_map/ppermute | solution.py:92
  598.8 55.9 %collective-permute-start.11 = (bf16[2,768,768]{2,1,0:T(8,128)(2,1)}, bf16[2,768,768]{2,1,0:T(8,128)(2,1)}, u32[]{:S(2)}, u32[]{:S(2)}) collective-permute-start(bf16[2,768,768]{2,1,0:T(8,128)(2,1)} %collective-permute-done.10.refs_2_), channel_id=1, source_target_pairs={{0,1},{1,0},{2,3},{3,2},{4,5},{5,4},{6,7},{7,6},{8,9},{9,8},{10,11... | collective-permute-start | bytes 7077896 | tf_op jit(solution)/shard_map/ppermute | solution.py:92
  617.6 37.2 %collective-permute-start.12 = (bf16[2,768,512]{2,1,0:T(8,128)(2,1)}, bf16[2,768,512]{2,1,0:T(8,128)(2,1)}, u32[]{:S(2)}, u32[]{:S(2)}) collective-permute-start(bf16[2,768,512]{2,1,0:T(8,128)(2,1)} %get-tuple-element.40.refs_0_), channel_id=1, source_target_pairs={{0,2},{1,3},{2,0},{3,1},{4,6},{5,7},{6,4},{7,5},{8,10},{9,11},{10,... | collective-permute-start | bytes 4718600 | tf_op jit(solution)/shard_map/ppermute | solution.py:92
  617.9 69.5 %collective-permute-start.13 = (bf16[2,768,512]{2,1,0:T(8,128)(2,1)}, bf16[2,768,512]{2,1,0:T(8,128)(2,1)}, u32[]{:S(2)}, u32[]{:S(2)}) collective-permute-start(bf16[2,768,512]{2,1,0:T(8,128)(2,1)} %get-tuple-element.40.refs_0_), channel_id=1, source_target_pairs={{0,1},{1,0},{2,3},{3,2},{4,5},{5,4},{6,7},{7,6},{8,9},{9,8},{10,11... | collective-permute-start | bytes 4718600 | tf_op jit(solution)/shard_map/ppermute | solution.py:92
  654.7 32.7 %collective-permute-start.14 = (bf16[2,768,512]{2,1,0:T(8,128)(2,1)}, bf16[2,768,512]{2,1,0:T(8,128)(2,1)}, u32[]{:S(2)}, u32[]{:S(2)}) collective-permute-start(bf16[2,768,512]{2,1,0:T(8,128)(2,1)} %collective-permute-done.12.refs_2_), channel_id=1, source_target_pairs={{0,1},{1,0},{2,3},{3,2},{4,5},{5,4},{6,7},{7,6},{8,9},{9,8},{10,11... | collective-permute-start | bytes 4718600 | tf_op jit(solution)/shard_map/ppermute | solution.py:92
  687.1 20.0 %collective-permute-start.16 = (bf16[2,768,256]{2,1,0:T(8,128)(2,1)S(1)}, bf16[2,768,256]{2,1,0:T(8,128)(2,1)S(1)}, u32[]{:S(2)}, u32[]{:S(2)}) collective-permute-start(bf16[2,768,256]{2,1,0:T(8,128)(2,1)S(1)} %get-tuple-element.42.refs_0_), channel_id=1, source_target_pairs={{0,2},{1,3},{2,0},{3,1},{4,6},{5,7},{6,4},{7,5},{8,10},{9,11},{10,... | collective-permute-start | bytes 2359304 | tf_op jit(solution)/shard_map/ppermute | solution.py:92
  707.1 2.3 collective-permute-start.15
  707.1 3.4 collective-permute-start.17
  (11 other events, 235.9 us)
Sparse Core Ops, SparseCore 0:
  136.1 131.8 all-gather.6
  377.6 158.2 all-gather.10
  537.5 66.5 all-gather.8

commit v11 on v10

--- a/solution.py
+++ b/solution.py
@@ -289,13 +289,14 @@
 
     tiles, lefts = [], []
     pair = None
+    sent = [bin_rows(picker, data, f, n_row, n_col) for f in range(FREQ)]
+    sent[0] = after(sent[0], places)
     for f in range(FREQ):
-        sent = bin_rows(picker, data, f, n_row, n_col)
+        got = lax.all_to_all(
+            sent[f].reshape(n_row * n_col, cap, 2 * tile_cols), ("row", "col"), split_axis=0, concat_axis=0, tiled=True
+        ).reshape(-1, 2 * tile_cols)
         if f == 0:
-            sent = after(sent, places)
-        got = lax.all_to_all(
-            sent.reshape(n_row * n_col, cap, 2 * tile_cols), ("row", "col"), split_axis=0, concat_axis=0, tiled=True
-        ).reshape(-1, 2 * tile_cols)
+            got = after(got, sent[1])
         if pair is not None:
             got, pair, _ = lax.optimization_barrier((got, pair, lefts[0][0]))
         tile, *cut = place_rows(placer, got, (THIRDS - 1, 1) if f else ())
@@ -320,7 +321,7 @@
             second = pair if k == 2 else second
             right0 += list(pair)
             ups += [k, -k]
-        cut = [after(part, second) for part in cut]
+        cut[1] = after(cut[1], second)
     else:
         right0, ups = [gather_rows(tiles[0])], [None]
     right1 = [gather_rows(part) for part in cut]
@@ -331,14 +332,13 @@
     product = functools.partial(complex_product, where)
     shape = (2, planes, block_rows, tile_cols)
     result, piece = product([lefts[0]], right0, views0, shape, (), (0, 0, 0))
-    found = gather_cols(piece, n_col)
     result, most = product([lefts[1]], right1[:1], views1[:-1], shape, (result,), (0, 1, 0))
-    most = gather_cols(most, n_col)
-    found[0] = after(found[0], right1[1])
+    found = gather_cols(piece, n_col, most)
+    result, rest = product([lefts[1]], right1[1:], [([(0, None)], 0)], shape, (result,), (0, 1, THIRDS - 1))
     (result,) = product([(found, everything)], right0, views0, shape, (result,), (1, 0, 0))
-    result, rest = product([lefts[1]], right1[1:], [([(0, None)], 0)], shape, (result,), (0, 1, THIRDS - 1))
+    most = gather_cols(most, n_col, result)
     (sums,) = product([(most, everything[:-1])], right1, views1, shape, (), None)
-    rest = gather_cols(after(rest, most[n_col // 2]), n_col, sums)
+    rest = gather_cols(rest, n_col, sums)
     return product([(rest, everything[-1:])], right1, views1, shape, (result,), (1, 1, 0), before=sums)[0]
 
 

time: 737 us -> 691 us (0.938)
  waiting for transfers between devices: 509 us -> 465 us
    ppermute x3, waiting for transfers between devices: 168 us -> 267 us  [hop(): lax.ppermute(pair[0], 'row', down)]
    ppermute x12, waiting for transfers between devices: 134 us -> 43.3 us  [gather_cols(): arrived = {d ^ bit: lax.ppermute(a, 'col', pairs) for d, a in held.items()}]
    ppermute x3, waiting for transfers between devices: 40.8 us -> 0.01 us  [hop(): lax.ppermute(pair[1], 'row', up)]
    all_to_all x2, waiting for transfers between devices: 165 us -> 155 us  [per_device(): lax.all_to_all(sent[f].reshape(n_row * n_col, cap, 2 * tile_cols), ('row'...]
    unnamed x23 -> x21, local copies, waits for them, and re-layouts: 27.8 us -> 26.6 us
  transfers between devices with their start and end apart: 24 -> 24, of which waited for: 12 -> 11; matrix products, arithmetic and copies ran while one was open for 2% -> 2% of each run, Pallas kernels for 14% -> 14%
where the time goes in v11:
time: 691 us; the launch traced here: 690 us
  waiting for transfers between devices  465 us (67%)
  Pallas kernels  124 us (18%)
  starting transfers between devices  57.2 us (8%)
  local copies, waits for them, and re-layouts  27.8 us (4%)
  between operations  14 us (2%)
    ppermute x3, waiting for transfers between devices, hop(): lax.ppermute(pair[0], 'row', down)  267 us
    all_to_all x2, waiting for transfers between devices, per_device(): lax.all_to_all(sent[f].reshape(n_row * n_col, cap, 2 * tile_cols), ('row'...  155 us
    pallas_call x6, Pallas kernels, complex_product(): pl.pallas_call(functools.partial(product_kernel, opts), grid_spec=pltpu.P...  103 us
    ppermute x12, waiting for transfers between devices, gather_cols(): arrived = {d ^ bit: lax.ppermute(a, 'col', pairs) for d, a in held.items()}  43.3 us
    all_to_all x2, starting transfers between devices, per_device(): lax.all_to_all(sent[f].reshape(n_row * n_col, cap, 2 * tile_cols), ('row'...  27.9 us
    unnamed x21, local copies, waits for them, and re-layouts  26.6 us
  transfers between devices with their start and end apart: 24, of which 11 were waited for; matrix products, arithmetic and copies ran while one was open for 2% of the time, Pallas kernels for 14%

profile of v11, /device:TPU:0, one launch (start us, length us, event | category | flops | bytes accessed | tf_op | source)
XLA Modules:
  0.0 690.4 jit_solution(6511019314119473498)
XLA Ops:
  9.0 7.4 %all-to-all-start = ((s32[16,1,96]{2,1,0:T(1,128)}), s32[16,1,96]{2,1,0:T(1,128)S(1)}, u32[]{:S(2)}, u32[]{:S(2)}) async-start(s32[16,1,96]{2,1,0:T(1,128)} %bitcast.3), calls=%async_computation | async-start | bytes 16384 | tf_op jit(solution)/shard_map/all_to_all | solution.py:285
  16.4 10.4 %copy.12 = bf16[384,4,3072]{2,0,1:T(8,128)(2,1)} copy(bf16[384,4,3072]{2,1,0:T(4,128)(2,1)} %param.3) | data formatting | bytes 18874368 | tf_op args[0]
  26.8 3.7 copy-done
  30.5 3.7 shard_map.38
  36.4 6.0 all-to-all-start.2
  42.5 3.7 copy-done.1
  46.2 3.7 shard_map.37
  54.0 75.2 %all-to-all-done.2 = bf16[16,96,1536]{2,1,0:T(8,128)(2,1)} async-done(((bf16[16,96,1536]{2,1,0:T(8,128)(2,1)}), bf16[16,96,1536]{2,1,0:T(8,128)(2,1)}, u32[]{:S(2)}, u32[]{:S(2)}) %all-to-all-start.2) | async-done | bytes 4718624 | tf_op jit(solution)/shard_map/all_to_all | solution.py:295
  129.3 6.7 shard_map.39.refs_1_.refs_4_
  136.0 21.8 %all-to-all-start.1 = ((bf16[16,96,1536]{2,1,0:T(8,128)(2,1)}), bf16[16,96,1536]{2,1,0:T(8,128)(2,1)}, u32[]{:S(2)}, u32[]{:S(2)}) async-start(bf16[16,96,1536]{2,1,0:T(8,128)(2,1)} %bitcast.20), calls=%async_computation.1 | async-start | bytes 9437184 | tf_op jit(solution)/shard_map/all_to_all | solution.py:295
  159.1 6.1 collective-permute-start.1
  165.3 79.6 %all-to-all-done.1 = bf16[16,96,1536]{2,1,0:T(8,128)(2,1)} async-done(((bf16[16,96,1536]{2,1,0:T(8,128)(2,1)}), bf16[16,96,1536]{2,1,0:T(8,128)(2,1)}, u32[]{:S(2)}, u32[]{:S(2)}) %all-to-all-start.1) | async-done | bytes 4718624 | tf_op jit(solution)/shard_map/all_to_all | solution.py:295
  244.9 42.6 %collective-permute-done.refs_2_.refs_5_ = bf16[2,768,768]{2,1,0:T(8,128)(2,1)} collective-permute-done((bf16[2,768,768]{2,1,0:T(8,128)(2,1)}, bf16[2,768,768]{2,1,0:T(8,128)(2,1)}, u32[]{:S(2)}, u32[]{:S(2)}) %collective-permute-start) | collective-permute-done | bytes 2359328 | tf_op jit(solution)/shard_map/ppermute | solution.py:21
  287.5 6.4 shard_map.40
  300.0 157.5 %collective-permute-done.2.refs_4_.refs_7_ = bf16[2,768,768]{2,1,0:T(8,128)(2,1)S(1)} collective-permute-done((bf16[2,768,768]{2,1,0:T(8,128)(2,1)}, bf16[2,768,768]{2,1,0:T(8,128)(2,1)S(1)}, u32[]{:S(2)}, u32[]{:S(2)}) %collective-permute-start.2) | collective-permute-done | bytes 2359328 | tf_op jit(solution)/shard_map/ppermute | solution.py:21
  462.5 66.7 %collective-permute-done.3.refs_6_.refs_9_ = bf16[2,768,768]{2,1,0:T(8,128)(2,1)} collective-permute-done((bf16[2,768,768]{2,1,0:T(8,128)(2,1)S(1)}, bf16[2,768,768]{2,1,0:T(8,128)(2,1)}, u32[]{:S(2)}, u32[]{:S(2)}) %collective-permute-start.3) | collective-permute-done | bytes 2359328 | tf_op jit(solution)/shard_map/ppermute | solution.py:21
  529.8 24.2 %shard_map.41 = (bf16[2,4,768,768]{3,2,1,0:T(8,128)(2,1)}, bf16[2,768,768]{2,1,0:T(8,128)(2,1)}) custom-call(s32[2]{0:T(128)S(1)} %pad_add_fusion.where, bf16[4,2,768,768]{3,2,1,0:T(8,128)(2,1)} %bitcast.25, bf16[2,768,768]{2,1,0:T(8,128)(2,1)} %shard_map.39.refs_1_.refs_4_, bf16[2,768,768]{2,1,0:T(8,128)(2,1)} %collective-permute-done.refs_2_.refs_5_, ...), custom_call_target="tpu_custom_call" | custom-call | flops 1000 | bytes 1000 | tf_op jit(solution)/shard_map/pallas_call | solution.py:240
  555.6 15.6 %shard_map.42 = (bf16[2,4,768,768]{3,2,1,0:T(8,128)(2,1)}, bf16[2,768,512]{2,1,0:T(8,128)(2,1)}) custom-call(s32[2]{0:T(128)S(1)} %pad_add_fusion.where, bf16[2,768,768]{2,1,0:T(8,128)(2,1)S(1)} %copy-done.7, bf16[2,768,768]{2,1,0:T(8,128)(2,1)} %collective-permute-done.6.refs_1_, ...), custom_call_target="tpu_custom_call", output_to_operand_aliasing={{0}: (6, {})} | custom-call | flops 1000 | bytes 1000 | tf_op jit(solution)/shard_map/pallas_call | solution.py:240
  571.3 36.3 %collective-permute-done.10.refs_2_ = bf16[2,768,768]{2,1,0:T(8,128)(2,1)} collective-permute-done((bf16[2,768,768]{2,1,0:T(8,128)(2,1)}, bf16[2,768,768]{2,1,0:T(8,128)(2,1)}, u32[]{:S(2)}, u32[]{:S(2)}) %collective-permute-start.10) | collective-permute-done | bytes 2359328 | tf_op jit(solution)/shard_map/ppermute | solution.py:92
  611.0 8.2 %shard_map.43 = (bf16[2,4,768,768]{3,2,1,0:T(8,128)(2,1)}, bf16[2,768,256]{2,1,0:T(8,128)(2,1)S(1)}) custom-call(s32[2]{0:T(128)S(1)} %pad_add_fusion.where, bf16[2,768,768]{2,1,0:T(8,128)(2,1)S(1)} %copy-done.7, bf16[2,768,768]{2,1,0:T(8,128)(2,1)} %collective-permute-done.6.refs_1_, ...), custom_call_target="tpu_custom_call", output_to_operand_aliasing={{0}: (6, {})} | custom-call | flops 1000 | bytes 1000 | tf_op jit(solution)/shard_map/pallas_call | solution.py:240
  619.3 24.0 %shard_map.44.refs_7_ = bf16[2,4,768,768]{3,2,1,0:T(8,128)(2,1)} custom-call(s32[2]{0:T(128)S(1)} %pad_add_fusion.where, bf16[2,768,768]{2,1,0:T(8,128)(2,1)} %get-tuple-element.42.refs_0_, bf16[2,768,768]{2,1,0:T(8,128)(2,1)} %collective-permute-done.9.refs_1_, ...), custom_call_target="tpu_custom_call", output_to_operand_aliasing={{}: (12, {})} | custom-call | flops 1000 | bytes 1000 | tf_op jit(solution)/shard_map/pallas_call | solution.py:240
  646.9 2.2 collective-permute-done.14.refs_3_
  649.2 17.4 %shard_map.45.refs_6_ = f32[2,768,768]{2,1,0:T(8,128)} custom-call(s32[2]{0:T(128)S(1)} %pad_add_fusion.where, bf16[2,768,512]{2,1,0:T(8,128)(2,1)} %get-tuple-element.45.refs_0_, bf16[2,768,512]{2,1,0:T(8,128)(2,1)S(1)} %collective-permute-done.12.refs_1_, bf16[2,768,512]{2,1,0:T(8,128)(2,1)} %collective-permute-done.13.refs_2_, ...), custom_call_target="tpu_custom_call" | custom-call | flops 1000 | bytes 1000 | tf_op jit(solution)/shard_map/pallas_call | solution.py:240
  670.1 13.8 %shard_map.46 = bf16[2,4,768,768]{3,2,1,0:T(8,128)(2,1)} custom-call(s32[2]{0:T(128)S(1)} %pad_add_fusion.where, bf16[2,768,256]{2,1,0:T(8,128)(2,1)S(1)} %get-tuple-element.47.refs_0_, bf16[2,768,256]{2,1,0:T(8,128)(2,1)S(1)} %collective-permute-done.15.refs_1_, ...), custom_call_target="tpu_custom_call", output_to_operand_aliasing={{}: (8, {})} | custom-call | flops 1000 | bytes 1000 | tf_op jit(solution)/shard_map/pallas_call | solution.py:240
  (71 shorter events, 33.4 us)
Async XLA Ops:
  9.0 27.4 %all-to-all-start = ((s32[16,1,96]{2,1,0:T(1,128)}), s32[16,1,96]{2,1,0:T(1,128)S(1)}, u32[]{:S(2)}, u32[]{:S(2)}) async-start(s32[16,1,96]{2,1,0:T(1,128)} %bitcast.3), calls=%async_computation | async-start | bytes 16384 | tf_op jit(solution)/shard_map/all_to_all | solution.py:285
  36.4 92.9 %all-to-all-start.2 = ((bf16[16,96,1536]{2,1,0:T(8,128)(2,1)}), bf16[16,96,1536]{2,1,0:T(8,128)(2,1)}, u32[]{:S(2)}, u32[]{:S(2)}) async-start(bf16[16,96,1536]{2,1,0:T(8,128)(2,1)} %bitcast.21), calls=%async_computation.2 | async-start | bytes 9437184 | tf_op jit(solution)/shard_map/all_to_all | solution.py:295
  42.4 245.0 %all-gather.7.cloned.1.call-start = ((), (), s32[]{:S(2)}) async-start(), calls=%async_computation.3 | async-start | bytes 11796480 | tf_op jit(solution)/shard_map/all_gather | solution.py:307
  136.0 108.9 %all-to-all-start.1 = ((bf16[16,96,1536]{2,1,0:T(8,128)(2,1)}), bf16[16,96,1536]{2,1,0:T(8,128)(2,1)}, u32[]{:S(2)}, u32[]{:S(2)}) async-start(bf16[16,96,1536]{2,1,0:T(8,128)(2,1)} %bitcast.20), calls=%async_computation.1 | async-start | bytes 9437184 | tf_op jit(solution)/shard_map/all_to_all | solution.py:295
  157.8 397.8 %all-gather.11.cloned.1.call-start = ((), (), s32[]{:S(2)}) async-start(), calls=%async_computation.5 | async-start | bytes 7864320 | tf_op jit(solution)/shard_map/all_gather | solution.py:311
  157.8 129.6 %collective-permute-start = (bf16[2,768,768]{2,1,0:T(8,128)(2,1)}, bf16[2,768,768]{2,1,0:T(8,128)(2,1)}, u32[]{:S(2)}, u32[]{:S(2)}) collective-permute-start(bf16[2,768,768]{2,1,0:T(8,128)(2,1)} %shard_map.39.refs_1_.refs_4_), channel_id=1, source_target_pairs={{4,0},{8,4},{12,8},{5,1},{9,5},{13,9},{6,2},{10,6},{14,10},{7,3},{... | collective-permute-start | bytes 7077896 | tf_op jit(solution)/shard_map/ppermute | solution.py:21
  159.1 128.3 %collective-permute-start.1 = (bf16[2,768,768]{2,1,0:T(8,128)(2,1)}, bf16[2,768,768]{2,1,0:T(8,128)(2,1)}, u32[]{:S(2)}, u32[]{:S(2)}) collective-permute-start(bf16[2,768,768]{2,1,0:T(8,128)(2,1)} %shard_map.39.refs_1_.refs_4_), channel_id=1, source_target_pairs={{0,4},{4,8},{8,12},{1,5},{5,9},{9,13},{2,6},{6,10},{10,14},{3,7},{... | collective-permute-start | bytes 7077896 | tf_op jit(solution)/shard_map/ppermute | solution.py:21
  296.5 312.6 %all-gather.9.cloned.1.call-start = ((), (), s32[]{:S(2)}) async-start(), calls=%async_computation.4 | async-start | bytes 3932160 | tf_op jit(solution)/shard_map/all_gather | solution.py:311
  296.6 160.9 %collective-permute-start.2 = (bf16[2,768,768]{2,1,0:T(8,128)(2,1)}, bf16[2,768,768]{2,1,0:T(8,128)(2,1)S(1)}, u32[]{:S(2)}, u32[]{:S(2)}) collective-permute-start(bf16[2,768,768]{2,1,0:T(8,128)(2,1)} %collective-permute-done.refs_2_.refs_5_), channel_id=1, source_target_pairs={{4,0},{8,4},{5,1},{9,5},{6,2},{10,6},{7,3},{11,7},{20,16},{24,20},... | collective-permute-start | bytes 7077896 | tf_op jit(solution)/shard_map/ppermute | solution.py:21
  297.9 160.9 %collective-permute-start.4 = (bf16[2,768,768]{2,1,0:T(8,128)(2,1)}, bf16[2,768,768]{2,1,0:T(8,128)(2,1)}, u32[]{:S(2)}, u32[]{:S(2)}) collective-permute-start(bf16[2,768,768]{2,1,0:T(8,128)(2,1)} %collective-permute-done.1.refs_3_.refs_6_), channel_id=1, source_target_pairs={{4,8},{8,12},{5,9},{9,13},{6,10},{10,14},{7,11},{11,15},{20,24},{2... | collective-permute-start | bytes 7077896 | tf_op jit(solution)/shard_map/ppermute | solution.py:21
  457.5 71.7 %collective-permute-start.3 = (bf16[2,768,768]{2,1,0:T(8,128)(2,1)S(1)}, bf16[2,768,768]{2,1,0:T(8,128)(2,1)}, u32[]{:S(2)}, u32[]{:S(2)}) collective-permute-start(bf16[2,768,768]{2,1,0:T(8,128)(2,1)S(1)} %collective-permute-done.2.refs_4_.refs_7_), channel_id=1, source_target_pairs={{4,0},{5,1},{6,2},{7,3},{20,16},{21,17},{22,18},{23,19}} | collective-permute-start | bytes 7077896 | tf_op jit(solution)/shard_map/ppermute | solution.py:21
  458.8 70.4 %collective-permute-start.5 = (bf16[2,768,768]{2,1,0:T(8,128)(2,1)}, bf16[2,768,768]{2,1,0:T(8,128)(2,1)}, u32[]{:S(2)}, u32[]{:S(2)}) collective-permute-start(bf16[2,768,768]{2,1,0:T(8,128)(2,1)} %collective-permute-done.4.refs_5_.refs_8_), channel_id=1, source_target_pairs={{8,12},{9,13},{10,14},{11,15},{24,28},{25,29},{26,30},{27,31}} | collective-permute-start | bytes 7077896 | tf_op jit(solution)/shard_map/ppermute | solution.py:21
  460.8 68.4 %collective-permute-start.7 = (bf16[2,768,768]{2,1,0:T(8,128)(2,1)}, bf16[2,768,768]{2,1,0:T(8,128)(2,1)}, u32[]{:S(2)}, u32[]{:S(2)}) collective-permute-start(bf16[2,768,768]{2,1,0:T(8,128)(2,1)} %copy-done.6), channel_id=1, source_target_pairs={{0,2},{1,3},{2,0},{3,1},{4,6},{5,7},{6,4},{7,5},{8,10},{9,11},{10,... | collective-permute-start | bytes 7077896 | tf_op jit(solution)/shard_map/ppermute | solution.py:92
  529.2 26.4 %collective-permute-start.6 = (bf16[2,768,768]{2,1,0:T(8,128)(2,1)}, bf16[2,768,768]{2,1,0:T(8,128)(2,1)}, u32[]{:S(2)}, u32[]{:S(2)}) collective-permute-start(bf16[2,768,768]{2,1,0:T(8,128)(2,1)} %copy-done.6), channel_id=1, source_target_pairs={{0,1},{1,0},{2,3},{3,2},{4,5},{5,4},{6,7},{7,6},{8,9},{9,8},{10,11... | collective-permute-start | bytes 7077896 | tf_op jit(solution)/shard_map/ppermute | solution.py:92
  529.2 26.4 %collective-permute-start.8 = (bf16[2,768,768]{2,1,0:T(8,128)(2,1)}, bf16[2,768,768]{2,1,0:T(8,128)(2,1)}, u32[]{:S(2)}, u32[]{:S(2)}) collective-permute-start(bf16[2,768,768]{2,1,0:T(8,128)(2,1)} %collective-permute-done.7.refs_2_), channel_id=1, source_target_pairs={{0,1},{1,0},{2,3},{3,2},{4,5},{5,4},{6,7},{7,6},{8,9},{9,8},{10,11... | collective-permute-start | bytes 7077896 | tf_op jit(solution)/shard_map/ppermute | solution.py:92
  554.0 53.6 %collective-permute-start.10 = (bf16[2,768,768]{2,1,0:T(8,128)(2,1)}, bf16[2,768,768]{2,1,0:T(8,128)(2,1)}, u32[]{:S(2)}, u32[]{:S(2)}) collective-permute-start(bf16[2,768,768]{2,1,0:T(8,128)(2,1)} %get-tuple-element.42.refs_0_), channel_id=1, source_target_pairs={{0,2},{1,3},{2,0},{3,1},{4,6},{5,7},{6,4},{7,5},{8,10},{9,11},{10,... | collective-permute-start | bytes 7077896 | tf_op jit(solution)/shard_map/ppermute | solution.py:92
  571.3 48.0 %collective-permute-start.9 = (bf16[2,768,768]{2,1,0:T(8,128)(2,1)}, bf16[2,768,768]{2,1,0:T(8,128)(2,1)}, u32[]{:S(2)}, u32[]{:S(2)}) collective-permute-start(bf16[2,768,768]{2,1,0:T(8,128)(2,1)} %get-tuple-element.42.refs_0_), channel_id=1, source_target_pairs={{0,1},{1,0},{2,3},{3,2},{4,5},{5,4},{6,7},{7,6},{8,9},{9,8},{10,11... | collective-permute-start | bytes 7077896 | tf_op jit(solution)/shard_map/ppermute | solution.py:92
  607.6 11.6 %collective-permute-start.11 = (bf16[2,768,768]{2,1,0:T(8,128)(2,1)}, bf16[2,768,768]{2,1,0:T(8,128)(2,1)}, u32[]{:S(2)}, u32[]{:S(2)}) collective-permute-start(bf16[2,768,768]{2,1,0:T(8,128)(2,1)} %collective-permute-done.10.refs_2_), channel_id=1, source_target_pairs={{0,1},{1,0},{2,3},{3,2},{4,5},{5,4},{6,7},{7,6},{8,9},{9,8},{10,11... | collective-permute-start | bytes 7077896 | tf_op jit(solution)/shard_map/ppermute | solution.py:92
  607.6 37.1 %collective-permute-start.13 = (bf16[2,768,512]{2,1,0:T(8,128)(2,1)}, bf16[2,768,512]{2,1,0:T(8,128)(2,1)}, u32[]{:S(2)}, u32[]{:S(2)}) collective-permute-start(bf16[2,768,512]{2,1,0:T(8,128)(2,1)} %get-tuple-element.45.refs_0_), channel_id=1, source_target_pairs={{0,2},{1,3},{2,0},{3,1},{4,6},{5,7},{6,4},{7,5},{8,10},{9,11},{10,... | collective-permute-start | bytes 4718600 | tf_op jit(solution)/shard_map/ppermute | solution.py:92
  643.2 3.7 collective-permute-start.12
  644.7 4.4 collective-permute-start.14
  644.8 22.2 %collective-permute-start.16 = (bf16[2,768,256]{2,1,0:T(8,128)(2,1)S(1)}, bf16[2,768,256]{2,1,0:T(8,128)(2,1)S(1)}, u32[]{:S(2)}, u32[]{:S(2)}) collective-permute-start(bf16[2,768,256]{2,1,0:T(8,128)(2,1)S(1)} %get-tuple-element.47.refs_0_), channel_id=1, source_target_pairs={{0,2},{1,3},{2,0},{3,1},{4,6},{5,7},{6,4},{7,5},{8,10},{9,11},{10,... | collective-permute-start | bytes 2359304 | tf_op jit(solution)/shard_map/ppermute | solution.py:92
  666.6 2.4 collective-permute-start.15
  666.9 3.2 collective-permute-start.17
  (10 other events, 144.2 us)
Sparse Core Ops, SparseCore 0:
  136.1 127.6 all-gather.6
  296.6 182.6 all-gather.10
  530.0 65.6 all-gather.8

commit v12 on v11

--- a/solution.py
+++ b/solution.py
@@ -313,15 +313,13 @@
 
     sub = tile_cols // THIRDS
     views1 = [([(0, None)], j * sub) for j in everything[:-1]] + [([(1, None)], 0)]
-    second = None
     if line:
         right0, ups = [tiles[0], *pair], [0, 1, -1]
         for k in range(2, n_row):
             pair = hop(pair, k, n_row)
-            second = pair if k == 2 else second
             right0 += list(pair)
             ups += [k, -k]
-        cut[1] = after(cut[1], second)
+        cut = [after(part, pair) for part in cut]
     else:
         right0, ups = [gather_rows(tiles[0])], [None]
     right1 = [gather_rows(part) for part in cut]
@@ -332,11 +330,11 @@
     product = functools.partial(complex_product, where)
     shape = (2, planes, block_rows, tile_cols)
     result, piece = product([lefts[0]], right0, views0, shape, (), (0, 0, 0))
+    found = gather_cols(piece, n_col)
+    (result,) = product([(found, everything)], right0, views0, shape, (result,), (1, 0, 0))
     result, most = product([lefts[1]], right1[:1], views1[:-1], shape, (result,), (0, 1, 0))
-    found = gather_cols(piece, n_col, most)
+    most = gather_cols(most, n_col)
     result, rest = product([lefts[1]], right1[1:], [([(0, None)], 0)], shape, (result,), (0, 1, THIRDS - 1))
-    (result,) = product([(found, everything)], right0, views0, shape, (result,), (1, 0, 0))
-    most = gather_cols(most, n_col, result)
     (sums,) = product([(most, everything[:-1])], right1, views1, shape, (), None)
     rest = gather_cols(rest, n_col, sums)
     return product([(rest, everything[-1:])], right1, views1, shape, (result,), (1, 1, 0), before=sums)[0]

time: 691 us -> 666 us (0.964)
  waiting for transfers between devices: 465 us -> 441 us
    ppermute x3, waiting for transfers between devices: 267 us -> 163 us  [hop(): lax.ppermute(pair[0], 'row', down)]
    ppermute x12, waiting for transfers between devices: 43.3 us -> 123 us  [gather_cols(): arrived = {d ^ bit: lax.ppermute(a, 'col', pairs) for d, a in held.items()}]
    unnamed x21 -> x27, local copies, waits for them, and re-layouts: 26.6 us -> 29.4 us
  transfers between devices with their start and end apart: 24 -> 24, of which waited for: 11 -> 12; matrix products, arithmetic and copies ran while one was open for 2% -> 2% of each run, Pallas kernels for 14% -> 15%
where the time goes in v12:
time: 666 us; the launch traced here: 665 us
  waiting for transfers between devices  441 us (66%)
  Pallas kernels  124 us (19%)
  starting transfers between devices  53.5 us (8%)
  local copies, waits for them, and re-layouts  30.7 us (5%)
  between operations  14 us (2%)
    ppermute x3, waiting for transfers between devices, hop(): lax.ppermute(pair[0], 'row', down)  163 us
    all_to_all x2, waiting for transfers between devices, per_device(): lax.all_to_all(sent[f].reshape(n_row * n_col, cap, 2 * tile_cols), ('row'...  155 us
    ppermute x12, waiting for transfers between devices, gather_cols(): arrived = {d ^ bit: lax.ppermute(a, 'col', pairs) for d, a in held.items()}  123 us
    pallas_call x6, Pallas kernels, complex_product(): pl.pallas_call(functools.partial(product_kernel, opts), grid_spec=pltpu.P...  103 us
    unnamed x27, local copies, waits for them, and re-layouts  29.4 us
    all_to_all x2, starting transfers between devices, per_device(): lax.all_to_all(sent[f].reshape(n_row * n_col, cap, 2 * tile_cols), ('row'...  27.9 us
  transfers between devices with their start and end apart: 24, of which 12 were waited for; matrix products, arithmetic and copies ran while one was open for 2% of the time, Pallas kernels for 15%

profile of v12, /device:TPU:0, one launch (start us, length us, event | category | flops | bytes accessed | tf_op | source)
XLA Modules:
  0.0 665.4 jit_solution(18158255317818227968)
XLA Ops:
  9.0 7.4 %all-to-all-start = ((s32[16,1,96]{2,1,0:T(1,128)}), s32[16,1,96]{2,1,0:T(1,128)S(1)}, u32[]{:S(2)}, u32[]{:S(2)}) async-start(s32[16,1,96]{2,1,0:T(1,128)} %bitcast.3), calls=%async_computation | async-start | bytes 16384 | tf_op jit(solution)/shard_map/all_to_all | solution.py:285
  16.4 10.4 %copy.12 = bf16[384,4,3072]{2,0,1:T(8,128)(2,1)} copy(bf16[384,4,3072]{2,1,0:T(4,128)(2,1)} %param.3) | data formatting | bytes 18874368 | tf_op args[0]
  30.5 3.7 shard_map.38
  36.4 6.1 all-to-all-start.2
  46.2 3.7 shard_map.37
  54.2 75.1 %all-to-all-done.2 = bf16[16,96,1536]{2,1,0:T(8,128)(2,1)} async-done(((bf16[16,96,1536]{2,1,0:T(8,128)(2,1)}), bf16[16,96,1536]{2,1,0:T(8,128)(2,1)}, u32[]{:S(2)}, u32[]{:S(2)}) %all-to-all-start.2) | async-done | bytes 4718624 | tf_op jit(solution)/shard_map/all_to_all | solution.py:295
  129.3 6.7 %shard_map.39.refs_1_.refs_4_ = bf16[2,768,768]{2,1,0:T(8,128)(2,1)} custom-call(bf16[768,1536]{1,0:T(8,128)(2,1)S(1)} %fusion.placer, bf16[1536,1536]{1,0:T(8,128)(2,1)} %bitcast.8.got), custom_call_target="tpu_custom_call" | custom-call | flops 1000 | bytes 1000 | tf_op jit(solution)/shard_map/pallas_call | solution.py:67
  136.0 21.8 %all-to-all-start.1 = ((bf16[16,96,1536]{2,1,0:T(8,128)(2,1)}), bf16[16,96,1536]{2,1,0:T(8,128)(2,1)}, u32[]{:S(2)}, u32[]{:S(2)}) async-start(bf16[16,96,1536]{2,1,0:T(8,128)(2,1)} %bitcast.20), calls=%async_computation.1 | async-start | bytes 9437184 | tf_op jit(solution)/shard_map/all_to_all | solution.py:295
  159.1 6.1 collective-permute-start.1
  165.3 79.6 %all-to-all-done.1 = bf16[16,96,1536]{2,1,0:T(8,128)(2,1)} async-done(((bf16[16,96,1536]{2,1,0:T(8,128)(2,1)}), bf16[16,96,1536]{2,1,0:T(8,128)(2,1)}, u32[]{:S(2)}, u32[]{:S(2)}) %all-to-all-start.1) | async-done | bytes 4718624 | tf_op jit(solution)/shard_map/all_to_all | solution.py:295
  244.9 42.6 %collective-permute-done.refs_2_.refs_5_ = bf16[2,768,768]{2,1,0:T(8,128)(2,1)} collective-permute-done((bf16[2,768,768]{2,1,0:T(8,128)(2,1)}, bf16[2,768,768]{2,1,0:T(8,128)(2,1)}, u32[]{:S(2)}, u32[]{:S(2)}) %collective-permute-start) | collective-permute-done | bytes 2359328 | tf_op jit(solution)/shard_map/ppermute | solution.py:21
  289.6 78.0 %collective-permute-done.2.refs_4_.refs_7_ = bf16[2,768,768]{2,1,0:T(8,128)(2,1)S(1)} collective-permute-done((bf16[2,768,768]{2,1,0:T(8,128)(2,1)}, bf16[2,768,768]{2,1,0:T(8,128)(2,1)S(1)}, u32[]{:S(2)}, u32[]{:S(2)}) %collective-permute-start.2) | collective-permute-done | bytes 2359328 | tf_op jit(solution)/shard_map/ppermute | solution.py:21
  369.7 6.4 shard_map.40
  378.8 42.9 %collective-permute-done.3.refs_6_.refs_9_ = bf16[2,768,768]{2,1,0:T(8,128)(2,1)S(1)} collective-permute-done((bf16[2,768,768]{2,1,0:T(8,128)(2,1)S(1)}, bf16[2,768,768]{2,1,0:T(8,128)(2,1)S(1)}, u32[]{:S(2)}, u32[]{:S(2)}) %collective-permute-start.3) | collective-permute-done | bytes 2359328 | tf_op jit(solution)/shard_map/ppermute | solution.py:21
  426.4 24.2 %shard_map.41 = (bf16[2,4,768,768]{3,2,1,0:T(8,128)(2,1)}, bf16[2,768,768]{2,1,0:T(8,128)(2,1)}) custom-call(s32[2]{0:T(128)S(1)} %pad_add_fusion.where, bf16[4,2,768,768]{3,2,1,0:T(8,128)(2,1)} %bitcast.25, bf16[2,768,768]{2,1,0:T(8,128)(2,1)} %shard_map.39.refs_1_.refs_4_, bf16[2,768,768]{2,1,0:T(8,128)(2,1)} %collective-permute-done.refs_2_.refs_5_, ...), custom_call_target="tpu_custom_call" | custom-call | flops 1000 | bytes 1000 | tf_op jit(solution)/shard_map/pallas_call | solution.py:240
  451.1 28.2 %collective-permute-done.7.refs_2_ = bf16[2,768,768]{2,1,0:T(8,128)(2,1)} collective-permute-done((bf16[2,768,768]{2,1,0:T(8,128)(2,1)}, bf16[2,768,768]{2,1,0:T(8,128)(2,1)}, u32[]{:S(2)}, u32[]{:S(2)}) %collective-permute-start.7) | collective-permute-done | bytes 2359328 | tf_op jit(solution)/shard_map/ppermute | solution.py:92
  479.3 47.7 %collective-permute-done.10.refs_2_ = bf16[2,768,768]{2,1,0:T(8,128)(2,1)} collective-permute-done((bf16[2,768,768]{2,1,0:T(8,128)(2,1)}, bf16[2,768,768]{2,1,0:T(8,128)(2,1)}, u32[]{:S(2)}, u32[]{:S(2)}) %collective-permute-start.10) | collective-permute-done | bytes 2359328 | tf_op jit(solution)/shard_map/ppermute | solution.py:92
  527.5 7.6 %collective-permute-done.11.refs_3_ = bf16[2,768,768]{2,1,0:T(8,128)(2,1)} collective-permute-done((bf16[2,768,768]{2,1,0:T(8,128)(2,1)}, bf16[2,768,768]{2,1,0:T(8,128)(2,1)}, u32[]{:S(2)}, u32[]{:S(2)}) %collective-permute-start.11) | collective-permute-done | bytes 2359328 | tf_op jit(solution)/shard_map/ppermute | solution.py:92
  535.1 23.7 %shard_map.42.refs_5_ = bf16[2,4,768,768]{3,2,1,0:T(8,128)(2,1)} custom-call(s32[2]{0:T(128)S(1)} %pad_add_fusion.where, bf16[2,768,768]{2,1,0:T(8,128)(2,1)} %get-tuple-element.35.refs_0_, bf16[2,768,768]{2,1,0:T(8,128)(2,1)} %collective-permute-done.9.refs_1_, ...), custom_call_target="tpu_custom_call", output_to_operand_aliasing={{}: (12, {})} | custom-call | flops 1000 | bytes 1000 | tf_op jit(solution)/shard_map/pallas_call | solution.py:240
  558.9 15.6 %shard_map.43 = (bf16[2,4,768,768]{3,2,1,0:T(8,128)(2,1)}, bf16[2,768,512]{2,1,0:T(8,128)(2,1)}) custom-call(s32[2]{0:T(128)S(1)} %pad_add_fusion.where, bf16[2,768,768]{2,1,0:T(8,128)(2,1)S(1)} %copy-done.7, bf16[2,768,768]{2,1,0:T(8,128)(2,1)} %collective-permute-done.6.refs_1_, ...), custom_call_target="tpu_custom_call", output_to_operand_aliasing={{0}: (6, {})} | custom-call | flops 1000 | bytes 1000 | tf_op jit(solution)/shard_map/pallas_call | solution.py:240
  576.1 35.2 %collective-permute-done.13.refs_2_ = bf16[2,768,512]{2,1,0:T(8,128)(2,1)} collective-permute-done((bf16[2,768,512]{2,1,0:T(8,128)(2,1)}, bf16[2,768,512]{2,1,0:T(8,128)(2,1)}, u32[]{:S(2)}, u32[]{:S(2)}) %collective-permute-start.13) | collective-permute-done | bytes 1572896 | tf_op jit(solution)/shard_map/ppermute | solution.py:92
  613.2 8.3 %shard_map.44 = (bf16[2,4,768,768]{3,2,1,0:T(8,128)(2,1)}, bf16[2,768,256]{2,1,0:T(8,128)(2,1)S(1)}) custom-call(s32[2]{0:T(128)S(1)} %pad_add_fusion.where, bf16[2,768,768]{2,1,0:T(8,128)(2,1)S(1)} %copy-done.7, bf16[2,768,768]{2,1,0:T(8,128)(2,1)} %collective-permute-done.6.refs_1_, ...), custom_call_target="tpu_custom_call", output_to_operand_aliasing={{0}: (6, {})} | custom-call | flops 1000 | bytes 1000 | tf_op jit(solution)/shard_map/pallas_call | solution.py:240
  623.2 17.4 %shard_map.45.refs_6_ = f32[2,768,768]{2,1,0:T(8,128)} custom-call(s32[2]{0:T(128)S(1)} %pad_add_fusion.where, bf16[2,768,512]{2,1,0:T(8,128)(2,1)} %get-tuple-element.39.refs_0_, bf16[2,768,512]{2,1,0:T(8,128)(2,1)} %collective-permute-done.12.refs_1_, bf16[2,768,512]{2,1,0:T(8,128)(2,1)} %collective-permute-done.13.refs_2_, ...), custom_call_target="tpu_custom_call" | custom-call | flops 1000 | bytes 1000 | tf_op jit(solution)/shard_map/pallas_call | solution.py:240
  645.0 13.8 %shard_map.46 = bf16[2,4,768,768]{3,2,1,0:T(8,128)(2,1)} custom-call(s32[2]{0:T(128)S(1)} %pad_add_fusion.where, bf16[2,768,256]{2,1,0:T(8,128)(2,1)S(1)} %get-tuple-element.40.refs_0_, bf16[2,768,256]{2,1,0:T(8,128)(2,1)S(1)} %collective-permute-done.15.refs_1_, ...), custom_call_target="tpu_custom_call", output_to_operand_aliasing={{}: (8, {})} | custom-call | flops 1000 | bytes 1000 | tf_op jit(solution)/shard_map/pallas_call | solution.py:240
  (77 shorter events, 39.2 us)
Async XLA Ops:
  9.0 27.4 %all-to-all-start = ((s32[16,1,96]{2,1,0:T(1,128)}), s32[16,1,96]{2,1,0:T(1,128)S(1)}, u32[]{:S(2)}, u32[]{:S(2)}) async-start(s32[16,1,96]{2,1,0:T(1,128)} %bitcast.3), calls=%async_computation | async-start | bytes 16384 | tf_op jit(solution)/shard_map/all_to_all | solution.py:285
  36.4 92.9 %all-to-all-start.2 = ((bf16[16,96,1536]{2,1,0:T(8,128)(2,1)}), bf16[16,96,1536]{2,1,0:T(8,128)(2,1)}, u32[]{:S(2)}, u32[]{:S(2)}) async-start(bf16[16,96,1536]{2,1,0:T(8,128)(2,1)} %bitcast.21), calls=%async_computation.2 | async-start | bytes 9437184 | tf_op jit(solution)/shard_map/all_to_all | solution.py:295
  42.5 245.0 %all-gather.7.cloned.1.call-start = ((), (), s32[]{:S(2)}) async-start(), calls=%async_computation.3 | async-start | bytes 11796480 | tf_op jit(solution)/shard_map/all_gather | solution.py:307
  136.0 108.9 %all-to-all-start.1 = ((bf16[16,96,1536]{2,1,0:T(8,128)(2,1)}), bf16[16,96,1536]{2,1,0:T(8,128)(2,1)}, u32[]{:S(2)}, u32[]{:S(2)}) async-start(bf16[16,96,1536]{2,1,0:T(8,128)(2,1)} %bitcast.20), calls=%async_computation.1 | async-start | bytes 9437184 | tf_op jit(solution)/shard_map/all_to_all | solution.py:295
  157.8 401.1 %all-gather.11.cloned.1.call-start = ((), (), s32[]{:S(2)}) async-start(), calls=%async_computation.5 | async-start | bytes 7864320 | tf_op jit(solution)/shard_map/all_gather | solution.py:311
  157.8 129.6 %collective-permute-start = (bf16[2,768,768]{2,1,0:T(8,128)(2,1)}, bf16[2,768,768]{2,1,0:T(8,128)(2,1)}, u32[]{:S(2)}, u32[]{:S(2)}) collective-permute-start(bf16[2,768,768]{2,1,0:T(8,128)(2,1)} %shard_map.39.refs_1_.refs_4_), channel_id=1, source_target_pairs={{4,0},{8,4},{12,8},{5,1},{9,5},{13,9},{6,2},{10,6},{14,10},{7,3},{... | collective-permute-start | bytes 7077896 | tf_op jit(solution)/shard_map/ppermute | solution.py:21
  159.1 128.3 %collective-permute-start.1 = (bf16[2,768,768]{2,1,0:T(8,128)(2,1)}, bf16[2,768,768]{2,1,0:T(8,128)(2,1)}, u32[]{:S(2)}, u32[]{:S(2)}) collective-permute-start(bf16[2,768,768]{2,1,0:T(8,128)(2,1)} %shard_map.39.refs_1_.refs_4_), channel_id=1, source_target_pairs={{0,4},{4,8},{8,12},{1,5},{5,9},{9,13},{2,6},{6,10},{10,14},{3,7},{... | collective-permute-start | bytes 7077896 | tf_op jit(solution)/shard_map/ppermute | solution.py:21
  287.5 80.1 %collective-permute-start.2 = (bf16[2,768,768]{2,1,0:T(8,128)(2,1)}, bf16[2,768,768]{2,1,0:T(8,128)(2,1)S(1)}, u32[]{:S(2)}, u32[]{:S(2)}) collective-permute-start(bf16[2,768,768]{2,1,0:T(8,128)(2,1)} %collective-permute-done.refs_2_.refs_5_), channel_id=1, source_target_pairs={{4,0},{8,4},{5,1},{9,5},{6,2},{10,6},{7,3},{11,7},{20,16},{24,20},... | collective-permute-start | bytes 7077896 | tf_op jit(solution)/shard_map/ppermute | solution.py:21
  288.7 80.1 %collective-permute-start.4 = (bf16[2,768,768]{2,1,0:T(8,128)(2,1)}, bf16[2,768,768]{2,1,0:T(8,128)(2,1)S(1)}, u32[]{:S(2)}, u32[]{:S(2)}) collective-permute-start(bf16[2,768,768]{2,1,0:T(8,128)(2,1)} %collective-permute-done.1.refs_3_.refs_6_), channel_id=1, source_target_pairs={{4,8},{8,12},{5,9},{9,13},{6,10},{10,14},{7,11},{11,15},{20,24},{2... | collective-permute-start | bytes 7077896 | tf_op jit(solution)/shard_map/ppermute | solution.py:21
  367.6 54.1 %collective-permute-start.3 = (bf16[2,768,768]{2,1,0:T(8,128)(2,1)S(1)}, bf16[2,768,768]{2,1,0:T(8,128)(2,1)S(1)}, u32[]{:S(2)}, u32[]{:S(2)}) collective-permute-start(bf16[2,768,768]{2,1,0:T(8,128)(2,1)S(1)} %collective-permute-done.2.refs_4_.refs_7_), channel_id=1, source_target_pairs={{4,0},{5,1},{6,2},{7,3},{20,16},{21,17},{22,18},{23,19}} | collective-permute-start | bytes 7077896 | tf_op jit(solution)/shard_map/ppermute | solution.py:21
  368.9 52.8 %collective-permute-start.5 = (bf16[2,768,768]{2,1,0:T(8,128)(2,1)S(1)}, bf16[2,768,768]{2,1,0:T(8,128)(2,1)S(1)}, u32[]{:S(2)}, u32[]{:S(2)}) collective-permute-start(bf16[2,768,768]{2,1,0:T(8,128)(2,1)S(1)} %collective-permute-done.4.refs_5_.refs_8_), channel_id=1, source_target_pairs={{8,12},{9,13},{10,14},{11,15},{24,28},{25,29},{26,30},{27,31}} | collective-permute-start | bytes 7077896 | tf_op jit(solution)/shard_map/ppermute | solution.py:21
  424.5 186.9 %all-gather.9.cloned.1.call-start = ((), (), s32[]{:S(2)}) async-start(), calls=%async_computation.4 | async-start | bytes 3932160 | tf_op jit(solution)/shard_map/all_gather | solution.py:311
  424.7 54.6 %collective-permute-start.7 = (bf16[2,768,768]{2,1,0:T(8,128)(2,1)}, bf16[2,768,768]{2,1,0:T(8,128)(2,1)}, u32[]{:S(2)}, u32[]{:S(2)}) collective-permute-start(bf16[2,768,768]{2,1,0:T(8,128)(2,1)} %copy-done.6), channel_id=1, source_target_pairs={{0,2},{1,3},{2,0},{3,1},{4,6},{5,7},{6,4},{7,5},{8,10},{9,11},{10,... | collective-permute-start | bytes 7077896 | tf_op jit(solution)/shard_map/ppermute | solution.py:92
  450.5 76.4 %collective-permute-start.10 = (bf16[2,768,768]{2,1,0:T(8,128)(2,1)}, bf16[2,768,768]{2,1,0:T(8,128)(2,1)}, u32[]{:S(2)}, u32[]{:S(2)}) collective-permute-start(bf16[2,768,768]{2,1,0:T(8,128)(2,1)} %get-tuple-element.35.refs_0_), channel_id=1, source_target_pairs={{0,2},{1,3},{2,0},{3,1},{4,6},{5,7},{6,4},{7,5},{8,10},{9,11},{10,... | collective-permute-start | bytes 7077896 | tf_op jit(solution)/shard_map/ppermute | solution.py:92
  451.1 76.4 %collective-permute-start.9 = (bf16[2,768,768]{2,1,0:T(8,128)(2,1)}, bf16[2,768,768]{2,1,0:T(8,128)(2,1)}, u32[]{:S(2)}, u32[]{:S(2)}) collective-permute-start(bf16[2,768,768]{2,1,0:T(8,128)(2,1)} %get-tuple-element.35.refs_0_), channel_id=1, source_target_pairs={{0,1},{1,0},{2,3},{3,2},{4,5},{5,4},{6,7},{7,6},{8,9},{9,8},{10,11... | collective-permute-start | bytes 7077896 | tf_op jit(solution)/shard_map/ppermute | solution.py:92
  479.3 79.6 %collective-permute-start.8 = (bf16[2,768,768]{2,1,0:T(8,128)(2,1)}, bf16[2,768,768]{2,1,0:T(8,128)(2,1)}, u32[]{:S(2)}, u32[]{:S(2)}) collective-permute-start(bf16[2,768,768]{2,1,0:T(8,128)(2,1)} %collective-permute-done.7.refs_2_), channel_id=1, source_target_pairs={{0,1},{1,0},{2,3},{3,2},{4,5},{5,4},{6,7},{7,6},{8,9},{9,8},{10,11... | collective-permute-start | bytes 7077896 | tf_op jit(solution)/shard_map/ppermute | solution.py:92
  526.9 8.2 %collective-permute-start.11 = (bf16[2,768,768]{2,1,0:T(8,128)(2,1)}, bf16[2,768,768]{2,1,0:T(8,128)(2,1)}, u32[]{:S(2)}, u32[]{:S(2)}) collective-permute-start(bf16[2,768,768]{2,1,0:T(8,128)(2,1)} %collective-permute-done.10.refs_2_), channel_id=1, source_target_pairs={{0,1},{1,0},{2,3},{3,2},{4,5},{5,4},{6,7},{7,6},{8,9},{9,8},{10,11... | collective-permute-start | bytes 7077896 | tf_op jit(solution)/shard_map/ppermute | solution.py:92
  526.9 31.9 %collective-permute-start.6 = (bf16[2,768,768]{2,1,0:T(8,128)(2,1)S(1)}, bf16[2,768,768]{2,1,0:T(8,128)(2,1)}, u32[]{:S(2)}, u32[]{:S(2)}) collective-permute-start(bf16[2,768,768]{2,1,0:T(8,128)(2,1)S(1)} %copy-done.7), channel_id=1, source_target_pairs={{0,1},{1,0},{2,3},{3,2},{4,5},{5,4},{6,7},{7,6},{8,9},{9,8},{10,11... | collective-permute-start | bytes 7077896 | tf_op jit(solution)/shard_map/ppermute | solution.py:92
  574.5 36.8 %collective-permute-start.13 = (bf16[2,768,512]{2,1,0:T(8,128)(2,1)}, bf16[2,768,512]{2,1,0:T(8,128)(2,1)}, u32[]{:S(2)}, u32[]{:S(2)}) collective-permute-start(bf16[2,768,512]{2,1,0:T(8,128)(2,1)} %get-tuple-element.39.refs_0_), channel_id=1, source_target_pairs={{0,2},{1,3},{2,0},{3,1},{4,6},{5,7},{6,4},{7,5},{8,10},{9,11},{10,... | collective-permute-start | bytes 4718600 | tf_op jit(solution)/shard_map/ppermute | solution.py:92
  576.1 47.1 %collective-permute-start.12 = (bf16[2,768,512]{2,1,0:T(8,128)(2,1)}, bf16[2,768,512]{2,1,0:T(8,128)(2,1)}, u32[]{:S(2)}, u32[]{:S(2)}) collective-permute-start(bf16[2,768,512]{2,1,0:T(8,128)(2,1)} %get-tuple-element.39.refs_0_), channel_id=1, source_target_pairs={{0,1},{1,0},{2,3},{3,2},{4,5},{5,4},{6,7},{7,6},{8,9},{9,8},{10,11... | collective-permute-start | bytes 4718600 | tf_op jit(solution)/shard_map/ppermute | solution.py:92
  611.3 11.8 %collective-permute-start.14 = (bf16[2,768,512]{2,1,0:T(8,128)(2,1)}, bf16[2,768,512]{2,1,0:T(8,128)(2,1)}, u32[]{:S(2)}, u32[]{:S(2)}) collective-permute-start(bf16[2,768,512]{2,1,0:T(8,128)(2,1)} %collective-permute-done.13.refs_2_), channel_id=1, source_target_pairs={{0,1},{1,0},{2,3},{3,2},{4,5},{5,4},{6,7},{7,6},{8,9},{9,8},{10,11... | collective-permute-start | bytes 4718600 | tf_op jit(solution)/shard_map/ppermute | solution.py:92
  621.6 20.0 %collective-permute-start.16 = (bf16[2,768,256]{2,1,0:T(8,128)(2,1)S(1)}, bf16[2,768,256]{2,1,0:T(8,128)(2,1)S(1)}, u32[]{:S(2)}, u32[]{:S(2)}) collective-permute-start(bf16[2,768,256]{2,1,0:T(8,128)(2,1)S(1)} %get-tuple-element.40.refs_0_), channel_id=1, source_target_pairs={{0,2},{1,3},{2,0},{3,1},{4,6},{5,7},{6,4},{7,5},{8,10},{9,11},{10,... | collective-permute-start | bytes 2359304 | tf_op jit(solution)/shard_map/ppermute | solution.py:92
  641.6 2.3 collective-permute-start.17
  641.6 3.4 collective-permute-start.15
  (13 other events, 145.4 us)
Sparse Core Ops, SparseCore 0:
  136.1 127.6 all-gather.6
  424.6 116.0 all-gather.10
  542.2 61.7 all-gather.8

commit v13 on v12

--- a/solution.py
+++ b/solution.py
@@ -331,10 +331,11 @@
     shape = (2, planes, block_rows, tile_cols)
     result, piece = product([lefts[0]], right0, views0, shape, (), (0, 0, 0))
     found = gather_cols(piece, n_col)
+    result, most = product([lefts[1]], right1[:1], views1[:-1], shape, (result,), (0, 1, 0))
     (result,) = product([(found, everything)], right0, views0, shape, (result,), (1, 0, 0))
-    result, most = product([lefts[1]], right1[:1], views1[:-1], shape, (result,), (0, 1, 0))
-    most = gather_cols(most, n_col)
+    most = gather_cols(most, n_col, result)
     result, rest = product([lefts[1]], right1[1:], [([(0, None)], 0)], shape, (result,), (0, 1, THIRDS - 1))
+    most[0] = after(most[0], rest)
     (sums,) = product([(most, everything[:-1])], right1, views1, shape, (), None)
     rest = gather_cols(rest, n_col, sums)
     return product([(rest, everything[-1:])], right1, views1, shape, (result,), (1, 1, 0), before=sums)[0]

time: 666 us -> 658 us (0.988)
  waiting for transfers between devices: 441 us -> 433 us
    ppermute x12, waiting for transfers between devices: 123 us -> 89.9 us  [gather_cols(): arrived = {d ^ bit: lax.ppermute(a, 'col', pairs) for d, a in held.items()}]
    all_gather x2, waiting for transfers between devices: 0.02 us -> 24.7 us  [gather_rows(): return lax.all_gather(part, 'row', axis=0)]
  transfers between devices with their start and end apart: 24 -> 24, of which waited for: 12 -> 13; matrix products, arithmetic and copies ran while one was open for 2% -> 2% of each run, Pallas kernels for 15% -> 16%
where the time goes in v13:
time: 658 us; the launch traced here: 657 us
  waiting for transfers between devices  433 us (66%)
  Pallas kernels  124 us (19%)
  starting transfers between devices  53.2 us (8%)
  local copies, waits for them, and re-layouts  30.7 us (5%)
  between operations  14 us (2%)
    ppermute x3, waiting for transfers between devices, hop(): lax.ppermute(pair[0], 'row', down)  164 us
    all_to_all x2, waiting for transfers between devices, per_device(): lax.all_to_all(sent[f].reshape(n_row * n_col, cap, 2 * tile_cols), ('row'...  155 us
    pallas_call x6, Pallas kernels, complex_product(): pl.pallas_call(functools.partial(product_kernel, opts), grid_spec=pltpu.P...  103 us
    ppermute x12, waiting for transfers between devices, gather_cols(): arrived = {d ^ bit: lax.ppermute(a, 'col', pairs) for d, a in held.items()}  89.9 us
    unnamed x27, local copies, waits for them, and re-layouts  29.4 us
    all_to_all x2, starting transfers between devices, per_device(): lax.all_to_all(sent[f].reshape(n_row * n_col, cap, 2 * tile_cols), ('row'...  27.9 us
    all_gather x2, waiting for transfers between devices, gather_rows(): return lax.all_gather(part, 'row', axis=0)  24.7 us
    pallas_call x2, Pallas kernels, place_rows(): pl.pallas_call(place_kernel, grid=(2,), in_specs=[pl.BlockSpec(placer.sha...  13.2 us
  transfers between devices with their start and end apart: 24, of which 13 were waited for; matrix products, arithmetic and copies ran while one was open for 2% of the time, Pallas kernels for 16%

profile of v13, /device:TPU:0, one launch (start us, length us, event | category | flops | bytes accessed | tf_op | source)
XLA Modules:
  0.0 657.0 jit_solution(5782038505729667554)
XLA Ops:
  9.0 7.4 %all-to-all-start = ((s32[16,1,96]{2,1,0:T(1,128)}), s32[16,1,96]{2,1,0:T(1,128)S(1)}, u32[]{:S(2)}, u32[]{:S(2)}) async-start(s32[16,1,96]{2,1,0:T(1,128)} %bitcast.3), calls=%async_computation | async-start | bytes 16384 | tf_op jit(solution)/shard_map/all_to_all | solution.py:285
  16.4 10.4 %copy.12 = bf16[384,4,3072]{2,0,1:T(8,128)(2,1)} copy(bf16[384,4,3072]{2,1,0:T(4,128)(2,1)} %param.3) | data formatting | bytes 18874368 | tf_op args[0]
  30.5 3.7 shard_map.38
  36.4 6.1 all-to-all-start.2
  54.2 75.1 %all-to-all-done.2 = bf16[16,96,1536]{2,1,0:T(8,128)(2,1)} async-done(((bf16[16,96,1536]{2,1,0:T(8,128)(2,1)}), bf16[16,96,1536]{2,1,0:T(8,128)(2,1)}, u32[]{:S(2)}, u32[]{:S(2)}) %all-to-all-start.2) | async-done | bytes 4718624 | tf_op jit(solution)/shard_map/all_to_all | solution.py:295
  129.3 6.7 %shard_map.39.refs_1_.refs_4_ = bf16[2,768,768]{2,1,0:T(8,128)(2,1)} custom-call(bf16[768,1536]{1,0:T(8,128)(2,1)S(1)} %fusion.placer, bf16[1536,1536]{1,0:T(8,128)(2,1)} %bitcast.8.got), custom_call_target="tpu_custom_call" | custom-call | flops 1000 | bytes 1000 | tf_op jit(solution)/shard_map/pallas_call | solution.py:67
  136.0 21.8 %all-to-all-start.1 = ((bf16[16,96,1536]{2,1,0:T(8,128)(2,1)}), bf16[16,96,1536]{2,1,0:T(8,128)(2,1)}, u32[]{:S(2)}, u32[]{:S(2)}) async-start(bf16[16,96,1536]{2,1,0:T(8,128)(2,1)} %bitcast.20), calls=%async_computation.1 | async-start | bytes 9437184 | tf_op jit(solution)/shard_map/all_to_all | solution.py:295
  159.2 6.1 collective-permute-start.1
  165.3 79.6 %all-to-all-done.1 = bf16[16,96,1536]{2,1,0:T(8,128)(2,1)} async-done(((bf16[16,96,1536]{2,1,0:T(8,128)(2,1)}), bf16[16,96,1536]{2,1,0:T(8,128)(2,1)}, u32[]{:S(2)}, u32[]{:S(2)}) %all-to-all-start.1) | async-done | bytes 4718624 | tf_op jit(solution)/shard_map/all_to_all | solution.py:295
  244.9 42.6 %collective-permute-done.refs_2_.refs_5_ = bf16[2,768,768]{2,1,0:T(8,128)(2,1)} collective-permute-done((bf16[2,768,768]{2,1,0:T(8,128)(2,1)}, bf16[2,768,768]{2,1,0:T(8,128)(2,1)}, u32[]{:S(2)}, u32[]{:S(2)}) %collective-permute-start) | collective-permute-done | bytes 2359328 | tf_op jit(solution)/shard_map/ppermute | solution.py:21
  289.6 78.0 %collective-permute-done.2.refs_4_.refs_7_ = bf16[2,768,768]{2,1,0:T(8,128)(2,1)S(1)} collective-permute-done((bf16[2,768,768]{2,1,0:T(8,128)(2,1)}, bf16[2,768,768]{2,1,0:T(8,128)(2,1)S(1)}, u32[]{:S(2)}, u32[]{:S(2)}) %collective-permute-start.2) | collective-permute-done | bytes 2359328 | tf_op jit(solution)/shard_map/ppermute | solution.py:21
  369.8 6.4 shard_map.40
  378.8 42.9 %collective-permute-done.3.refs_6_.refs_9_ = bf16[2,768,768]{2,1,0:T(8,128)(2,1)S(1)} collective-permute-done((bf16[2,768,768]{2,1,0:T(8,128)(2,1)S(1)}, bf16[2,768,768]{2,1,0:T(8,128)(2,1)S(1)}, u32[]{:S(2)}, u32[]{:S(2)}) %collective-permute-start.3) | collective-permute-done | bytes 2359328 | tf_op jit(solution)/shard_map/ppermute | solution.py:21
  426.5 24.1 %shard_map.41 = (bf16[2,4,768,768]{3,2,1,0:T(8,128)(2,1)}, bf16[2,768,768]{2,1,0:T(8,128)(2,1)}) custom-call(s32[2]{0:T(128)S(1)} %pad_add_fusion.where, bf16[4,2,768,768]{3,2,1,0:T(8,128)(2,1)} %bitcast.25, bf16[2,768,768]{2,1,0:T(8,128)(2,1)} %shard_map.39.refs_1_.refs_4_, bf16[2,768,768]{2,1,0:T(8,128)(2,1)} %collective-permute-done.refs_2_.refs_5_, ...), custom_call_target="tpu_custom_call" | custom-call | flops 1000 | bytes 1000 | tf_op jit(solution)/shard_map/pallas_call | solution.py:240
  451.2 28.2 %collective-permute-done.7.refs_2_ = bf16[2,768,768]{2,1,0:T(8,128)(2,1)} collective-permute-done((bf16[2,768,768]{2,1,0:T(8,128)(2,1)}, bf16[2,768,768]{2,1,0:T(8,128)(2,1)}, u32[]{:S(2)}, u32[]{:S(2)}) %collective-permute-start.7) | collective-permute-done | bytes 2359328 | tf_op jit(solution)/shard_map/ppermute | solution.py:92
  480.0 47.1 %collective-permute-done.10.refs_2_ = bf16[2,768,768]{2,1,0:T(8,128)(2,1)} collective-permute-done((bf16[2,768,768]{2,1,0:T(8,128)(2,1)}, bf16[2,768,768]{2,1,0:T(8,128)(2,1)}, u32[]{:S(2)}, u32[]{:S(2)}) %collective-permute-start.10) | collective-permute-done | bytes 2359328 | tf_op jit(solution)/shard_map/ppermute | solution.py:92
  527.0 13.7 %all-gather.11.cloned.1.call-done = bf16[8,768,512]{2,1,0:T(8,128)(2,1)} async-done(((bf16[2,768,512]{2,1,0:T(8,128)(2,1)}), bf16[8,768,512]{2,1,0:T(8,128)(2,1)}) %all-gather.11.cloned.1.call-update) | async-done | bytes 6291472 | tf_op jit(solution)/shard_map/all_gather | solution.py:311
  540.7 15.6 %shard_map.42 = (bf16[2,4,768,768]{3,2,1,0:T(8,128)(2,1)}, bf16[2,768,512]{2,1,0:T(8,128)(2,1)}) custom-call(s32[2]{0:T(128)S(1)} %pad_add_fusion.where, bf16[2,768,768]{2,1,0:T(8,128)(2,1)S(1)} %copy-done.7, bf16[2,768,768]{2,1,0:T(8,128)(2,1)} %collective-permute-done.6.refs_1_, ...), custom_call_target="tpu_custom_call", output_to_operand_aliasing={{0}: (6, {})} | custom-call | flops 1000 | bytes 1000 | tf_op jit(solution)/shard_map/pallas_call | solution.py:240
  557.9 23.7 %shard_map.43.refs_5_ = bf16[2,4,768,768]{3,2,1,0:T(8,128)(2,1)} custom-call(s32[2]{0:T(128)S(1)} %pad_add_fusion.where, bf16[2,768,768]{2,1,0:T(8,128)(2,1)} %get-tuple-element.36.refs_0_, bf16[2,768,768]{2,1,0:T(8,128)(2,1)} %collective-permute-done.9.refs_1_, ...), custom_call_target="tpu_custom_call", output_to_operand_aliasing={{}: (12, {})} | custom-call | flops 1000 | bytes 1000 | tf_op jit(solution)/shard_map/pallas_call | solution.py:240
  581.7 11.4 %collective-permute-done.13.refs_2_ = bf16[2,768,512]{2,1,0:T(8,128)(2,1)} collective-permute-done((bf16[2,768,512]{2,1,0:T(8,128)(2,1)}, bf16[2,768,512]{2,1,0:T(8,128)(2,1)}, u32[]{:S(2)}, u32[]{:S(2)}) %collective-permute-start.13) | collective-permute-done | bytes 1572896 | tf_op jit(solution)/shard_map/ppermute | solution.py:92
  593.1 11.0 %all-gather.9.cloned.1.call-done = bf16[8,768,256]{2,1,0:T(8,128)(2,1)} async-done(((bf16[2,768,256]{2,1,0:T(8,128)(2,1)}), bf16[8,768,256]{2,1,0:T(8,128)(2,1)}) %all-gather.9.cloned.1.call-update) | async-done | bytes 3145744 | tf_op jit(solution)/shard_map/all_gather | solution.py:311
  606.0 8.4 %shard_map.44 = (bf16[2,4,768,768]{3,2,1,0:T(8,128)(2,1)}, bf16[2,768,256]{2,1,0:T(8,128)(2,1)S(1)}) custom-call(s32[2]{0:T(128)S(1)} %pad_add_fusion.where, bf16[2,768,768]{2,1,0:T(8,128)(2,1)S(1)} %copy-done.7, bf16[2,768,768]{2,1,0:T(8,128)(2,1)} %collective-permute-done.6.refs_1_, ...), custom_call_target="tpu_custom_call", output_to_operand_aliasing={{0}: (6, {})} | custom-call | flops 1000 | bytes 1000 | tf_op jit(solution)/shard_map/pallas_call | solution.py:240
  615.9 17.3 %shard_map.45.refs_6_ = f32[2,768,768]{2,1,0:T(8,128)} custom-call(s32[2]{0:T(128)S(1)} %pad_add_fusion.where, bf16[2,768,512]{2,1,0:T(8,128)(2,1)} %get-tuple-element.44.refs_0_, bf16[2,768,512]{2,1,0:T(8,128)(2,1)} %collective-permute-done.12.refs_1_, bf16[2,768,512]{2,1,0:T(8,128)(2,1)} %collective-permute-done.13.refs_2_, ...), custom_call_target="tpu_custom_call" | custom-call | flops 1000 | bytes 1000 | tf_op jit(solution)/shard_map/pallas_call | solution.py:240
  636.7 13.8 %shard_map.46 = bf16[2,4,768,768]{3,2,1,0:T(8,128)(2,1)} custom-call(s32[2]{0:T(128)S(1)} %pad_add_fusion.where, bf16[2,768,256]{2,1,0:T(8,128)(2,1)S(1)} %get-tuple-element.46.refs_0_, bf16[2,768,256]{2,1,0:T(8,128)(2,1)S(1)} %collective-permute-done.15.refs_1_, ...), custom_call_target="tpu_custom_call", output_to_operand_aliasing={{}: (8, {})} | custom-call | flops 1000 | bytes 1000 | tf_op jit(solution)/shard_map/pallas_call | solution.py:240
  (77 shorter events, 41.9 us)
Async XLA Ops:
  9.0 27.4 %all-to-all-start = ((s32[16,1,96]{2,1,0:T(1,128)}), s32[16,1,96]{2,1,0:T(1,128)S(1)}, u32[]{:S(2)}, u32[]{:S(2)}) async-start(s32[16,1,96]{2,1,0:T(1,128)} %bitcast.3), calls=%async_computation | async-start | bytes 16384 | tf_op jit(solution)/shard_map/all_to_all | solution.py:285
  36.4 92.9 %all-to-all-start.2 = ((bf16[16,96,1536]{2,1,0:T(8,128)(2,1)}), bf16[16,96,1536]{2,1,0:T(8,128)(2,1)}, u32[]{:S(2)}, u32[]{:S(2)}) async-start(bf16[16,96,1536]{2,1,0:T(8,128)(2,1)} %bitcast.21), calls=%async_computation.2 | async-start | bytes 9437184 | tf_op jit(solution)/shard_map/all_to_all | solution.py:295
  42.5 245.1 %all-gather.7.cloned.1.call-start = ((), (), s32[]{:S(2)}) async-start(), calls=%async_computation.3 | async-start | bytes 11796480 | tf_op jit(solution)/shard_map/all_gather | solution.py:307
  136.0 108.9 %all-to-all-start.1 = ((bf16[16,96,1536]{2,1,0:T(8,128)(2,1)}), bf16[16,96,1536]{2,1,0:T(8,128)(2,1)}, u32[]{:S(2)}, u32[]{:S(2)}) async-start(bf16[16,96,1536]{2,1,0:T(8,128)(2,1)} %bitcast.20), calls=%async_computation.1 | async-start | bytes 9437184 | tf_op jit(solution)/shard_map/all_to_all | solution.py:295
  157.8 382.9 %all-gather.11.cloned.1.call-start = ((), (), s32[]{:S(2)}) async-start(), calls=%async_computation.5 | async-start | bytes 7864320 | tf_op jit(solution)/shard_map/all_gather | solution.py:311
  157.9 129.6 %collective-permute-start = (bf16[2,768,768]{2,1,0:T(8,128)(2,1)}, bf16[2,768,768]{2,1,0:T(8,128)(2,1)}, u32[]{:S(2)}, u32[]{:S(2)}) collective-permute-start(bf16[2,768,768]{2,1,0:T(8,128)(2,1)} %shard_map.39.refs_1_.refs_4_), channel_id=1, source_target_pairs={{4,0},{8,4},{12,8},{5,1},{9,5},{13,9},{6,2},{10,6},{14,10},{7,3},{... | collective-permute-start | bytes 7077896 | tf_op jit(solution)/shard_map/ppermute | solution.py:21
  159.2 128.3 %collective-permute-start.1 = (bf16[2,768,768]{2,1,0:T(8,128)(2,1)}, bf16[2,768,768]{2,1,0:T(8,128)(2,1)}, u32[]{:S(2)}, u32[]{:S(2)}) collective-permute-start(bf16[2,768,768]{2,1,0:T(8,128)(2,1)} %shard_map.39.refs_1_.refs_4_), channel_id=1, source_target_pairs={{0,4},{4,8},{8,12},{1,5},{5,9},{9,13},{2,6},{6,10},{10,14},{3,7},{... | collective-permute-start | bytes 7077896 | tf_op jit(solution)/shard_map/ppermute | solution.py:21
  287.5 80.1 %collective-permute-start.2 = (bf16[2,768,768]{2,1,0:T(8,128)(2,1)}, bf16[2,768,768]{2,1,0:T(8,128)(2,1)S(1)}, u32[]{:S(2)}, u32[]{:S(2)}) collective-permute-start(bf16[2,768,768]{2,1,0:T(8,128)(2,1)} %collective-permute-done.refs_2_.refs_5_), channel_id=1, source_target_pairs={{4,0},{8,4},{5,1},{9,5},{6,2},{10,6},{7,3},{11,7},{20,16},{24,20},... | collective-permute-start | bytes 7077896 | tf_op jit(solution)/shard_map/ppermute | solution.py:21
  288.8 80.1 %collective-permute-start.4 = (bf16[2,768,768]{2,1,0:T(8,128)(2,1)}, bf16[2,768,768]{2,1,0:T(8,128)(2,1)S(1)}, u32[]{:S(2)}, u32[]{:S(2)}) collective-permute-start(bf16[2,768,768]{2,1,0:T(8,128)(2,1)} %collective-permute-done.1.refs_3_.refs_6_), channel_id=1, source_target_pairs={{4,8},{8,12},{5,9},{9,13},{6,10},{10,14},{7,11},{11,15},{20,24},{2... | collective-permute-start | bytes 7077896 | tf_op jit(solution)/shard_map/ppermute | solution.py:21
  367.6 54.1 %collective-permute-start.3 = (bf16[2,768,768]{2,1,0:T(8,128)(2,1)S(1)}, bf16[2,768,768]{2,1,0:T(8,128)(2,1)S(1)}, u32[]{:S(2)}, u32[]{:S(2)}) collective-permute-start(bf16[2,768,768]{2,1,0:T(8,128)(2,1)S(1)} %collective-permute-done.2.refs_4_.refs_7_), channel_id=1, source_target_pairs={{4,0},{5,1},{6,2},{7,3},{20,16},{21,17},{22,18},{23,19}} | collective-permute-start | bytes 7077896 | tf_op jit(solution)/shard_map/ppermute | solution.py:21
  369.0 52.8 %collective-permute-start.5 = (bf16[2,768,768]{2,1,0:T(8,128)(2,1)S(1)}, bf16[2,768,768]{2,1,0:T(8,128)(2,1)S(1)}, u32[]{:S(2)}, u32[]{:S(2)}) collective-permute-start(bf16[2,768,768]{2,1,0:T(8,128)(2,1)S(1)} %collective-permute-done.4.refs_5_.refs_8_), channel_id=1, source_target_pairs={{8,12},{9,13},{10,14},{11,15},{24,28},{25,29},{26,30},{27,31}} | collective-permute-start | bytes 7077896 | tf_op jit(solution)/shard_map/ppermute | solution.py:21
  424.6 179.5 %all-gather.9.cloned.1.call-start = ((), (), s32[]{:S(2)}) async-start(), calls=%async_computation.4 | async-start | bytes 3932160 | tf_op jit(solution)/shard_map/all_gather | solution.py:311
  424.8 54.6 %collective-permute-start.7 = (bf16[2,768,768]{2,1,0:T(8,128)(2,1)}, bf16[2,768,768]{2,1,0:T(8,128)(2,1)}, u32[]{:S(2)}, u32[]{:S(2)}) collective-permute-start(bf16[2,768,768]{2,1,0:T(8,128)(2,1)} %copy-done.6), channel_id=1, source_target_pairs={{0,2},{1,3},{2,0},{3,1},{4,6},{5,7},{6,4},{7,5},{8,10},{9,11},{10,... | collective-permute-start | bytes 7077896 | tf_op jit(solution)/shard_map/ppermute | solution.py:92
  450.6 76.4 %collective-permute-start.10 = (bf16[2,768,768]{2,1,0:T(8,128)(2,1)}, bf16[2,768,768]{2,1,0:T(8,128)(2,1)}, u32[]{:S(2)}, u32[]{:S(2)}) collective-permute-start(bf16[2,768,768]{2,1,0:T(8,128)(2,1)} %get-tuple-element.36.refs_0_), channel_id=1, source_target_pairs={{0,2},{1,3},{2,0},{3,1},{4,6},{5,7},{6,4},{7,5},{8,10},{9,11},{10,... | collective-permute-start | bytes 7077896 | tf_op jit(solution)/shard_map/ppermute | solution.py:92
  451.2 75.9 %collective-permute-start.6 = (bf16[2,768,768]{2,1,0:T(8,128)(2,1)S(1)}, bf16[2,768,768]{2,1,0:T(8,128)(2,1)}, u32[]{:S(2)}, u32[]{:S(2)}) collective-permute-start(bf16[2,768,768]{2,1,0:T(8,128)(2,1)S(1)} %copy-done.7), channel_id=1, source_target_pairs={{0,1},{1,0},{2,3},{3,2},{4,5},{5,4},{6,7},{7,6},{8,9},{9,8},{10,11... | collective-permute-start | bytes 7077896 | tf_op jit(solution)/shard_map/ppermute | solution.py:92
  479.4 47.7 %collective-permute-start.8 = (bf16[2,768,768]{2,1,0:T(8,128)(2,1)}, bf16[2,768,768]{2,1,0:T(8,128)(2,1)}, u32[]{:S(2)}, u32[]{:S(2)}) collective-permute-start(bf16[2,768,768]{2,1,0:T(8,128)(2,1)} %collective-permute-done.7.refs_2_), channel_id=1, source_target_pairs={{0,1},{1,0},{2,3},{3,2},{4,5},{5,4},{6,7},{7,6},{8,9},{9,8},{10,11... | collective-permute-start | bytes 7077896 | tf_op jit(solution)/shard_map/ppermute | solution.py:92
  479.4 78.5 %collective-permute-start.9 = (bf16[2,768,768]{2,1,0:T(8,128)(2,1)}, bf16[2,768,768]{2,1,0:T(8,128)(2,1)}, u32[]{:S(2)}, u32[]{:S(2)}) collective-permute-start(bf16[2,768,768]{2,1,0:T(8,128)(2,1)} %get-tuple-element.36.refs_0_), channel_id=1, source_target_pairs={{0,1},{1,0},{2,3},{3,2},{4,5},{5,4},{6,7},{7,6},{8,9},{9,8},{10,11... | collective-permute-start | bytes 7077896 | tf_op jit(solution)/shard_map/ppermute | solution.py:92
  527.0 30.8 %collective-permute-start.11 = (bf16[2,768,768]{2,1,0:T(8,128)(2,1)}, bf16[2,768,768]{2,1,0:T(8,128)(2,1)}, u32[]{:S(2)}, u32[]{:S(2)}) collective-permute-start(bf16[2,768,768]{2,1,0:T(8,128)(2,1)} %collective-permute-done.10.refs_2_), channel_id=1, source_target_pairs={{0,1},{1,0},{2,3},{3,2},{4,5},{5,4},{6,7},{7,6},{8,9},{9,8},{10,11... | collective-permute-start | bytes 7077896 | tf_op jit(solution)/shard_map/ppermute | solution.py:92
  556.3 36.7 %collective-permute-start.13 = (bf16[2,768,512]{2,1,0:T(8,128)(2,1)}, bf16[2,768,512]{2,1,0:T(8,128)(2,1)}, u32[]{:S(2)}, u32[]{:S(2)}) collective-permute-start(bf16[2,768,512]{2,1,0:T(8,128)(2,1)} %get-tuple-element.44.refs_0_), channel_id=1, source_target_pairs={{0,2},{1,3},{2,0},{3,1},{4,6},{5,7},{6,4},{7,5},{8,10},{9,11},{10,... | collective-permute-start | bytes 4718600 | tf_op jit(solution)/shard_map/ppermute | solution.py:92
  581.6 34.2 %collective-permute-start.12 = (bf16[2,768,512]{2,1,0:T(8,128)(2,1)}, bf16[2,768,512]{2,1,0:T(8,128)(2,1)}, u32[]{:S(2)}, u32[]{:S(2)}) collective-permute-start(bf16[2,768,512]{2,1,0:T(8,128)(2,1)} %get-tuple-element.44.refs_0_), channel_id=1, source_target_pairs={{0,1},{1,0},{2,3},{3,2},{4,5},{5,4},{6,7},{7,6},{8,9},{9,8},{10,11... | collective-permute-start | bytes 4718600 | tf_op jit(solution)/shard_map/ppermute | solution.py:92
  593.1 22.8 %collective-permute-start.14 = (bf16[2,768,512]{2,1,0:T(8,128)(2,1)}, bf16[2,768,512]{2,1,0:T(8,128)(2,1)}, u32[]{:S(2)}, u32[]{:S(2)}) collective-permute-start(bf16[2,768,512]{2,1,0:T(8,128)(2,1)} %collective-permute-done.13.refs_2_), channel_id=1, source_target_pairs={{0,1},{1,0},{2,3},{3,2},{4,5},{5,4},{6,7},{7,6},{8,9},{9,8},{10,11... | collective-permute-start | bytes 4718600 | tf_op jit(solution)/shard_map/ppermute | solution.py:92
  614.3 19.3 %collective-permute-start.16 = (bf16[2,768,256]{2,1,0:T(8,128)(2,1)S(1)}, bf16[2,768,256]{2,1,0:T(8,128)(2,1)S(1)}, u32[]{:S(2)}, u32[]{:S(2)}) collective-permute-start(bf16[2,768,256]{2,1,0:T(8,128)(2,1)S(1)} %get-tuple-element.46.refs_0_), channel_id=1, source_target_pairs={{0,2},{1,3},{2,0},{3,1},{4,6},{5,7},{6,4},{7,5},{8,10},{9,11},{10,... | collective-permute-start | bytes 2359304 | tf_op jit(solution)/shard_map/ppermute | solution.py:92
  633.2 2.4 collective-permute-start.15
  633.6 3.1 collective-permute-start.17
  (13 other events, 69.5 us)
Sparse Core Ops, SparseCore 0:
  136.1 127.6 all-gather.6
  424.7 115.9 all-gather.10
  542.3 61.7 all-gather.8

commit v14 on v13

--- a/solution.py
+++ b/solution.py
@@ -299,7 +299,7 @@
             got = after(got, sent[1])
         if pair is not None:
             got, pair, _ = lax.optimization_barrier((got, pair, lefts[0][0]))
-        tile, *cut = place_rows(placer, got, (THIRDS - 1, 1) if f else ())
+        tile, *cut = place_rows(placer, got, (1,) * THIRDS if f else ())
         if line and f == 0:
             pair = hop((tile, tile), 1, n_row)
         tiles.append(tile)
@@ -312,14 +312,16 @@
         return lax.all_gather(part, "row", axis=1, tiled=True)
 
     sub = tile_cols // THIRDS
-    views1 = [([(0, None)], j * sub) for j in everything[:-1]] + [([(1, None)], 0)]
+    views1 = [([(j, None)], 0) for j in everything]
     if line:
         right0, ups = [tiles[0], *pair], [0, 1, -1]
+        second = pair
         for k in range(2, n_row):
             pair = hop(pair, k, n_row)
+            second = pair if k == 2 else second
             right0 += list(pair)
             ups += [k, -k]
-        cut = [after(part, pair) for part in cut]
+        cut = [after(part, pair if j else second) for j, part in enumerate(cut)]
     else:
         right0, ups = [gather_rows(tiles[0])], [None]
     right1 = [gather_rows(part) for part in cut]
@@ -331,10 +333,10 @@
     shape = (2, planes, block_rows, tile_cols)
     result, piece = product([lefts[0]], right0, views0, shape, (), (0, 0, 0))
     found = gather_cols(piece, n_col)
-    result, most = product([lefts[1]], right1[:1], views1[:-1], shape, (result,), (0, 1, 0))
+    result, most = product([lefts[1]], right1[:-1], views1[:-1], shape, (result,), (0, 1, 0))
     (result,) = product([(found, everything)], right0, views0, shape, (result,), (1, 0, 0))
     most = gather_cols(most, n_col, result)
-    result, rest = product([lefts[1]], right1[1:], [([(0, None)], 0)], shape, (result,), (0, 1, THIRDS - 1))
+    result, rest = product([lefts[1]], right1[-1:], views1[:1], shape, (result,), (0, 1, THIRDS - 1))
     most[0] = after(most[0], rest)
     (sums,) = product([(most, everything[:-1])], right1, views1, shape, (), None)
     rest = gather_cols(rest, n_col, sums)

time: 658 us -> 684 us (1.040)
  waiting for transfers between devices: 433 us -> 459 us
    ppermute x3, waiting for transfers between devices: 164 us -> 214 us  [hop(): lax.ppermute(pair[0], 'row', down)]
    all_gather x2 -> x3, waiting for transfers between devices: 24.7 us -> 0.02 us  [gather_rows(): return lax.all_gather(part, 'row', axis=0)]
    unnamed x27 -> x19, local copies, waits for them, and re-layouts: 29.4 us -> 25.4 us
  transfers between devices with their start and end apart: 24 -> 25, of which waited for: 13 -> 11; matrix products, arithmetic and copies ran while one was open for 2% -> 2% of each run, Pallas kernels for 16% -> 15%
where the time goes in v14:
time: 684 us; the launch traced here: 681 us
  waiting for transfers between devices  459 us (67%)
  Pallas kernels  123 us (18%)
  starting transfers between devices  56.3 us (8%)
  local copies, waits for them, and re-layouts  26.7 us (4%)
  between operations  14 us (2%)
    ppermute x3, waiting for transfers between devices, hop(): lax.ppermute(pair[0], 'row', down)  214 us
    all_to_all x2, waiting for transfers between devices, per_device(): lax.all_to_all(sent[f].reshape(n_row * n_col, cap, 2 * tile_cols), ('row'...  155 us
    pallas_call x6, Pallas kernels, complex_product(): pl.pallas_call(functools.partial(product_kernel, opts), grid_spec=pltpu.P...  102 us
    ppermute x12, waiting for transfers between devices, gather_cols(): arrived = {d ^ bit: lax.ppermute(a, 'col', pairs) for d, a in held.items()}  89.9 us
    all_to_all x2, starting transfers between devices, per_device(): lax.all_to_all(sent[f].reshape(n_row * n_col, cap, 2 * tile_cols), ('row'...  27.9 us
    unnamed x19, local copies, waits for them, and re-layouts  25.4 us
  transfers between devices with their start and end apart: 25, of which 11 were waited for; matrix products, arithmetic and copies ran while one was open for 2% of the time, Pallas kernels for 15%

profile of v14, /device:TPU:0, one launch (start us, length us, event | category | flops | bytes accessed | tf_op | source)
XLA Modules:
  0.0 681.3 jit_solution(13383130548396743803)
XLA Ops:
  9.0 7.4 %all-to-all-start = ((s32[16,1,96]{2,1,0:T(1,128)}), s32[16,1,96]{2,1,0:T(1,128)S(1)}, u32[]{:S(2)}, u32[]{:S(2)}) async-start(s32[16,1,96]{2,1,0:T(1,128)} %bitcast.3), calls=%async_computation | async-start | bytes 16384 | tf_op jit(solution)/shard_map/all_to_all | solution.py:285
  16.4 10.4 %copy.12 = bf16[384,4,3072]{2,0,1:T(8,128)(2,1)} copy(bf16[384,4,3072]{2,1,0:T(4,128)(2,1)} %param.3) | data formatting | bytes 18874368 | tf_op args[0]
  26.8 3.7 copy-done
  30.5 3.7 shard_map.38
  36.4 6.0 all-to-all-start.2
  46.2 3.7 shard_map.37
  54.2 75.1 %all-to-all-done.2 = bf16[16,96,1536]{2,1,0:T(8,128)(2,1)} async-done(((bf16[16,96,1536]{2,1,0:T(8,128)(2,1)}), bf16[16,96,1536]{2,1,0:T(8,128)(2,1)}, u32[]{:S(2)}, u32[]{:S(2)}) %all-to-all-start.2) | async-done | bytes 4718624 | tf_op jit(solution)/shard_map/all_to_all | solution.py:295
  129.3 6.7 shard_map.39.refs_1_.refs_4_
  136.0 21.8 %all-to-all-start.1 = ((bf16[16,96,1536]{2,1,0:T(8,128)(2,1)}), bf16[16,96,1536]{2,1,0:T(8,128)(2,1)}, u32[]{:S(2)}, u32[]{:S(2)}) async-start(bf16[16,96,1536]{2,1,0:T(8,128)(2,1)} %bitcast.27), calls=%async_computation.1 | async-start | bytes 9437184 | tf_op jit(solution)/shard_map/all_to_all | solution.py:295
  159.2 6.1 collective-permute-start.1
  165.3 79.6 %all-to-all-done.1 = bf16[16,96,1536]{2,1,0:T(8,128)(2,1)} async-done(((bf16[16,96,1536]{2,1,0:T(8,128)(2,1)}), bf16[16,96,1536]{2,1,0:T(8,128)(2,1)}, u32[]{:S(2)}, u32[]{:S(2)}) %all-to-all-start.1) | async-done | bytes 4718624 | tf_op jit(solution)/shard_map/all_to_all | solution.py:295
  244.9 42.6 %collective-permute-done.refs_2_.refs_5_ = bf16[2,768,768]{2,1,0:T(8,128)(2,1)} collective-permute-done((bf16[2,768,768]{2,1,0:T(8,128)(2,1)}, bf16[2,768,768]{2,1,0:T(8,128)(2,1)}, u32[]{:S(2)}, u32[]{:S(2)}) %collective-permute-start) | collective-permute-done | bytes 2359328 | tf_op jit(solution)/shard_map/ppermute | solution.py:21
  291.0 6.6 shard_map.40
  299.0 68.7 %collective-permute-done.2.refs_4_.refs_7_ = bf16[2,768,768]{2,1,0:T(8,128)(2,1)} collective-permute-done((bf16[2,768,768]{2,1,0:T(8,128)(2,1)}, bf16[2,768,768]{2,1,0:T(8,128)(2,1)}, u32[]{:S(2)}, u32[]{:S(2)}) %collective-permute-start.2) | collective-permute-done | bytes 2359328 | tf_op jit(solution)/shard_map/ppermute | solution.py:21
  371.2 103.0 %collective-permute-done.3.refs_6_.refs_9_ = bf16[2,768,768]{2,1,0:T(8,128)(2,1)} collective-permute-done((bf16[2,768,768]{2,1,0:T(8,128)(2,1)}, bf16[2,768,768]{2,1,0:T(8,128)(2,1)}, u32[]{:S(2)}, u32[]{:S(2)}) %collective-permute-start.3) | collective-permute-done | bytes 2359328 | tf_op jit(solution)/shard_map/ppermute | solution.py:21
  476.1 24.2 %shard_map.41 = (bf16[2,4,768,768]{3,2,1,0:T(8,128)(2,1)}, bf16[2,768,768]{2,1,0:T(8,128)(2,1)}) custom-call(s32[2]{0:T(128)S(1)} %pad_add_fusion.where, bf16[4,2,768,768]{3,2,1,0:T(8,128)(2,1)} %bitcast.29, bf16[2,768,768]{2,1,0:T(8,128)(2,1)} %shard_map.39.refs_1_.refs_4_, bf16[2,768,768]{2,1,0:T(8,128)(2,1)} %collective-permute-done.refs_2_.refs_5_, ...), custom_call_target="tpu_custom_call" | custom-call | flops 1000 | bytes 1000 | tf_op jit(solution)/shard_map/pallas_call | solution.py:240
  500.9 28.1 %collective-permute-done.7.refs_2_ = bf16[2,768,768]{2,1,0:T(8,128)(2,1)} collective-permute-done((bf16[2,768,768]{2,1,0:T(8,128)(2,1)}, bf16[2,768,768]{2,1,0:T(8,128)(2,1)}, u32[]{:S(2)}, u32[]{:S(2)}) %collective-permute-start.7) | collective-permute-done | bytes 2359328 | tf_op jit(solution)/shard_map/ppermute | solution.py:92
  529.6 46.7 %collective-permute-done.10.refs_2_ = bf16[2,768,768]{2,1,0:T(8,128)(2,1)} collective-permute-done((bf16[2,768,768]{2,1,0:T(8,128)(2,1)}, bf16[2,768,768]{2,1,0:T(8,128)(2,1)}, u32[]{:S(2)}, u32[]{:S(2)}) %collective-permute-start.10) | collective-permute-done | bytes 2359328 | tf_op jit(solution)/shard_map/ppermute | solution.py:92
  576.3 15.6 %shard_map.42 = (bf16[2,4,768,768]{3,2,1,0:T(8,128)(2,1)}, bf16[2,768,512]{2,1,0:T(8,128)(2,1)}) custom-call(s32[2]{0:T(128)S(1)} %pad_add_fusion.where, bf16[2,768,768]{2,1,0:T(8,128)(2,1)S(1)} %copy-done.8, bf16[2,768,768]{2,1,0:T(8,128)(2,1)} %collective-permute-done.6.refs_1_, ...), custom_call_target="tpu_custom_call", output_to_operand_aliasing={{0}: (7, {})} | custom-call | flops 1000 | bytes 1000 | tf_op jit(solution)/shard_map/pallas_call | solution.py:240
  593.5 23.7 %shard_map.43.refs_5_ = bf16[2,4,768,768]{3,2,1,0:T(8,128)(2,1)} custom-call(s32[2]{0:T(128)S(1)} %pad_add_fusion.where, bf16[2,768,768]{2,1,0:T(8,128)(2,1)} %get-tuple-element.38.refs_0_, bf16[2,768,768]{2,1,0:T(8,128)(2,1)} %collective-permute-done.9.refs_1_, ...), custom_call_target="tpu_custom_call", output_to_operand_aliasing={{}: (12, {})} | custom-call | flops 1000 | bytes 1000 | tf_op jit(solution)/shard_map/pallas_call | solution.py:240
  617.5 11.6 %collective-permute-done.13.refs_2_ = bf16[2,768,512]{2,1,0:T(8,128)(2,1)} collective-permute-done((bf16[2,768,512]{2,1,0:T(8,128)(2,1)}, bf16[2,768,512]{2,1,0:T(8,128)(2,1)}, u32[]{:S(2)}, u32[]{:S(2)}) %collective-permute-start.13) | collective-permute-done | bytes 1572896 | tf_op jit(solution)/shard_map/ppermute | solution.py:92
  631.0 8.4 %shard_map.44 = (bf16[2,4,768,768]{3,2,1,0:T(8,128)(2,1)}, bf16[2,768,256]{2,1,0:T(8,128)(2,1)S(1)}) custom-call(s32[2]{0:T(128)S(1)} %pad_add_fusion.where, bf16[2,768,768]{2,1,0:T(8,128)(2,1)S(1)} %copy-done.8, bf16[2,768,768]{2,1,0:T(8,128)(2,1)} %collective-permute-done.6.refs_1_, ...), custom_call_target="tpu_custom_call", output_to_operand_aliasing={{0}: (6, {})} | custom-call | flops 1000 | bytes 1000 | tf_op jit(solution)/shard_map/pallas_call | solution.py:240
  641.0 17.0 %shard_map.45.refs_7_ = f32[2,768,768]{2,1,0:T(8,128)} custom-call(s32[2]{0:T(128)S(1)} %pad_add_fusion.where, bf16[2,768,512]{2,1,0:T(8,128)(2,1)} %get-tuple-element.48.refs_0_, bf16[2,768,512]{2,1,0:T(8,128)(2,1)} %collective-permute-done.12.refs_1_, bf16[2,768,512]{2,1,0:T(8,128)(2,1)} %collective-permute-done.13.refs_2_, ...), custom_call_target="tpu_custom_call" | custom-call | flops 1000 | bytes 1000 | tf_op jit(solution)/shard_map/pallas_call | solution.py:240
  661.7 13.1 %shard_map.46 = bf16[2,4,768,768]{3,2,1,0:T(8,128)(2,1)} custom-call(s32[2]{0:T(128)S(1)} %pad_add_fusion.where, bf16[2,768,256]{2,1,0:T(8,128)(2,1)S(1)} %get-tuple-element.50.refs_0_, bf16[2,768,256]{2,1,0:T(8,128)(2,1)S(1)} %collective-permute-done.15.refs_1_, ...), custom_call_target="tpu_custom_call", output_to_operand_aliasing={{}: (9, {})} | custom-call | flops 1000 | bytes 1000 | tf_op jit(solution)/shard_map/pallas_call | solution.py:240
  (72 shorter events, 33.8 us)
Async XLA Ops:
  9.0 27.4 %all-to-all-start = ((s32[16,1,96]{2,1,0:T(1,128)}), s32[16,1,96]{2,1,0:T(1,128)S(1)}, u32[]{:S(2)}, u32[]{:S(2)}) async-start(s32[16,1,96]{2,1,0:T(1,128)} %bitcast.3), calls=%async_computation | async-start | bytes 16384 | tf_op jit(solution)/shard_map/all_to_all | solution.py:285
  36.4 92.9 %all-to-all-start.2 = ((bf16[16,96,1536]{2,1,0:T(8,128)(2,1)}), bf16[16,96,1536]{2,1,0:T(8,128)(2,1)}, u32[]{:S(2)}, u32[]{:S(2)}) async-start(bf16[16,96,1536]{2,1,0:T(8,128)(2,1)} %bitcast.28), calls=%async_computation.2 | async-start | bytes 9437184 | tf_op jit(solution)/shard_map/all_to_all | solution.py:295
  42.4 245.0 %all-gather.9.cloned.1.call-start = ((), (), s32[]{:S(2)}) async-start(), calls=%async_computation.3 | async-start | bytes 11796480 | tf_op jit(solution)/shard_map/all_gather | solution.py:307
  136.0 108.9 %all-to-all-start.1 = ((bf16[16,96,1536]{2,1,0:T(8,128)(2,1)}), bf16[16,96,1536]{2,1,0:T(8,128)(2,1)}, u32[]{:S(2)}, u32[]{:S(2)}) async-start(bf16[16,96,1536]{2,1,0:T(8,128)(2,1)} %bitcast.27), calls=%async_computation.1 | async-start | bytes 9437184 | tf_op jit(solution)/shard_map/all_to_all | solution.py:295
  157.8 418.5 %all-gather.13.cloned.1.call-start = ((), (), s32[]{:S(2)}) async-start(), calls=%async_computation.5 | async-start | bytes 3932160 | tf_op jit(solution)/shard_map/all_gather | solution.py:311
  157.9 129.6 %collective-permute-start = (bf16[2,768,768]{2,1,0:T(8,128)(2,1)}, bf16[2,768,768]{2,1,0:T(8,128)(2,1)}, u32[]{:S(2)}, u32[]{:S(2)}) collective-permute-start(bf16[2,768,768]{2,1,0:T(8,128)(2,1)} %shard_map.39.refs_1_.refs_4_), channel_id=1, source_target_pairs={{4,0},{8,4},{12,8},{5,1},{9,5},{13,9},{6,2},{10,6},{14,10},{7,3},{... | collective-permute-start | bytes 7077896 | tf_op jit(solution)/shard_map/ppermute | solution.py:21
  159.2 128.3 %collective-permute-start.1 = (bf16[2,768,768]{2,1,0:T(8,128)(2,1)}, bf16[2,768,768]{2,1,0:T(8,128)(2,1)}, u32[]{:S(2)}, u32[]{:S(2)}) collective-permute-start(bf16[2,768,768]{2,1,0:T(8,128)(2,1)} %shard_map.39.refs_1_.refs_4_), channel_id=1, source_target_pairs={{0,4},{4,8},{8,12},{1,5},{5,9},{9,13},{2,6},{6,10},{10,14},{3,7},{... | collective-permute-start | bytes 7077896 | tf_op jit(solution)/shard_map/ppermute | solution.py:21
  287.5 80.2 %collective-permute-start.2 = (bf16[2,768,768]{2,1,0:T(8,128)(2,1)}, bf16[2,768,768]{2,1,0:T(8,128)(2,1)}, u32[]{:S(2)}, u32[]{:S(2)}) collective-permute-start(bf16[2,768,768]{2,1,0:T(8,128)(2,1)} %collective-permute-done.refs_2_.refs_5_), channel_id=1, source_target_pairs={{4,0},{8,4},{5,1},{9,5},{6,2},{10,6},{7,3},{11,7},{20,16},{24,20},... | collective-permute-start | bytes 7077896 | tf_op jit(solution)/shard_map/ppermute | solution.py:21
  288.8 78.9 %collective-permute-start.4 = (bf16[2,768,768]{2,1,0:T(8,128)(2,1)}, bf16[2,768,768]{2,1,0:T(8,128)(2,1)}, u32[]{:S(2)}, u32[]{:S(2)}) collective-permute-start(bf16[2,768,768]{2,1,0:T(8,128)(2,1)} %collective-permute-done.1.refs_3_.refs_6_), channel_id=1, source_target_pairs={{4,8},{8,12},{5,9},{9,13},{6,10},{10,14},{7,11},{11,15},{20,24},{2... | collective-permute-start | bytes 7077896 | tf_op jit(solution)/shard_map/ppermute | solution.py:21
  367.8 208.6 %all-gather.15.cloned.1.call-start = ((), (), s32[]{:S(2)}) async-start(), calls=%async_computation.6 | async-start | bytes 3932160 | tf_op jit(solution)/shard_map/all_gather | solution.py:311
  367.8 106.3 %collective-permute-start.3 = (bf16[2,768,768]{2,1,0:T(8,128)(2,1)}, bf16[2,768,768]{2,1,0:T(8,128)(2,1)}, u32[]{:S(2)}, u32[]{:S(2)}) collective-permute-start(bf16[2,768,768]{2,1,0:T(8,128)(2,1)} %collective-permute-done.2.refs_4_.refs_7_), channel_id=1, source_target_pairs={{4,0},{5,1},{6,2},{7,3},{20,16},{21,17},{22,18},{23,19}} | collective-permute-start | bytes 7077896 | tf_op jit(solution)/shard_map/ppermute | solution.py:21
  369.1 105.0 %collective-permute-start.5 = (bf16[2,768,768]{2,1,0:T(8,128)(2,1)}, bf16[2,768,768]{2,1,0:T(8,128)(2,1)}, u32[]{:S(2)}, u32[]{:S(2)}) collective-permute-start(bf16[2,768,768]{2,1,0:T(8,128)(2,1)} %collective-permute-done.4.refs_5_.refs_8_), channel_id=1, source_target_pairs={{8,12},{9,13},{10,14},{11,15},{24,28},{25,29},{26,30},{27,31}} | collective-permute-start | bytes 7077896 | tf_op jit(solution)/shard_map/ppermute | solution.py:21
  474.2 155.0 %all-gather.11.cloned.1.call-start = ((), (), s32[]{:S(2)}) async-start(), calls=%async_computation.4 | async-start | bytes 3932160 | tf_op jit(solution)/shard_map/all_gather | solution.py:311
  474.4 54.6 %collective-permute-start.7 = (bf16[2,768,768]{2,1,0:T(8,128)(2,1)}, bf16[2,768,768]{2,1,0:T(8,128)(2,1)}, u32[]{:S(2)}, u32[]{:S(2)}) collective-permute-start(bf16[2,768,768]{2,1,0:T(8,128)(2,1)} %copy-done.7), channel_id=1, source_target_pairs={{0,2},{1,3},{2,0},{3,1},{4,6},{5,7},{6,4},{7,5},{8,10},{9,11},{10,... | collective-permute-start | bytes 7077896 | tf_op jit(solution)/shard_map/ppermute | solution.py:92
  500.3 76.0 %collective-permute-start.10 = (bf16[2,768,768]{2,1,0:T(8,128)(2,1)}, bf16[2,768,768]{2,1,0:T(8,128)(2,1)}, u32[]{:S(2)}, u32[]{:S(2)}) collective-permute-start(bf16[2,768,768]{2,1,0:T(8,128)(2,1)} %get-tuple-element.38.refs_0_), channel_id=1, source_target_pairs={{0,2},{1,3},{2,0},{3,1},{4,6},{5,7},{6,4},{7,5},{8,10},{9,11},{10,... | collective-permute-start | bytes 7077896 | tf_op jit(solution)/shard_map/ppermute | solution.py:92
  500.9 75.4 %collective-permute-start.6 = (bf16[2,768,768]{2,1,0:T(8,128)(2,1)S(1)}, bf16[2,768,768]{2,1,0:T(8,128)(2,1)}, u32[]{:S(2)}, u32[]{:S(2)}) collective-permute-start(bf16[2,768,768]{2,1,0:T(8,128)(2,1)S(1)} %copy-done.8), channel_id=1, source_target_pairs={{0,1},{1,0},{2,3},{3,2},{4,5},{5,4},{6,7},{7,6},{8,9},{9,8},{10,11... | collective-permute-start | bytes 7077896 | tf_op jit(solution)/shard_map/ppermute | solution.py:92
  529.0 47.3 %collective-permute-start.8 = (bf16[2,768,768]{2,1,0:T(8,128)(2,1)}, bf16[2,768,768]{2,1,0:T(8,128)(2,1)}, u32[]{:S(2)}, u32[]{:S(2)}) collective-permute-start(bf16[2,768,768]{2,1,0:T(8,128)(2,1)} %collective-permute-done.7.refs_2_), channel_id=1, source_target_pairs={{0,1},{1,0},{2,3},{3,2},{4,5},{5,4},{6,7},{7,6},{8,9},{9,8},{10,11... | collective-permute-start | bytes 7077896 | tf_op jit(solution)/shard_map/ppermute | solution.py:92
  529.0 64.5 %collective-permute-start.9 = (bf16[2,768,768]{2,1,0:T(8,128)(2,1)}, bf16[2,768,768]{2,1,0:T(8,128)(2,1)}, u32[]{:S(2)}, u32[]{:S(2)}) collective-permute-start(bf16[2,768,768]{2,1,0:T(8,128)(2,1)} %get-tuple-element.38.refs_0_), channel_id=1, source_target_pairs={{0,1},{1,0},{2,3},{3,2},{4,5},{5,4},{6,7},{7,6},{8,9},{9,8},{10,11... | collective-permute-start | bytes 7077896 | tf_op jit(solution)/shard_map/ppermute | solution.py:92
  576.3 17.3 %collective-permute-start.11 = (bf16[2,768,768]{2,1,0:T(8,128)(2,1)}, bf16[2,768,768]{2,1,0:T(8,128)(2,1)}, u32[]{:S(2)}, u32[]{:S(2)}) collective-permute-start(bf16[2,768,768]{2,1,0:T(8,128)(2,1)} %collective-permute-done.10.refs_2_), channel_id=1, source_target_pairs={{0,1},{1,0},{2,3},{3,2},{4,5},{5,4},{6,7},{7,6},{8,9},{9,8},{10,11... | collective-permute-start | bytes 7077896 | tf_op jit(solution)/shard_map/ppermute | solution.py:92
  592.0 37.2 %collective-permute-start.13 = (bf16[2,768,512]{2,1,0:T(8,128)(2,1)}, bf16[2,768,512]{2,1,0:T(8,128)(2,1)}, u32[]{:S(2)}, u32[]{:S(2)}) collective-permute-start(bf16[2,768,512]{2,1,0:T(8,128)(2,1)} %get-tuple-element.48.refs_0_), channel_id=1, source_target_pairs={{0,2},{1,3},{2,0},{3,1},{4,6},{5,7},{6,4},{7,5},{8,10},{9,11},{10,... | collective-permute-start | bytes 4718600 | tf_op jit(solution)/shard_map/ppermute | solution.py:92
  617.3 23.7 %collective-permute-start.12 = (bf16[2,768,512]{2,1,0:T(8,128)(2,1)}, bf16[2,768,512]{2,1,0:T(8,128)(2,1)}, u32[]{:S(2)}, u32[]{:S(2)}) collective-permute-start(bf16[2,768,512]{2,1,0:T(8,128)(2,1)} %get-tuple-element.48.refs_0_), channel_id=1, source_target_pairs={{0,1},{1,0},{2,3},{3,2},{4,5},{5,4},{6,7},{7,6},{8,9},{9,8},{10,11... | collective-permute-start | bytes 4718600 | tf_op jit(solution)/shard_map/ppermute | solution.py:92
  629.1 11.9 %collective-permute-start.14 = (bf16[2,768,512]{2,1,0:T(8,128)(2,1)}, bf16[2,768,512]{2,1,0:T(8,128)(2,1)}, u32[]{:S(2)}, u32[]{:S(2)}) collective-permute-start(bf16[2,768,512]{2,1,0:T(8,128)(2,1)} %collective-permute-done.13.refs_2_), channel_id=1, source_target_pairs={{0,1},{1,0},{2,3},{3,2},{4,5},{5,4},{6,7},{7,6},{8,9},{9,8},{10,11... | collective-permute-start | bytes 4718600 | tf_op jit(solution)/shard_map/ppermute | solution.py:92
  639.4 20.0 %collective-permute-start.16 = (bf16[2,768,256]{2,1,0:T(8,128)(2,1)S(1)}, bf16[2,768,256]{2,1,0:T(8,128)(2,1)S(1)}, u32[]{:S(2)}, u32[]{:S(2)}) collective-permute-start(bf16[2,768,256]{2,1,0:T(8,128)(2,1)S(1)} %get-tuple-element.50.refs_0_), channel_id=1, source_target_pairs={{0,2},{1,3},{2,0},{3,1},{4,6},{5,7},{6,4},{7,5},{8,10},{9,11},{10,... | collective-permute-start | bytes 2359304 | tf_op jit(solution)/shard_map/ppermute | solution.py:92
  658.0 2.4 collective-permute-start.15
  (10 other events, 74.4 us)
Sparse Core Ops, SparseCore 0:
  136.1 127.6 all-gather.8
  367.9 90.9 all-gather.12
  474.3 67.5 all-gather.14
  543.3 62.1 all-gather.10
